TPU v7x, 32 devices: a whole 2x2x4 slice. The times are simulated.
32 devices in a mesh: grp: 4 (over x, core), blk: 8 (over z, y).
Axes of the slice: x: 2, y: 2, z: 4, core: 2. Of those that a mesh axis runs over, the one named last changes fastest.
Arguments:
- obs: bfloat16 [196608, 256], P(('grp', 'blk')), may hold values from -6 to 6
- mask_bits: int32 [196608, 32], P(('grp', 'blk')), may hold values from 0 to 255
- factors: bfloat16 [196608, 256], P(('grp', 'blk')), may hold values from -0.375 to 0.375
- x_blocks: float32 [4, 256, 2048], P('grp', None, 'blk'), may hold values from -6 to 6
- first_moment: float32 [4, 256, 2048], P('grp', None, 'blk'), may hold values from -0.6 to 0.6
- second_moment: float32 [4, 256, 2048], P('grp', None, 'blk'), may hold values from 0.001 to 0.1
- ar_weights: float32 [25, 256], replicated, may hold values from -0.25 to 0.25
- stratum: int32 [1], replicated, may hold values from 0 to 7
Outputs:
- factors_next: bfloat16 [196608, 256], P(('grp', 'blk'))
- x_next: float32 [4, 256, 2048], P('grp', None, 'blk')
- first_next: float32 [4, 256, 2048], P('grp', None, 'blk')
- second_next: float32 [4, 256, 2048], P('grp', None, 'blk')
All inputs are finite; a program needn't handle non-finite values.
Results may differ from a plain program's by a relative error of at most 0.0013.
Values sent between devices are 32-bit elements; how exact they have to be, the bound alone decides.
No kernel may reach another device: no remote copies, remote signals or barrier semaphores. Data moves between devices by JAX's collectives and lax.ppermute only.
A program may use at most 64 MiB of HBM per device.

v0:
```python
import jax
import jax.numpy as jnp
from jax import lax
from jax.sharding import PartitionSpec as P

SHORT = 24
SEASON = 168


beta_one = 0.9
beta_two = 0.999
adam_eps = 1e-08
step_rate = 0.05
factor_rate = 0.002
data_scale = 0.25


def shifted(value, axis, steps):
    count = lax.axis_size(axis)
    pairs = [(source, (source + steps) % count) for source in range(count)]
    return lax.ppermute(value, axis, pairs)


def unpack_mask(bits):
    shifts = jnp.arange(8, dtype=jnp.int32)
    flags = jnp.bitwise_and(jnp.right_shift(bits[:, :, None], shifts[None, None, :]), 1)
    return flags.reshape(bits.shape[0], bits.shape[1] * 8).astype(jnp.float32)


def local_update(obs_tile, bits, factor_tile, block, first, second, halo, ar_weights):
    width = block.shape[1]
    mask = unpack_mask(bits)
    block_half = block.astype(jnp.bfloat16)
    predicted = jnp.dot(factor_tile, block_half, preferred_element_type=jnp.float32)
    error = (mask * (predicted - obs_tile.astype(jnp.float32))).astype(jnp.bfloat16)
    grad_factor = lax.dot_general(
        error, block_half, (((1,), (1,)), ((), ())), preferred_element_type=jnp.float32
    )
    grad_data = lax.dot_general(
        factor_tile, error, (((0,), (0,)), ((), ())), preferred_element_type=jnp.float32
    )
    extended = jnp.concatenate([halo, block], axis=1)
    lag_list = list(range(1, SHORT + 1)) + [SEASON]
    fitted = jnp.zeros_like(block)
    for index, lag in enumerate(lag_list):
        fitted = (
            fitted + ar_weights[index][:, None] * extended[:, SEASON - lag : SEASON - lag + width]
        )
    resid = block - fitted
    backward = jnp.zeros_like(block)
    for index, lag in enumerate(lag_list):
        later = jnp.pad(resid[:, lag:], ((0, 0), (0, lag)))
        backward = backward + ar_weights[index][:, None] * later
    gradient = data_scale * grad_data + resid - backward
    first_new = beta_one * first + (1.0 - beta_one) * gradient
    second_new = beta_two * second + (1.0 - beta_two) * gradient * gradient
    block_new = block - step_rate * first_new / (jnp.sqrt(second_new) + adam_eps)
    factor_new = (factor_tile.astype(jnp.float32) - factor_rate * grad_factor).astype(jnp.bfloat16)
    return (factor_new, block_new, first_new, second_new)


def body(obs, mask_bits, factors, x_blocks, first_moment, second_moment, ar_weights, stratum):
    cycle_count = lax.axis_size("blk")
    group_count = lax.axis_size("grp")
    position = lax.axis_index("blk")
    block_index = (position + stratum[0]) % cycle_count
    own_block = x_blocks[0]
    own_first = first_moment[0]
    own_second = second_moment[0]
    tail = own_block[:, own_block.shape[1] - SEASON :]
    halo = shifted(tail, "blk", 1)
    halo = jnp.where(block_index == 0, jnp.zeros_like(halo), halo)
    factor_new, block_new, first_new, second_new = local_update(
        obs, mask_bits, factors, own_block, own_first, own_second, halo, ar_weights
    )
    stacked = jnp.stack([block_new, first_new, second_new], axis=0)
    shares = lax.psum_scatter(stacked, "grp", scatter_dimension=1, tiled=True)
    means = shares / group_count
    moved = shifted(means, "blk", -1)
    turned = lax.all_gather(moved, "grp", axis=1, tiled=True)
    return (factor_new, turned[0][None], turned[1][None], turned[2][None])


def solution(mesh):
    placed = (
        P(("grp", "blk"), None),
        P(("grp", "blk"), None),
        P(("grp", "blk"), None),
        P("grp", None, "blk"),
        P("grp", None, "blk"),
        P("grp", None, "blk"),
        P(),
        P(),
    )
    return jax.shard_map(
        body,
        mesh=mesh,
        in_specs=placed,
        out_specs=(
            P(("grp", "blk"), None),
            P("grp", None, "blk"),
            P("grp", None, "blk"),
            P("grp", None, "blk"),
        ),
        check_vma=False,
    )
```

profile of v0, /device:TPU:0, one launch (start us, length us, event | category | flops | bytes accessed | tf_op | source)
XLA Modules:
  0.0 98.0 jit_solution(16520933926707197561)
XLA Ops:
  7.2 0.0 copy-start
  7.2 0.0 all-reduce.28.cloned.1.call-start
  7.2 1.1 %copy.27 = f32[1,256,256]{1,2,0:T(8,128)S(1)} copy(f32[1,256,256]{2,1,0:T(8,128)} %param.11) | data formatting | bytes 524288 | tf_op args[3]
  8.4 3.0 %collective-permute-start = (f32[256,168]{0,1:T(8,128)S(1)}, f32[256,168]{0,1:T(8,128)S(1)}, u32[]{:S(2)}, u32[]{:S(2)}) collective-permute-start(f32[256,168]{0,1:T(8,128)S(1)} %slice.341), channel_id=1, source_target_pairs={{0,1},{1,2},{2,3},{3,4},{4,5},{5,6},{6,7},{7,0},{8,9},{9,10},{10,1... | collective-permute-start | bytes 516104 | tf_op jit(solution)/shard_map/ppermute | solution.py:21
  12.1 0.0 copy-done
  12.1 3.4 %broadcast_bitcast_fusion = s32[6144,256]{0,1:T(8,128)} fusion(s32[6144,32]{0,1:T(8,128)S(1)} %copy-done), kind=kLoop, calls=%fused_computation.6 | loop fusion | bytes 7077888 | tf_op jit(solution)/shard_map/shift_right_arithmetic | solution.py:26
  15.5 0.0 copy-start.3
  15.5 0.0 copy-start.4
  15.5 0.0 copy-start.5
  15.5 6.6 %copy.26 = s32[6144,256]{1,0:T(8,128)} copy(s32[6144,256]{0,1:T(8,128)} %broadcast_bitcast_fusion) | data formatting | bytes 12582912 | tf_op jit(solution)/shard_map/shift_right_arithmetic | solution.py:26
  22.1 0.1 shift_right_arithmetic.23
  22.2 0.0 copy-done.3
  22.2 0.1 copy.28
  22.4 0.0 copy-done.4
  22.4 0.1 copy.29
  22.5 0.0 copy-done.5
  22.6 6.2 %fusion.2 = bf16[6144,256]{1,0:T(8,128)(2,1)S(1)} fusion(bf16[6144,256]{1,0:T(8,128)(2,1)} %param.10, bf16[6144,256]{1,0:T(8,128)(2,1)} %param.8, s32[6144,256]{1,0:T(8,128)} %copy.26, s32[256]{0:T(256)S(1)} %shift_right_arithmetic.23, f32[1,256,256]{1,2,0:T(8,128)S(1)} %copy.27), kind=kOutput, calls=%fused_computation.4 | convolution fusion | flops 816316416 | bytes 15991808 | tf_op jit(solution)/shard_map/dot_general | solution.py:34
  28.7 0.0 copy-start.2
  28.8 0.0 collective-permute-done
  28.8 0.6 fusion.12
  29.7 0.0 copy-start.1
  30.1 0.3 copy-done.2
  30.4 1.3 %copy-done.1 = bf16[6144,256]{1,0:T(8,128)(2,1)S(1)} copy-done((bf16[6144,256]{1,0:T(8,128)(2,1)S(1)}, bf16[6144,256]{1,0:T(8,128)(2,1)}, u32[]{:S(2)}) %copy-start.1) | copy-done | bytes 3145752
  31.7 1.8 %subtract_bitcast_fusion = (f32[1,256,256]{1,2,0:T(8,128)S(1)}, f32[1,256,256]{1,2,0:T(8,128)S(1)}, f32[1,256,256]{1,2,0:T(8,128)S(1)}) fusion(f32[1,256,256]{1,2,0:T(8,128)S(1)} %copy.28, f32[1,256,256]{1,2,0:T(8,128)S(1)} %copy.29, f32[1,256,256]{1,2,0:T(8,128)S(1)} %copy.27, f32[256,88]{0,1:T(8,128)S(1)} %slice.414, f32[256]{0:T(256)S(1)} %bitcast.137, ...), kind=kOutput, calls=%fused_computation.139 | convolution fusion | flops 809435136 | bytes 14226432 | tf_op jit(solution)/shard_map/dot_general | solution.py:39
  33.5 0.0 copy-start.6
  33.5 0.1 pad_maximum_fusion
  33.6 1.3 %copy.30 = f32[3,256,256]{2,0,1:T(4,128)} copy(f32[3,256,256]{1,2,0:T(8,128)S(1)} %pad_maximum_fusion) | data formatting | bytes 1572864 | tf_op jit(solution)/shard_map/stack | solution.py:76
  34.9 0.0 all-reduce.28.cloned.1.call-update
  34.9 0.0 copy-done.6
  34.9 0.6 dynamic-slice
  36.1 35.3 %all-reduce.28.cloned.1.call-done = f32[3,256,256]{2,0,1:T(4,128)} async-done(((f32[3,256,256]{2,0,1:T(4,128)}), f32[3,256,256]{2,0,1:T(4,128)}) %all-reduce.28.cloned.1.call-update) | async-done | bytes 786448
  71.4 1.0 %dynamic-slice_multiply_fusion = f32[3,64,256]{2,0,1:T(4,128)S(1)} fusion(f32[3,256,256]{2,0,1:T(4,128)} %all-reduce.28.cloned.1.call-done, u32[]{:T(128)S(6)} %multiply.2), kind=kLoop, calls=%fused_computation.137 | loop fusion | flops 49152 | bytes 393220 | tf_op jit(solution)/shard_map/div | solution.py:78
  72.4 4.3 %collective-permute-start.1 = (f32[3,64,256]{2,0,1:T(4,128)S(1)}, f32[3,64,256]{2,0,1:T(4,128)S(1)}, u32[]{:S(2)}, u32[]{:S(2)}) collective-permute-start(f32[3,64,256]{2,0,1:T(4,128)S(1)} %dynamic-slice_multiply_fusion), channel_id=1, source_target_pairs={{0,7},{1,0},{2,1},{3,2},{4,3},{5,4},{6,5},{7,6},{8,15},{9,8},{10,9... | collective-permute-start | bytes 589832 | tf_op jit(solution)/shard_map/ppermute | solution.py:21
  76.7 5.5 %fusion.3 = bf16[6144,256]{1,0:T(8,128)(2,1)} fusion(bf16[6144,256]{1,0:T(8,128)(2,1)} %copy-done.2, bf16[6144,256]{1,0:T(8,128)(2,1)} %param.10, f32[1,256,256]{1,2,0:T(8,128)S(1)} %copy.27), kind=kOutput, calls=%fused_computation.5 | convolution fusion | flops 811597824 | bytes 9699328 | tf_op jit(solution)/shard_map/dot_general | solution.py:36
  82.2 0.0 collective-permute-done.1
  82.2 8.1 %all_gather.3 = f32[3,256,256]{2,1,0:T(8,128)S(1)} all-gather(f32[3,64,256]{2,1,0:T(8,128)S(1)} %copy.31), channel_id=1, replica_groups=mesh['grp'=4,'blk'=8] {'grp'}, dimensions={1}, use_global_device_ids=true | all-gather | bytes 983040 | tf_op jit(solution)/shard_map/all_gather | solution.py:80
  90.3 0.9 fusion.90
  (31 shorter events, 0.6 us)
Async XLA Ops:
  7.2 4.9 %copy-start = (s32[6144,32]{0,1:T(8,128)S(1)}, s32[6144,32]{0,1:T(8,128)}, u32[]{:S(2)}) copy-start(s32[6144,32]{0,1:T(8,128)} %param.9) | copy-start | bytes 2359300
  7.2 64.2 %all-reduce.28.cloned.1.call-start = ((), (), s32[]{:S(2)}) async-start(), calls=%async_computation | async-start | bytes 2097152
  8.4 20.4 %collective-permute-start = (f32[256,168]{0,1:T(8,128)S(1)}, f32[256,168]{0,1:T(8,128)S(1)}, u32[]{:S(2)}, u32[]{:S(2)}) collective-permute-start(f32[256,168]{0,1:T(8,128)S(1)} %slice.341), channel_id=1, source_target_pairs={{0,1},{1,2},{2,3},{3,4},{4,5},{5,6},{6,7},{7,0},{8,9},{9,10},{10,1... | collective-permute-start | bytes 516104 | tf_op jit(solution)/shard_map/ppermute | solution.py:21
  15.5 6.7 %copy-start.3 = (f32[1,256,256]{2,1,0:T(8,128)S(1)}, f32[1,256,256]{2,1,0:T(8,128)}, u32[]{:S(2)}) copy-start(f32[1,256,256]{2,1,0:T(8,128)} %param.12) | copy-start | bytes 786436
  15.5 6.9 %copy-start.4 = (f32[1,256,256]{2,1,0:T(8,128)S(1)}, f32[1,256,256]{2,1,0:T(8,128)}, u32[]{:S(2)}) copy-start(f32[1,256,256]{2,1,0:T(8,128)} %param.13) | copy-start | bytes 786436
  15.5 7.0 %copy-start.5 = (f32[25,256]{1,0:T(8,128)S(1)}, f32[25,256]{1,0:T(8,128)}, u32[]{:S(2)}) copy-start(f32[25,256]{1,0:T(8,128)} %param.14) | copy-start | bytes 76804
  28.7 1.6 %copy-start.2 = (bf16[6144,256]{1,0:T(8,128)(2,1)}, bf16[6144,256]{1,0:T(8,128)(2,1)S(1)}, u32[]{:S(2)}) copy-start(bf16[6144,256]{1,0:T(8,128)(2,1)S(1)} %fusion.2) | copy-start | bytes 9437188
  29.7 2.0 %copy-start.1 = (bf16[6144,256]{1,0:T(8,128)(2,1)S(1)}, bf16[6144,256]{1,0:T(8,128)(2,1)}, u32[]{:S(2)}) copy-start(bf16[6144,256]{1,0:T(8,128)(2,1)} %param.10) | copy-start | bytes 9437188
  33.5 1.4 %copy-start.6 = (u32[32]{0:T(128)S(1)}, u32[32]{0:T(128)}, u32[]{:S(2)}) copy-start(u32[32]{0:T(128)} %constant.96) | copy-start | bytes 388
  72.4 9.8 %collective-permute-start.1 = (f32[3,64,256]{2,0,1:T(4,128)S(1)}, f32[3,64,256]{2,0,1:T(4,128)S(1)}, u32[]{:S(2)}, u32[]{:S(2)}) collective-permute-start(f32[3,64,256]{2,0,1:T(4,128)S(1)} %dynamic-slice_multiply_fusion), channel_id=1, source_target_pairs={{0,7},{1,0},{2,1},{3,2},{4,3},{5,4},{6,5},{7,6},{8,15},{9,8},{10,9... | collective-permute-start | bytes 589832 | tf_op jit(solution)/shard_map/ppermute | solution.py:21
Sparse Core Ops, SparseCore 0:
  35.0 36.3 all-reduce.27
where the time goes:
time: 98.3 us; the launch traced here: 98 us
  waiting for transfers between devices  35.3 us (36%)
  local copies, waits for them, and re-layouts  16.5 us (17%)
  between operations  15.7 us (16%)
  matrix products  13.4 us (14%)
  blocking collectives  8.05 us (8%)
  starting transfers between devices  7.35 us (7%)
  other arithmetic  1.66 us (2%)
    unnamed x2, waiting for transfers between devices  35.3 us
    shift_right_arithmetic x4, local copies, waits for them, and re-layouts, unpack_mask(): jnp.right_shift(bits[:, :, None], shifts[None, None, :])  10.1 us
    all_gather x1, blocking collectives, body(): turned = lax.all_gather(moved, 'grp', axis=1, tiled=True)  8.05 us
    ppermute x2, starting transfers between devices, shifted(): return lax.ppermute(value, axis, pairs)  7.31 us
    dot_general x1, matrix products, local_update(): jnp.dot(factor_tile, block_half, preferred_element_type=jnp.float32)  6.15 us
    dot_general x1, matrix products, local_update(): lax.dot_general(error, block_half, (((1,), (1,)), ((), ())), preferred_el...  5.48 us
    unnamed x18, local copies, waits for them, and re-layouts  3.62 us
  transfers between devices with their start and end apart: 3, of which 1 were waited for; matrix products, arithmetic and copies ran while one was open for 23% of the time, Pallas kernels for 0%

commit v1 on v0

v1 whole, which is shorter than its diff:
```python
import functools

import jax
import jax.numpy as jnp
from jax import lax
from jax.experimental import pallas as pl
from jax.experimental.pallas import tpu as pltpu
from jax.sharding import PartitionSpec as P

SEASON = 168

beta_one = 0.9
beta_two = 0.999
adam_eps = 1e-08
step_rate = 0.05
factor_rate = 0.002
data_scale = 0.25

LIMIT = 32 * 1024 * 1024
F32 = jnp.float32
BF16 = jnp.bfloat16


def whole():
    return pl.BlockSpec(memory_space=pltpu.VMEM)


def scalars():
    return pl.BlockSpec(memory_space=pltpu.SMEM)


def params(**more):
    return pltpu.CompilerParams(vmem_limit_bytes=LIMIT, **more)


def cost(flops, moved):
    return pl.CostEstimate(flops=int(flops), bytes_accessed=int(moved), transcendentals=0)


def rows_of(total, most):
    best = total
    for rows in range(128, most + 1, 128):
        if total % rows == 0:
            best = rows
    return best


def prepare_kernel(share, count, here, x_ref, m_ref, v_ref, tail_ref, *early):
    group = here[0]
    tail_ref[...] = x_ref[0, :, :].T[x_ref.shape[2] - SEASON :, :]
    for step in range(1, count):
        start = pl.multiple_of((group ^ step) * share, share)
        early[step - 1][0] = x_ref[0, pl.ds(start, share), :]
        early[step - 1][1] = m_ref[0, pl.ds(start, share), :]
        early[step - 1][2] = v_ref[0, pl.ds(start, share), :]


def prepare(here, x, m, v, count):
    rank, width = x.shape[1:]
    share = rank // count
    outs = [jax.ShapeDtypeStruct((SEASON, rank), F32)]
    outs += [jax.ShapeDtypeStruct((3, share, width), F32)] * (count - 1)
    return pl.pallas_call(
        functools.partial(prepare_kernel, share, count),
        out_shape=tuple(outs),
        in_specs=[scalars()] + [whole()] * 3,
        out_specs=tuple([whole()] * count),
        compiler_params=params(),
        cost_estimate=cost(0, 6 * rank * width * 4),
        name="prepare",
    )(here, x, m, v)


def error_kernel(obs_ref, bits_ref, f_ref, x_ref, err_ref, gd_ref, half_ref):
    step = pl.program_id(0)
    words, rows = bits_ref.shape
    width = obs_ref.shape[1]
    per = width // words

    @pl.when(step == 0)
    def _():
        half_ref[...] = x_ref[0].astype(BF16)

    lane = lax.broadcasted_iota(jnp.int32, (words, width), 1)
    word = lax.broadcasted_iota(jnp.int32, (words, width), 0)
    spread = (lane // per == word).astype(BF16)
    value = lax.dot_general(
        bits_ref[...].astype(F32).astype(BF16),
        spread,
        (((0,), (0,)), ((), ())),
        preferred_element_type=F32,
    ).astype(jnp.int32)
    flag = jnp.left_shift(1, lax.broadcasted_iota(jnp.int32, (1, width), 1) % per)
    predicted = jnp.dot(f_ref[...], half_ref[...], preferred_element_type=F32)
    error = jnp.where(
        jnp.bitwise_and(value, flag) != 0, predicted - obs_ref[...].astype(F32), 0.0
    ).astype(BF16)
    err_ref[...] = error
    part = lax.dot_general(
        f_ref[...], error, (((0,), (0,)), ((), ())), preferred_element_type=F32
    )

    @pl.when(step == 0)
    def _():
        gd_ref[...] = part

    @pl.when(step != 0)
    def _():
        gd_ref[...] += part


def error_step(obs, bits, factors, x):
    series, width = obs.shape
    rank = factors.shape[1]
    words = bits.shape[0]
    rows = rows_of(series, 1024)
    return pl.pallas_call(
        error_kernel,
        out_shape=(
            jax.ShapeDtypeStruct((series, width), BF16),
            jax.ShapeDtypeStruct((rank, width), F32),
        ),
        grid=(series // rows,),
        in_specs=[
            pl.BlockSpec((rows, width), lambda i: (i, 0)),
            pl.BlockSpec((words, rows), lambda i: (0, i)),
            pl.BlockSpec((rows, rank), lambda i: (i, 0)),
            pl.BlockSpec((1, rank, width), lambda i: (0, 0, 0)),
        ],
        out_specs=(
            pl.BlockSpec((rows, width), lambda i: (i, 0)),
            pl.BlockSpec((rank, width), lambda i: (0, 0)),
        ),
        scratch_shapes=[pltpu.VMEM((rank, width), BF16)],
        compiler_params=params(),
        cost_estimate=cost(6 * series * width * rank, series * (3 * width * 2 + words * 4)),
        name="errors",
    )(obs, bits, factors, x)


def factor_kernel(f_ref, err_ref, x_ref, out_ref, half_ref):
    @pl.when(pl.program_id(0) == 0)
    def _():
        half_ref[...] = x_ref[0].astype(BF16)

    gradient = lax.dot_general(
        err_ref[...], half_ref[...], (((1,), (1,)), ((), ())), preferred_element_type=F32
    )
    out_ref[...] = (f_ref[...].astype(F32) - factor_rate * gradient).astype(BF16)


def factor_step(factors, err, x):
    series, rank = factors.shape
    width = err.shape[1]
    rows = rows_of(series, 1024)
    return pl.pallas_call(
        factor_kernel,
        out_shape=jax.ShapeDtypeStruct((series, rank), BF16),
        grid=(series // rows,),
        in_specs=[
            pl.BlockSpec((rows, rank), lambda i: (i, 0)),
            pl.BlockSpec((rows, width), lambda i: (i, 0)),
            pl.BlockSpec((1, rank, width), lambda i: (0, 0, 0)),
        ],
        out_specs=pl.BlockSpec((rows, rank), lambda i: (i, 0)),
        scratch_shapes=[pltpu.VMEM((rank, width), BF16)],
        compiler_params=params(),
        cost_estimate=cost(2 * series * width * rank, series * 3 * width * 2),
        name="factors",
    )(factors, err, x)


def gradient_kernel(share, count, lanes, here, halo_ref, x_ref, w_ref, gd_ref, *rest):
    outs, (z_ref, r_ref) = rest[:count], rest[count:]
    group, first_block = here[0], here[1]
    rank, width = x_ref.shape[1:]
    lags = list(range(1, w_ref.shape[0])) + [SEASON]
    turned = x_ref[0].T
    for part in range(rank // lanes):
        columns = slice(part * lanes, (part + 1) * lanes)
        halo = halo_ref[:, columns]
        z_ref[part, :SEASON, :] = jnp.where(first_block == 0, 0.0, halo)
        z_ref[part, SEASON:, :] = turned[:, columns]
        resid = z_ref[part, SEASON:, :]
        for index, lag in enumerate(lags):
            begin = SEASON - lag
            resid = resid - w_ref[index : index + 1, columns] * z_ref[part, begin : begin + width, :]
        r_ref[part, :width, :] = resid
        r_ref[part, width:, :] = jnp.zeros((SEASON, lanes), F32)
        back = resid
        for index, lag in enumerate(lags):
            back = back - w_ref[index : index + 1, columns] * r_ref[part, lag : lag + width, :]
        z_ref[part, :width, :] = back
    for part in range(rank // lanes):
        rows = slice(part * lanes, (part + 1) * lanes)
        gd_ref[rows, :] = data_scale * gd_ref[rows, :] + z_ref[part, :width, :].T
    for step in range(count):
        start = pl.multiple_of((group ^ step) * share, share)
        outs[step][...] = gd_ref[pl.ds(start, share), :]


def gradient_step(here, halo, x, weights, gd, count):
    rank, width = gd.shape
    share = rank // count
    lanes = 128 if rank % 128 == 0 else rank

    def kernel(here, halo_ref, x_ref, w_ref, gd_ref, *rest):
        work = rest[-1]
        work[...] = gd_ref[...]
        gradient_kernel(share, count, lanes, here, halo_ref, x_ref, w_ref, work, *rest[:-1])

    return pl.pallas_call(
        kernel,
        out_shape=tuple([jax.ShapeDtypeStruct((share, width), F32)] * count),
        in_specs=[scalars()] + [whole()] * 4,
        out_specs=tuple([whole()] * count),
        scratch_shapes=[
            pltpu.VMEM((rank // lanes, SEASON + width, lanes), F32),
            pltpu.VMEM((rank // lanes, SEASON + width, lanes), F32),
            pltpu.VMEM((rank, width), F32),
        ],
        compiler_params=params(),
        cost_estimate=cost(100 * rank * width, 4 * rank * width * 4),
        name="gradient",
    )(here, halo, x, weights, gd)


def adam_kernel(share, count, here, x_ref, m_ref, v_ref, *rest):
    grads, early, out_ref = rest[:count], rest[count:-1], rest[-1]
    start = pl.multiple_of(here[0] * share, share)
    total = [0.0, 0.0, 0.0]
    for step in range(count):
        if step == 0:
            own = [ref[0, pl.ds(start, share), :] for ref in (x_ref, m_ref, v_ref)]
        else:
            own = [early[step - 1][which] for which in range(3)]
        block, first, second = own
        gradient = grads[step][...]
        first = beta_one * first + (1.0 - beta_one) * gradient
        second = beta_two * second + (1.0 - beta_two) * gradient * gradient
        block = block - step_rate * first / (jnp.sqrt(second) + adam_eps)
        total = [total[0] + block, total[1] + first, total[2] + second]
    for which in range(3):
        out_ref[which] = total[which] / count


def adam_step(here, x, m, v, grads, early):
    count = len(grads)
    share, width = grads[0].shape
    return pl.pallas_call(
        functools.partial(adam_kernel, share, count),
        out_shape=jax.ShapeDtypeStruct((3, share, width), F32),
        in_specs=[scalars()] + [whole()] * (3 + count + count - 1),
        out_specs=whole(),
        compiler_params=params(),
        cost_estimate=cost(80 * share * width, 20 * share * width * 4),
        name="adam",
    )(here, x, m, v, *grads, *early)


def place_kernel(share, here, *rest):
    parts, outs = rest[:-3], rest[-3:]
    for step, part in enumerate(parts):
        start = pl.multiple_of((here[0] ^ step) * share, share)
        for which in range(3):
            outs[which][0, pl.ds(start, share), :] = part[which]


def place(here, parts):
    count = len(parts)
    _, share, width = parts[0].shape
    out = jax.ShapeDtypeStruct((1, count * share, width), F32)
    return pl.pallas_call(
        functools.partial(place_kernel, share),
        out_shape=(out, out, out),
        in_specs=[scalars()] + [whole()] * count,
        out_specs=(whole(), whole(), whole()),
        compiler_params=params(),
        cost_estimate=cost(0, 6 * count * share * width * 4),
        name="place",
    )(here, *parts)


def crossed(value, step):
    count = lax.axis_size("grp")
    return lax.ppermute(value, "grp", [(source, source ^ step) for source in range(count)])


def shifted(value, steps):
    count = lax.axis_size("blk")
    return lax.ppermute(value, "blk", [(source, (source + steps) % count) for source in range(count)])


def body(obs, mask_bits, factors, x_blocks, first_moment, second_moment, ar_weights, stratum):
    cycle = lax.axis_size("blk")
    count = lax.axis_size("grp")
    group = lax.axis_index("grp")
    block_index = (lax.axis_index("blk") + stratum[0]) % cycle
    here = jnp.stack([group, block_index]).astype(jnp.int32)

    tail, *early = prepare(here, x_blocks, first_moment, second_moment, count)
    halo = shifted(tail, 1)
    early = [crossed(value, step + 1) for step, value in enumerate(early)]
    err, gd = error_step(obs, mask_bits.T, factors, x_blocks)
    grads = gradient_step(here, halo, x_blocks, ar_weights, gd, count)
    grads = [grads[0]] + [crossed(grads[step], step) for step in range(1, count)]
    means = adam_step(here, x_blocks, first_moment, second_moment, grads, early)
    moved = shifted(means, -1)
    factor_new = factor_step(factors, err, x_blocks)
    parts = [moved]
    span = 1
    while span < count:
        span *= 2
    level = span // 2
    known = {0: moved}
    while level >= 1:
        for key in list(known):
            known[key ^ level] = crossed(known[key], level)
        level //= 2
    parts = [known[key] for key in range(count)]
    outs = place(here, parts)
    return (factor_new, *outs)


def solution(mesh):
    rows = P(("grp", "blk"), None)
    blocks = P("grp", None, "blk")
    return jax.shard_map(
        body,
        mesh=mesh,
        in_specs=(rows, rows, rows, blocks, blocks, blocks, P(), P()),
        out_specs=(rows, blocks, blocks, blocks),
        check_vma=False,
    )
```

time: 98.3 us -> 49 us (0.50)
  waiting for transfers between devices: 35.3 us -> 13.6 us
  between operations: 15.7 us -> 1.36 us
  Pallas kernels: 0 us -> 13.7 us
  matrix products: 13.4 us -> 0 us
  blocking collectives: 8.05 us -> 0 us
  local copies, waits for them, and re-layouts: 16.5 us -> 8.72 us
  starting transfers between devices: 7.35 us -> 11.1 us
  other arithmetic: 1.66 us -> 0.08 us
    unnamed x2 -> x0, waiting for transfers between devices: 35.3 us -> none
    pallas_call x0 -> x6, Pallas kernels: none -> 13.7 us  [the longest x1 5.17 us: error_step(): pl.pallas_call(error_kernel, out_shape=(jax.ShapeDtypeStruct((series, wid...]
    ppermute x2 -> x11, waiting for transfers between devices: 0.01 us -> 13.6 us  [the longest x9 9.21 us: crossed(): lax.ppermute(value, 'grp', [(source, source ^ step) for source in range(c...]
    dot_general x3 -> x0, matrix products: 13.4 us -> none  [the longest x1 6.15 us: local_update(): jnp.dot(factor_tile, block_half, preferred_element_type=jnp.float32)]
    shift_right_arithmetic x4 -> x0, local copies, waits for them, and re-layouts: 10.1 us -> none  [unpack_mask(): jnp.right_shift(bits[:, :, None], shifts[None, None, :])]
    all_gather x1 -> x0, blocking collectives: 8.05 us -> none  [body(): turned = lax.all_gather(moved, 'grp', axis=1, tiled=True)]
    unnamed x18 -> x22, local copies, waits for them, and re-layouts: 3.62 us -> 8.72 us
    ppermute x2 -> x11, starting transfers between devices: 7.31 us -> 11.1 us  [the longest x2 6.28 us: shifted(): lax.ppermute(value, 'blk', [(source, (source + steps) % count) for source...]
  transfers between devices with their start and end apart: 3 -> 11, of which waited for: 1 -> 4; matrix products, arithmetic and copies ran while one was open for 23% -> 0% of each run, Pallas kernels for 0% -> 22%
where the time goes in v1:
time: 49 us; the launch traced here: 48.6 us
  Pallas kernels  13.7 us (28%)
  waiting for transfers between devices  13.6 us (28%)
  starting transfers between devices  11.1 us (23%)
  local copies, waits for them, and re-layouts  8.72 us (18%)
  between operations  1.36 us (3%)
    ppermute x9, waiting for transfers between devices, crossed(): lax.ppermute(value, 'grp', [(source, source ^ step) for source in range(c...  9.21 us
    unnamed x22, local copies, waits for them, and re-layouts  8.72 us
    ppermute x2, starting transfers between devices, shifted(): lax.ppermute(value, 'blk', [(source, (source + steps) % count) for source...  6.28 us
    pallas_call x1, Pallas kernels, error_step(): pl.pallas_call(error_kernel, out_shape=(jax.ShapeDtypeStruct((series, wid...  5.17 us
    ppermute x9, starting transfers between devices, crossed(): lax.ppermute(value, 'grp', [(source, source ^ step) for source in range(c...  4.85 us
    ppermute x2, waiting for transfers between devices, shifted(): lax.ppermute(value, 'blk', [(source, (source + steps) % count) for source...  4.44 us
    pallas_call x1, Pallas kernels, factor_step(): pl.pallas_call(factor_kernel, out_shape=jax.ShapeDtypeStruct((series, ran...  3.75 us
    pallas_call x1, Pallas kernels, gradient_step(): pl.pallas_call(kernel, out_shape=tuple([jax.ShapeDtypeStruct((share, widt...  1.86 us
  transfers between devices with their start and end apart: 11, of which 4 were waited for; matrix products, arithmetic and copies ran while one was open for 0% of the time, Pallas kernels for 22%

profile of v1, /device:TPU:0, one launch (start us, length us, event | category | flops | bytes accessed | tf_op | source)
XLA Modules:
  0.0 48.6 jit_solution(17731290595478211429)
XLA Ops:
  1.3 0.1 pad_add_fusion.here
  1.4 0.0 copy-start
  1.4 0.9 %copy-done = f32[1,256,256]{2,1,0:T(8,128)S(1)} copy-done((f32[1,256,256]{2,1,0:T(8,128)S(1)}, f32[1,256,256]{2,1,0:T(8,128)}, u32[]{:S(2)}) %copy-start) | copy-done | bytes 262168
  2.3 0.0 copy-start.4
  2.3 0.9 %copy-done.4 = f32[1,256,256]{2,1,0:T(8,128)S(1)} copy-done((f32[1,256,256]{2,1,0:T(8,128)S(1)}, f32[1,256,256]{2,1,0:T(8,128)}, u32[]{:S(2)}) %copy-start.4) | copy-done | bytes 262168
  3.3 0.0 copy-start.6
  3.3 0.9 %copy-done.6 = f32[1,256,256]{2,1,0:T(8,128)S(1)} copy-done((f32[1,256,256]{2,1,0:T(8,128)S(1)}, f32[1,256,256]{2,1,0:T(8,128)}, u32[]{:S(2)}) %copy-start.6) | copy-done | bytes 262168
  4.2 0.7 %prepare.1 = (f32[168,256]{1,0:T(8,128)S(1)}, f32[3,64,256]{2,1,0:T(8,128)S(1)}, f32[3,64,256]{2,1,0:T(8,128)S(1)}, f32[3,64,256]{2,1,0:T(8,128)S(1)}) custom-call(s32[2]{0:T(128)S(1)} %pad_add_fusion.here, f32[1,256,256]{2,1,0:T(8,128)S(1)} %copy-done, f32[1,256,256]{2,1,0:T(8,128)S(1)} %copy-done.4, f32[1,256,256]{2,1,0:T(8,128)S(1)} %copy-done.6), custom_call_target="tpu_custom_call" | custom-call | bytes 1572864 | tf_op jit(solution)/shard_map/prepare/pallas_call | solution.py:63
  4.9 3.0 %collective-permute-start = (f32[168,256]{1,0:T(8,128)S(1)}, f32[168,256]{1,0:T(8,128)S(1)}, u32[]{:S(2)}, u32[]{:S(2)}) collective-permute-start(f32[168,256]{1,0:T(8,128)S(1)} %get-tuple-element.18), channel_id=1, source_target_pairs={{0,1},{1,2},{2,3},{3,4},{4,5},{5,6},{6,7},{7,0},{8,9},{9,10},{10,1... | collective-permute-start | bytes 516104 | tf_op jit(solution)/shard_map/ppermute | solution.py:291
  7.9 0.0 collective-permute-start.4
  7.9 1.5 %collective-permute-start.5 = (f32[3,64,256]{2,1,0:T(8,128)S(1)}, f32[3,64,256]{2,1,0:T(8,128)S(1)}, u32[]{:S(2)}, u32[]{:S(2)}) collective-permute-start(f32[3,64,256]{2,1,0:T(8,128)S(1)} %get-tuple-element.25), channel_id=1, source_target_pairs={{0,16},{8,24},{16,0},{24,8},{1,17},{9,25},{17,1},{25,9},{2,18},{10... | collective-permute-start | bytes 589832 | tf_op jit(solution)/shard_map/ppermute | solution.py:286
  9.4 0.4 collective-permute-start.6
  9.8 0.0 copy-start.1
  9.8 0.9 %copy-done.1 = f32[1,256,256]{2,1,0:T(8,128)S(1)} copy-done((f32[1,256,256]{2,1,0:T(8,128)S(1)}, f32[1,256,256]{2,1,0:T(8,128)}, u32[]{:S(2)}) %copy-start.1) | copy-done | bytes 262168
  10.7 0.0 copy-start.2
  10.7 1.9 %copy-done.2 = bf16[6144,256]{1,0:T(8,128)(2,1)S(1)} copy-done((bf16[6144,256]{1,0:T(8,128)(2,1)S(1)}, bf16[6144,256]{1,0:T(8,128)(2,1)}, u32[]{:S(2)}) %copy-start.2) | copy-done | bytes 3145752
  12.6 0.0 copy-start.9
  12.6 1.9 %copy-done.9 = bf16[6144,256]{1,0:T(8,128)(2,1)S(1)} copy-done((bf16[6144,256]{1,0:T(8,128)(2,1)S(1)}, bf16[6144,256]{1,0:T(8,128)(2,1)}, u32[]{:S(2)}) %copy-start.9) | copy-done | bytes 3145752
  14.5 0.0 copy-start.10
  14.5 1.1 %copy-done.10 = s32[6144,32]{0,1:T(8,128)S(1)} copy-done((s32[6144,32]{0,1:T(8,128)S(1)}, s32[6144,32]{0,1:T(8,128)}, u32[]{:S(2)}) %copy-start.10) | copy-done | bytes 786456
  15.6 0.0 copy-start.8
  15.6 0.0 copy-start.5
  15.6 0.0 copy-start.7
  15.6 0.0 copy-start.3
  15.6 5.2 %errors.1 = (bf16[6144,256]{1,0:T(8,128)(2,1)S(1)}, f32[256,256]{1,0:T(8,128)S(1)}) custom-call(bf16[6144,256]{1,0:T(8,128)(2,1)S(1)} %copy-done.9, s32[32,6144]{1,0:T(8,128)S(1)} %bitcast.5, bf16[6144,256]{1,0:T(8,128)(2,1)S(1)} %copy-done.2, f32[1,256,256]{2,1,0:T(8,128)S(1)} %copy-done.1), custom_call_target="tpu_custom_call" | custom-call | flops 2415919104 | bytes 10223616 | tf_op jit(solution)/shard_map/errors/pallas_call | solution.py:117
  20.8 0.0 collective-permute-done.halo_ref
  20.8 0.0 copy-done.8
  20.8 1.9 %gradient.1 = (f32[64,256]{1,0:T(8,128)S(1)}, f32[64,256]{1,0:T(8,128)S(1)}, f32[64,256]{1,0:T(8,128)S(1)}, f32[64,256]{1,0:T(8,128)S(1)}) custom-call(s32[2]{0:T(128)S(1)} %pad_add_fusion.here, f32[168,256]{1,0:T(8,128)S(1)} %collective-permute-done.halo_ref, f32[1,256,256]{2,1,0:T(8,128)S(1)} %copy-done.1, f32[25,256]{1,0:T(8,128)S(1)} %copy-done.8, ...), custom_call_target="tpu_custom_call" | custom-call | flops 6553600 | bytes 1048576 | tf_op jit(solution)/shard_map/gradient/pallas_call | solution.py:212
  22.7 0.3 collective-permute-start.1
  23.1 1.5 %collective-permute-start.2 = (f32[64,256]{1,0:T(8,128)S(1)}, f32[64,256]{1,0:T(8,128)S(1)}, u32[]{:S(2)}, u32[]{:S(2)}) collective-permute-start(f32[64,256]{1,0:T(8,128)S(1)} %get-tuple-element.22), channel_id=1, source_target_pairs={{0,16},{8,24},{16,0},{24,8},{1,17},{9,25},{17,1},{25,9},{2,18},{10... | collective-permute-start | bytes 196616 | tf_op jit(solution)/shard_map/ppermute | solution.py:286
  24.6 0.0 collective-permute-done.4.rest_4_
  24.6 0.1 collective-permute-start.3
  24.7 0.0 collective-permute-done.5.rest_5_
  24.7 0.0 collective-permute-done.6.rest_6_
  24.7 0.0 collective-permute-done.1.rest_1_
  24.7 2.7 %collective-permute-done.2.rest_2_ = f32[64,256]{1,0:T(8,128)S(1)} collective-permute-done((f32[64,256]{1,0:T(8,128)S(1)}, f32[64,256]{1,0:T(8,128)S(1)}, u32[]{:S(2)}, u32[]{:S(2)}) %collective-permute-start.2) | collective-permute-done | bytes 65568 | tf_op jit(solution)/shard_map/ppermute | solution.py:286
  27.3 1.5 %collective-permute-done.3.rest_3_ = f32[64,256]{1,0:T(8,128)S(1)} collective-permute-done((f32[64,256]{1,0:T(8,128)S(1)}, f32[64,256]{1,0:T(8,128)S(1)}, u32[]{:S(2)}, u32[]{:S(2)}) %collective-permute-start.3) | collective-permute-done | bytes 65568 | tf_op jit(solution)/shard_map/ppermute | solution.py:286
  28.8 0.0 copy-done.5
  28.8 0.0 copy-done.7
  28.8 0.7 %adam.1 = f32[3,64,256]{2,1,0:T(8,128)S(1)} custom-call(s32[2]{0:T(128)S(1)} %pad_add_fusion.here, f32[1,256,256]{2,1,0:T(8,128)S(1)} %copy-done.1, f32[1,256,256]{2,1,0:T(8,128)S(1)} %copy-done.5, f32[1,256,256]{2,1,0:T(8,128)S(1)} %copy-done.7, f32[64,256]{1,0:T(8,128)S(1)} %get-tuple-element.20.rest_0_, f32[64,256]{1,0:T(8,128)S(1)} %collective-permute-done.1.rest_1_, ...), custom_call_target="tpu_custom_call" | custom-call | flops 1310720 | bytes 1310720 | tf_op jit(solution)/shard_map/adam/pallas_call | solution.py:250
  29.6 3.3 %collective-permute-start.7 = (f32[3,64,256]{2,1,0:T(8,128)S(1)}, f32[3,64,256]{2,1,0:T(8,128)S(1)}, u32[]{:S(2)}, u32[]{:S(2)}) collective-permute-start(f32[3,64,256]{2,1,0:T(8,128)S(1)} %adam.1), channel_id=1, source_target_pairs={{0,7},{1,0},{2,1},{3,2},{4,3},{5,4},{6,5},{7,6},{8,15},{9,8},{10,9... | collective-permute-start | bytes 589832 | tf_op jit(solution)/shard_map/ppermute | solution.py:291
  32.8 4.4 %collective-permute-done.7.rest_0_ = f32[3,64,256]{2,1,0:T(8,128)S(1)} collective-permute-done((f32[3,64,256]{2,1,0:T(8,128)S(1)}, f32[3,64,256]{2,1,0:T(8,128)S(1)}, u32[]{:S(2)}, u32[]{:S(2)}) %collective-permute-start.7) | collective-permute-done | bytes 196640 | tf_op jit(solution)/shard_map/ppermute | solution.py:291
  37.3 1.1 %collective-permute-start.9 = (f32[3,64,256]{2,1,0:T(8,128)S(1)}, f32[3,64,256]{2,1,0:T(8,128)S(1)}, u32[]{:S(2)}, u32[]{:S(2)}) collective-permute-start(f32[3,64,256]{2,1,0:T(8,128)S(1)} %collective-permute-done.7.rest_0_), channel_id=1, source_target_pairs={{0,16},{8,24},{16,0},{24,8},{1,17},{9,25},{17,1},{25,9},{2,18},{10... | collective-permute-start | bytes 589832 | tf_op jit(solution)/shard_map/ppermute | solution.py:286
  38.3 0.0 collective-permute-start.8
  38.3 5.0 %collective-permute-done.9.rest_2_ = f32[3,64,256]{2,1,0:T(8,128)S(1)} collective-permute-done((f32[3,64,256]{2,1,0:T(8,128)S(1)}, f32[3,64,256]{2,1,0:T(8,128)S(1)}, u32[]{:S(2)}, u32[]{:S(2)}) %collective-permute-start.9) | collective-permute-done | bytes 196640 | tf_op jit(solution)/shard_map/ppermute | solution.py:286
  43.4 0.0 collective-permute-start.10
  43.4 0.0 copy-done.3
  43.4 3.7 %factors.1 = bf16[6144,256]{1,0:T(8,128)(2,1)} custom-call(bf16[6144,256]{1,0:T(8,128)(2,1)S(1)} %copy-done.3, bf16[6144,256]{1,0:T(8,128)(2,1)S(1)} %get-tuple-element.17.err_ref, f32[1,256,256]{2,1,0:T(8,128)S(1)} %copy-done.1), custom_call_target="tpu_custom_call" | custom-call | flops 805306368 | bytes 9437184 | tf_op jit(solution)/shard_map/factors/pallas_call | solution.py:156
  47.1 0.0 collective-permute-done.8.rest_1_
  47.1 0.0 collective-permute-done.10.rest_3_
  47.1 1.5 %place.1 = (f32[1,256,256]{2,1,0:T(8,128)}, f32[1,256,256]{2,1,0:T(8,128)}, f32[1,256,256]{2,1,0:T(8,128)}) custom-call(s32[2]{0:T(128)S(1)} %pad_add_fusion.here, f32[3,64,256]{2,1,0:T(8,128)S(1)} %collective-permute-done.7.rest_0_, f32[3,64,256]{2,1,0:T(8,128)S(1)} %collective-permute-done.8.rest_1_, f32[3,64,256]{2,1,0:T(8,128)S(1)} %collective-permute-done.9.rest_2_, ...), custom_call_target="tpu_custom_call" | custom-call | bytes 1572864 | tf_op jit(solution)/shard_map/place/pallas_call | solution.py:273
Async XLA Ops:
  1.4 1.0 %copy-start = (f32[1,256,256]{2,1,0:T(8,128)S(1)}, f32[1,256,256]{2,1,0:T(8,128)}, u32[]{:S(2)}) copy-start(f32[1,256,256]{2,1,0:T(8,128)} %x_ref.9) | copy-start | bytes 786436
  2.3 0.9 %copy-start.4 = (f32[1,256,256]{2,1,0:T(8,128)S(1)}, f32[1,256,256]{2,1,0:T(8,128)}, u32[]{:S(2)}) copy-start(f32[1,256,256]{2,1,0:T(8,128)} %m_ref.3) | copy-start | bytes 786436
  3.3 0.9 %copy-start.6 = (f32[1,256,256]{2,1,0:T(8,128)S(1)}, f32[1,256,256]{2,1,0:T(8,128)}, u32[]{:S(2)}) copy-start(f32[1,256,256]{2,1,0:T(8,128)} %v_ref.3) | copy-start | bytes 786436
  4.9 15.9 %collective-permute-start = (f32[168,256]{1,0:T(8,128)S(1)}, f32[168,256]{1,0:T(8,128)S(1)}, u32[]{:S(2)}, u32[]{:S(2)}) collective-permute-start(f32[168,256]{1,0:T(8,128)S(1)} %get-tuple-element.18), channel_id=1, source_target_pairs={{0,1},{1,2},{2,3},{3,4},{4,5},{5,6},{6,7},{7,0},{8,9},{9,10},{10,1... | collective-permute-start | bytes 516104 | tf_op jit(solution)/shard_map/ppermute | solution.py:291
  7.9 16.7 %collective-permute-start.4 = (f32[3,64,256]{2,1,0:T(8,128)S(1)}, f32[3,64,256]{2,1,0:T(8,128)S(1)}, u32[]{:S(2)}, u32[]{:S(2)}) collective-permute-start(f32[3,64,256]{2,1,0:T(8,128)S(1)} %get-tuple-element.24), channel_id=1, source_target_pairs={{0,8},{8,0},{16,24},{24,16},{1,9},{9,1},{17,25},{25,17},{2,10},{10... | collective-permute-start | bytes 589832 | tf_op jit(solution)/shard_map/ppermute | solution.py:286
  7.9 16.7 %collective-permute-start.5 = (f32[3,64,256]{2,1,0:T(8,128)S(1)}, f32[3,64,256]{2,1,0:T(8,128)S(1)}, u32[]{:S(2)}, u32[]{:S(2)}) collective-permute-start(f32[3,64,256]{2,1,0:T(8,128)S(1)} %get-tuple-element.25), channel_id=1, source_target_pairs={{0,16},{8,24},{16,0},{24,8},{1,17},{9,25},{17,1},{25,9},{2,18},{10... | collective-permute-start | bytes 589832 | tf_op jit(solution)/shard_map/ppermute | solution.py:286
  9.4 15.3 %collective-permute-start.6 = (f32[3,64,256]{2,1,0:T(8,128)S(1)}, f32[3,64,256]{2,1,0:T(8,128)S(1)}, u32[]{:S(2)}, u32[]{:S(2)}) collective-permute-start(f32[3,64,256]{2,1,0:T(8,128)S(1)} %get-tuple-element.26), channel_id=1, source_target_pairs={{0,24},{8,16},{16,8},{24,0},{1,25},{9,17},{17,9},{25,1},{2,26},{10... | collective-permute-start | bytes 589832 | tf_op jit(solution)/shard_map/ppermute | solution.py:286
  9.8 0.9 %copy-start.1 = (f32[1,256,256]{2,1,0:T(8,128)S(1)}, f32[1,256,256]{2,1,0:T(8,128)}, u32[]{:S(2)}) copy-start(f32[1,256,256]{2,1,0:T(8,128)} %x_ref.9) | copy-start | bytes 786436
  10.7 1.9 %copy-start.2 = (bf16[6144,256]{1,0:T(8,128)(2,1)S(1)}, bf16[6144,256]{1,0:T(8,128)(2,1)}, u32[]{:S(2)}) copy-start(bf16[6144,256]{1,0:T(8,128)(2,1)} %f_ref.3) | copy-start | bytes 9437188
  12.6 1.9 %copy-start.9 = (bf16[6144,256]{1,0:T(8,128)(2,1)S(1)}, bf16[6144,256]{1,0:T(8,128)(2,1)}, u32[]{:S(2)}) copy-start(bf16[6144,256]{1,0:T(8,128)(2,1)} %obs_ref.1) | copy-start | bytes 9437188
  14.5 1.1 %copy-start.10 = (s32[6144,32]{0,1:T(8,128)S(1)}, s32[6144,32]{0,1:T(8,128)}, u32[]{:S(2)}) copy-start(s32[6144,32]{0,1:T(8,128)} %param.9) | copy-start | bytes 2359300
  15.6 5.2 %copy-start.8 = (f32[25,256]{1,0:T(8,128)S(1)}, f32[25,256]{1,0:T(8,128)}, u32[]{:S(2)}) copy-start(f32[25,256]{1,0:T(8,128)} %w_ref.1) | copy-start | bytes 76804
  15.6 13.2 %copy-start.5 = (f32[1,256,256]{2,1,0:T(8,128)S(1)}, f32[1,256,256]{2,1,0:T(8,128)}, u32[]{:S(2)}) copy-start(f32[1,256,256]{2,1,0:T(8,128)} %m_ref.3) | copy-start | bytes 786436
  15.6 13.2 %copy-start.7 = (f32[1,256,256]{2,1,0:T(8,128)S(1)}, f32[1,256,256]{2,1,0:T(8,128)}, u32[]{:S(2)}) copy-start(f32[1,256,256]{2,1,0:T(8,128)} %v_ref.3) | copy-start | bytes 786436
  15.6 27.7 %copy-start.3 = (bf16[6144,256]{1,0:T(8,128)(2,1)S(1)}, bf16[6144,256]{1,0:T(8,128)(2,1)}, u32[]{:S(2)}) copy-start(bf16[6144,256]{1,0:T(8,128)(2,1)} %f_ref.3) | copy-start | bytes 9437188
  22.7 1.9 %collective-permute-start.1 = (f32[64,256]{1,0:T(8,128)S(1)}, f32[64,256]{1,0:T(8,128)S(1)}, u32[]{:S(2)}, u32[]{:S(2)}) collective-permute-start(f32[64,256]{1,0:T(8,128)S(1)} %get-tuple-element.21), channel_id=1, source_target_pairs={{0,8},{8,0},{16,24},{24,16},{1,9},{9,1},{17,25},{25,17},{2,10},{10... | collective-permute-start | bytes 196616 | tf_op jit(solution)/shard_map/ppermute | solution.py:286
  23.1 4.3 %collective-permute-start.2 = (f32[64,256]{1,0:T(8,128)S(1)}, f32[64,256]{1,0:T(8,128)S(1)}, u32[]{:S(2)}, u32[]{:S(2)}) collective-permute-start(f32[64,256]{1,0:T(8,128)S(1)} %get-tuple-element.22), channel_id=1, source_target_pairs={{0,16},{8,24},{16,0},{24,8},{1,17},{9,25},{17,1},{25,9},{2,18},{10... | collective-permute-start | bytes 196616 | tf_op jit(solution)/shard_map/ppermute | solution.py:286
  24.6 4.3 %collective-permute-start.3 = (f32[64,256]{1,0:T(8,128)S(1)}, f32[64,256]{1,0:T(8,128)S(1)}, u32[]{:S(2)}, u32[]{:S(2)}) collective-permute-start(f32[64,256]{1,0:T(8,128)S(1)} %get-tuple-element.23), channel_id=1, source_target_pairs={{0,24},{8,16},{16,8},{24,0},{1,25},{9,17},{17,9},{25,1},{2,26},{10... | collective-permute-start | bytes 196616 | tf_op jit(solution)/shard_map/ppermute | solution.py:286
  29.6 7.7 %collective-permute-start.7 = (f32[3,64,256]{2,1,0:T(8,128)S(1)}, f32[3,64,256]{2,1,0:T(8,128)S(1)}, u32[]{:S(2)}, u32[]{:S(2)}) collective-permute-start(f32[3,64,256]{2,1,0:T(8,128)S(1)} %adam.1), channel_id=1, source_target_pairs={{0,7},{1,0},{2,1},{3,2},{4,3},{5,4},{6,5},{7,6},{8,15},{9,8},{10,9... | collective-permute-start | bytes 589832 | tf_op jit(solution)/shard_map/ppermute | solution.py:291
  37.3 6.1 %collective-permute-start.9 = (f32[3,64,256]{2,1,0:T(8,128)S(1)}, f32[3,64,256]{2,1,0:T(8,128)S(1)}, u32[]{:S(2)}, u32[]{:S(2)}) collective-permute-start(f32[3,64,256]{2,1,0:T(8,128)S(1)} %collective-permute-done.7.rest_0_), channel_id=1, source_target_pairs={{0,16},{8,24},{16,0},{24,8},{1,17},{9,25},{17,1},{25,9},{2,18},{10... | collective-permute-start | bytes 589832 | tf_op jit(solution)/shard_map/ppermute | solution.py:286
  38.3 8.8 %collective-permute-start.8 = (f32[3,64,256]{2,1,0:T(8,128)S(1)}, f32[3,64,256]{2,1,0:T(8,128)S(1)}, u32[]{:S(2)}, u32[]{:S(2)}) collective-permute-start(f32[3,64,256]{2,1,0:T(8,128)S(1)} %collective-permute-done.7.rest_0_), channel_id=1, source_target_pairs={{0,8},{8,0},{16,24},{24,16},{1,9},{9,1},{17,25},{25,17},{2,10},{10... | collective-permute-start | bytes 589832 | tf_op jit(solution)/shard_map/ppermute | solution.py:286
  43.4 3.8 %collective-permute-start.10 = (f32[3,64,256]{2,1,0:T(8,128)S(1)}, f32[3,64,256]{2,1,0:T(8,128)S(1)}, u32[]{:S(2)}, u32[]{:S(2)}) collective-permute-start(f32[3,64,256]{2,1,0:T(8,128)S(1)} %collective-permute-done.9.rest_2_), channel_id=1, source_target_pairs={{0,8},{8,0},{16,24},{24,16},{1,9},{9,1},{17,25},{25,17},{2,10},{10... | collective-permute-start | bytes 589832 | tf_op jit(solution)/shard_map/ppermute | solution.py:286

commit v2 on v1

v2 whole, which is shorter than its diff:
```python
import functools

import jax
import jax.numpy as jnp
from jax import lax
from jax.experimental import pallas as pl
from jax.experimental.pallas import tpu as pltpu
from jax.sharding import PartitionSpec as P

SEASON = 168

beta_one = 0.9
beta_two = 0.999
adam_eps = 1e-08
step_rate = 0.05
factor_rate = 0.002
data_scale = 0.25

LIMIT = 32 * 1024 * 1024
F32 = jnp.float32
BF16 = jnp.bfloat16


def whole():
    return pl.BlockSpec(memory_space=pltpu.VMEM)


def far():
    return pl.BlockSpec(memory_space=pltpu.HBM)


def held(value):
    return pltpu.with_memory_space_constraint(value, pltpu.HBM)


def scalars():
    return pl.BlockSpec(memory_space=pltpu.SMEM)


def params(**more):
    return pltpu.CompilerParams(vmem_limit_bytes=LIMIT, **more)


def cost(flops, moved):
    return pl.CostEstimate(flops=int(flops), bytes_accessed=int(moved), transcendentals=0)


def rows_of(total, most):
    best = total
    for rows in range(128, most + 1, 128):
        if total % rows == 0:
            best = rows
    return best


def prepare_kernel(share, count, here, x_hbm, m_hbm, v_hbm, tail_ref, turned_ref, x_ref, own_ref, *rest):
    early, (x_sem, sems) = rest[:-2], rest[-2:]
    group = here[0]
    whole_copy = pltpu.make_async_copy(x_hbm.at[0], x_ref, x_sem)
    whole_copy.start()
    copies = []
    for step in range(count):
        target = own_ref if step == 0 else early[step - 1]
        start = pl.multiple_of((group ^ step) * share, share)
        for which, source in enumerate((x_hbm, m_hbm, v_hbm)):
            copies.append(
                pltpu.make_async_copy(
                    source.at[0, pl.ds(start, share), :], target.at[which], sems.at[step, which]
                )
            )
    for copy in copies:
        copy.start()
    whole_copy.wait()
    turned_ref[...] = x_ref[...].T
    tail_ref[...] = turned_ref[turned_ref.shape[0] - SEASON :, :]
    for copy in copies:
        copy.wait()


def prepare(here, x, m, v, count):
    rank, width = x.shape[1:]
    share = rank // count
    outs = [
        jax.ShapeDtypeStruct((SEASON, rank), F32),
        jax.ShapeDtypeStruct((width, rank), F32),
        jax.ShapeDtypeStruct((rank, width), F32),
    ]
    outs += [jax.ShapeDtypeStruct((3, share, width), F32)] * count
    return pl.pallas_call(
        functools.partial(prepare_kernel, share, count),
        out_shape=tuple(outs),
        in_specs=[scalars()] + [far()] * 3,
        out_specs=tuple([whole()] * len(outs)),
        scratch_shapes=[pltpu.SemaphoreType.DMA(()), pltpu.SemaphoreType.DMA((count, 3))],
        compiler_params=params(),
        cost_estimate=cost(0, 6 * rank * width * 4),
        name="prepare",
    )(here, held(x), held(m), held(v))


def error_kernel(chunks, obs_hbm, bits_hbm, f_hbm, x_ref, err_ref, f_ref, gd_ref, obs_ref, bits_ref, sems):
    words, series = bits_ref.shape
    width = obs_ref.shape[1]
    per = width // words
    rows = series // chunks

    def copies(index):
        part = pl.ds(index * rows, rows)
        return (
            pltpu.make_async_copy(bits_hbm.at[:, part], bits_ref.at[:, part], sems.at[index, 0]),
            pltpu.make_async_copy(f_hbm.at[part, :], f_ref.at[part, :], sems.at[index, 1]),
            pltpu.make_async_copy(obs_hbm.at[part, :], obs_ref.at[part, :], sems.at[index, 2]),
        )

    for index in range(chunks):
        for copy in copies(index):
            copy.start()
    half = x_ref[...].astype(BF16)
    lane = lax.broadcasted_iota(jnp.int32, (words, width), 1)
    word = lax.broadcasted_iota(jnp.int32, (words, width), 0)
    spread = (lane // per == word).astype(BF16)
    flag = jnp.left_shift(1, lax.broadcasted_iota(jnp.int32, (1, width), 1) % per)
    for index in range(chunks):
        for copy in copies(index):
            copy.wait()
        part = pl.ds(index * rows, rows)
        value = lax.dot_general(
            bits_ref[:, part].astype(F32).astype(BF16),
            spread,
            (((0,), (0,)), ((), ())),
            preferred_element_type=F32,
        ).astype(jnp.int32)
        predicted = jnp.dot(f_ref[part, :], half, preferred_element_type=F32)
        error = jnp.where(
            jnp.bitwise_and(value, flag) != 0, predicted - obs_ref[part, :].astype(F32), 0.0
        ).astype(BF16)
        err_ref[part, :] = error
        term = lax.dot_general(
            f_ref[part, :], error, (((0,), (0,)), ((), ())), preferred_element_type=F32
        )
        if index == 0:
            gd_ref[...] = term
        else:
            gd_ref[...] += term


def error_step(obs, bits, factors, x):
    series, width = obs.shape
    rank = factors.shape[1]
    words = bits.shape[0]
    chunks = series // rows_of(series, 1024)
    return pl.pallas_call(
        functools.partial(error_kernel, chunks),
        out_shape=(
            jax.ShapeDtypeStruct((series, width), BF16),
            jax.ShapeDtypeStruct((series, rank), BF16),
            jax.ShapeDtypeStruct((rank, width), F32),
        ),
        in_specs=[far(), far(), far(), whole()],
        out_specs=(whole(), whole(), whole()),
        scratch_shapes=[
            pltpu.VMEM((series, width), BF16),
            pltpu.VMEM((words, series), jnp.int32),
            pltpu.SemaphoreType.DMA((chunks, 3)),
        ],
        compiler_params=params(),
        cost_estimate=cost(6 * series * width * rank, series * (3 * width * 2 + words * 4)),
        name="errors",
    )(held(obs), held(bits), held(factors), x)


def factor_kernel(f_ref, err_ref, x_ref, after, out_ref, half_ref):
    @pl.when(pl.program_id(0) == 0)
    def _():
        half_ref[...] = x_ref[...].astype(BF16)

    gradient = lax.dot_general(
        err_ref[...], half_ref[...], (((1,), (1,)), ((), ())), preferred_element_type=F32
    )
    out_ref[...] = (f_ref[...].astype(F32) - factor_rate * gradient).astype(BF16)


def factor_step(factors, err, x, after):
    series, rank = factors.shape
    width = err.shape[1]
    rows = rows_of(series, 1024)
    return pl.pallas_call(
        factor_kernel,
        out_shape=jax.ShapeDtypeStruct((series, rank), BF16),
        grid=(series // rows,),
        in_specs=[
            pl.BlockSpec((rows, rank), lambda i: (i, 0)),
            pl.BlockSpec((rows, width), lambda i: (i, 0)),
            pl.BlockSpec((rank, width), lambda i: (0, 0)),
            pl.BlockSpec(memory_space=pl.ANY),
        ],
        out_specs=pl.BlockSpec((rows, rank), lambda i: (i, 0)),
        scratch_shapes=[pltpu.VMEM((rank, width), BF16)],
        compiler_params=params(),
        cost_estimate=cost(2 * series * width * rank, series * 3 * width * 2),
        name="factors",
    )(factors, err, x, after)


def gradient_kernel(share, count, lanes, block_index, halo_ref, turned_ref, w_ref, gd_ref, out_ref, z_ref, r_ref):
    width, rank = turned_ref.shape
    lags = list(range(1, w_ref.shape[0])) + [SEASON]
    for part in range(rank // lanes):
        columns = slice(part * lanes, (part + 1) * lanes)
        z_ref[part, :SEASON, :] = jnp.where(block_index[0] == 0, 0.0, halo_ref[:, columns])
        z_ref[part, SEASON:, :] = turned_ref[:, columns]
        resid = turned_ref[:, columns]
        for index, lag in enumerate(lags):
            begin = SEASON - lag
            resid = resid - w_ref[index : index + 1, columns] * z_ref[part, begin : begin + width, :]
        r_ref[part, :width, :] = resid
        r_ref[part, width:, :] = jnp.zeros((SEASON, lanes), F32)
        back = resid
        for index, lag in enumerate(lags):
            back = back - w_ref[index : index + 1, columns] * r_ref[part, lag : lag + width, :]
        back = back.T
        for line in range(0, lanes, share):
            which = (part * lanes + line) // share
            at = which * share
            out_ref[which] = data_scale * gd_ref[at : at + share, :] + back[line : line + share, :]


def gradient_step(block_index, halo, turned, weights, gd, count):
    rank, width = gd.shape
    share = rank // count
    lanes = 128
    return pl.pallas_call(
        functools.partial(gradient_kernel, share, count, lanes),
        out_shape=jax.ShapeDtypeStruct((count, share, width), F32),
        in_specs=[scalars()] + [whole()] * 4,
        out_specs=whole(),
        scratch_shapes=[
            pltpu.VMEM((rank // lanes, SEASON + width, lanes), F32),
            pltpu.VMEM((rank // lanes, SEASON + width, lanes), F32),
        ],
        compiler_params=params(),
        cost_estimate=cost(100 * rank * width, 4 * rank * width * 4),
        name="gradient",
    )(block_index, halo, turned, weights, gd)


def adam_kernel(count, here, grads_ref, *rest):
    early, out_ref = rest[:-1], rest[-1]
    total = [0.0, 0.0, 0.0]
    for step in range(count):
        block, first, second = [early[step][which] for which in range(3)]
        gradient = grads_ref[here[0] ^ step]
        first = beta_one * first + (1.0 - beta_one) * gradient
        second = beta_two * second + (1.0 - beta_two) * gradient * gradient
        block = block - step_rate * first / (jnp.sqrt(second) + adam_eps)
        total = [total[0] + block, total[1] + first, total[2] + second]
    for which in range(3):
        out_ref[which] = total[which] / count


def adam_step(here, grads, early):
    count, share, width = grads.shape
    return pl.pallas_call(
        functools.partial(adam_kernel, count),
        out_shape=jax.ShapeDtypeStruct((3, share, width), F32),
        in_specs=[scalars()] + [whole()] * (1 + count),
        out_specs=whole(),
        compiler_params=params(),
        cost_estimate=cost(80 * share * width, 20 * share * width * 4),
        name="adam",
    )(here, grads, *early)


def place_kernel(share, count, here, *rest):
    parts, outs, sems = rest[:count], rest[count : count + 3], rest[count + 3]
    copies = []
    for step, part in enumerate(parts):
        start = pl.multiple_of((here[0] ^ step) * share, share)
        for which in range(3):
            copies.append(
                pltpu.make_async_copy(
                    part.at[which], outs[which].at[0, pl.ds(start, share), :], sems.at[step, which]
                )
            )
    for copy in copies:
        copy.start()
    for copy in copies:
        copy.wait()


def place(here, parts):
    count = len(parts)
    _, share, width = parts[0].shape
    out = jax.ShapeDtypeStruct((1, count * share, width), F32)
    return pl.pallas_call(
        functools.partial(place_kernel, share, count),
        out_shape=(out, out, out),
        in_specs=[scalars()] + [pl.BlockSpec(memory_space=pl.ANY)] * count,
        out_specs=(far(), far(), far()),
        scratch_shapes=[pltpu.SemaphoreType.DMA((count, 3))],
        compiler_params=params(),
        cost_estimate=cost(0, 6 * count * share * width * 4),
        name="place",
    )(here, *parts)


def crossed(value, step):
    count = lax.axis_size("grp")
    return lax.ppermute(value, "grp", [(source, source ^ step) for source in range(count)])


def shifted(value, steps):
    count = lax.axis_size("blk")
    return lax.ppermute(value, "blk", [(source, (source + steps) % count) for source in range(count)])


def body(obs, mask_bits, factors, x_blocks, first_moment, second_moment, ar_weights, stratum):
    cycle = lax.axis_size("blk")
    count = lax.axis_size("grp")
    group = lax.axis_index("grp")
    block_index = (lax.axis_index("blk") + stratum[0]) % cycle
    here = group.astype(jnp.int32).reshape(1)

    tail, turned, x, own, *early = prepare(here, x_blocks, first_moment, second_moment, count)
    halo = shifted(tail, 1)
    early = [own] + [crossed(value, step + 1) for step, value in enumerate(early)]
    err, kept, gd = error_step(obs, mask_bits.T, factors, x)
    grads = gradient_step(block_index.reshape(1), halo, turned, ar_weights, gd, count)
    grads = lax.all_to_all(grads, "grp", 0, 0, tiled=True)
    means = adam_step(here, grads, early)
    moved = shifted(means, -1)
    factor_new = factor_step(kept, err, x, means)
    moved, factor_new = lax.optimization_barrier((moved, factor_new))
    span = 1
    while span < count:
        span *= 2
    level = span // 2
    known = {0: moved}
    while level >= 1:
        for key in list(known):
            known[key ^ level] = crossed(known[key], level)
        level //= 2
    parts = [known[key] for key in range(count)]
    outs = place(here, parts)
    return (factor_new, *outs)


def solution(mesh):
    rows = P(("grp", "blk"), None)
    blocks = P("grp", None, "blk")
    return jax.shard_map(
        body,
        mesh=mesh,
        in_specs=(rows, rows, rows, blocks, blocks, blocks, P(), P()),
        out_specs=(rows, blocks, blocks, blocks),
        check_vma=False,
    )
```

time: 49 us -> 50.5 us (1.031)
  Pallas kernels: 13.7 us -> 17 us
  local copies, waits for them, and re-layouts: 8.72 us -> 6.82 us
  starting transfers between devices: 11.1 us -> 11.7 us
    all_to_all x0 -> x1, waiting for transfers between devices: none -> 5.97 us  [body(): grads = lax.all_to_all(grads, 'grp', 0, 0, tiled=True)]
    ppermute x2, waiting for transfers between devices: 4.44 us -> 0.01 us  [shifted(): lax.ppermute(value, 'blk', [(source, (source + steps) % count) for source...]
    all_to_all x0 -> x1, starting transfers between devices: none -> 3.41 us  [body(): grads = lax.all_to_all(grads, 'grp', 0, 0, tiled=True)]
    ppermute x9 -> x6, starting transfers between devices: 4.85 us -> 2.22 us  [crossed(): lax.ppermute(value, 'grp', [(source, source ^ step) for source in range(c...]
    ppermute x9 -> x6, waiting for transfers between devices: 9.21 us -> 7.26 us  [crossed(): lax.ppermute(value, 'grp', [(source, source ^ step) for source in range(c...]
    unnamed x22 -> x18, local copies, waits for them, and re-layouts: 8.72 us -> 6.82 us
    pallas_call x1, Pallas kernels: 0.67 us -> 2.4 us  [prepare(): pl.pallas_call(functools.partial(prepare_kernel, share, count), out_shape...]
    pallas_call x4, Pallas kernels: 9.24 us -> 10.9 us  [the longest x1 5.84 us: error_step(): pl.pallas_call(functools.partial(error_kernel, chunks), out_shape=(jax.Sh...]
  transfers between devices with their start and end apart: 11 -> 9, of which waited for: 4 -> 3; matrix products, arithmetic and copies ran while one was open for 0% -> 0% of each run, Pallas kernels for 22% -> 25%
where the time goes in v2:
time: 50.5 us; the launch traced here: 50.2 us
  Pallas kernels  17 us (34%)
  waiting for transfers between devices  13.2 us (26%)
  starting transfers between devices  11.7 us (23%)
  local copies, waits for them, and re-layouts  6.82 us (14%)
  between operations  1.41 us (3%)
    ppermute x6, waiting for transfers between devices, crossed(): lax.ppermute(value, 'grp', [(source, source ^ step) for source in range(c...  7.26 us
    unnamed x18, local copies, waits for them, and re-layouts  6.82 us
    ppermute x2, starting transfers between devices, shifted(): lax.ppermute(value, 'blk', [(source, (source + steps) % count) for source...  6.06 us
    all_to_all x1, waiting for transfers between devices, body(): grads = lax.all_to_all(grads, 'grp', 0, 0, tiled=True)  5.97 us
    pallas_call x1, Pallas kernels, error_step(): pl.pallas_call(functools.partial(error_kernel, chunks), out_shape=(jax.Sh...  5.84 us
    pallas_call x1, Pallas kernels, factor_step(): pl.pallas_call(factor_kernel, out_shape=jax.ShapeDtypeStruct((series, ran...  3.75 us
    all_to_all x1, starting transfers between devices, body(): grads = lax.all_to_all(grads, 'grp', 0, 0, tiled=True)  3.41 us
    pallas_call x1, Pallas kernels, gradient_step(): pl.pallas_call(functools.partial(gradient_kernel, share, count, lanes), o...  2.74 us
  transfers between devices with their start and end apart: 9, of which 3 were waited for; matrix products, arithmetic and copies ran while one was open for 0% of the time, Pallas kernels for 25%

profile of v2, /device:TPU:0, one launch (start us, length us, event | category | flops | bytes accessed | tf_op | source)
XLA Modules:
  0.0 50.2 jit_solution(12433783017768193288)
XLA Ops:
  0.6 2.4 %prepare.1 = (f32[168,256]{1,0:T(8,128)}, f32[256,256]{1,0:T(8,128)S(1)}, f32[256,256]{1,0:T(8,128)S(1)}, f32[3,64,256]{2,1,0:T(8,128)S(1)}, f32[3,64,256]{2,1,0...) custom-call(s32[1]{0:T(128)} %bitcast.here, f32[1,256,256]{2,1,0:T(8,128)} %x_hbm.1, f32[1,256,256]{2,1,0:T(8,128)} %m_hbm.1, ...), custom_call_target="tpu_custom_call" | custom-call | bytes 1572864 | tf_op jit(solution)/shard_map/prepare/pallas_call | solution.py:89
  3.0 0.0 copy-start.4
  3.1 0.7 %copy-done.4 = f32[256,256]{1,0:T(8,128)} copy-done((f32[256,256]{1,0:T(8,128)}, f32[256,256]{1,0:T(8,128)S(1)}, u32[]{:S(2)}) %copy-start.4) | copy-done | bytes 262168
  3.8 0.0 copy-start.6
  3.8 0.7 %copy-done.6 = f32[3,64,256]{2,1,0:T(8,128)} copy-done((f32[3,64,256]{2,1,0:T(8,128)}, f32[3,64,256]{2,1,0:T(8,128)S(1)}, u32[]{:S(2)}) %copy-start.6) | copy-done | bytes 196632
  4.4 0.0 copy-start.2
  4.4 3.0 %collective-permute-start = (f32[168,256]{1,0:T(8,128)}, f32[168,256]{1,0:T(8,128)}, u32[]{:S(2)}, u32[]{:S(2)}) collective-permute-start(f32[168,256]{1,0:T(8,128)} %get-tuple-element.19), channel_id=1, source_target_pairs={{0,1},{1,2},{2,3},{3,4},{4,5},{5,6},{6,7},{7,0},{8,9},{9,10},{10,1... | collective-permute-start | bytes 516104 | tf_op jit(solution)/shard_map/ppermute | solution.py:314
  7.4 0.0 collective-permute-start.1
  7.4 1.5 %collective-permute-start.2 = (f32[3,64,256]{2,1,0:T(8,128)}, f32[3,64,256]{2,1,0:T(8,128)}, u32[]{:S(2)}, u32[]{:S(2)}) collective-permute-start(f32[3,64,256]{2,1,0:T(8,128)} %get-tuple-element.25), channel_id=1, source_target_pairs={{0,16},{8,24},{16,0},{24,8},{1,17},{9,25},{17,1},{25,9},{2,18},{10... | collective-permute-start | bytes 589832 | tf_op jit(solution)/shard_map/ppermute | solution.py:309
  8.9 0.4 collective-permute-start.3
  9.9 0.0 copy-start.5
  9.9 0.0 copy-start.8
  10.0 5.8 %errors.1 = (bf16[6144,256]{1,0:T(8,128)(2,1)S(1)}, bf16[6144,256]{1,0:T(8,128)(2,1)S(1)}, f32[256,256]{1,0:T(8,128)S(1)}) custom-call(bf16[6144,256]{1,0:T(8,128)(2,1)} %obs_hbm.1, s32[32,6144]{1,0:T(8,128)} %bitcast.5, bf16[6144,256]{1,0:T(8,128)(2,1)} %f_hbm.1, f32[256,256]{1,0:T(8,128)S(1)} %get-tuple-element.21.x_ref), custom_call_target="tpu_custom_call" | custom-call | flops 2415919104 | bytes 10223616 | tf_op jit(solution)/shard_map/errors/pallas_call | solution.py:152
  15.8 0.0 copy-done.2
  15.8 0.0 copy-start
  15.8 1.7 %copy-done = bf16[6144,256]{1,0:T(8,128)(2,1)} copy-done((bf16[6144,256]{1,0:T(8,128)(2,1)}, bf16[6144,256]{1,0:T(8,128)(2,1)S(1)}, u32[]{:S(2)}) %copy-start) | copy-done | bytes 3145752
  17.5 0.0 collective-permute-done.halo_ref
  17.5 0.0 copy-done.5
  17.5 0.0 copy-done.8
  17.5 2.7 %gradient.1 = f32[4,64,256]{2,1,0:T(8,128)} custom-call(s32[1]{0:T(128)} %bitcast.2.block_index, f32[168,256]{1,0:T(8,128)} %collective-permute-done.halo_ref, f32[256,256]{1,0:T(8,128)S(1)} %copy-done.5, f32[25,256]{1,0:T(8,128)S(1)} %copy-done.8, f32[256,256]{1,0:T(8,128)S(1)} %get-tuple-element.22.gd_ref), custom_call_target="tpu_custom_call" | custom-call | flops 6553600 | bytes 1048576 | tf_op jit(solution)/shard_map/gradient/pallas_call | solution.py:232
  20.2 3.4 %all-to-all-start = ((f32[4,64,256]{2,1,0:T(8,128)}), f32[4,64,256]{2,1,0:T(8,128)S(1)}, u32[]{:S(2)}, u32[]{:S(2)}) async-start(f32[4,64,256]{2,1,0:T(8,128)} %gradient.1), calls=%async_computation | async-start | bytes 524288 | tf_op jit(solution)/shard_map/all_to_all | solution.py:329
  23.6 0.0 collective-permute-done.1.rest_1_
  23.7 0.0 collective-permute-done.2.rest_2_
  23.7 0.0 collective-permute-done.3.rest_3_
  23.7 6.0 %all-to-all-done.grads_ref = f32[4,64,256]{2,1,0:T(8,128)S(1)} async-done(((f32[4,64,256]{2,1,0:T(8,128)}), f32[4,64,256]{2,1,0:T(8,128)S(1)}, u32[]{:S(2)}, u32[]{:S(2)}) %all-to-all-start) | async-done | bytes 262176 | tf_op jit(solution)/shard_map/all_to_all | solution.py:329
  29.6 0.0 copy-start.7
  29.7 0.9 %copy-done.7 = f32[3,64,256]{2,1,0:T(8,128)S(1)} copy-done((f32[3,64,256]{2,1,0:T(8,128)S(1)}, f32[3,64,256]{2,1,0:T(8,128)}, u32[]{:S(2)}) %copy-start.7) | copy-done | bytes 196632
  30.6 1.3 %adam.1.after = f32[3,64,256]{2,1,0:T(8,128)S(1)} custom-call(s32[1]{0:T(128)} %bitcast.here, f32[4,64,256]{2,1,0:T(8,128)S(1)} %all-to-all-done.grads_ref, f32[3,64,256]{2,1,0:T(8,128)S(1)} %copy-done.7, f32[3,64,256]{2,1,0:T(8,128)} %collective-permute-done.1.rest_1_, f32[3,64,256]{2,1,0:T(8,128)} %collective-permute-done.2.rest_2_, ...), custom_call_target="tpu_custom_call" | custom-call | flops 1310720 | bytes 1310720 | tf_op jit(solution)/shard_map/adam/pallas_call | solution.py:263
  31.9 3.1 %collective-permute-start.4 = (f32[3,64,256]{2,1,0:T(8,128)S(1)}, f32[3,64,256]{2,1,0:T(8,128)S(1)}, u32[]{:S(2)}, u32[]{:S(2)}) collective-permute-start(f32[3,64,256]{2,1,0:T(8,128)S(1)} %adam.1.after), channel_id=1, source_target_pairs={{0,7},{1,0},{2,1},{3,2},{4,3},{5,4},{6,5},{7,6},{8,15},{9,8},{10,9... | collective-permute-start | bytes 589832 | tf_op jit(solution)/shard_map/ppermute | solution.py:314
  35.0 0.0 copy-start.1
  35.0 1.9 %copy-done.1 = bf16[6144,256]{1,0:T(8,128)(2,1)S(1)} copy-done((bf16[6144,256]{1,0:T(8,128)(2,1)S(1)}, bf16[6144,256]{1,0:T(8,128)(2,1)}, u32[]{:S(2)}) %copy-start.1) | copy-done | bytes 3145752
  36.9 0.0 copy-start.3
  36.9 0.9 %copy-done.3 = f32[256,256]{1,0:T(8,128)S(1)} copy-done((f32[256,256]{1,0:T(8,128)S(1)}, f32[256,256]{1,0:T(8,128)}, u32[]{:S(2)}) %copy-start.3) | copy-done | bytes 262168
  37.8 3.8 %factors.1 = bf16[6144,256]{1,0:T(8,128)(2,1)} custom-call(bf16[6144,256]{1,0:T(8,128)(2,1)S(1)} %copy-done.1, bf16[6144,256]{1,0:T(8,128)(2,1)S(1)} %get-tuple-element.28.err_ref, f32[256,256]{1,0:T(8,128)S(1)} %copy-done.3, f32[3,64,256]{2,1,0:T(8,128)S(1)} %adam.1.after), custom_call_target="tpu_custom_call" | custom-call | flops 805306368 | bytes 9437184 | tf_op jit(solution)/shard_map/factors/pallas_call | solution.py:187
  41.6 0.0 collective-permute-done.4.rest_0_
  41.6 0.4 collective-permute-start.6
  41.9 0.0 collective-permute-start.5
  41.9 5.8 %collective-permute-done.6.rest_2_ = f32[3,64,256]{2,1,0:T(8,128)S(1)} collective-permute-done((f32[3,64,256]{2,1,0:T(8,128)S(1)}, f32[3,64,256]{2,1,0:T(8,128)S(1)}, u32[]{:S(2)}, u32[]{:S(2)}) %collective-permute-start.6) | collective-permute-done | bytes 196640 | tf_op jit(solution)/shard_map/ppermute | solution.py:309
  47.7 0.0 collective-permute-start.7
  47.8 0.0 collective-permute-done.5.rest_1_
  47.8 1.4 %collective-permute-done.7.rest_3_ = f32[3,64,256]{2,1,0:T(8,128)S(1)} collective-permute-done((f32[3,64,256]{2,1,0:T(8,128)S(1)}, f32[3,64,256]{2,1,0:T(8,128)S(1)}, u32[]{:S(2)}, u32[]{:S(2)}) %collective-permute-start.7) | collective-permute-done | bytes 196640 | tf_op jit(solution)/shard_map/ppermute | solution.py:309
  49.2 1.0 %place.1 = (f32[1,256,256]{2,1,0:T(8,128)}, f32[1,256,256]{2,1,0:T(8,128)}, f32[1,256,256]{2,1,0:T(8,128)}) custom-call(s32[1]{0:T(128)} %bitcast.here, f32[3,64,256]{2,1,0:T(8,128)S(1)} %collective-permute-done.4.rest_0_, f32[3,64,256]{2,1,0:T(8,128)S(1)} %collective-permute-done.5.rest_1_, f32[3,64,256]{2,1,0:T(8,128)S(1)} %collective-permute-done.6.rest_2_, ...), custom_call_target="tpu_custom_call" | custom-call | bytes 1572864 | tf_op jit(solution)/shard_map/place/pallas_call | solution.py:295
Async XLA Ops:
  3.0 0.7 %copy-start.4 = (f32[256,256]{1,0:T(8,128)}, f32[256,256]{1,0:T(8,128)S(1)}, u32[]{:S(2)}) copy-start(f32[256,256]{1,0:T(8,128)S(1)} %get-tuple-element.20.turned_ref) | copy-start | bytes 786436
  3.8 0.7 %copy-start.6 = (f32[3,64,256]{2,1,0:T(8,128)}, f32[3,64,256]{2,1,0:T(8,128)S(1)}, u32[]{:S(2)}) copy-start(f32[3,64,256]{2,1,0:T(8,128)S(1)} %get-tuple-element.23.rest_0_) | copy-start | bytes 589828
  4.4 11.4 %copy-start.2 = (f32[256,256]{1,0:T(8,128)}, f32[256,256]{1,0:T(8,128)S(1)}, u32[]{:S(2)}) copy-start(f32[256,256]{1,0:T(8,128)S(1)} %get-tuple-element.21.x_ref) | copy-start | bytes 786436
  4.4 13.1 %collective-permute-start = (f32[168,256]{1,0:T(8,128)}, f32[168,256]{1,0:T(8,128)}, u32[]{:S(2)}, u32[]{:S(2)}) collective-permute-start(f32[168,256]{1,0:T(8,128)} %get-tuple-element.19), channel_id=1, source_target_pairs={{0,1},{1,2},{2,3},{3,4},{4,5},{5,6},{6,7},{7,0},{8,9},{9,10},{10,1... | collective-permute-start | bytes 516104 | tf_op jit(solution)/shard_map/ppermute | solution.py:314
  7.4 16.2 %collective-permute-start.1 = (f32[3,64,256]{2,1,0:T(8,128)}, f32[3,64,256]{2,1,0:T(8,128)}, u32[]{:S(2)}, u32[]{:S(2)}) collective-permute-start(f32[3,64,256]{2,1,0:T(8,128)} %get-tuple-element.24), channel_id=1, source_target_pairs={{0,8},{8,0},{16,24},{24,16},{1,9},{9,1},{17,25},{25,17},{2,10},{10... | collective-permute-start | bytes 589832 | tf_op jit(solution)/shard_map/ppermute | solution.py:309
  7.4 16.3 %collective-permute-start.2 = (f32[3,64,256]{2,1,0:T(8,128)}, f32[3,64,256]{2,1,0:T(8,128)}, u32[]{:S(2)}, u32[]{:S(2)}) collective-permute-start(f32[3,64,256]{2,1,0:T(8,128)} %get-tuple-element.25), channel_id=1, source_target_pairs={{0,16},{8,24},{16,0},{24,8},{1,17},{9,25},{17,1},{25,9},{2,18},{10... | collective-permute-start | bytes 589832 | tf_op jit(solution)/shard_map/ppermute | solution.py:309
  8.9 14.8 %collective-permute-start.3 = (f32[3,64,256]{2,1,0:T(8,128)}, f32[3,64,256]{2,1,0:T(8,128)}, u32[]{:S(2)}, u32[]{:S(2)}) collective-permute-start(f32[3,64,256]{2,1,0:T(8,128)} %get-tuple-element.26), channel_id=1, source_target_pairs={{0,24},{8,16},{16,8},{24,0},{1,25},{9,17},{17,9},{25,1},{2,26},{10... | collective-permute-start | bytes 589832 | tf_op jit(solution)/shard_map/ppermute | solution.py:309
  9.9 7.6 %copy-start.5 = (f32[256,256]{1,0:T(8,128)S(1)}, f32[256,256]{1,0:T(8,128)}, u32[]{:S(2)}) copy-start(f32[256,256]{1,0:T(8,128)} %copy-done.4) | copy-start | bytes 786436
  9.9 7.5 %copy-start.8 = (f32[25,256]{1,0:T(8,128)S(1)}, f32[25,256]{1,0:T(8,128)}, u32[]{:S(2)}) copy-start(f32[25,256]{1,0:T(8,128)} %w_ref.1) | copy-start | bytes 76804
  15.8 1.7 %copy-start = (bf16[6144,256]{1,0:T(8,128)(2,1)}, bf16[6144,256]{1,0:T(8,128)(2,1)S(1)}, u32[]{:S(2)}) copy-start(bf16[6144,256]{1,0:T(8,128)(2,1)S(1)} %get-tuple-element.27.f_ref) | copy-start | bytes 9437188
  20.2 9.4 %all-to-all-start = ((f32[4,64,256]{2,1,0:T(8,128)}), f32[4,64,256]{2,1,0:T(8,128)S(1)}, u32[]{:S(2)}, u32[]{:S(2)}) async-start(f32[4,64,256]{2,1,0:T(8,128)} %gradient.1), calls=%async_computation | async-start | bytes 524288 | tf_op jit(solution)/shard_map/all_to_all | solution.py:329
  29.6 0.9 %copy-start.7 = (f32[3,64,256]{2,1,0:T(8,128)S(1)}, f32[3,64,256]{2,1,0:T(8,128)}, u32[]{:S(2)}) copy-start(f32[3,64,256]{2,1,0:T(8,128)} %copy-done.6) | copy-start | bytes 589828
  31.9 9.7 %collective-permute-start.4 = (f32[3,64,256]{2,1,0:T(8,128)S(1)}, f32[3,64,256]{2,1,0:T(8,128)S(1)}, u32[]{:S(2)}, u32[]{:S(2)}) collective-permute-start(f32[3,64,256]{2,1,0:T(8,128)S(1)} %adam.1.after), channel_id=1, source_target_pairs={{0,7},{1,0},{2,1},{3,2},{4,3},{5,4},{6,5},{7,6},{8,15},{9,8},{10,9... | collective-permute-start | bytes 589832 | tf_op jit(solution)/shard_map/ppermute | solution.py:314
  35.0 1.9 %copy-start.1 = (bf16[6144,256]{1,0:T(8,128)(2,1)S(1)}, bf16[6144,256]{1,0:T(8,128)(2,1)}, u32[]{:S(2)}) copy-start(bf16[6144,256]{1,0:T(8,128)(2,1)} %copy-done) | copy-start | bytes 9437188
  36.9 0.9 %copy-start.3 = (f32[256,256]{1,0:T(8,128)S(1)}, f32[256,256]{1,0:T(8,128)}, u32[]{:S(2)}) copy-start(f32[256,256]{1,0:T(8,128)} %copy-done.2) | copy-start | bytes 786436
  41.6 6.2 %collective-permute-start.6 = (f32[3,64,256]{2,1,0:T(8,128)S(1)}, f32[3,64,256]{2,1,0:T(8,128)S(1)}, u32[]{:S(2)}, u32[]{:S(2)}) collective-permute-start(f32[3,64,256]{2,1,0:T(8,128)S(1)} %collective-permute-done.4.rest_0_), channel_id=1, source_target_pairs={{0,16},{8,24},{16,0},{24,8},{1,17},{9,25},{17,1},{25,9},{2,18},{10... | collective-permute-start | bytes 589832 | tf_op jit(solution)/shard_map/ppermute | solution.py:309
  41.9 5.8 %collective-permute-start.5 = (f32[3,64,256]{2,1,0:T(8,128)S(1)}, f32[3,64,256]{2,1,0:T(8,128)S(1)}, u32[]{:S(2)}, u32[]{:S(2)}) collective-permute-start(f32[3,64,256]{2,1,0:T(8,128)S(1)} %collective-permute-done.4.rest_0_), channel_id=1, source_target_pairs={{0,8},{8,0},{16,24},{24,16},{1,9},{9,1},{17,25},{25,17},{2,10},{10... | collective-permute-start | bytes 589832 | tf_op jit(solution)/shard_map/ppermute | solution.py:309
  47.7 1.4 %collective-permute-start.7 = (f32[3,64,256]{2,1,0:T(8,128)S(1)}, f32[3,64,256]{2,1,0:T(8,128)S(1)}, u32[]{:S(2)}, u32[]{:S(2)}) collective-permute-start(f32[3,64,256]{2,1,0:T(8,128)S(1)} %collective-permute-done.6.rest_2_), channel_id=1, source_target_pairs={{0,8},{8,0},{16,24},{24,16},{1,9},{9,1},{17,25},{25,17},{2,10},{10... | collective-permute-start | bytes 589832 | tf_op jit(solution)/shard_map/ppermute | solution.py:309

commit v3 on v2

v3 whole, which is shorter than its diff:
```python
import functools

import jax
import jax.numpy as jnp
from jax import lax
from jax.experimental import pallas as pl
from jax.experimental.pallas import tpu as pltpu
from jax.sharding import PartitionSpec as P

SEASON = 168

beta_one = 0.9
beta_two = 0.999
adam_eps = 1e-08
step_rate = 0.05
factor_rate = 0.002
data_scale = 0.25

LIMIT = 32 * 1024 * 1024
F32 = jnp.float32
BF16 = jnp.bfloat16


def whole():
    return pl.BlockSpec(memory_space=pltpu.VMEM)


def far():
    return pl.BlockSpec(memory_space=pltpu.HBM)


def held(value):
    return pltpu.with_memory_space_constraint(value, pltpu.HBM)


def scalars():
    return pl.BlockSpec(memory_space=pltpu.SMEM)


def params(**more):
    return pltpu.CompilerParams(vmem_limit_bytes=LIMIT, **more)


def cost(flops, moved):
    return pl.CostEstimate(flops=int(flops), bytes_accessed=int(moved), transcendentals=0)


def rows_of(total, most):
    best = total
    for rows in range(128, most + 1, 128):
        if total % rows == 0:
            best = rows
    return best


def prepare_kernel(share, count, x_hbm, m_hbm, v_hbm, tail_ref, turned_ref, x_ref, own_ref, *rest):
    early, (x_sem, sems) = rest[:-2], rest[-2:]
    group = lax.axis_index("grp")
    whole_copy = pltpu.make_async_copy(x_hbm.at[0], x_ref, x_sem)
    whole_copy.start()
    copies = []
    for step in range(count):
        target = own_ref if step == 0 else early[step - 1]
        start = pl.multiple_of((group ^ step) * share, share)
        for which, source in enumerate((x_hbm, m_hbm, v_hbm)):
            copies.append(
                pltpu.make_async_copy(
                    source.at[0, pl.ds(start, share), :], target.at[which], sems.at[step, which]
                )
            )
    for copy in copies:
        copy.start()
    whole_copy.wait()
    turned_ref[...] = x_ref[...].T
    tail_ref[...] = turned_ref[turned_ref.shape[0] - SEASON :, :]
    for copy in copies:
        copy.wait()


def prepare(x, m, v, count):
    rank, width = x.shape[1:]
    share = rank // count
    outs = [
        jax.ShapeDtypeStruct((SEASON, rank), F32),
        jax.ShapeDtypeStruct((width, rank), F32),
        jax.ShapeDtypeStruct((rank, width), F32),
    ]
    outs += [jax.ShapeDtypeStruct((3, share, width), F32)] * count
    return pl.pallas_call(
        functools.partial(prepare_kernel, share, count),
        out_shape=tuple(outs),
        in_specs=[far()] * 3,
        out_specs=tuple([whole()] * len(outs)),
        scratch_shapes=[pltpu.SemaphoreType.DMA(()), pltpu.SemaphoreType.DMA((count, 3))],
        compiler_params=params(),
        cost_estimate=cost(0, 6 * rank * width * 4),
        name="prepare",
    )(held(x), held(m), held(v))


def error_kernel(chunks, obs_hbm, bits_hbm, f_hbm, x_ref, err_ref, f_ref, gd_ref, obs_ref, bits_ref, sems):
    words, series = bits_ref.shape
    width = obs_ref.shape[1]
    per = width // words
    rows = series // chunks

    def copies(index):
        part = pl.ds(index * rows, rows)
        return (
            pltpu.make_async_copy(bits_hbm.at[:, part], bits_ref.at[:, part], sems.at[index, 0]),
            pltpu.make_async_copy(f_hbm.at[part, :], f_ref.at[part, :], sems.at[index, 1]),
            pltpu.make_async_copy(obs_hbm.at[part, :], obs_ref.at[part, :], sems.at[index, 2]),
        )

    for index in range(chunks):
        for copy in copies(index):
            copy.start()
    half = x_ref[...].astype(BF16)
    lane = lax.broadcasted_iota(jnp.int32, (words, width), 1)
    word = lax.broadcasted_iota(jnp.int32, (words, width), 0)
    spread = (lane // per == word).astype(BF16)
    flag = jnp.left_shift(1, lax.broadcasted_iota(jnp.int32, (1, width), 1) % per)

    def arrive(index):
        for copy in copies(index):
            copy.wait()

    def predict(index):
        part = pl.ds(index * rows, rows)
        value = lax.dot_general(
            bits_ref[:, part].astype(F32).astype(BF16),
            spread,
            (((0,), (0,)), ((), ())),
            preferred_element_type=F32,
        )
        return value, jnp.dot(f_ref[part, :], half, preferred_element_type=F32)

    def settle(index, value, predicted):
        part = pl.ds(index * rows, rows)
        error = jnp.where(
            jnp.bitwise_and(value.astype(jnp.int32), flag) != 0,
            predicted - obs_ref[part, :].astype(F32),
            0.0,
        ).astype(BF16)
        err_ref[part, :] = error
        term = lax.dot_general(
            f_ref[part, :], error, (((0,), (0,)), ((), ())), preferred_element_type=F32
        )
        if index == 0:
            gd_ref[...] = term
        else:
            gd_ref[...] += term

    arrive(0)
    ready = predict(0)
    for index in range(chunks):
        if index + 1 < chunks:
            arrive(index + 1)
            later = predict(index + 1)
        settle(index, *ready)
        ready = later


def error_step(obs, bits, factors, x):
    series, width = obs.shape
    rank = factors.shape[1]
    words = bits.shape[0]
    chunks = series // rows_of(series, 1024)
    return pl.pallas_call(
        functools.partial(error_kernel, chunks),
        out_shape=(
            jax.ShapeDtypeStruct((series, width), BF16),
            jax.ShapeDtypeStruct((series, rank), BF16),
            jax.ShapeDtypeStruct((rank, width), F32),
        ),
        in_specs=[far(), far(), far(), whole()],
        out_specs=(whole(), whole(), whole()),
        scratch_shapes=[
            pltpu.VMEM((series, width), BF16),
            pltpu.VMEM((words, series), jnp.int32),
            pltpu.SemaphoreType.DMA((chunks, 3)),
        ],
        compiler_params=params(),
        cost_estimate=cost(6 * series * width * rank, series * (3 * width * 2 + words * 4)),
        name="errors",
    )(held(obs), held(bits), held(factors), x)


def factor_kernel(begin, rows, chunks, f_ref, err_ref, turned_ref, *rest):
    out_hbm, out_ref, sems = rest[-3:]
    half = turned_ref[...].astype(BF16)
    size = rows // chunks

    def copy(index):
        return pltpu.make_async_copy(
            out_ref.at[pl.ds(index * size, size), :],
            out_hbm.at[pl.ds(begin + index * size, size), :],
            sems.at[index],
        )

    for index in range(chunks):
        part = pl.ds(begin + index * size, size)
        gradient = jnp.dot(err_ref[part, :], half, preferred_element_type=F32)
        out_ref[pl.ds(index * size, size), :] = (
            f_ref[part, :].astype(F32) - factor_rate * gradient
        ).astype(BF16)
        copy(index).start()
    for index in range(chunks):
        copy(index).wait()


def factor_step(factors, err, turned, after, sofar, begin, rows):
    series, rank = factors.shape
    width = err.shape[1]
    chunks = rows // rows_of(rows, 1024)
    rest = (after,) if sofar is None else (after, sofar)
    return pl.pallas_call(
        functools.partial(factor_kernel, begin, rows, chunks),
        out_shape=jax.ShapeDtypeStruct((series, rank), BF16),
        in_specs=[whole()] * 3 + [pl.BlockSpec(memory_space=pl.ANY)] * len(rest),
        out_specs=far(),
        input_output_aliases={} if sofar is None else {4: 0},
        scratch_shapes=[pltpu.VMEM((rows, rank), BF16), pltpu.SemaphoreType.DMA((chunks,))],
        compiler_params=params(),
        cost_estimate=cost(2 * rows * width * rank, rows * 3 * width * 2),
        name="factors",
    )(factors, err, turned, *rest)


def gradient_kernel(share, count, parts, lanes, stratum, halo_ref, turned_ref, w_ref, gd_ref, *rest):
    outs, (z_ref, r_ref) = rest[: count * parts], rest[count * parts :]
    width, rank = turned_ref.shape
    group = lax.axis_index("grp")
    block_index = lax.rem(lax.axis_index("blk") + stratum[0], lax.axis_size("blk"))
    lags = list(range(1, w_ref.shape[0])) + [SEASON]
    for part in range(rank // lanes):
        columns = slice(part * lanes, (part + 1) * lanes)
        z_ref[part, :SEASON, :] = jnp.where(block_index == 0, 0.0, halo_ref[:, columns])
        z_ref[part, SEASON:, :] = turned_ref[:, columns]
        resid = turned_ref[:, columns]
        for index, lag in enumerate(lags):
            begin = SEASON - lag
            resid = resid - w_ref[index : index + 1, columns] * z_ref[part, begin : begin + width, :]
        r_ref[part, :width, :] = resid
        r_ref[part, width:, :] = jnp.zeros((SEASON, lanes), F32)
        back = resid
        for index, lag in enumerate(lags):
            back = back - w_ref[index : index + 1, columns] * r_ref[part, lag : lag + width, :]
        rows = slice(part * lanes, (part + 1) * lanes)
        gd_ref[rows, :] = data_scale * gd_ref[rows, :] + back.T
    size = share // parts
    for step in range(count):
        start = (group ^ step) * share
        for part in range(parts):
            at = pl.multiple_of(start + part * size, size)
            outs[step * parts + part][...] = gd_ref[pl.ds(at, size), :]


def gradient_step(stratum, halo, turned, weights, gd, count, parts):
    rank, width = gd.shape
    share = rank // count
    lanes = 128
    size = share // parts

    def kernel(stratum, halo_ref, turned_ref, w_ref, gd_ref, *rest):
        work = rest[-1]
        work[...] = gd_ref[...]
        gradient_kernel(share, count, parts, lanes, stratum, halo_ref, turned_ref, w_ref, work, *rest[:-1])

    outs = pl.pallas_call(
        kernel,
        out_shape=tuple([jax.ShapeDtypeStruct((size, width), F32)] * (count * parts)),
        in_specs=[scalars()] + [whole()] * 4,
        out_specs=tuple([whole()] * (count * parts)),
        scratch_shapes=[
            pltpu.VMEM((rank // lanes, SEASON + width, lanes), F32),
            pltpu.VMEM((rank // lanes, SEASON + width, lanes), F32),
            pltpu.VMEM((rank, width), F32),
        ],
        compiler_params=params(),
        cost_estimate=cost(100 * rank * width, 4 * rank * width * 4),
        name="gradient",
    )(stratum, halo, turned, weights, gd)
    return [[outs[step * parts + part] for step in range(count)] for part in range(parts)]


def adam_kernel(part, count, *rest):
    grads, early, out_ref = rest[:count], rest[count : 2 * count], rest[2 * count]
    size = out_ref.shape[1]
    rows = slice(part * size, (part + 1) * size)
    total = [0.0, 0.0, 0.0]
    for step in range(count):
        block, first, second = [early[step][which, rows, :] for which in range(3)]
        gradient = grads[step][...]
        first = beta_one * first + (1.0 - beta_one) * gradient
        second = beta_two * second + (1.0 - beta_two) * gradient * gradient
        block = block - step_rate * first / (jnp.sqrt(second) + adam_eps)
        total = [total[0] + block, total[1] + first, total[2] + second]
    for which in range(3):
        out_ref[which] = total[which] / count


def adam_step(grads, early, part):
    count = len(grads)
    size, width = grads[0].shape
    return pl.pallas_call(
        functools.partial(adam_kernel, part, count),
        out_shape=jax.ShapeDtypeStruct((3, size, width), F32),
        in_specs=[whole()] * (2 * count),
        out_specs=whole(),
        compiler_params=params(),
        cost_estimate=cost(80 * size * width, 20 * size * width * 4),
        name="adam",
    )(*grads, *early)


def place_kernel(base, share, *rest):
    outs, sems = rest[-4:-1], rest[-1]
    count, size = sems.shape[0], rest[0].shape[1]
    group = lax.axis_index("grp")
    copies = []
    for step, part in enumerate(rest[:count]):
        start = pl.multiple_of((group ^ step) * share + base, size)
        for which in range(3):
            copies.append(
                pltpu.make_async_copy(
                    part.at[which], outs[which].at[0, pl.ds(start, size), :], sems.at[step, which]
                )
            )
    for copy in copies:
        copy.start()
    for copy in copies:
        copy.wait()


def place(parts, base, share, sofar):
    count = len(parts)
    width = parts[0].shape[2]
    out = jax.ShapeDtypeStruct((1, count * share, width), F32)
    return pl.pallas_call(
        functools.partial(place_kernel, base, share),
        out_shape=(out, out, out),
        in_specs=[pl.BlockSpec(memory_space=pl.ANY)] * (count + len(sofar)),
        out_specs=(far(), far(), far()),
        input_output_aliases={count + which: which for which in range(len(sofar))},
        scratch_shapes=[pltpu.SemaphoreType.DMA((count, 3))],
        compiler_params=params(),
        cost_estimate=cost(0, 6 * count * parts[0].size * 4),
        name="place",
    )(*parts, *sofar)


def crossed(value, step):
    count = lax.axis_size("grp")
    return lax.ppermute(value, "grp", [(source, source ^ step) for source in range(count)])


def shifted(value, steps):
    count = lax.axis_size("blk")
    return lax.ppermute(value, "blk", [(source, (source + steps) % count) for source in range(count)])


def delivered(value, step):
    groups, slots = lax.axis_size("grp"), lax.axis_size("blk")
    pairs = [
        (group * slots + slot, (group ^ step) * slots + (slot - 1) % slots)
        for group in range(groups)
        for slot in range(slots)
    ]
    return lax.ppermute(value, ("grp", "blk"), pairs)


def body(obs, mask_bits, factors, x_blocks, first_moment, second_moment, ar_weights, stratum):
    count = lax.axis_size("grp")
    pieces = 2

    tail, turned, x, own, *early = prepare(x_blocks, first_moment, second_moment, count)
    halo = shifted(tail, 1)
    early = [own] + [crossed(value, step + 1) for step, value in enumerate(early)]
    err, kept, gd = error_step(obs, mask_bits.T, factors, x)
    grads = gradient_step(stratum, halo, turned, ar_weights, gd, count, pieces)
    grads = [
        [part if step == 0 else crossed(part, step) for step, part in enumerate(row)]
        for row in grads
    ]
    series = obs.shape[0]
    third = series // 3 // 128 * 128

    factor_new = factor_step(kept, err, turned, grads[0][0], None, 0, third)
    grads[0][-1], factor_new = lax.optimization_barrier((grads[0][-1], factor_new))
    means = [adam_step(row, early, index) for index, row in enumerate(grads)]
    direct = [step for step in range(count) if step % 2 == 0]
    moved = [{step: delivered(part, step) for step in direct} for part in means]
    factor_new = factor_step(
        kept, err, turned, means[-1], factor_new, third, series - third
    )
    moved[0], factor_new = lax.optimization_barrier((moved[0], factor_new))
    share = own.shape[1]
    outs = ()
    for index, known in enumerate(moved):
        for step in direct:
            if step + 1 < count:
                known[step + 1] = crossed(known[step], 1)
        parts = [known[step] for step in range(count)]
        outs = place(parts, index * parts[0].shape[1], share, outs)
    return (factor_new, *outs)


def solution(mesh):
    rows = P(("grp", "blk"), None)
    blocks = P("grp", None, "blk")
    return jax.shard_map(
        body,
        mesh=mesh,
        in_specs=(rows, rows, rows, blocks, blocks, blocks, P(), P()),
        out_specs=(rows, blocks, blocks, blocks),
        check_vma=False,
    )
```

time: 50.5 us -> 36.8 us (0.73)
  waiting for transfers between devices: 13.2 us -> 2.5 us
  starting transfers between devices: 11.7 us -> 19 us
  local copies, waits for them, and re-layouts: 6.82 us -> 0.01 us
  Pallas kernels: 17 us -> 13.7 us
    ppermute x0 -> x4, starting transfers between devices: none -> 7.99 us  [delivered(): return lax.ppermute(value, ('grp', 'blk'), pairs)]
    ppermute x6 -> x13, waiting for transfers between devices: 7.26 us -> 0.11 us  [crossed(): lax.ppermute(value, 'grp', [(source, source ^ step) for source in range(c...]
    unnamed x18 -> x2, local copies, waits for them, and re-layouts: 6.82 us -> 0.01 us
    all_to_all x1 -> x0, waiting for transfers between devices: 5.97 us -> none  [body(): grads = lax.all_to_all(grads, 'grp', 0, 0, tiled=True)]
    ppermute x6 -> x13, starting transfers between devices: 2.22 us -> 8 us  [crossed(): lax.ppermute(value, 'grp', [(source, source ^ step) for source in range(c...]
    all_to_all x1 -> x0, starting transfers between devices: 3.41 us -> none  [body(): grads = lax.all_to_all(grads, 'grp', 0, 0, tiled=True)]
    ppermute x2 -> x1, starting transfers between devices: 6.06 us -> 3.02 us  [shifted(): lax.ppermute(value, 'blk', [(source, (source + steps) % count) for source...]
    pallas_call x4 -> x7, Pallas kernels: 8.76 us -> 6.34 us  [the longest x2 3.2 us: factor_step(): pl.pallas_call(functools.partial(factor_kernel, begin, rows, chunks), out...]
  transfers between devices with their start and end apart: 9 -> 18, of which waited for: 3 -> 2; matrix products, arithmetic and copies ran while one was open for 0% -> 0% of each run, Pallas kernels for 25% -> 31%
where the time goes in v3:
time: 36.8 us; the launch traced here: 36.6 us
  starting transfers between devices  19 us (52%)
  Pallas kernels  13.7 us (37%)
  waiting for transfers between devices  2.5 us (7%)
  between operations  1.43 us (4%)
    ppermute x13, starting transfers between devices, crossed(): lax.ppermute(value, 'grp', [(source, source ^ step) for source in range(c...  8 us
    ppermute x4, starting transfers between devices, delivered(): return lax.ppermute(value, ('grp', 'blk'), pairs)  7.99 us
    pallas_call x1, Pallas kernels, error_step(): pl.pallas_call(functools.partial(error_kernel, chunks), out_shape=(jax.Sh...  5.82 us
    pallas_call x2, Pallas kernels, factor_step(): pl.pallas_call(functools.partial(factor_kernel, begin, rows, chunks), out...  3.2 us
    ppermute x1, starting transfers between devices, shifted(): lax.ppermute(value, 'blk', [(source, (source + steps) % count) for source...  3.02 us
    ppermute x4, waiting for transfers between devices, delivered(): return lax.ppermute(value, ('grp', 'blk'), pairs)  2.38 us
    pallas_call x2, Pallas kernels, place(): pl.pallas_call(functools.partial(place_kernel, base, share), out_shape=(o...  1.67 us
    pallas_call x1, Pallas kernels, prepare(): pl.pallas_call(functools.partial(prepare_kernel, share, count), out_shape...  1.56 us
  transfers between devices with their start and end apart: 18, of which 2 were waited for; matrix products, arithmetic and copies ran while one was open for 0% of the time, Pallas kernels for 31%

profile of v3, /device:TPU:0, one launch (start us, length us, event | category | flops | bytes accessed | tf_op | source)
XLA Modules:
  0.0 36.6 jit_solution(763132617025659633)
XLA Ops:
  0.6 1.6 %prepare.1 = (f32[168,256]{1,0:T(8,128)S(1)}, f32[256,256]{1,0:T(8,128)S(1)}, f32[256,256]{1,0:T(8,128)S(1)}, f32[3,64,256]{2,1,0:T(8,128)S(1)}, f32[3,64,256]{2...) custom-call(f32[1,256,256]{2,1,0:T(8,128)} %x_hbm.1, f32[1,256,256]{2,1,0:T(8,128)} %m_hbm.1, ...), custom_call_target="tpu_custom_call" | custom-call | bytes 1572864 | tf_op jit(solution)/shard_map/prepare/pallas_call | solution.py:89
  2.2 3.0 %collective-permute-start = (f32[168,256]{1,0:T(8,128)S(1)}, f32[168,256]{1,0:T(8,128)S(1)}, u32[]{:S(2)}, u32[]{:S(2)}) collective-permute-start(f32[168,256]{1,0:T(8,128)S(1)} %get-tuple-element.33), channel_id=1, source_target_pairs={{0,1},{1,2},{2,3},{3,4},{4,5},{5,6},{6,7},{7,0},{8,9},{9,10},{10,1... | collective-permute-start | bytes 516104 | tf_op jit(solution)/shard_map/ppermute | solution.py:360
  5.2 0.0 collective-permute-start.4
  5.2 1.5 %collective-permute-start.5 = (f32[3,64,256]{2,1,0:T(8,128)S(1)}, f32[3,64,256]{2,1,0:T(8,128)S(1)}, u32[]{:S(2)}, u32[]{:S(2)}) collective-permute-start(f32[3,64,256]{2,1,0:T(8,128)S(1)} %get-tuple-element.46), channel_id=1, source_target_pairs={{0,16},{8,24},{16,0},{24,8},{1,17},{9,25},{17,1},{25,9},{2,18},{10... | collective-permute-start | bytes 589832 | tf_op jit(solution)/shard_map/ppermute | solution.py:355
  6.7 0.4 %collective-permute-start.6 = (f32[3,64,256]{2,1,0:T(8,128)S(1)}, f32[3,64,256]{2,1,0:T(8,128)S(1)}, u32[]{:S(2)}, u32[]{:S(2)}) collective-permute-start(f32[3,64,256]{2,1,0:T(8,128)S(1)} %get-tuple-element.47), channel_id=1, source_target_pairs={{0,24},{8,16},{16,8},{24,0},{1,25},{9,17},{17,9},{25,1},{2,26},{10... | collective-permute-start | bytes 589832 | tf_op jit(solution)/shard_map/ppermute | solution.py:355
  7.7 0.0 copy-start
  7.7 5.8 %errors.1 = (bf16[6144,256]{1,0:T(8,128)(2,1)S(1)}, bf16[6144,256]{1,0:T(8,128)(2,1)S(1)}, f32[256,256]{1,0:T(8,128)S(1)}) custom-call(bf16[6144,256]{1,0:T(8,128)(2,1)} %obs_hbm.1, s32[32,6144]{1,0:T(8,128)} %bitcast.1, bf16[6144,256]{1,0:T(8,128)(2,1)} %f_hbm.1, f32[256,256]{1,0:T(8,128)S(1)} %get-tuple-element.35.x_ref), custom_call_target="tpu_custom_call" | custom-call | flops 2415919104 | bytes 10223616 | tf_op jit(solution)/shard_map/errors/pallas_call | solution.py:169
  13.6 0.0 collective-permute-done.halo_ref
  13.6 0.0 copy-done
  13.6 1.2 %gradient.1 = (f32[32,256]{1,0:T(8,128)S(1)}, f32[32,256]{1,0:T(8,128)S(1)}, f32[32,256]{1,0:T(8,128)S(1)}, f32[32,256]{1,0:T(8,128)S(1)}, f32[32,256]{1,0:T(8,1...) custom-call(s32[1]{0:T(128)S(6)} %copy.20.stratum, ...), custom_call_target="tpu_custom_call" | custom-call | flops 6553600 | bytes 1048576 | tf_op jit(solution)/shard_map/gradient/pallas_call | solution.py:270
  14.8 1.5 %collective-permute-start.3 = (f32[32,256]{1,0:T(8,128)S(1)}, f32[32,256]{1,0:T(8,128)S(1)}, u32[]{:S(2)}, u32[]{:S(2)}) collective-permute-start(f32[32,256]{1,0:T(8,128)S(1)} %get-tuple-element.40), channel_id=1, source_target_pairs={{0,24},{8,16},{16,8},{24,0},{1,25},{9,17},{17,9},{25,1},{2,26},{10... | collective-permute-start | bytes 98312 | tf_op jit(solution)/shard_map/ppermute | solution.py:355
  16.3 0.2 collective-permute-start.1
  16.5 0.0 collective-permute-done.4.rest_5_
  16.5 0.5 %collective-permute-start.2 = (f32[32,256]{1,0:T(8,128)S(1)}, f32[32,256]{1,0:T(8,128)S(1)}, u32[]{:S(2)}, u32[]{:S(2)}) collective-permute-start(f32[32,256]{1,0:T(8,128)S(1)} %get-tuple-element.39), channel_id=1, source_target_pairs={{0,16},{8,24},{16,0},{24,8},{1,17},{9,25},{17,1},{25,9},{2,18},{10... | collective-permute-start | bytes 98312 | tf_op jit(solution)/shard_map/ppermute | solution.py:355
  17.1 0.0 collective-permute-done.5.rest_6_
  17.1 0.0 collective-permute-start.9
  17.1 0.0 collective-permute-done.6.rest_7_
  17.1 1.6 %collective-permute-start.10 = (f32[32,256]{1,0:T(8,128)S(1)}, f32[32,256]{1,0:T(8,128)S(1)}, u32[]{:S(2)}, u32[]{:S(2)}) collective-permute-start(f32[32,256]{1,0:T(8,128)S(1)} %get-tuple-element.50), channel_id=1, source_target_pairs={{0,16},{8,24},{16,0},{24,8},{1,17},{9,25},{17,1},{25,9},{2,18},{10... | collective-permute-start | bytes 98312 | tf_op jit(solution)/shard_map/ppermute | solution.py:355
  18.6 0.0 collective-permute-done.3.rest_3_
  18.6 1.3 %collective-permute-start.11 = (f32[32,256]{1,0:T(8,128)S(1)}, f32[32,256]{1,0:T(8,128)S(1)}, u32[]{:S(2)}, u32[]{:S(2)}) collective-permute-start(f32[32,256]{1,0:T(8,128)S(1)} %get-tuple-element.51), channel_id=1, source_target_pairs={{0,24},{8,16},{16,8},{24,0},{1,25},{9,17},{17,9},{25,1},{2,26},{10... | collective-permute-start | bytes 98312 | tf_op jit(solution)/shard_map/ppermute | solution.py:355
  19.9 1.4 %factors.2.rest_1_ = bf16[6144,256]{1,0:T(8,128)(2,1)} custom-call(bf16[6144,256]{1,0:T(8,128)(2,1)S(1)} %get-tuple-element.41.f_ref, bf16[6144,256]{1,0:T(8,128)(2,1)S(1)} %get-tuple-element.42.err_ref, f32[256,256]{1,0:T(8,128)S(1)} %get-tuple-element.34.turned_ref, f32[32,256]{1,0:T(8,128)S(1)} %get-tuple-element.37.rest_0_), custom_call_target="tpu_custom_call" | custom-call | flops 268435456 | bytes 3145728 | tf_op jit(solution)/shard_map/factors/pallas_call | solution.py:217
  21.3 0.0 collective-permute-done.1.rest_1_
  21.4 0.0 collective-permute-done.2.rest_2_
  21.4 0.1 adam.2
  21.5 3.3 %collective-permute-start.7 = (f32[3,32,256]{2,1,0:T(8,128)S(1)}, f32[3,32,256]{2,1,0:T(8,128)S(1)}, u32[]{:S(2)}, u32[]{:S(2)}) collective-permute-start(f32[3,32,256]{2,1,0:T(8,128)S(1)} %adam.2), channel_id=1, source_target_pairs={{0,7},{1,0},{2,1},{3,2},{4,3},{5,4},{6,5},{7,6},{8,15},{9,8},{10,9... | collective-permute-start | bytes 294920 | tf_op jit(solution)/shard_map/ppermute | solution.py:370
  24.7 1.8 %collective-permute-start.8 = (f32[3,32,256]{2,1,0:T(8,128)S(1)}, f32[3,32,256]{2,1,0:T(8,128)S(1)}, u32[]{:S(2)}, u32[]{:S(2)}) collective-permute-start(f32[3,32,256]{2,1,0:T(8,128)S(1)} %adam.2), channel_id=1, source_target_pairs={{0,23},{1,16},{2,17},{3,18},{4,19},{5,20},{6,21},{7,22},{8,31},{9,... | collective-permute-start | bytes 294920 | tf_op jit(solution)/shard_map/ppermute | solution.py:370
  26.5 0.0 collective-permute-done.9.rest_1_
  26.5 0.0 collective-permute-done.10.rest_2_
  26.5 0.0 collective-permute-done.11.rest_3_
  26.5 0.1 adam.3.rest_0_
  26.6 1.5 %collective-permute-start.12 = (f32[3,32,256]{2,1,0:T(8,128)S(1)}, f32[3,32,256]{2,1,0:T(8,128)S(1)}, u32[]{:S(2)}, u32[]{:S(2)}) collective-permute-start(f32[3,32,256]{2,1,0:T(8,128)S(1)} %adam.3.rest_0_), channel_id=1, source_target_pairs={{0,7},{1,0},{2,1},{3,2},{4,3},{5,4},{6,5},{7,6},{8,15},{9,8},{10,9... | collective-permute-start | bytes 294920 | tf_op jit(solution)/shard_map/ppermute | solution.py:370
  28.1 1.5 %collective-permute-start.14 = (f32[3,32,256]{2,1,0:T(8,128)S(1)}, f32[3,32,256]{2,1,0:T(8,128)S(1)}, u32[]{:S(2)}, u32[]{:S(2)}) collective-permute-start(f32[3,32,256]{2,1,0:T(8,128)S(1)} %adam.3.rest_0_), channel_id=1, source_target_pairs={{0,23},{1,16},{2,17},{3,18},{4,19},{5,20},{6,21},{7,22},{8,31},{9,... | collective-permute-start | bytes 294920 | tf_op jit(solution)/shard_map/ppermute | solution.py:370
  29.6 1.8 %factors.3 = bf16[6144,256]{1,0:T(8,128)(2,1)} custom-call(bf16[6144,256]{1,0:T(8,128)(2,1)S(1)} %get-tuple-element.41.f_ref, bf16[6144,256]{1,0:T(8,128)(2,1)S(1)} %get-tuple-element.42.err_ref, f32[256,256]{1,0:T(8,128)S(1)} %get-tuple-element.34.turned_ref, f32[3,32,256]{2,1,0:T(8,128)S(1)} %adam.3.rest_0_, ...), custom_call_target="tpu_custom_call", output_to_operand_aliasing={{}: (4, {})} | custom-call | flops 536870912 | bytes 6291456 | tf_op jit(solution)/shard_map/factors/pallas_call | solution.py:217
  31.4 0.0 collective-permute-done.7.rest_0_
  31.4 0.0 collective-permute-done.8.rest_2_
  31.4 0.1 collective-permute-start.16
  31.5 0.5 %collective-permute-start.17 = (f32[3,32,256]{2,1,0:T(8,128)S(1)}, f32[3,32,256]{2,1,0:T(8,128)S(1)}, u32[]{:S(2)}, u32[]{:S(2)}) collective-permute-start(f32[3,32,256]{2,1,0:T(8,128)S(1)} %collective-permute-done.8.rest_2_), channel_id=1, source_target_pairs={{0,8},{8,0},{16,24},{24,16},{1,9},{9,1},{17,25},{25,17},{2,10},{10... | collective-permute-start | bytes 294920 | tf_op jit(solution)/shard_map/ppermute | solution.py:355
  32.0 2.4 %collective-permute-done.12.rest_0_ = f32[3,32,256]{2,1,0:T(8,128)S(1)} collective-permute-done((f32[3,32,256]{2,1,0:T(8,128)S(1)}, f32[3,32,256]{2,1,0:T(8,128)S(1)}, u32[]{:S(2)}, u32[]{:S(2)}) %collective-permute-start.12) | collective-permute-done | bytes 98336 | tf_op jit(solution)/shard_map/ppermute | solution.py:370
  34.3 0.0 collective-permute-start.13
  34.4 0.0 collective-permute-done.14.rest_2_
  34.4 0.5 %collective-permute-start.15 = (f32[3,32,256]{2,1,0:T(8,128)S(1)}, f32[3,32,256]{2,1,0:T(8,128)S(1)}, u32[]{:S(2)}, u32[]{:S(2)}) collective-permute-start(f32[3,32,256]{2,1,0:T(8,128)S(1)} %collective-permute-done.14.rest_2_), channel_id=1, source_target_pairs={{0,8},{8,0},{16,24},{24,16},{1,9},{9,1},{17,25},{25,17},{2,10},{10... | collective-permute-start | bytes 294920 | tf_op jit(solution)/shard_map/ppermute | solution.py:355
  34.9 0.0 collective-permute-done.16.rest_1_
  34.9 0.0 collective-permute-done.17.rest_3_
  34.9 0.8 %place.2 = (f32[1,256,256]{2,1,0:T(8,128)}, f32[1,256,256]{2,1,0:T(8,128)}, f32[1,256,256]{2,1,0:T(8,128)}) custom-call(f32[3,32,256]{2,1,0:T(8,128)S(1)} %collective-permute-done.7.rest_0_, f32[3,32,256]{2,1,0:T(8,128)S(1)} %collective-permute-done.16.rest_1_, f32[3,32,256]{2,1,0:T(8,128)S(1)} %collective-permute-done.8.rest_2_, ...), custom_call_target="tpu_custom_call" | custom-call | bytes 2359296 | tf_op jit(solution)/shard_map/place/pallas_call | solution.py:340
  35.7 0.0 collective-permute-done.13.rest_1_
  35.7 0.1 collective-permute-done.15.rest_3_
  35.8 0.8 %place.3 = (f32[1,256,256]{2,1,0:T(8,128)}, f32[1,256,256]{2,1,0:T(8,128)}, f32[1,256,256]{2,1,0:T(8,128)}) custom-call(f32[3,32,256]{2,1,0:T(8,128)S(1)} %collective-permute-done.12.rest_0_, f32[3,32,256]{2,1,0:T(8,128)S(1)} %collective-permute-done.13.rest_1_, ...), custom_call_target="tpu_custom_call", output_to_operand_aliasing={{0}: (4, {}), {1}: (5, {}), {2}: (6, {})} | custom-call | bytes 2359296 | tf_op jit(solution)/shard_map/place/pallas_call | solution.py:340
Async XLA Ops:
  2.2 11.4 %collective-permute-start = (f32[168,256]{1,0:T(8,128)S(1)}, f32[168,256]{1,0:T(8,128)S(1)}, u32[]{:S(2)}, u32[]{:S(2)}) collective-permute-start(f32[168,256]{1,0:T(8,128)S(1)} %get-tuple-element.33), channel_id=1, source_target_pairs={{0,1},{1,2},{2,3},{3,4},{4,5},{5,6},{6,7},{7,0},{8,9},{9,10},{10,1... | collective-permute-start | bytes 516104 | tf_op jit(solution)/shard_map/ppermute | solution.py:360
  5.2 11.3 %collective-permute-start.4 = (f32[3,64,256]{2,1,0:T(8,128)S(1)}, f32[3,64,256]{2,1,0:T(8,128)S(1)}, u32[]{:S(2)}, u32[]{:S(2)}) collective-permute-start(f32[3,64,256]{2,1,0:T(8,128)S(1)} %get-tuple-element.45), channel_id=1, source_target_pairs={{0,8},{8,0},{16,24},{24,16},{1,9},{9,1},{17,25},{25,17},{2,10},{10... | collective-permute-start | bytes 589832 | tf_op jit(solution)/shard_map/ppermute | solution.py:355
  5.2 11.8 %collective-permute-start.5 = (f32[3,64,256]{2,1,0:T(8,128)S(1)}, f32[3,64,256]{2,1,0:T(8,128)S(1)}, u32[]{:S(2)}, u32[]{:S(2)}) collective-permute-start(f32[3,64,256]{2,1,0:T(8,128)S(1)} %get-tuple-element.46), channel_id=1, source_target_pairs={{0,16},{8,24},{16,0},{24,8},{1,17},{9,25},{17,1},{25,9},{2,18},{10... | collective-permute-start | bytes 589832 | tf_op jit(solution)/shard_map/ppermute | solution.py:355
  6.7 10.4 %collective-permute-start.6 = (f32[3,64,256]{2,1,0:T(8,128)S(1)}, f32[3,64,256]{2,1,0:T(8,128)S(1)}, u32[]{:S(2)}, u32[]{:S(2)}) collective-permute-start(f32[3,64,256]{2,1,0:T(8,128)S(1)} %get-tuple-element.47), channel_id=1, source_target_pairs={{0,24},{8,16},{16,8},{24,0},{1,25},{9,17},{17,9},{25,1},{2,26},{10... | collective-permute-start | bytes 589832 | tf_op jit(solution)/shard_map/ppermute | solution.py:355
  7.7 5.9 %copy-start = (f32[25,256]{1,0:T(8,128)S(1)}, f32[25,256]{1,0:T(8,128)}, u32[]{:S(2)}) copy-start(f32[25,256]{1,0:T(8,128)} %w_ref.1) | copy-start | bytes 76804
  14.8 3.8 %collective-permute-start.3 = (f32[32,256]{1,0:T(8,128)S(1)}, f32[32,256]{1,0:T(8,128)S(1)}, u32[]{:S(2)}, u32[]{:S(2)}) collective-permute-start(f32[32,256]{1,0:T(8,128)S(1)} %get-tuple-element.40), channel_id=1, source_target_pairs={{0,24},{8,16},{16,8},{24,0},{1,25},{9,17},{17,9},{25,1},{2,26},{10... | collective-permute-start | bytes 98312 | tf_op jit(solution)/shard_map/ppermute | solution.py:355
  16.3 5.0 %collective-permute-start.1 = (f32[32,256]{1,0:T(8,128)S(1)}, f32[32,256]{1,0:T(8,128)S(1)}, u32[]{:S(2)}, u32[]{:S(2)}) collective-permute-start(f32[32,256]{1,0:T(8,128)S(1)} %get-tuple-element.38), channel_id=1, source_target_pairs={{0,8},{8,0},{16,24},{24,16},{1,9},{9,1},{17,25},{25,17},{2,10},{10... | collective-permute-start | bytes 98312 | tf_op jit(solution)/shard_map/ppermute | solution.py:355
  16.5 4.8 %collective-permute-start.2 = (f32[32,256]{1,0:T(8,128)S(1)}, f32[32,256]{1,0:T(8,128)S(1)}, u32[]{:S(2)}, u32[]{:S(2)}) collective-permute-start(f32[32,256]{1,0:T(8,128)S(1)} %get-tuple-element.39), channel_id=1, source_target_pairs={{0,16},{8,24},{16,0},{24,8},{1,17},{9,25},{17,1},{25,9},{2,18},{10... | collective-permute-start | bytes 98312 | tf_op jit(solution)/shard_map/ppermute | solution.py:355
  17.1 9.5 %collective-permute-start.9 = (f32[32,256]{1,0:T(8,128)S(1)}, f32[32,256]{1,0:T(8,128)S(1)}, u32[]{:S(2)}, u32[]{:S(2)}) collective-permute-start(f32[32,256]{1,0:T(8,128)S(1)} %get-tuple-element.49), channel_id=1, source_target_pairs={{0,8},{8,0},{16,24},{24,16},{1,9},{9,1},{17,25},{25,17},{2,10},{10... | collective-permute-start | bytes 98312 | tf_op jit(solution)/shard_map/ppermute | solution.py:355
  17.1 9.5 %collective-permute-start.10 = (f32[32,256]{1,0:T(8,128)S(1)}, f32[32,256]{1,0:T(8,128)S(1)}, u32[]{:S(2)}, u32[]{:S(2)}) collective-permute-start(f32[32,256]{1,0:T(8,128)S(1)} %get-tuple-element.50), channel_id=1, source_target_pairs={{0,16},{8,24},{16,0},{24,8},{1,17},{9,25},{17,1},{25,9},{2,18},{10... | collective-permute-start | bytes 98312 | tf_op jit(solution)/shard_map/ppermute | solution.py:355
  18.6 7.9 %collective-permute-start.11 = (f32[32,256]{1,0:T(8,128)S(1)}, f32[32,256]{1,0:T(8,128)S(1)}, u32[]{:S(2)}, u32[]{:S(2)}) collective-permute-start(f32[32,256]{1,0:T(8,128)S(1)} %get-tuple-element.51), channel_id=1, source_target_pairs={{0,24},{8,16},{16,8},{24,0},{1,25},{9,17},{17,9},{25,1},{2,26},{10... | collective-permute-start | bytes 98312 | tf_op jit(solution)/shard_map/ppermute | solution.py:355
  21.5 9.9 %collective-permute-start.7 = (f32[3,32,256]{2,1,0:T(8,128)S(1)}, f32[3,32,256]{2,1,0:T(8,128)S(1)}, u32[]{:S(2)}, u32[]{:S(2)}) collective-permute-start(f32[3,32,256]{2,1,0:T(8,128)S(1)} %adam.2), channel_id=1, source_target_pairs={{0,7},{1,0},{2,1},{3,2},{4,3},{5,4},{6,5},{7,6},{8,15},{9,8},{10,9... | collective-permute-start | bytes 294920 | tf_op jit(solution)/shard_map/ppermute | solution.py:370
  24.7 6.6 %collective-permute-start.8 = (f32[3,32,256]{2,1,0:T(8,128)S(1)}, f32[3,32,256]{2,1,0:T(8,128)S(1)}, u32[]{:S(2)}, u32[]{:S(2)}) collective-permute-start(f32[3,32,256]{2,1,0:T(8,128)S(1)} %adam.2), channel_id=1, source_target_pairs={{0,23},{1,16},{2,17},{3,18},{4,19},{5,20},{6,21},{7,22},{8,31},{9,... | collective-permute-start | bytes 294920 | tf_op jit(solution)/shard_map/ppermute | solution.py:370
  26.6 7.7 %collective-permute-start.12 = (f32[3,32,256]{2,1,0:T(8,128)S(1)}, f32[3,32,256]{2,1,0:T(8,128)S(1)}, u32[]{:S(2)}, u32[]{:S(2)}) collective-permute-start(f32[3,32,256]{2,1,0:T(8,128)S(1)} %adam.3.rest_0_), channel_id=1, source_target_pairs={{0,7},{1,0},{2,1},{3,2},{4,3},{5,4},{6,5},{7,6},{8,15},{9,8},{10,9... | collective-permute-start | bytes 294920 | tf_op jit(solution)/shard_map/ppermute | solution.py:370
  28.1 6.2 %collective-permute-start.14 = (f32[3,32,256]{2,1,0:T(8,128)S(1)}, f32[3,32,256]{2,1,0:T(8,128)S(1)}, u32[]{:S(2)}, u32[]{:S(2)}) collective-permute-start(f32[3,32,256]{2,1,0:T(8,128)S(1)} %adam.3.rest_0_), channel_id=1, source_target_pairs={{0,23},{1,16},{2,17},{3,18},{4,19},{5,20},{6,21},{7,22},{8,31},{9,... | collective-permute-start | bytes 294920 | tf_op jit(solution)/shard_map/ppermute | solution.py:370
  31.4 3.5 %collective-permute-start.16 = (f32[3,32,256]{2,1,0:T(8,128)S(1)}, f32[3,32,256]{2,1,0:T(8,128)S(1)}, u32[]{:S(2)}, u32[]{:S(2)}) collective-permute-start(f32[3,32,256]{2,1,0:T(8,128)S(1)} %collective-permute-done.7.rest_0_), channel_id=1, source_target_pairs={{0,8},{8,0},{16,24},{24,16},{1,9},{9,1},{17,25},{25,17},{2,10},{10... | collective-permute-start | bytes 294920 | tf_op jit(solution)/shard_map/ppermute | solution.py:355
  31.5 3.4 %collective-permute-start.17 = (f32[3,32,256]{2,1,0:T(8,128)S(1)}, f32[3,32,256]{2,1,0:T(8,128)S(1)}, u32[]{:S(2)}, u32[]{:S(2)}) collective-permute-start(f32[3,32,256]{2,1,0:T(8,128)S(1)} %collective-permute-done.8.rest_2_), channel_id=1, source_target_pairs={{0,8},{8,0},{16,24},{24,16},{1,9},{9,1},{17,25},{25,17},{2,10},{10... | collective-permute-start | bytes 294920 | tf_op jit(solution)/shard_map/ppermute | solution.py:355
  34.3 1.4 %collective-permute-start.13 = (f32[3,32,256]{2,1,0:T(8,128)S(1)}, f32[3,32,256]{2,1,0:T(8,128)S(1)}, u32[]{:S(2)}, u32[]{:S(2)}) collective-permute-start(f32[3,32,256]{2,1,0:T(8,128)S(1)} %collective-permute-done.12.rest_0_), channel_id=1, source_target_pairs={{0,8},{8,0},{16,24},{24,16},{1,9},{9,1},{17,25},{25,17},{2,10},{10... | collective-permute-start | bytes 294920 | tf_op jit(solution)/shard_map/ppermute | solution.py:355
  34.4 1.5 %collective-permute-start.15 = (f32[3,32,256]{2,1,0:T(8,128)S(1)}, f32[3,32,256]{2,1,0:T(8,128)S(1)}, u32[]{:S(2)}, u32[]{:S(2)}) collective-permute-start(f32[3,32,256]{2,1,0:T(8,128)S(1)} %collective-permute-done.14.rest_2_), channel_id=1, source_target_pairs={{0,8},{8,0},{16,24},{24,16},{1,9},{9,1},{17,25},{25,17},{2,10},{10... | collective-permute-start | bytes 294920 | tf_op jit(solution)/shard_map/ppermute | solution.py:355

commit v4 on v3

v4 whole, which is shorter than its diff:
```python
import functools

import jax
import jax.numpy as jnp
from jax import lax
from jax.experimental import pallas as pl
from jax.experimental.pallas import tpu as pltpu
from jax.sharding import PartitionSpec as P

SEASON = 168

beta_one = 0.9
beta_two = 0.999
adam_eps = 1e-08
step_rate = 0.05
factor_rate = 0.002
data_scale = 0.25

LIMIT = 32 * 1024 * 1024
F32 = jnp.float32
BF16 = jnp.bfloat16


def whole():
    return pl.BlockSpec(memory_space=pltpu.VMEM)


def far():
    return pl.BlockSpec(memory_space=pltpu.HBM)


def held(value):
    return pltpu.with_memory_space_constraint(value, pltpu.HBM)


def scalars():
    return pl.BlockSpec(memory_space=pltpu.SMEM)


def params(**more):
    return pltpu.CompilerParams(vmem_limit_bytes=LIMIT, **more)


def cost(flops, moved):
    return pl.CostEstimate(flops=int(flops), bytes_accessed=int(moved), transcendentals=0)


def rows_of(total, most):
    best = total
    for rows in range(128, most + 1, 128):
        if total % rows == 0:
            best = rows
    return best


def prepare_kernel(x_hbm, tail_ref, turned_ref, x_ref, sem):
    copy = pltpu.make_async_copy(x_hbm.at[0], x_ref, sem)
    copy.start()
    copy.wait()
    turned_ref[...] = x_ref[...].T
    tail_ref[...] = turned_ref[turned_ref.shape[0] - SEASON :, :]


def prepare(x):
    rank, width = x.shape[1:]
    return pl.pallas_call(
        prepare_kernel,
        out_shape=(
            jax.ShapeDtypeStruct((SEASON, rank), F32),
            jax.ShapeDtypeStruct((width, rank), F32),
            jax.ShapeDtypeStruct((rank, width), F32),
        ),
        in_specs=[far()],
        out_specs=(whole(), whole(), whole()),
        scratch_shapes=[pltpu.SemaphoreType.DMA(())],
        compiler_params=params(),
        cost_estimate=cost(0, 4 * rank * width * 4),
        name="prepare",
    )(held(x))


def error_kernel(rows, obs_hbm, bits_hbm, f_hbm, x_ref, err_ref, f_ref, gd_ref, obs_ref, bits_ref, *rest):
    (value_a, value_b, predicted_a, predicted_b), sems = rest[:4], rest[4]
    words, series = bits_ref.shape
    width = obs_ref.shape[1]
    per = width // words
    chunks = series // rows

    def lines(index):
        return pl.ds(pl.multiple_of(index * rows, rows), rows)

    def copies(index):
        part = lines(index)
        return (
            pltpu.make_async_copy(bits_hbm.at[:, part], bits_ref.at[:, part], sems.at[index, 0]),
            pltpu.make_async_copy(f_hbm.at[part, :], f_ref.at[part, :], sems.at[index, 1]),
            pltpu.make_async_copy(obs_hbm.at[part, :], obs_ref.at[part, :], sems.at[index, 2]),
        )

    @pl.loop(0, chunks)
    def _(index):
        for copy in copies(index):
            copy.start()

    half = x_ref[...].astype(BF16)
    lane = lax.broadcasted_iota(jnp.int32, (words, width), 1)
    word = lax.broadcasted_iota(jnp.int32, (words, width), 0)
    spread = (lane // per == word).astype(BF16)
    flag = jnp.left_shift(1, lax.broadcasted_iota(jnp.int32, (1, width), 1) % per)
    gd_ref[...] = jnp.zeros_like(gd_ref)

    def predict(index, value_ref, predicted_ref):
        for copy in copies(index):
            copy.wait()
        part = lines(index)
        value_ref[...] = lax.dot_general(
            bits_ref[:, part].astype(F32).astype(BF16),
            spread,
            (((0,), (0,)), ((), ())),
            preferred_element_type=F32,
        )
        predicted_ref[...] = jnp.dot(f_ref[part, :], half, preferred_element_type=F32)

    def settle(index, value_ref, predicted_ref):
        part = lines(index)
        error = jnp.where(
            jnp.bitwise_and(value_ref[...].astype(jnp.int32), flag) != 0,
            predicted_ref[...] - obs_ref[part, :].astype(F32),
            0.0,
        ).astype(BF16)
        err_ref[part, :] = error
        gd_ref[...] += lax.dot_general(
            f_ref[part, :], error, (((0,), (0,)), ((), ())), preferred_element_type=F32
        )

    predict(0, value_a, predicted_a)

    @pl.loop(0, (chunks - 1) // 2)
    def _(pair):
        predict(2 * pair + 1, value_b, predicted_b)
        settle(2 * pair, value_a, predicted_a)
        predict(2 * pair + 2, value_a, predicted_a)
        settle(2 * pair + 1, value_b, predicted_b)

    if chunks % 2 == 0:
        predict(chunks - 1, value_b, predicted_b)
        settle(chunks - 2, value_a, predicted_a)
        settle(chunks - 1, value_b, predicted_b)
    else:
        settle(chunks - 1, value_a, predicted_a)


def error_step(obs, bits, factors, x):
    series, width = obs.shape
    rank = factors.shape[1]
    words = bits.shape[0]
    rows = rows_of(series, 512)
    return pl.pallas_call(
        functools.partial(error_kernel, rows),
        out_shape=(
            jax.ShapeDtypeStruct((series, width), BF16),
            jax.ShapeDtypeStruct((series, rank), BF16),
            jax.ShapeDtypeStruct((rank, width), F32),
        ),
        in_specs=[far(), far(), far(), whole()],
        out_specs=(whole(), whole(), whole()),
        scratch_shapes=[
            pltpu.VMEM((series, width), BF16),
            pltpu.VMEM((words, series), jnp.int32),
            pltpu.VMEM((rows, width), F32),
            pltpu.VMEM((rows, width), F32),
            pltpu.VMEM((rows, width), F32),
            pltpu.VMEM((rows, width), F32),
            pltpu.SemaphoreType.DMA((series // rows, 3)),
        ],
        compiler_params=params(),
        cost_estimate=cost(6 * series * width * rank, series * (3 * width * 2 + words * 4)),
        name="errors",
    )(held(obs), held(bits), held(factors), x)


def factor_kernel(begin, rows, chunks, f_ref, err_ref, turned_ref, *rest):
    out_hbm, out_ref, sems = rest[-3:]
    half = turned_ref[...].astype(BF16)
    size = rows // chunks

    def copy(index):
        return pltpu.make_async_copy(
            out_ref.at[pl.ds(index * size, size), :],
            out_hbm.at[pl.ds(begin + index * size, size), :],
            sems.at[index],
        )

    for index in range(chunks):
        part = pl.ds(begin + index * size, size)
        gradient = jnp.dot(err_ref[part, :], half, preferred_element_type=F32)
        out_ref[pl.ds(index * size, size), :] = (
            f_ref[part, :].astype(F32) - factor_rate * gradient
        ).astype(BF16)
        copy(index).start()
    for index in range(chunks):
        copy(index).wait()


def factor_step(factors, err, turned, after, sofar, begin, rows):
    series, rank = factors.shape
    width = err.shape[1]
    chunks = rows // rows_of(rows, 1024)
    rest = (after,) if sofar is None else (after, sofar)
    return pl.pallas_call(
        functools.partial(factor_kernel, begin, rows, chunks),
        out_shape=jax.ShapeDtypeStruct((series, rank), BF16),
        in_specs=[whole()] * 3 + [pl.BlockSpec(memory_space=pl.ANY)] * len(rest),
        out_specs=far(),
        input_output_aliases={} if sofar is None else {4: 0},
        scratch_shapes=[pltpu.VMEM((rows, rank), BF16), pltpu.SemaphoreType.DMA((chunks,))],
        compiler_params=params(),
        cost_estimate=cost(2 * rows * width * rank, rows * 3 * width * 2),
        name="factors",
    )(factors, err, turned, *rest)


def update_kernel(
    count, pieces, lanes, stratum, halo_ref, turned_ref, w_ref, gd_ref, x_ref, m_hbm, v_hbm, *rest
):
    outs, (z_ref, r_ref, m_ref, v_ref, new_ref, sems) = rest[: 2 * pieces], rest[2 * pieces :]
    m_copy = pltpu.make_async_copy(m_hbm.at[0], m_ref, sems.at[0])
    v_copy = pltpu.make_async_copy(v_hbm.at[0], v_ref, sems.at[1])
    m_copy.start()
    v_copy.start()
    width, rank = turned_ref.shape
    share = rank // count
    block_index = lax.rem(lax.axis_index("blk") + stratum[0], lax.axis_size("blk"))
    lags = list(range(1, w_ref.shape[0])) + [SEASON]
    for part in range(rank // lanes):
        columns = slice(part * lanes, (part + 1) * lanes)
        z_ref[part, :SEASON, :] = jnp.where(block_index == 0, 0.0, halo_ref[:, columns])
        z_ref[part, SEASON:, :] = turned_ref[:, columns]
        resid = turned_ref[:, columns]
        for index, lag in enumerate(lags):
            begin = SEASON - lag
            resid = resid - w_ref[index : index + 1, columns] * z_ref[part, begin : begin + width, :]
        r_ref[part, :width, :] = resid
        r_ref[part, width:, :] = jnp.zeros((SEASON, lanes), F32)
        back = resid
        for index, lag in enumerate(lags):
            back = back - w_ref[index : index + 1, columns] * r_ref[part, lag : lag + width, :]
        z_ref[part, :width, :] = back
    m_copy.wait()
    v_copy.wait()
    for part in range(rank // lanes):
        rows = slice(part * lanes, (part + 1) * lanes)
        gradient = data_scale * gd_ref[rows, :] + z_ref[part, :width, :].T
        first = beta_one * m_ref[rows, :] + (1.0 - beta_one) * gradient
        second = beta_two * v_ref[rows, :] + (1.0 - beta_two) * gradient * gradient
        new_ref[0, rows, :] = x_ref[rows, :] - step_rate * first / (jnp.sqrt(second) + adam_eps)
        new_ref[1, rows, :] = first
        new_ref[2, rows, :] = second
    size = share // pieces
    odd = lax.axis_index("grp") % 2
    for piece in range(pieces):
        for line in range(count // 2):
            for side in range(2):
                one = 2 * line + (odd if side == 0 else 1 - odd)
                start = pl.multiple_of(one * share + piece * size, size)
                for which in range(3):
                    outs[2 * piece + side][which, line] = new_ref[which, pl.ds(start, size), :]


def update_step(stratum, halo, turned, weights, gd, x, m, v, count, pieces):
    rank, width = gd.shape
    lanes = 128
    size = rank // count // pieces
    out = jax.ShapeDtypeStruct((3, count // 2, size, width), F32)
    outs = pl.pallas_call(
        functools.partial(update_kernel, count, pieces, lanes),
        out_shape=(out,) * (2 * pieces),
        in_specs=[scalars()] + [whole()] * 5 + [far()] * 2,
        out_specs=(whole(),) * (2 * pieces),
        scratch_shapes=[
            pltpu.VMEM((rank // lanes, SEASON + width, lanes), F32),
            pltpu.VMEM((rank // lanes, SEASON + width, lanes), F32),
            pltpu.VMEM((rank, width), F32),
            pltpu.VMEM((rank, width), F32),
            pltpu.VMEM((3, rank, width), F32),
            pltpu.SemaphoreType.DMA((2,)),
        ],
        compiler_params=params(),
        cost_estimate=cost(120 * rank * width, 10 * rank * width * 4),
        name="update",
    )(stratum, halo, turned, weights, gd, x, held(m), held(v))
    return [(outs[2 * piece], outs[2 * piece + 1]) for piece in range(pieces)]


def halve_kernel(level, kept_ref, got_ref, keep_ref, send_ref):
    mine = (lax.axis_index("grp") // level) % 2
    for line in range(keep_ref.shape[1]):
        for out, side in ((keep_ref, mine), (send_ref, 1 - mine)):
            for which in range(3):
                out[which, line] = kept_ref[which, 2 * line + side] + got_ref[which, 2 * line + side]


def halve(kept, got, level):
    _, lines, size, width = kept.shape
    out = jax.ShapeDtypeStruct((3, lines // 2, size, width), F32)
    return pl.pallas_call(
        functools.partial(halve_kernel, level),
        out_shape=(out, out),
        in_specs=[whole(), whole()],
        out_specs=(whole(), whole()),
        compiler_params=params(),
        cost_estimate=cost(kept.size, 3 * kept.size * 4),
        name="halve",
    )(kept, got)


def mean_kernel(count, kept_ref, got_ref, out_ref):
    for which in range(3):
        out_ref[which] = (kept_ref[which, 0] + got_ref[which, 0]) / count


def mean(kept, got, count):
    _, _, size, width = kept.shape
    return pl.pallas_call(
        functools.partial(mean_kernel, count),
        out_shape=jax.ShapeDtypeStruct((3, size, width), F32),
        in_specs=[whole(), whole()],
        out_specs=whole(),
        compiler_params=params(),
        cost_estimate=cost(2 * kept.size, 3 * kept.size * 4),
        name="mean",
    )(kept, got)


def place_kernel(count, share, *rest):
    parts, outs, sems = rest[:-4], rest[-4:-1], rest[-1]
    size = parts[0].shape[1]
    group = lax.axis_index("grp")
    copies = []
    for index, part in enumerate(parts):
        piece, step = divmod(index, count)
        start = pl.multiple_of((group ^ step) * share + piece * size, size)
        for which in range(3):
            copies.append(
                pltpu.make_async_copy(
                    part.at[which], outs[which].at[0, pl.ds(start, size), :], sems.at[index, which]
                )
            )
    for copy in copies:
        copy.start()
    for copy in copies:
        copy.wait()


def place(pieces):
    parts = [part for piece in pieces for part in piece]
    count = len(pieces[0])
    _, size, width = parts[0].shape
    share = size * len(pieces)
    out = jax.ShapeDtypeStruct((1, count * share, width), F32)
    return pl.pallas_call(
        functools.partial(place_kernel, count, share),
        out_shape=(out, out, out),
        in_specs=[pl.BlockSpec(memory_space=pl.ANY)] * len(parts),
        out_specs=(far(), far(), far()),
        scratch_shapes=[pltpu.SemaphoreType.DMA((len(parts), 3))],
        compiler_params=params(),
        cost_estimate=cost(0, 6 * count * share * width * 4),
        name="place",
    )(*parts)


def crossed(value, step):
    count = lax.axis_size("grp")
    return lax.ppermute(value, "grp", [(source, source ^ step) for source in range(count)])


def shifted(value, steps):
    count = lax.axis_size("blk")
    return lax.ppermute(value, "blk", [(source, (source + steps) % count) for source in range(count)])


def delivered(value, step):
    groups, slots = lax.axis_size("grp"), lax.axis_size("blk")
    pairs = [
        (group * slots + slot, (group ^ step) * slots + (slot - 1) % slots)
        for group in range(groups)
        for slot in range(slots)
    ]
    return lax.ppermute(value, ("grp", "blk"), pairs)


def body(obs, mask_bits, factors, x_blocks, first_moment, second_moment, ar_weights, stratum):
    count = lax.axis_size("grp")
    series = obs.shape[0]
    third = series // 3 // 128 * 128

    tail, turned, x = prepare(x_blocks)
    halo = shifted(tail, 1)
    err, kept, gd = error_step(obs, mask_bits.T, factors, x)
    (keep0, send0), (keep1, send1) = update_step(
        stratum, halo, turned, ar_weights, gd, x, first_moment, second_moment, count, 2
    )

    got0 = crossed(send0, 1)
    got1 = crossed(send1, 1)
    keep0, send0 = halve(keep0, got0, 2)
    far0 = crossed(send0, 2)
    factor_new = factor_step(kept, err, turned, send0, None, 0, third)
    got1, factor_new = lax.optimization_barrier((got1, factor_new))
    keep1, send1 = halve(keep1, got1, 2)
    far1 = crossed(send1, 2)
    mean0 = mean(keep0, far0, count)

    near0 = delivered(mean0, 0)
    mean1 = mean(keep1, far1, count)
    near1 = delivered(mean1, 0)
    side1 = delivered(mean1, 2)
    side0 = crossed(near0, 2)
    factor_new = factor_step(kept, err, turned, near0, factor_new, third, series - third)
    near1, side0, side1, factor_new = lax.optimization_barrier((near1, side0, side1, factor_new))
    pieces = [
        [near0, crossed(near0, 1), side0, crossed(side0, 1)],
        [near1, crossed(near1, 1), side1, crossed(side1, 1)],
    ]
    return (factor_new, *place(pieces))


def solution(mesh):
    rows = P(("grp", "blk"), None)
    blocks = P("grp", None, "blk")
    return jax.shard_map(
        body,
        mesh=mesh,
        in_specs=(rows, rows, rows, blocks, blocks, blocks, P(), P()),
        out_specs=(rows, blocks, blocks, blocks),
        check_vma=False,
    )
```

time: 36.8 us -> 36.3 us (0.986)
  starting transfers between devices: 19 us -> 15.6 us
  waiting for transfers between devices: 2.5 us -> 5.24 us
    ppermute x13 -> x9, waiting for transfers between devices: 0.11 us -> 4.84 us  [crossed(): lax.ppermute(value, 'grp', [(source, source ^ step) for source in range(c...]
    ppermute x13 -> x9, starting transfers between devices: 8 us -> 4.49 us  [crossed(): lax.ppermute(value, 'grp', [(source, source ^ step) for source in range(c...]
    ppermute x4 -> x3, waiting for transfers between devices: 2.38 us -> 0.4 us  [delivered(): return lax.ppermute(value, ('grp', 'blk'), pairs)]
    pallas_call x7 -> x8, Pallas kernels: 10.5 us -> 10.7 us  [the longest x1 6.83 us: error_step(): pl.pallas_call(functools.partial(error_kernel, rows), out_shape=(jax.Shap...]
    ppermute x4 -> x3, starting transfers between devices: 7.99 us -> 8.13 us  [delivered(): return lax.ppermute(value, ('grp', 'blk'), pairs)]
  transfers between devices with their start and end apart: 18 -> 13, of which waited for: 2 -> 7; matrix products, arithmetic and copies ran while one was open for 0% -> 0% of each run, Pallas kernels for 31% -> 28%
where the time goes in v4:
time: 36.3 us; the launch traced here: 36.2 us
  starting transfers between devices  15.6 us (43%)
  Pallas kernels  13.9 us (38%)
  waiting for transfers between devices  5.24 us (14%)
  between operations  1.4 us (4%)
    ppermute x3, starting transfers between devices, delivered(): return lax.ppermute(value, ('grp', 'blk'), pairs)  8.13 us
    pallas_call x1, Pallas kernels, error_step(): pl.pallas_call(functools.partial(error_kernel, rows), out_shape=(jax.Shap...  6.83 us
    ppermute x9, waiting for transfers between devices, crossed(): lax.ppermute(value, 'grp', [(source, source ^ step) for source in range(c...  4.84 us
    ppermute x9, starting transfers between devices, crossed(): lax.ppermute(value, 'grp', [(source, source ^ step) for source in range(c...  4.49 us
    pallas_call x2, Pallas kernels, factor_step(): pl.pallas_call(functools.partial(factor_kernel, begin, rows, chunks), out...  3.21 us
    ppermute x1, starting transfers between devices, shifted(): lax.ppermute(value, 'blk', [(source, (source + steps) % count) for source...  3.02 us
    pallas_call x1, Pallas kernels, update_step(): pl.pallas_call(functools.partial(update_kernel, count, pieces, lanes), ou...  1.6 us
    pallas_call x1, Pallas kernels, prepare(): pl.pallas_call(prepare_kernel, out_shape=(jax.ShapeDtypeStruct((SEASON, r...  1.09 us
  transfers between devices with their start and end apart: 13, of which 7 were waited for; matrix products, arithmetic and copies ran while one was open for 0% of the time, Pallas kernels for 28%

profile of v4, /device:TPU:0, one launch (start us, length us, event | category | flops | bytes accessed | tf_op | source)
XLA Modules:
  0.0 36.2 jit_solution(8083892975183754521)
XLA Ops:
  0.6 1.1 %prepare.1 = (f32[168,256]{1,0:T(8,128)S(1)}, f32[256,256]{1,0:T(8,128)S(1)}, f32[256,256]{1,0:T(8,128)S(1)}) custom-call(f32[1,256,256]{2,1,0:T(8,128)} %x_hbm.1), custom_call_target="tpu_custom_call" | custom-call | bytes 1048576 | tf_op jit(solution)/shard_map/prepare/pallas_call | solution.py:66
  1.7 3.0 %collective-permute-start = (f32[168,256]{1,0:T(8,128)S(1)}, f32[168,256]{1,0:T(8,128)S(1)}, u32[]{:S(2)}, u32[]{:S(2)}) collective-permute-start(f32[168,256]{1,0:T(8,128)S(1)} %get-tuple-element.27), channel_id=1, source_target_pairs={{0,1},{1,2},{2,3},{3,4},{4,5},{5,6},{6,7},{7,0},{8,9},{9,10},{10,1... | collective-permute-start | bytes 516104 | tf_op jit(solution)/shard_map/ppermute | solution.py:380
  5.4 0.0 copy-start
  5.4 6.8 %errors.1 = (bf16[6144,256]{1,0:T(8,128)(2,1)S(1)}, bf16[6144,256]{1,0:T(8,128)(2,1)S(1)}, f32[256,256]{1,0:T(8,128)S(1)}) custom-call(bf16[6144,256]{1,0:T(8,128)(2,1)} %obs_hbm.1, s32[32,6144]{1,0:T(8,128)} %bitcast.1, bf16[6144,256]{1,0:T(8,128)(2,1)} %f_hbm.1, f32[256,256]{1,0:T(8,128)S(1)} %get-tuple-element.29.x_ref), custom_call_target="tpu_custom_call" | custom-call | flops 2415919104 | bytes 10223616 | tf_op jit(solution)/shard_map/errors/pallas_call | solution.py:158
  12.3 0.0 collective-permute-done.halo_ref
  12.3 0.0 copy-done
  12.3 1.6 %update.1 = (f32[3,2,32,256]{3,2,1,0:T(8,128)S(1)}, f32[3,2,32,256]{3,2,1,0:T(8,128)S(1)}, f32[3,2,32,256]{3,2,1,0:T(8,128)S(1)}, f32[3,2,32,256]{3,2,1,0:T(8,128)S(1)}) custom-call(s32[1]{0:T(128)S(6)} %copy.14.stratum, f32[168,256]{1,0:T(8,128)S(1)} %collective-permute-done.halo_ref, f32[256,256]{1,0:T(8,128)S(1)} %get-tuple-element.28.turned_ref, ...), custom_call_target="tpu_custom_call" | custom-call | flops 7864320 | bytes 2621440 | tf_op jit(solution)/shard_map/update/pallas_call | solution.py:275
  13.9 0.1 collective-permute-start.2
  14.0 0.5 %collective-permute-start.1 = (f32[3,2,32,256]{3,2,1,0:T(8,128)S(1)}, f32[3,2,32,256]{3,2,1,0:T(8,128)S(1)}, u32[]{:S(2)}, u32[]{:S(2)}) collective-permute-start(f32[3,2,32,256]{3,2,1,0:T(8,128)S(1)} %get-tuple-element.32), channel_id=1, source_target_pairs={{0,8},{8,0},{16,24},{24,16},{1,9},{9,1},{17,25},{25,17},{2,10},{10... | collective-permute-start | bytes 589832 | tf_op jit(solution)/shard_map/ppermute | solution.py:375
  14.5 0.9 %collective-permute-done.2.got_ref = f32[3,2,32,256]{3,2,1,0:T(8,128)S(1)} collective-permute-done((f32[3,2,32,256]{3,2,1,0:T(8,128)S(1)}, f32[3,2,32,256]{3,2,1,0:T(8,128)S(1)}, u32[]{:S(2)}, u32[]{:S(2)}) %collective-permute-start.2) | collective-permute-done | bytes 196640 | tf_op jit(solution)/shard_map/ppermute | solution.py:375
  15.4 1.6 %collective-permute-start.5 = (f32[3,1,32,256]{3,2,1,0:T(8,128)S(1)}, f32[3,1,32,256]{3,2,1,0:T(8,128)S(1)}, u32[]{:S(2)}, u32[]{:S(2)}) collective-permute-start(f32[3,1,32,256]{3,2,1,0:T(8,128)S(1)} %get-tuple-element.37.rest_0_), channel_id=1, source_target_pairs={{0,16},{8,24},{16,0},{24,8},{1,17},{9,25},{17,1},{25,9},{2,18},{10... | collective-permute-start | bytes 294920 | tf_op jit(solution)/shard_map/ppermute | solution.py:375
  17.0 1.4 %factors.2.rest_1_ = bf16[6144,256]{1,0:T(8,128)(2,1)} custom-call(bf16[6144,256]{1,0:T(8,128)(2,1)S(1)} %get-tuple-element.33.f_ref, bf16[6144,256]{1,0:T(8,128)(2,1)S(1)} %get-tuple-element.34.err_ref, f32[256,256]{1,0:T(8,128)S(1)} %get-tuple-element.28.turned_ref, f32[3,1,32,256]{3,2,1,0:T(8,128)S(1)} %get-tuple-element.37.rest_0_), custom_call_target="tpu_custom_call" | custom-call | flops 268435456 | bytes 3145728 | tf_op jit(solution)/shard_map/factors/pallas_call | solution.py:210
  18.4 0.0 collective-permute-done.1.got_ref
  18.5 0.6 %collective-permute-start.3 = (f32[3,1,32,256]{3,2,1,0:T(8,128)S(1)}, f32[3,1,32,256]{3,2,1,0:T(8,128)S(1)}, u32[]{:S(2)}, u32[]{:S(2)}) collective-permute-start(f32[3,1,32,256]{3,2,1,0:T(8,128)S(1)} %get-tuple-element.40), channel_id=1, source_target_pairs={{0,16},{8,24},{16,0},{24,8},{1,17},{9,25},{17,1},{25,9},{2,18},{10... | collective-permute-start | bytes 294920 | tf_op jit(solution)/shard_map/ppermute | solution.py:375
  19.1 1.3 %collective-permute-done.5.got_ref = f32[3,1,32,256]{3,2,1,0:T(8,128)S(1)} collective-permute-done((f32[3,1,32,256]{3,2,1,0:T(8,128)S(1)}, f32[3,1,32,256]{3,2,1,0:T(8,128)S(1)}, u32[]{:S(2)}, u32[]{:S(2)}) %collective-permute-start.5) | collective-permute-done | bytes 98336 | tf_op jit(solution)/shard_map/ppermute | solution.py:375
  20.3 3.1 %collective-permute-start.6 = (f32[3,32,256]{2,1,0:T(8,128)S(1)}, f32[3,32,256]{2,1,0:T(8,128)S(1)}, u32[]{:S(2)}, u32[]{:S(2)}) collective-permute-start(f32[3,32,256]{2,1,0:T(8,128)S(1)} %mean.3), channel_id=1, source_target_pairs={{0,7},{1,0},{2,1},{3,2},{4,3},{5,4},{6,5},{7,6},{8,15},{9,8},{10,9... | collective-permute-start | bytes 294920 | tf_op jit(solution)/shard_map/ppermute | solution.py:390
  23.5 0.0 collective-permute-done.3.got_ref
  23.5 3.0 %collective-permute-start.4 = (f32[3,32,256]{2,1,0:T(8,128)S(1)}, f32[3,32,256]{2,1,0:T(8,128)S(1)}, u32[]{:S(2)}, u32[]{:S(2)}) collective-permute-start(f32[3,32,256]{2,1,0:T(8,128)S(1)} %mean.2), channel_id=1, source_target_pairs={{0,7},{1,0},{2,1},{3,2},{4,3},{5,4},{6,5},{7,6},{8,15},{9,8},{10,9... | collective-permute-start | bytes 294920 | tf_op jit(solution)/shard_map/ppermute | solution.py:390
  26.4 2.1 %collective-permute-start.8 = (f32[3,32,256]{2,1,0:T(8,128)S(1)}, f32[3,32,256]{2,1,0:T(8,128)S(1)}, u32[]{:S(2)}, u32[]{:S(2)}) collective-permute-start(f32[3,32,256]{2,1,0:T(8,128)S(1)} %mean.2), channel_id=1, source_target_pairs={{0,23},{1,16},{2,17},{3,18},{4,19},{5,20},{6,21},{7,22},{8,31},{9,... | collective-permute-start | bytes 294920 | tf_op jit(solution)/shard_map/ppermute | solution.py:390
  28.5 0.0 collective-permute-done.6.rest_0_
  28.5 1.2 %collective-permute-start.7 = (f32[3,32,256]{2,1,0:T(8,128)S(1)}, f32[3,32,256]{2,1,0:T(8,128)S(1)}, u32[]{:S(2)}, u32[]{:S(2)}) collective-permute-start(f32[3,32,256]{2,1,0:T(8,128)S(1)} %collective-permute-done.6.rest_0_), channel_id=1, source_target_pairs={{0,16},{8,24},{16,0},{24,8},{1,17},{9,25},{17,1},{25,9},{2,18},{10... | collective-permute-start | bytes 294920 | tf_op jit(solution)/shard_map/ppermute | solution.py:375
  29.8 0.0 collective-permute-start.9
  29.8 1.8 %factors.3 = bf16[6144,256]{1,0:T(8,128)(2,1)} custom-call(bf16[6144,256]{1,0:T(8,128)(2,1)S(1)} %get-tuple-element.33.f_ref, bf16[6144,256]{1,0:T(8,128)(2,1)S(1)} %get-tuple-element.34.err_ref, f32[256,256]{1,0:T(8,128)S(1)} %get-tuple-element.28.turned_ref, f32[3,32,256]{2,1,0:T(8,128)S(1)} %collective-permute-done.6.rest_0_, ...), custom_call_target="tpu_custom_call", output_to_operand_aliasing={{}: (4, {})} | custom-call | flops 536870912 | bytes 6291456 | tf_op jit(solution)/shard_map/factors/pallas_call | solution.py:210
  31.5 0.0 collective-permute-done.4.rest_4_
  31.6 0.4 %collective-permute-done.8.rest_6_ = f32[3,32,256]{2,1,0:T(8,128)S(1)} collective-permute-done((f32[3,32,256]{2,1,0:T(8,128)S(1)}, f32[3,32,256]{2,1,0:T(8,128)S(1)}, u32[]{:S(2)}, u32[]{:S(2)}) %collective-permute-start.8) | collective-permute-done | bytes 98336 | tf_op jit(solution)/shard_map/ppermute | solution.py:390
  32.0 1.4 %collective-permute-done.7.rest_2_ = f32[3,32,256]{2,1,0:T(8,128)S(1)} collective-permute-done((f32[3,32,256]{2,1,0:T(8,128)S(1)}, f32[3,32,256]{2,1,0:T(8,128)S(1)}, u32[]{:S(2)}, u32[]{:S(2)}) %collective-permute-start.7) | collective-permute-done | bytes 98336 | tf_op jit(solution)/shard_map/ppermute | solution.py:375
  33.3 0.0 collective-permute-start.10
  33.3 0.5 %collective-permute-start.11 = (f32[3,32,256]{2,1,0:T(8,128)S(1)}, f32[3,32,256]{2,1,0:T(8,128)S(1)}, u32[]{:S(2)}, u32[]{:S(2)}) collective-permute-start(f32[3,32,256]{2,1,0:T(8,128)S(1)} %collective-permute-done.4.rest_4_), channel_id=1, source_target_pairs={{0,8},{8,0},{16,24},{24,16},{1,9},{9,1},{17,25},{25,17},{2,10},{10... | collective-permute-start | bytes 294920 | tf_op jit(solution)/shard_map/ppermute | solution.py:375
  33.8 0.0 collective-permute-start.12
  33.8 0.0 collective-permute-done.9.rest_1_
  33.8 0.8 %collective-permute-done.10.rest_3_ = f32[3,32,256]{2,1,0:T(8,128)S(1)} collective-permute-done((f32[3,32,256]{2,1,0:T(8,128)S(1)}, f32[3,32,256]{2,1,0:T(8,128)S(1)}, u32[]{:S(2)}, u32[]{:S(2)}) %collective-permute-start.10) | collective-permute-done | bytes 98336 | tf_op jit(solution)/shard_map/ppermute | solution.py:375
  34.6 0.2 collective-permute-done.11.rest_5_
  34.8 0.4 collective-permute-done.12.rest_7_
  35.1 1.1 %place.1 = (f32[1,256,256]{2,1,0:T(8,128)}, f32[1,256,256]{2,1,0:T(8,128)}, f32[1,256,256]{2,1,0:T(8,128)}) custom-call(f32[3,32,256]{2,1,0:T(8,128)S(1)} %collective-permute-done.6.rest_0_, f32[3,32,256]{2,1,0:T(8,128)S(1)} %collective-permute-done.9.rest_1_, f32[3,32,256]{2,1,0:T(8,128)S(1)} %collective-permute-done.7.rest_2_, ...), custom_call_target="tpu_custom_call" | custom-call | bytes 1572864 | tf_op jit(solution)/shard_map/place/pallas_call | solution.py:361
  (4 shorter events, 0.1 us)
Async XLA Ops:
  1.7 10.5 %collective-permute-start = (f32[168,256]{1,0:T(8,128)S(1)}, f32[168,256]{1,0:T(8,128)S(1)}, u32[]{:S(2)}, u32[]{:S(2)}) collective-permute-start(f32[168,256]{1,0:T(8,128)S(1)} %get-tuple-element.27), channel_id=1, source_target_pairs={{0,1},{1,2},{2,3},{3,4},{4,5},{5,6},{6,7},{7,0},{8,9},{9,10},{10,1... | collective-permute-start | bytes 516104 | tf_op jit(solution)/shard_map/ppermute | solution.py:380
  5.4 6.9 %copy-start = (f32[25,256]{1,0:T(8,128)S(1)}, f32[25,256]{1,0:T(8,128)}, u32[]{:S(2)}) copy-start(f32[25,256]{1,0:T(8,128)} %w_ref.1) | copy-start | bytes 76804
  13.9 1.5 %collective-permute-start.2 = (f32[3,2,32,256]{3,2,1,0:T(8,128)S(1)}, f32[3,2,32,256]{3,2,1,0:T(8,128)S(1)}, u32[]{:S(2)}, u32[]{:S(2)}) collective-permute-start(f32[3,2,32,256]{3,2,1,0:T(8,128)S(1)} %get-tuple-element.36), channel_id=1, source_target_pairs={{0,8},{8,0},{16,24},{24,16},{1,9},{9,1},{17,25},{25,17},{2,10},{10... | collective-permute-start | bytes 589832 | tf_op jit(solution)/shard_map/ppermute | solution.py:375
  14.0 4.5 %collective-permute-start.1 = (f32[3,2,32,256]{3,2,1,0:T(8,128)S(1)}, f32[3,2,32,256]{3,2,1,0:T(8,128)S(1)}, u32[]{:S(2)}, u32[]{:S(2)}) collective-permute-start(f32[3,2,32,256]{3,2,1,0:T(8,128)S(1)} %get-tuple-element.32), channel_id=1, source_target_pairs={{0,8},{8,0},{16,24},{24,16},{1,9},{9,1},{17,25},{25,17},{2,10},{10... | collective-permute-start | bytes 589832 | tf_op jit(solution)/shard_map/ppermute | solution.py:375
  15.4 4.9 %collective-permute-start.5 = (f32[3,1,32,256]{3,2,1,0:T(8,128)S(1)}, f32[3,1,32,256]{3,2,1,0:T(8,128)S(1)}, u32[]{:S(2)}, u32[]{:S(2)}) collective-permute-start(f32[3,1,32,256]{3,2,1,0:T(8,128)S(1)} %get-tuple-element.37.rest_0_), channel_id=1, source_target_pairs={{0,16},{8,24},{16,0},{24,8},{1,17},{9,25},{17,1},{25,9},{2,18},{10... | collective-permute-start | bytes 294920 | tf_op jit(solution)/shard_map/ppermute | solution.py:375
  18.5 5.0 %collective-permute-start.3 = (f32[3,1,32,256]{3,2,1,0:T(8,128)S(1)}, f32[3,1,32,256]{3,2,1,0:T(8,128)S(1)}, u32[]{:S(2)}, u32[]{:S(2)}) collective-permute-start(f32[3,1,32,256]{3,2,1,0:T(8,128)S(1)} %get-tuple-element.40), channel_id=1, source_target_pairs={{0,16},{8,24},{16,0},{24,8},{1,17},{9,25},{17,1},{25,9},{2,18},{10... | collective-permute-start | bytes 294920 | tf_op jit(solution)/shard_map/ppermute | solution.py:375
  20.3 8.2 %collective-permute-start.6 = (f32[3,32,256]{2,1,0:T(8,128)S(1)}, f32[3,32,256]{2,1,0:T(8,128)S(1)}, u32[]{:S(2)}, u32[]{:S(2)}) collective-permute-start(f32[3,32,256]{2,1,0:T(8,128)S(1)} %mean.3), channel_id=1, source_target_pairs={{0,7},{1,0},{2,1},{3,2},{4,3},{5,4},{6,5},{7,6},{8,15},{9,8},{10,9... | collective-permute-start | bytes 294920 | tf_op jit(solution)/shard_map/ppermute | solution.py:390
  23.5 8.1 %collective-permute-start.4 = (f32[3,32,256]{2,1,0:T(8,128)S(1)}, f32[3,32,256]{2,1,0:T(8,128)S(1)}, u32[]{:S(2)}, u32[]{:S(2)}) collective-permute-start(f32[3,32,256]{2,1,0:T(8,128)S(1)} %mean.2), channel_id=1, source_target_pairs={{0,7},{1,0},{2,1},{3,2},{4,3},{5,4},{6,5},{7,6},{8,15},{9,8},{10,9... | collective-permute-start | bytes 294920 | tf_op jit(solution)/shard_map/ppermute | solution.py:390
  26.4 5.5 %collective-permute-start.8 = (f32[3,32,256]{2,1,0:T(8,128)S(1)}, f32[3,32,256]{2,1,0:T(8,128)S(1)}, u32[]{:S(2)}, u32[]{:S(2)}) collective-permute-start(f32[3,32,256]{2,1,0:T(8,128)S(1)} %mean.2), channel_id=1, source_target_pairs={{0,23},{1,16},{2,17},{3,18},{4,19},{5,20},{6,21},{7,22},{8,31},{9,... | collective-permute-start | bytes 294920 | tf_op jit(solution)/shard_map/ppermute | solution.py:390
  28.5 4.8 %collective-permute-start.7 = (f32[3,32,256]{2,1,0:T(8,128)S(1)}, f32[3,32,256]{2,1,0:T(8,128)S(1)}, u32[]{:S(2)}, u32[]{:S(2)}) collective-permute-start(f32[3,32,256]{2,1,0:T(8,128)S(1)} %collective-permute-done.6.rest_0_), channel_id=1, source_target_pairs={{0,16},{8,24},{16,0},{24,8},{1,17},{9,25},{17,1},{25,9},{2,18},{10... | collective-permute-start | bytes 294920 | tf_op jit(solution)/shard_map/ppermute | solution.py:375
  29.8 4.1 %collective-permute-start.9 = (f32[3,32,256]{2,1,0:T(8,128)S(1)}, f32[3,32,256]{2,1,0:T(8,128)S(1)}, u32[]{:S(2)}, u32[]{:S(2)}) collective-permute-start(f32[3,32,256]{2,1,0:T(8,128)S(1)} %collective-permute-done.6.rest_0_), channel_id=1, source_target_pairs={{0,8},{8,0},{16,24},{24,16},{1,9},{9,1},{17,25},{25,17},{2,10},{10... | collective-permute-start | bytes 294920 | tf_op jit(solution)/shard_map/ppermute | solution.py:375
  33.3 1.3 %collective-permute-start.10 = (f32[3,32,256]{2,1,0:T(8,128)S(1)}, f32[3,32,256]{2,1,0:T(8,128)S(1)}, u32[]{:S(2)}, u32[]{:S(2)}) collective-permute-start(f32[3,32,256]{2,1,0:T(8,128)S(1)} %collective-permute-done.7.rest_2_), channel_id=1, source_target_pairs={{0,8},{8,0},{16,24},{24,16},{1,9},{9,1},{17,25},{25,17},{2,10},{10... | collective-permute-start | bytes 294920 | tf_op jit(solution)/shard_map/ppermute | solution.py:375
  33.3 1.5 %collective-permute-start.11 = (f32[3,32,256]{2,1,0:T(8,128)S(1)}, f32[3,32,256]{2,1,0:T(8,128)S(1)}, u32[]{:S(2)}, u32[]{:S(2)}) collective-permute-start(f32[3,32,256]{2,1,0:T(8,128)S(1)} %collective-permute-done.4.rest_4_), channel_id=1, source_target_pairs={{0,8},{8,0},{16,24},{24,16},{1,9},{9,1},{17,25},{25,17},{2,10},{10... | collective-permute-start | bytes 294920 | tf_op jit(solution)/shard_map/ppermute | solution.py:375
  33.8 1.3 %collective-permute-start.12 = (f32[3,32,256]{2,1,0:T(8,128)S(1)}, f32[3,32,256]{2,1,0:T(8,128)S(1)}, u32[]{:S(2)}, u32[]{:S(2)}) collective-permute-start(f32[3,32,256]{2,1,0:T(8,128)S(1)} %collective-permute-done.8.rest_6_), channel_id=1, source_target_pairs={{0,8},{8,0},{16,24},{24,16},{1,9},{9,1},{17,25},{25,17},{2,10},{10... | collective-permute-start | bytes 294920 | tf_op jit(solution)/shard_map/ppermute | solution.py:375

commit v5 on v4

--- a/solution.py
+++ b/solution.py
@@ -79,107 +79,87 @@
     )(held(x))
 
 
-def error_kernel(rows, obs_hbm, bits_hbm, f_hbm, x_ref, err_ref, f_ref, gd_ref, obs_ref, bits_ref, *rest):
-    (value_a, value_b, predicted_a, predicted_b), sems = rest[:4], rest[4]
-    words, series = bits_ref.shape
-    width = obs_ref.shape[1]
+def error_kernel(rows, obs_hbm, bits_hbm, f_hbm, turned_ref, err_ref, both_ref, gd_ref, bits_ref, sems):
+    width, series = err_ref.shape
+    rank = turned_ref.shape[1]
+    words = bits_ref.shape[0]
     per = width // words
     chunks = series // rows
 
-    def lines(index):
-        return pl.ds(pl.multiple_of(index * rows, rows), rows)
-
     def copies(index):
-        part = lines(index)
+        part = pl.ds(index * rows, rows)
         return (
             pltpu.make_async_copy(bits_hbm.at[:, part], bits_ref.at[:, part], sems.at[index, 0]),
-            pltpu.make_async_copy(f_hbm.at[part, :], f_ref.at[part, :], sems.at[index, 1]),
-            pltpu.make_async_copy(obs_hbm.at[part, :], obs_ref.at[part, :], sems.at[index, 2]),
+            pltpu.make_async_copy(
+                f_hbm.at[part, :], both_ref.at[part, pl.ds(0, rank)], sems.at[index, 1]
+            ),
+            pltpu.make_async_copy(
+                obs_hbm.at[part, :], both_ref.at[part, pl.ds(rank, width)], sems.at[index, 2]
+            ),
         )
 
-    @pl.loop(0, chunks)
-    def _(index):
+    for index in range(chunks):
         for copy in copies(index):
             copy.start()
-
-    half = x_ref[...].astype(BF16)
-    lane = lax.broadcasted_iota(jnp.int32, (words, width), 1)
-    word = lax.broadcasted_iota(jnp.int32, (words, width), 0)
-    spread = (lane // per == word).astype(BF16)
-    flag = jnp.left_shift(1, lax.broadcasted_iota(jnp.int32, (1, width), 1) % per)
-    gd_ref[...] = jnp.zeros_like(gd_ref)
-
-    def predict(index, value_ref, predicted_ref):
+    row = lax.broadcasted_iota(jnp.int32, (width, width), 0)
+    column = lax.broadcasted_iota(jnp.int32, (width, width), 1)
+    weights = jnp.concatenate(
+        [turned_ref[...].astype(BF16), jnp.where(row == column, -1.0, 0.0).astype(BF16)], axis=1
+    )
+    flag = jnp.left_shift(1, lax.broadcasted_iota(jnp.int32, (1, per, 1), 1))
+
+    def compare(index):
         for copy in copies(index):
             copy.wait()
-        part = lines(index)
-        value_ref[...] = lax.dot_general(
-            bits_ref[:, part].astype(F32).astype(BF16),
-            spread,
-            (((0,), (0,)), ((), ())),
-            preferred_element_type=F32,
+        part = pl.ds(index * rows, rows)
+        return lax.dot_general(
+            weights, both_ref[part, :], (((1,), (1,)), ((), ())), preferred_element_type=F32
         )
-        predicted_ref[...] = jnp.dot(f_ref[part, :], half, preferred_element_type=F32)
-
-    def settle(index, value_ref, predicted_ref):
-        part = lines(index)
-        error = jnp.where(
-            jnp.bitwise_and(value_ref[...].astype(jnp.int32), flag) != 0,
-            predicted_ref[...] - obs_ref[part, :].astype(F32),
-            0.0,
-        ).astype(BF16)
-        err_ref[part, :] = error
-        gd_ref[...] += lax.dot_general(
-            f_ref[part, :], error, (((0,), (0,)), ((), ())), preferred_element_type=F32
-        )
-
-    predict(0, value_a, predicted_a)
-
-    @pl.loop(0, (chunks - 1) // 2)
-    def _(pair):
-        predict(2 * pair + 1, value_b, predicted_b)
-        settle(2 * pair, value_a, predicted_a)
-        predict(2 * pair + 2, value_a, predicted_a)
-        settle(2 * pair + 1, value_b, predicted_b)
-
-    if chunks % 2 == 0:
-        predict(chunks - 1, value_b, predicted_b)
-        settle(chunks - 2, value_a, predicted_a)
-        settle(chunks - 1, value_b, predicted_b)
-    else:
-        settle(chunks - 1, value_a, predicted_a)
-
-
-def error_step(obs, bits, factors, x):
+
+    def settle(index, gap):
+        part = pl.ds(index * rows, rows)
+        seen = jnp.bitwise_and(bits_ref[:, part][:, None, :], flag) != 0
+        error = jnp.where(seen, gap.reshape(words, per, rows), 0.0).reshape(width, rows)
+        error = error.astype(BF16)
+        err_ref[:, part] = error
+        term = jnp.dot(error, both_ref[part, pl.ds(0, rank)], preferred_element_type=F32)
+        if index == 0:
+            gd_ref[...] = term
+        else:
+            gd_ref[...] += term
+
+    gap = compare(0)
+    for index in range(chunks):
+        later = compare(index + 1) if index + 1 < chunks else None
+        settle(index, gap)
+        gap = later
+
+
+def error_step(obs, bits, factors, turned):
     series, width = obs.shape
     rank = factors.shape[1]
     words = bits.shape[0]
-    rows = rows_of(series, 512)
+    rows = rows_of(series, 1024)
     return pl.pallas_call(
         functools.partial(error_kernel, rows),
         out_shape=(
-            jax.ShapeDtypeStruct((series, width), BF16),
-            jax.ShapeDtypeStruct((series, rank), BF16),
-            jax.ShapeDtypeStruct((rank, width), F32),
+            jax.ShapeDtypeStruct((width, series), BF16),
+            jax.ShapeDtypeStruct((series, rank + width), BF16),
+            jax.ShapeDtypeStruct((width, rank), F32),
         ),
         in_specs=[far(), far(), far(), whole()],
         out_specs=(whole(), whole(), whole()),
         scratch_shapes=[
-            pltpu.VMEM((series, width), BF16),
             pltpu.VMEM((words, series), jnp.int32),
-            pltpu.VMEM((rows, width), F32),
-            pltpu.VMEM((rows, width), F32),
-            pltpu.VMEM((rows, width), F32),
-            pltpu.VMEM((rows, width), F32),
             pltpu.SemaphoreType.DMA((series // rows, 3)),
         ],
         compiler_params=params(),
-        cost_estimate=cost(6 * series * width * rank, series * (3 * width * 2 + words * 4)),
+        cost_estimate=cost(8 * series * width * rank, series * (3 * width * 2 + words * 4)),
         name="errors",
-    )(held(obs), held(bits), held(factors), x)
-
-
-def factor_kernel(begin, rows, chunks, f_ref, err_ref, turned_ref, *rest):
+    )(held(obs), held(bits), held(factors), turned)
+
+
+def factor_kernel(begin, rows, chunks, both_ref, err_ref, turned_ref, *rest):
     out_hbm, out_ref, sems = rest[-3:]
     half = turned_ref[...].astype(BF16)
     size = rows // chunks
@@ -193,18 +173,20 @@
 
     for index in range(chunks):
         part = pl.ds(begin + index * size, size)
-        gradient = jnp.dot(err_ref[part, :], half, preferred_element_type=F32)
+        gradient = lax.dot_general(
+            err_ref[:, part], half, (((0,), (0,)), ((), ())), preferred_element_type=F32
+        )
         out_ref[pl.ds(index * size, size), :] = (
-            f_ref[part, :].astype(F32) - factor_rate * gradient
+            both_ref[part, pl.ds(0, half.shape[1])].astype(F32) - factor_rate * gradient
         ).astype(BF16)
         copy(index).start()
     for index in range(chunks):
         copy(index).wait()
 
 
-def factor_step(factors, err, turned, after, sofar, begin, rows):
-    series, rank = factors.shape
-    width = err.shape[1]
+def factor_step(both, err, turned, after, sofar, begin, rows):
+    width, series = err.shape
+    rank = turned.shape[1]
     chunks = rows // rows_of(rows, 1024)
     rest = (after,) if sofar is None else (after, sofar)
     return pl.pallas_call(
@@ -217,20 +199,21 @@
         compiler_params=params(),
         cost_estimate=cost(2 * rows * width * rank, rows * 3 * width * 2),
         name="factors",
-    )(factors, err, turned, *rest)
+    )(both, err, turned, *rest)
 
 
 def update_kernel(
-    count, pieces, lanes, stratum, halo_ref, turned_ref, w_ref, gd_ref, x_ref, m_hbm, v_hbm, *rest
+    count, pieces, lanes, stratum_ref, halo_ref, turned_ref, w_ref, gd_ref, x_ref, m_hbm, v_hbm, *rest
 ):
-    outs, (z_ref, r_ref, m_ref, v_ref, new_ref, sems) = rest[: 2 * pieces], rest[2 * pieces :]
+    outs, scratch = rest[: 2 * pieces], rest[2 * pieces :]
+    z_ref, r_ref, m_ref, v_ref, new_ref, sems = scratch
     m_copy = pltpu.make_async_copy(m_hbm.at[0], m_ref, sems.at[0])
     v_copy = pltpu.make_async_copy(v_hbm.at[0], v_ref, sems.at[1])
     m_copy.start()
     v_copy.start()
     width, rank = turned_ref.shape
     share = rank // count
-    block_index = lax.rem(lax.axis_index("blk") + stratum[0], lax.axis_size("blk"))
+    block_index = lax.rem(lax.axis_index("blk") + stratum_ref[...], lax.axis_size("blk"))
     lags = list(range(1, w_ref.shape[0])) + [SEASON]
     for part in range(rank // lanes):
         columns = slice(part * lanes, (part + 1) * lanes)
@@ -245,12 +228,12 @@
         back = resid
         for index, lag in enumerate(lags):
             back = back - w_ref[index : index + 1, columns] * r_ref[part, lag : lag + width, :]
-        z_ref[part, :width, :] = back
+        z_ref[part, :width, :] = data_scale * gd_ref[:, columns] + back
     m_copy.wait()
     v_copy.wait()
     for part in range(rank // lanes):
         rows = slice(part * lanes, (part + 1) * lanes)
-        gradient = data_scale * gd_ref[rows, :] + z_ref[part, :width, :].T
+        gradient = z_ref[part, :width, :].T
         first = beta_one * m_ref[rows, :] + (1.0 - beta_one) * gradient
         second = beta_two * v_ref[rows, :] + (1.0 - beta_two) * gradient * gradient
         new_ref[0, rows, :] = x_ref[rows, :] - step_rate * first / (jnp.sqrt(second) + adam_eps)
@@ -268,14 +251,14 @@
 
 
 def update_step(stratum, halo, turned, weights, gd, x, m, v, count, pieces):
-    rank, width = gd.shape
+    width, rank = gd.shape
     lanes = 128
     size = rank // count // pieces
     out = jax.ShapeDtypeStruct((3, count // 2, size, width), F32)
     outs = pl.pallas_call(
         functools.partial(update_kernel, count, pieces, lanes),
         out_shape=(out,) * (2 * pieces),
-        in_specs=[scalars()] + [whole()] * 5 + [far()] * 2,
+        in_specs=[whole()] * 6 + [far()] * 2,
         out_specs=(whole(),) * (2 * pieces),
         scratch_shapes=[
             pltpu.VMEM((rank // lanes, SEASON + width, lanes), F32),
@@ -288,7 +271,7 @@
         compiler_params=params(),
         cost_estimate=cost(120 * rank * width, 10 * rank * width * 4),
         name="update",
-    )(stratum, halo, turned, weights, gd, x, held(m), held(v))
+    )(stratum.reshape(1, 1), halo, turned, weights, gd, x, held(m), held(v))
     return [(outs[2 * piece], outs[2 * piece + 1]) for piece in range(pieces)]
 
 
@@ -397,7 +380,7 @@
 
     tail, turned, x = prepare(x_blocks)
     halo = shifted(tail, 1)
-    err, kept, gd = error_step(obs, mask_bits.T, factors, x)
+    err, kept, gd = error_step(obs, mask_bits.T, factors, turned)
     (keep0, send0), (keep1, send1) = update_step(
         stratum, halo, turned, ar_weights, gd, x, first_moment, second_moment, count, 2
     )
@@ -415,10 +398,11 @@
     near0 = delivered(mean0, 0)
     mean1 = mean(keep1, far1, count)
     near1 = delivered(mean1, 0)
+    side0 = crossed(near0, 2)
+    mean1, _ = lax.optimization_barrier((mean1, near0))
     side1 = delivered(mean1, 2)
-    side0 = crossed(near0, 2)
     factor_new = factor_step(kept, err, turned, near0, factor_new, third, series - third)
-    near1, side0, side1, factor_new = lax.optimization_barrier((near1, side0, side1, factor_new))
+    near1, factor_new = lax.optimization_barrier((near1, factor_new))
     pieces = [
         [near0, crossed(near0, 1), side0, crossed(side0, 1)],
         [near1, crossed(near1, 1), side1, crossed(side1, 1)],

time: 36.3 us -> 37.6 us (1.036); the launches traced: 36.2 us -> 36.9 us
  starting transfers between devices: 15.6 us -> 17.5 us
  Pallas kernels: 13.9 us -> 12.7 us
    ppermute x9, starting transfers between devices: 4.49 us -> 5.97 us  [crossed(): lax.ppermute(value, 'grp', [(source, source ^ step) for source in range(c...]
    pallas_call x1, Pallas kernels: 6.83 us -> 5.57 us  [error_step(): pl.pallas_call(functools.partial(error_kernel, rows), out_shape=(jax.Shap...]
    ppermute x1, waiting for transfers between devices: 0.01 us -> 1.17 us  [shifted(): lax.ppermute(value, 'blk', [(source, (source + steps) % count) for source...]
    ppermute x9, waiting for transfers between devices: 4.84 us -> 3.98 us  [crossed(): lax.ppermute(value, 'grp', [(source, source ^ step) for source in range(c...]
  transfers between devices with their start and end apart: 13 -> 13, of which waited for: 7 -> 8; matrix products, arithmetic and copies ran while one was open for 0% -> 0% of each run, Pallas kernels for 28% -> 24%
where the time goes in v5:
time: 37.6 us; the launch traced here: 36.9 us
  starting transfers between devices  17.5 us (47%)
  Pallas kernels  12.7 us (34%)
  waiting for transfers between devices  5.33 us (14%)
  between operations  1.39 us (4%)
    ppermute x3, starting transfers between devices, delivered(): return lax.ppermute(value, ('grp', 'blk'), pairs)  8.48 us
    ppermute x9, starting transfers between devices, crossed(): lax.ppermute(value, 'grp', [(source, source ^ step) for source in range(c...  5.97 us
    pallas_call x1, Pallas kernels, error_step(): pl.pallas_call(functools.partial(error_kernel, rows), out_shape=(jax.Shap...  5.57 us
    ppermute x9, waiting for transfers between devices, crossed(): lax.ppermute(value, 'grp', [(source, source ^ step) for source in range(c...  3.98 us
    pallas_call x2, Pallas kernels, factor_step(): pl.pallas_call(functools.partial(factor_kernel, begin, rows, chunks), out...  3.32 us
    ppermute x1, starting transfers between devices, shifted(): lax.ppermute(value, 'blk', [(source, (source + steps) % count) for source...  3.02 us
    pallas_call x1, Pallas kernels, update_step(): pl.pallas_call(functools.partial(update_kernel, count, pieces, lanes), ou...  1.59 us
    ppermute x1, waiting for transfers between devices, shifted(): lax.ppermute(value, 'blk', [(source, (source + steps) % count) for source...  1.17 us
  transfers between devices with their start and end apart: 13, of which 8 were waited for; matrix products, arithmetic and copies ran while one was open for 0% of the time, Pallas kernels for 24%

profile of v5, /device:TPU:0, one launch (start us, length us, event | category | flops | bytes accessed | tf_op | source)
XLA Modules:
  0.0 36.9 jit_solution(7992470335868163672)
XLA Ops:
  0.6 1.1 %prepare.1 = (f32[168,256]{1,0:T(8,128)S(1)}, f32[256,256]{1,0:T(8,128)S(1)}, f32[256,256]{1,0:T(8,128)S(1)}) custom-call(f32[1,256,256]{2,1,0:T(8,128)} %x_hbm.1), custom_call_target="tpu_custom_call" | custom-call | bytes 1048576 | tf_op jit(solution)/shard_map/prepare/pallas_call | solution.py:66
  1.7 3.0 %collective-permute-start = (f32[168,256]{1,0:T(8,128)S(1)}, f32[168,256]{1,0:T(8,128)S(1)}, u32[]{:S(2)}, u32[]{:S(2)}) collective-permute-start(f32[168,256]{1,0:T(8,128)S(1)} %get-tuple-element.26), channel_id=1, source_target_pairs={{0,1},{1,2},{2,3},{3,4},{4,5},{5,6},{6,7},{7,0},{8,9},{9,10},{10,1... | collective-permute-start | bytes 516104 | tf_op jit(solution)/shard_map/ppermute | solution.py:363
  5.4 0.0 copy-start
  5.4 5.6 %errors.1 = (bf16[256,6144]{1,0:T(8,128)(2,1)S(1)}, bf16[6144,512]{1,0:T(8,128)(2,1)S(1)}, f32[256,256]{1,0:T(8,128)S(1)}) custom-call(bf16[6144,256]{1,0:T(8,128)(2,1)} %obs_hbm.1, s32[32,6144]{1,0:T(8,128)} %bitcast.3, bf16[6144,256]{1,0:T(8,128)(2,1)} %f_hbm.1, f32[256,256]{1,0:T(8,128)S(1)} %get-tuple-element.27.turned_ref), custom_call_target="tpu_custom_call" | custom-call | flops 3221225472 | bytes 10223616 | tf_op jit(solution)/shard_map/errors/pallas_call | solution.py:143
  11.0 1.2 %collective-permute-done.halo_ref = f32[168,256]{1,0:T(8,128)S(1)} collective-permute-done((f32[168,256]{1,0:T(8,128)S(1)}, f32[168,256]{1,0:T(8,128)S(1)}, u32[]{:S(2)}, u32[]{:S(2)}) %collective-permute-start) | collective-permute-done | bytes 172064 | tf_op jit(solution)/shard_map/ppermute | solution.py:363
  12.2 0.0 copy-done
  12.2 1.6 %update.1 = (f32[3,2,32,256]{3,2,1,0:T(8,128)S(1)}, f32[3,2,32,256]{3,2,1,0:T(8,128)S(1)}, f32[3,2,32,256]{3,2,1,0:T(8,128)S(1)}, f32[3,2,32,256]{3,2,1,0:T(8,128)S(1)}) custom-call(s32[1,1]{1,0:T(1,128)} %bitcast.2.stratum_ref, f32[168,256]{1,0:T(8,128)S(1)} %collective-permute-done.halo_ref, f32[256,256]{1,0:T(8,128)S(1)} %get-tuple-element.27.turned_ref, ...), custom_call_target="tpu_custom_call" | custom-call | flops 7864320 | bytes 2621440 | tf_op jit(solution)/shard_map/update/pallas_call | solution.py:258
  13.8 0.1 collective-permute-start.2
  13.8 0.5 %collective-permute-start.1 = (f32[3,2,32,256]{3,2,1,0:T(8,128)S(1)}, f32[3,2,32,256]{3,2,1,0:T(8,128)S(1)}, u32[]{:S(2)}, u32[]{:S(2)}) collective-permute-start(f32[3,2,32,256]{3,2,1,0:T(8,128)S(1)} %get-tuple-element.31), channel_id=1, source_target_pairs={{0,8},{8,0},{16,24},{24,16},{1,9},{9,1},{17,25},{25,17},{2,10},{10... | collective-permute-start | bytes 589832 | tf_op jit(solution)/shard_map/ppermute | solution.py:358
  14.3 0.9 %collective-permute-done.2.got_ref = f32[3,2,32,256]{3,2,1,0:T(8,128)S(1)} collective-permute-done((f32[3,2,32,256]{3,2,1,0:T(8,128)S(1)}, f32[3,2,32,256]{3,2,1,0:T(8,128)S(1)}, u32[]{:S(2)}, u32[]{:S(2)}) %collective-permute-start.2) | collective-permute-done | bytes 196640 | tf_op jit(solution)/shard_map/ppermute | solution.py:358
  15.3 1.6 %collective-permute-start.5 = (f32[3,1,32,256]{3,2,1,0:T(8,128)S(1)}, f32[3,1,32,256]{3,2,1,0:T(8,128)S(1)}, u32[]{:S(2)}, u32[]{:S(2)}) collective-permute-start(f32[3,1,32,256]{3,2,1,0:T(8,128)S(1)} %get-tuple-element.36.rest_0_), channel_id=1, source_target_pairs={{0,16},{8,24},{16,0},{24,8},{1,17},{9,25},{17,1},{25,9},{2,18},{10... | collective-permute-start | bytes 294920 | tf_op jit(solution)/shard_map/ppermute | solution.py:358
  16.9 1.5 %factors.2.rest_1_ = bf16[6144,256]{1,0:T(8,128)(2,1)} custom-call(bf16[6144,512]{1,0:T(8,128)(2,1)S(1)} %get-tuple-element.32.both_ref, bf16[256,6144]{1,0:T(8,128)(2,1)S(1)} %get-tuple-element.33.err_ref, f32[256,256]{1,0:T(8,128)S(1)} %get-tuple-element.27.turned_ref, f32[3,1,32,256]{3,2,1,0:T(8,128)S(1)} %get-tuple-element.36.rest_0_), custom_call_target="tpu_custom_call" | custom-call | flops 268435456 | bytes 3145728 | tf_op jit(solution)/shard_map/factors/pallas_call | solution.py:192
  18.3 0.0 collective-permute-done.1.got_ref
  18.4 0.6 %collective-permute-start.3 = (f32[3,1,32,256]{3,2,1,0:T(8,128)S(1)}, f32[3,1,32,256]{3,2,1,0:T(8,128)S(1)}, u32[]{:S(2)}, u32[]{:S(2)}) collective-permute-start(f32[3,1,32,256]{3,2,1,0:T(8,128)S(1)} %get-tuple-element.39), channel_id=1, source_target_pairs={{0,16},{8,24},{16,0},{24,8},{1,17},{9,25},{17,1},{25,9},{2,18},{10... | collective-permute-start | bytes 294920 | tf_op jit(solution)/shard_map/ppermute | solution.py:358
  19.0 1.2 %collective-permute-done.5.got_ref = f32[3,1,32,256]{3,2,1,0:T(8,128)S(1)} collective-permute-done((f32[3,1,32,256]{3,2,1,0:T(8,128)S(1)}, f32[3,1,32,256]{3,2,1,0:T(8,128)S(1)}, u32[]{:S(2)}, u32[]{:S(2)}) %collective-permute-start.5) | collective-permute-done | bytes 98336 | tf_op jit(solution)/shard_map/ppermute | solution.py:358
  20.2 2.0 %collective-permute-start.6 = (f32[3,32,256]{2,1,0:T(8,128)S(1)}, f32[3,32,256]{2,1,0:T(8,128)S(1)}, u32[]{:S(2)}, u32[]{:S(2)}) collective-permute-start(f32[3,32,256]{2,1,0:T(8,128)S(1)} %mean.3), channel_id=1, source_target_pairs={{0,7},{1,0},{2,1},{3,2},{4,3},{5,4},{6,5},{7,6},{8,15},{9,8},{10,9... | collective-permute-start | bytes 294920 | tf_op jit(solution)/shard_map/ppermute | solution.py:373
  22.2 0.9 %collective-permute-done.3.got_ref = f32[3,1,32,256]{3,2,1,0:T(8,128)S(1)} collective-permute-done((f32[3,1,32,256]{3,2,1,0:T(8,128)S(1)}, f32[3,1,32,256]{3,2,1,0:T(8,128)S(1)}, u32[]{:S(2)}, u32[]{:S(2)}) %collective-permute-start.3) | collective-permute-done | bytes 98336 | tf_op jit(solution)/shard_map/ppermute | solution.py:358
  23.1 2.1 %collective-permute-start.4 = (f32[3,32,256]{2,1,0:T(8,128)S(1)}, f32[3,32,256]{2,1,0:T(8,128)S(1)}, u32[]{:S(2)}, u32[]{:S(2)}) collective-permute-start(f32[3,32,256]{2,1,0:T(8,128)S(1)} %mean.2), channel_id=1, source_target_pairs={{0,7},{1,0},{2,1},{3,2},{4,3},{5,4},{6,5},{7,6},{8,15},{9,8},{10,9... | collective-permute-start | bytes 294920 | tf_op jit(solution)/shard_map/ppermute | solution.py:373
  25.2 0.2 collective-permute-done.6.rest_0_
  25.4 2.2 %collective-permute-start.8 = (f32[3,32,256]{2,1,0:T(8,128)S(1)}, f32[3,32,256]{2,1,0:T(8,128)S(1)}, u32[]{:S(2)}, u32[]{:S(2)}) collective-permute-start(f32[3,32,256]{2,1,0:T(8,128)S(1)} %collective-permute-done.6.rest_0_), channel_id=1, source_target_pairs={{0,16},{8,24},{16,0},{24,8},{1,17},{9,25},{17,1},{25,9},{2,18},{10... | collective-permute-start | bytes 294920 | tf_op jit(solution)/shard_map/ppermute | solution.py:358
  27.6 4.4 %collective-permute-start.11 = (f32[3,32,256]{2,1,0:T(8,128)S(1)}, f32[3,32,256]{2,1,0:T(8,128)S(1)}, u32[]{:S(2)}, u32[]{:S(2)}) collective-permute-start(f32[3,32,256]{2,1,0:T(8,128)S(1)} %mean.2), channel_id=1, source_target_pairs={{0,23},{1,16},{2,17},{3,18},{4,19},{5,20},{6,21},{7,22},{8,31},{9,... | collective-permute-start | bytes 294920 | tf_op jit(solution)/shard_map/ppermute | solution.py:373
  32.0 1.9 %factors.3 = bf16[6144,256]{1,0:T(8,128)(2,1)} custom-call(bf16[6144,512]{1,0:T(8,128)(2,1)S(1)} %get-tuple-element.32.both_ref, bf16[256,6144]{1,0:T(8,128)(2,1)S(1)} %get-tuple-element.33.err_ref, f32[256,256]{1,0:T(8,128)S(1)} %get-tuple-element.27.turned_ref, f32[3,32,256]{2,1,0:T(8,128)S(1)} %collective-permute-done.6.rest_0_, ...), custom_call_target="tpu_custom_call", output_to_operand_aliasing={{}: (4, {})} | custom-call | flops 536870912 | bytes 6291456 | tf_op jit(solution)/shard_map/factors/pallas_call | solution.py:192
  33.8 0.0 collective-permute-done.4.rest_4_
  33.8 0.1 collective-permute-start.10
  33.9 0.5 %collective-permute-start.7 = (f32[3,32,256]{2,1,0:T(8,128)S(1)}, f32[3,32,256]{2,1,0:T(8,128)S(1)}, u32[]{:S(2)}, u32[]{:S(2)}) collective-permute-start(f32[3,32,256]{2,1,0:T(8,128)S(1)} %collective-permute-done.6.rest_0_), channel_id=1, source_target_pairs={{0,8},{8,0},{16,24},{24,16},{1,9},{9,1},{17,25},{25,17},{2,10},{10... | collective-permute-start | bytes 294920 | tf_op jit(solution)/shard_map/ppermute | solution.py:358
  34.4 0.0 collective-permute-done.8.rest_2_
  34.4 0.1 collective-permute-start.9
  34.5 0.0 collective-permute-done.11.rest_6_
  34.5 0.4 %collective-permute-start.12 = (f32[3,32,256]{2,1,0:T(8,128)S(1)}, f32[3,32,256]{2,1,0:T(8,128)S(1)}, u32[]{:S(2)}, u32[]{:S(2)}) collective-permute-start(f32[3,32,256]{2,1,0:T(8,128)S(1)} %collective-permute-done.11.rest_6_), channel_id=1, source_target_pairs={{0,8},{8,0},{16,24},{24,16},{1,9},{9,1},{17,25},{25,17},{2,10},{10... | collective-permute-start | bytes 294920 | tf_op jit(solution)/shard_map/ppermute | solution.py:358
  34.9 0.4 %collective-permute-done.7.rest_1_ = f32[3,32,256]{2,1,0:T(8,128)S(1)} collective-permute-done((f32[3,32,256]{2,1,0:T(8,128)S(1)}, f32[3,32,256]{2,1,0:T(8,128)S(1)}, u32[]{:S(2)}, u32[]{:S(2)}) %collective-permute-start.7) | collective-permute-done | bytes 98336 | tf_op jit(solution)/shard_map/ppermute | solution.py:358
  35.4 0.0 collective-permute-done.10.rest_5_
  35.4 0.4 collective-permute-done.9.rest_3_
  35.7 0.2 collective-permute-done.12.rest_7_
  35.9 1.1 %place.1 = (f32[1,256,256]{2,1,0:T(8,128)}, f32[1,256,256]{2,1,0:T(8,128)}, f32[1,256,256]{2,1,0:T(8,128)}) custom-call(f32[3,32,256]{2,1,0:T(8,128)S(1)} %collective-permute-done.6.rest_0_, f32[3,32,256]{2,1,0:T(8,128)S(1)} %collective-permute-done.7.rest_1_, f32[3,32,256]{2,1,0:T(8,128)S(1)} %collective-permute-done.8.rest_2_, ...), custom_call_target="tpu_custom_call" | custom-call | bytes 1572864 | tf_op jit(solution)/shard_map/place/pallas_call | solution.py:344
  (4 shorter events, 0.1 us)
Async XLA Ops:
  1.7 10.4 %collective-permute-start = (f32[168,256]{1,0:T(8,128)S(1)}, f32[168,256]{1,0:T(8,128)S(1)}, u32[]{:S(2)}, u32[]{:S(2)}) collective-permute-start(f32[168,256]{1,0:T(8,128)S(1)} %get-tuple-element.26), channel_id=1, source_target_pairs={{0,1},{1,2},{2,3},{3,4},{4,5},{5,6},{6,7},{7,0},{8,9},{9,10},{10,1... | collective-permute-start | bytes 516104 | tf_op jit(solution)/shard_map/ppermute | solution.py:363
  5.4 6.8 %copy-start = (f32[25,256]{1,0:T(8,128)S(1)}, f32[25,256]{1,0:T(8,128)}, u32[]{:S(2)}) copy-start(f32[25,256]{1,0:T(8,128)} %w_ref.1) | copy-start | bytes 76804
  13.8 1.5 %collective-permute-start.2 = (f32[3,2,32,256]{3,2,1,0:T(8,128)S(1)}, f32[3,2,32,256]{3,2,1,0:T(8,128)S(1)}, u32[]{:S(2)}, u32[]{:S(2)}) collective-permute-start(f32[3,2,32,256]{3,2,1,0:T(8,128)S(1)} %get-tuple-element.35), channel_id=1, source_target_pairs={{0,8},{8,0},{16,24},{24,16},{1,9},{9,1},{17,25},{25,17},{2,10},{10... | collective-permute-start | bytes 589832 | tf_op jit(solution)/shard_map/ppermute | solution.py:358
  13.8 4.5 %collective-permute-start.1 = (f32[3,2,32,256]{3,2,1,0:T(8,128)S(1)}, f32[3,2,32,256]{3,2,1,0:T(8,128)S(1)}, u32[]{:S(2)}, u32[]{:S(2)}) collective-permute-start(f32[3,2,32,256]{3,2,1,0:T(8,128)S(1)} %get-tuple-element.31), channel_id=1, source_target_pairs={{0,8},{8,0},{16,24},{24,16},{1,9},{9,1},{17,25},{25,17},{2,10},{10... | collective-permute-start | bytes 589832 | tf_op jit(solution)/shard_map/ppermute | solution.py:358
  15.3 4.9 %collective-permute-start.5 = (f32[3,1,32,256]{3,2,1,0:T(8,128)S(1)}, f32[3,1,32,256]{3,2,1,0:T(8,128)S(1)}, u32[]{:S(2)}, u32[]{:S(2)}) collective-permute-start(f32[3,1,32,256]{3,2,1,0:T(8,128)S(1)} %get-tuple-element.36.rest_0_), channel_id=1, source_target_pairs={{0,16},{8,24},{16,0},{24,8},{1,17},{9,25},{17,1},{25,9},{2,18},{10... | collective-permute-start | bytes 294920 | tf_op jit(solution)/shard_map/ppermute | solution.py:358
  18.4 4.7 %collective-permute-start.3 = (f32[3,1,32,256]{3,2,1,0:T(8,128)S(1)}, f32[3,1,32,256]{3,2,1,0:T(8,128)S(1)}, u32[]{:S(2)}, u32[]{:S(2)}) collective-permute-start(f32[3,1,32,256]{3,2,1,0:T(8,128)S(1)} %get-tuple-element.39), channel_id=1, source_target_pairs={{0,16},{8,24},{16,0},{24,8},{1,17},{9,25},{17,1},{25,9},{2,18},{10... | collective-permute-start | bytes 294920 | tf_op jit(solution)/shard_map/ppermute | solution.py:358
  20.2 5.2 %collective-permute-start.6 = (f32[3,32,256]{2,1,0:T(8,128)S(1)}, f32[3,32,256]{2,1,0:T(8,128)S(1)}, u32[]{:S(2)}, u32[]{:S(2)}) collective-permute-start(f32[3,32,256]{2,1,0:T(8,128)S(1)} %mean.3), channel_id=1, source_target_pairs={{0,7},{1,0},{2,1},{3,2},{4,3},{5,4},{6,5},{7,6},{8,15},{9,8},{10,9... | collective-permute-start | bytes 294920 | tf_op jit(solution)/shard_map/ppermute | solution.py:373
  23.1 10.7 %collective-permute-start.4 = (f32[3,32,256]{2,1,0:T(8,128)S(1)}, f32[3,32,256]{2,1,0:T(8,128)S(1)}, u32[]{:S(2)}, u32[]{:S(2)}) collective-permute-start(f32[3,32,256]{2,1,0:T(8,128)S(1)} %mean.2), channel_id=1, source_target_pairs={{0,7},{1,0},{2,1},{3,2},{4,3},{5,4},{6,5},{7,6},{8,15},{9,8},{10,9... | collective-permute-start | bytes 294920 | tf_op jit(solution)/shard_map/ppermute | solution.py:373
  25.4 9.0 %collective-permute-start.8 = (f32[3,32,256]{2,1,0:T(8,128)S(1)}, f32[3,32,256]{2,1,0:T(8,128)S(1)}, u32[]{:S(2)}, u32[]{:S(2)}) collective-permute-start(f32[3,32,256]{2,1,0:T(8,128)S(1)} %collective-permute-done.6.rest_0_), channel_id=1, source_target_pairs={{0,16},{8,24},{16,0},{24,8},{1,17},{9,25},{17,1},{25,9},{2,18},{10... | collective-permute-start | bytes 294920 | tf_op jit(solution)/shard_map/ppermute | solution.py:358
  27.6 6.9 %collective-permute-start.11 = (f32[3,32,256]{2,1,0:T(8,128)S(1)}, f32[3,32,256]{2,1,0:T(8,128)S(1)}, u32[]{:S(2)}, u32[]{:S(2)}) collective-permute-start(f32[3,32,256]{2,1,0:T(8,128)S(1)} %mean.2), channel_id=1, source_target_pairs={{0,23},{1,16},{2,17},{3,18},{4,19},{5,20},{6,21},{7,22},{8,31},{9,... | collective-permute-start | bytes 294920 | tf_op jit(solution)/shard_map/ppermute | solution.py:373
  33.8 1.5 %collective-permute-start.10 = (f32[3,32,256]{2,1,0:T(8,128)S(1)}, f32[3,32,256]{2,1,0:T(8,128)S(1)}, u32[]{:S(2)}, u32[]{:S(2)}) collective-permute-start(f32[3,32,256]{2,1,0:T(8,128)S(1)} %collective-permute-done.4.rest_4_), channel_id=1, source_target_pairs={{0,8},{8,0},{16,24},{24,16},{1,9},{9,1},{17,25},{25,17},{2,10},{10... | collective-permute-start | bytes 294920 | tf_op jit(solution)/shard_map/ppermute | solution.py:358
  33.9 1.4 %collective-permute-start.7 = (f32[3,32,256]{2,1,0:T(8,128)S(1)}, f32[3,32,256]{2,1,0:T(8,128)S(1)}, u32[]{:S(2)}, u32[]{:S(2)}) collective-permute-start(f32[3,32,256]{2,1,0:T(8,128)S(1)} %collective-permute-done.6.rest_0_), channel_id=1, source_target_pairs={{0,8},{8,0},{16,24},{24,16},{1,9},{9,1},{17,25},{25,17},{2,10},{10... | collective-permute-start | bytes 294920 | tf_op jit(solution)/shard_map/ppermute | solution.py:358
  34.4 1.3 %collective-permute-start.9 = (f32[3,32,256]{2,1,0:T(8,128)S(1)}, f32[3,32,256]{2,1,0:T(8,128)S(1)}, u32[]{:S(2)}, u32[]{:S(2)}) collective-permute-start(f32[3,32,256]{2,1,0:T(8,128)S(1)} %collective-permute-done.8.rest_2_), channel_id=1, source_target_pairs={{0,8},{8,0},{16,24},{24,16},{1,9},{9,1},{17,25},{25,17},{2,10},{10... | collective-permute-start | bytes 294920 | tf_op jit(solution)/shard_map/ppermute | solution.py:358
  34.5 1.4 %collective-permute-start.12 = (f32[3,32,256]{2,1,0:T(8,128)S(1)}, f32[3,32,256]{2,1,0:T(8,128)S(1)}, u32[]{:S(2)}, u32[]{:S(2)}) collective-permute-start(f32[3,32,256]{2,1,0:T(8,128)S(1)} %collective-permute-done.11.rest_6_), channel_id=1, source_target_pairs={{0,8},{8,0},{16,24},{24,16},{1,9},{9,1},{17,25},{25,17},{2,10},{10... | collective-permute-start | bytes 294920 | tf_op jit(solution)/shard_map/ppermute | solution.py:358

commit v6 on v5

--- a/solution.py
+++ b/solution.py
@@ -98,7 +98,8 @@
             ),
         )
 
-    for index in range(chunks):
+    ahead = 3
+    for index in range(min(ahead, chunks)):
         for copy in copies(index):
             copy.start()
     row = lax.broadcasted_iota(jnp.int32, (width, width), 0)
@@ -111,6 +112,9 @@
     def compare(index):
         for copy in copies(index):
             copy.wait()
+        if index + ahead < chunks:
+            for copy in copies(index + ahead):
+                copy.start()
         part = pl.ds(index * rows, rows)
         return lax.dot_general(
             weights, both_ref[part, :], (((1,), (1,)), ((), ())), preferred_element_type=F32
@@ -399,10 +403,9 @@
     mean1 = mean(keep1, far1, count)
     near1 = delivered(mean1, 0)
     side0 = crossed(near0, 2)
-    mean1, _ = lax.optimization_barrier((mean1, near0))
-    side1 = delivered(mean1, 2)
     factor_new = factor_step(kept, err, turned, near0, factor_new, third, series - third)
-    near1, factor_new = lax.optimization_barrier((near1, factor_new))
+    near1, side0, factor_new = lax.optimization_barrier((near1, side0, factor_new))
+    side1 = crossed(near1, 2)
     pieces = [
         [near0, crossed(near0, 1), side0, crossed(side0, 1)],
         [near1, crossed(near1, 1), side1, crossed(side1, 1)],

time: 37.6 us -> 38 us (1.011); the launches traced: 36.9 us -> 37.9 us
  waiting for transfers between devices: 5.33 us -> 8.72 us
  starting transfers between devices: 17.5 us -> 15 us
    ppermute x3 -> x2, starting transfers between devices: 8.48 us -> 4.09 us  [delivered(): return lax.ppermute(value, ('grp', 'blk'), pairs)]
    ppermute x9 -> x10, waiting for transfers between devices: 3.98 us -> 7.4 us  [crossed(): lax.ppermute(value, 'grp', [(source, source ^ step) for source in range(c...]
    ppermute x9 -> x10, starting transfers between devices: 5.97 us -> 7.89 us  [crossed(): lax.ppermute(value, 'grp', [(source, source ^ step) for source in range(c...]
where the time goes in v6:
time: 38 us; the launch traced here: 37.9 us
  starting transfers between devices  15 us (39%)
  Pallas kernels  12.8 us (34%)
  waiting for transfers between devices  8.72 us (23%)
  between operations  1.39 us (4%)
    ppermute x10, starting transfers between devices, crossed(): lax.ppermute(value, 'grp', [(source, source ^ step) for source in range(c...  7.89 us
    ppermute x10, waiting for transfers between devices, crossed(): lax.ppermute(value, 'grp', [(source, source ^ step) for source in range(c...  7.4 us
    pallas_call x1, Pallas kernels, error_step(): pl.pallas_call(functools.partial(error_kernel, rows), out_shape=(jax.Shap...  5.59 us
    ppermute x2, starting transfers between devices, delivered(): return lax.ppermute(value, ('grp', 'blk'), pairs)  4.09 us
    pallas_call x2, Pallas kernels, factor_step(): pl.pallas_call(functools.partial(factor_kernel, begin, rows, chunks), out...  3.32 us
    ppermute x1, starting transfers between devices, shifted(): lax.ppermute(value, 'blk', [(source, (source + steps) % count) for source...  3.02 us
    pallas_call x1, Pallas kernels, update_step(): pl.pallas_call(functools.partial(update_kernel, count, pieces, lanes), ou...  1.59 us
    ppermute x1, waiting for transfers between devices, shifted(): lax.ppermute(value, 'blk', [(source, (source + steps) % count) for source...  1.15 us
  transfers between devices with their start and end apart: 13, of which 8 were waited for; matrix products, arithmetic and copies ran while one was open for 0% of the time, Pallas kernels for 24%

profile of v6, /device:TPU:0, one launch (start us, length us, event | category | flops | bytes accessed | tf_op | source)
XLA Modules:
  0.0 37.9 jit_solution(16124868106040025220)
XLA Ops:
  0.6 1.1 %prepare.1 = (f32[168,256]{1,0:T(8,128)S(1)}, f32[256,256]{1,0:T(8,128)S(1)}, f32[256,256]{1,0:T(8,128)S(1)}) custom-call(f32[1,256,256]{2,1,0:T(8,128)} %x_hbm.1), custom_call_target="tpu_custom_call" | custom-call | bytes 1048576 | tf_op jit(solution)/shard_map/prepare/pallas_call | solution.py:66
  1.7 3.0 %collective-permute-start = (f32[168,256]{1,0:T(8,128)S(1)}, f32[168,256]{1,0:T(8,128)S(1)}, u32[]{:S(2)}, u32[]{:S(2)}) collective-permute-start(f32[168,256]{1,0:T(8,128)S(1)} %get-tuple-element.26), channel_id=1, source_target_pairs={{0,1},{1,2},{2,3},{3,4},{4,5},{5,6},{6,7},{7,0},{8,9},{9,10},{10,1... | collective-permute-start | bytes 516104 | tf_op jit(solution)/shard_map/ppermute | solution.py:367
  5.4 0.0 copy-start
  5.4 5.6 %errors.1 = (bf16[256,6144]{1,0:T(8,128)(2,1)S(1)}, bf16[6144,512]{1,0:T(8,128)(2,1)S(1)}, f32[256,256]{1,0:T(8,128)S(1)}) custom-call(bf16[6144,256]{1,0:T(8,128)(2,1)} %obs_hbm.1, s32[32,6144]{1,0:T(8,128)} %bitcast.3, bf16[6144,256]{1,0:T(8,128)(2,1)} %f_hbm.1, f32[256,256]{1,0:T(8,128)S(1)} %get-tuple-element.27.turned_ref), custom_call_target="tpu_custom_call" | custom-call | flops 3221225472 | bytes 10223616 | tf_op jit(solution)/shard_map/errors/pallas_call | solution.py:147
  11.0 1.2 %collective-permute-done.halo_ref = f32[168,256]{1,0:T(8,128)S(1)} collective-permute-done((f32[168,256]{1,0:T(8,128)S(1)}, f32[168,256]{1,0:T(8,128)S(1)}, u32[]{:S(2)}, u32[]{:S(2)}) %collective-permute-start) | collective-permute-done | bytes 172064 | tf_op jit(solution)/shard_map/ppermute | solution.py:367
  12.2 0.0 copy-done
  12.2 1.6 %update.1 = (f32[3,2,32,256]{3,2,1,0:T(8,128)S(1)}, f32[3,2,32,256]{3,2,1,0:T(8,128)S(1)}, f32[3,2,32,256]{3,2,1,0:T(8,128)S(1)}, f32[3,2,32,256]{3,2,1,0:T(8,128)S(1)}) custom-call(s32[1,1]{1,0:T(1,128)} %bitcast.2.stratum_ref, f32[168,256]{1,0:T(8,128)S(1)} %collective-permute-done.halo_ref, f32[256,256]{1,0:T(8,128)S(1)} %get-tuple-element.27.turned_ref, ...), custom_call_target="tpu_custom_call" | custom-call | flops 7864320 | bytes 2621440 | tf_op jit(solution)/shard_map/update/pallas_call | solution.py:262
  13.8 0.1 collective-permute-start.2
  13.8 0.5 %collective-permute-start.1 = (f32[3,2,32,256]{3,2,1,0:T(8,128)S(1)}, f32[3,2,32,256]{3,2,1,0:T(8,128)S(1)}, u32[]{:S(2)}, u32[]{:S(2)}) collective-permute-start(f32[3,2,32,256]{3,2,1,0:T(8,128)S(1)} %get-tuple-element.31), channel_id=1, source_target_pairs={{0,8},{8,0},{16,24},{24,16},{1,9},{9,1},{17,25},{25,17},{2,10},{10... | collective-permute-start | bytes 589832 | tf_op jit(solution)/shard_map/ppermute | solution.py:362
  14.3 0.9 %collective-permute-done.2.got_ref = f32[3,2,32,256]{3,2,1,0:T(8,128)S(1)} collective-permute-done((f32[3,2,32,256]{3,2,1,0:T(8,128)S(1)}, f32[3,2,32,256]{3,2,1,0:T(8,128)S(1)}, u32[]{:S(2)}, u32[]{:S(2)}) %collective-permute-start.2) | collective-permute-done | bytes 196640 | tf_op jit(solution)/shard_map/ppermute | solution.py:362
  15.3 1.6 %collective-permute-start.5 = (f32[3,1,32,256]{3,2,1,0:T(8,128)S(1)}, f32[3,1,32,256]{3,2,1,0:T(8,128)S(1)}, u32[]{:S(2)}, u32[]{:S(2)}) collective-permute-start(f32[3,1,32,256]{3,2,1,0:T(8,128)S(1)} %get-tuple-element.36.rest_0_), channel_id=1, source_target_pairs={{0,16},{8,24},{16,0},{24,8},{1,17},{9,25},{17,1},{25,9},{2,18},{10... | collective-permute-start | bytes 294920 | tf_op jit(solution)/shard_map/ppermute | solution.py:362
  16.9 1.5 %factors.2.rest_1_ = bf16[6144,256]{1,0:T(8,128)(2,1)} custom-call(bf16[6144,512]{1,0:T(8,128)(2,1)S(1)} %get-tuple-element.32.both_ref, bf16[256,6144]{1,0:T(8,128)(2,1)S(1)} %get-tuple-element.33.err_ref, f32[256,256]{1,0:T(8,128)S(1)} %get-tuple-element.27.turned_ref, f32[3,1,32,256]{3,2,1,0:T(8,128)S(1)} %get-tuple-element.36.rest_0_), custom_call_target="tpu_custom_call" | custom-call | flops 268435456 | bytes 3145728 | tf_op jit(solution)/shard_map/factors/pallas_call | solution.py:196
  18.3 0.0 collective-permute-done.1.got_ref
  18.4 0.6 %collective-permute-start.3 = (f32[3,1,32,256]{3,2,1,0:T(8,128)S(1)}, f32[3,1,32,256]{3,2,1,0:T(8,128)S(1)}, u32[]{:S(2)}, u32[]{:S(2)}) collective-permute-start(f32[3,1,32,256]{3,2,1,0:T(8,128)S(1)} %get-tuple-element.39), channel_id=1, source_target_pairs={{0,16},{8,24},{16,0},{24,8},{1,17},{9,25},{17,1},{25,9},{2,18},{10... | collective-permute-start | bytes 294920 | tf_op jit(solution)/shard_map/ppermute | solution.py:362
  19.0 1.2 %collective-permute-done.5.got_ref = f32[3,1,32,256]{3,2,1,0:T(8,128)S(1)} collective-permute-done((f32[3,1,32,256]{3,2,1,0:T(8,128)S(1)}, f32[3,1,32,256]{3,2,1,0:T(8,128)S(1)}, u32[]{:S(2)}, u32[]{:S(2)}) %collective-permute-start.5) | collective-permute-done | bytes 98336 | tf_op jit(solution)/shard_map/ppermute | solution.py:362
  20.2 2.0 %collective-permute-start.6 = (f32[3,32,256]{2,1,0:T(8,128)S(1)}, f32[3,32,256]{2,1,0:T(8,128)S(1)}, u32[]{:S(2)}, u32[]{:S(2)}) collective-permute-start(f32[3,32,256]{2,1,0:T(8,128)S(1)} %mean.3), channel_id=1, source_target_pairs={{0,7},{1,0},{2,1},{3,2},{4,3},{5,4},{6,5},{7,6},{8,15},{9,8},{10,9... | collective-permute-start | bytes 294920 | tf_op jit(solution)/shard_map/ppermute | solution.py:377
  22.2 0.9 %collective-permute-done.3.got_ref = f32[3,1,32,256]{3,2,1,0:T(8,128)S(1)} collective-permute-done((f32[3,1,32,256]{3,2,1,0:T(8,128)S(1)}, f32[3,1,32,256]{3,2,1,0:T(8,128)S(1)}, u32[]{:S(2)}, u32[]{:S(2)}) %collective-permute-start.3) | collective-permute-done | bytes 98336 | tf_op jit(solution)/shard_map/ppermute | solution.py:362
  23.1 2.1 %collective-permute-start.4 = (f32[3,32,256]{2,1,0:T(8,128)S(1)}, f32[3,32,256]{2,1,0:T(8,128)S(1)}, u32[]{:S(2)}, u32[]{:S(2)}) collective-permute-start(f32[3,32,256]{2,1,0:T(8,128)S(1)} %mean.2), channel_id=1, source_target_pairs={{0,7},{1,0},{2,1},{3,2},{4,3},{5,4},{6,5},{7,6},{8,15},{9,8},{10,9... | collective-permute-start | bytes 294920 | tf_op jit(solution)/shard_map/ppermute | solution.py:377
  25.2 0.2 collective-permute-done.6.rest_0_
  25.4 2.2 %collective-permute-start.7 = (f32[3,32,256]{2,1,0:T(8,128)S(1)}, f32[3,32,256]{2,1,0:T(8,128)S(1)}, u32[]{:S(2)}, u32[]{:S(2)}) collective-permute-start(f32[3,32,256]{2,1,0:T(8,128)S(1)} %collective-permute-done.6.rest_0_), channel_id=1, source_target_pairs={{0,16},{8,24},{16,0},{24,8},{1,17},{9,25},{17,1},{25,9},{2,18},{10... | collective-permute-start | bytes 294920 | tf_op jit(solution)/shard_map/ppermute | solution.py:362
  27.6 1.9 %factors.3 = bf16[6144,256]{1,0:T(8,128)(2,1)} custom-call(bf16[6144,512]{1,0:T(8,128)(2,1)S(1)} %get-tuple-element.32.both_ref, bf16[256,6144]{1,0:T(8,128)(2,1)S(1)} %get-tuple-element.33.err_ref, f32[256,256]{1,0:T(8,128)S(1)} %get-tuple-element.27.turned_ref, f32[3,32,256]{2,1,0:T(8,128)S(1)} %collective-permute-done.6.rest_0_, ...), custom_call_target="tpu_custom_call", output_to_operand_aliasing={{}: (4, {})} | custom-call | flops 536870912 | bytes 6291456 | tf_op jit(solution)/shard_map/factors/pallas_call | solution.py:196
  29.4 0.0 collective-permute-done.4.rest_4_
  29.4 1.0 %collective-permute-done.7.rest_2_ = f32[3,32,256]{2,1,0:T(8,128)S(1)} collective-permute-done((f32[3,32,256]{2,1,0:T(8,128)S(1)}, f32[3,32,256]{2,1,0:T(8,128)S(1)}, u32[]{:S(2)}, u32[]{:S(2)}) %collective-permute-start.7) | collective-permute-done | bytes 98336 | tf_op jit(solution)/shard_map/ppermute | solution.py:362
  30.4 2.5 %collective-permute-start.11 = (f32[3,32,256]{2,1,0:T(8,128)S(1)}, f32[3,32,256]{2,1,0:T(8,128)S(1)}, u32[]{:S(2)}, u32[]{:S(2)}) collective-permute-start(f32[3,32,256]{2,1,0:T(8,128)S(1)} %collective-permute-done.4.rest_4_), channel_id=1, source_target_pairs={{0,16},{8,24},{16,0},{24,8},{1,17},{9,25},{17,1},{25,9},{2,18},{10... | collective-permute-start | bytes 294920 | tf_op jit(solution)/shard_map/ppermute | solution.py:362
  32.9 0.0 collective-permute-start.8
  32.9 0.5 %collective-permute-start.10 = (f32[3,32,256]{2,1,0:T(8,128)S(1)}, f32[3,32,256]{2,1,0:T(8,128)S(1)}, u32[]{:S(2)}, u32[]{:S(2)}) collective-permute-start(f32[3,32,256]{2,1,0:T(8,128)S(1)} %collective-permute-done.4.rest_4_), channel_id=1, source_target_pairs={{0,8},{8,0},{16,24},{24,16},{1,9},{9,1},{17,25},{25,17},{2,10},{10... | collective-permute-start | bytes 294920 | tf_op jit(solution)/shard_map/ppermute | solution.py:362
  33.4 0.0 collective-permute-start.9
  33.4 2.1 %collective-permute-done.11.rest_6_ = f32[3,32,256]{2,1,0:T(8,128)S(1)} collective-permute-done((f32[3,32,256]{2,1,0:T(8,128)S(1)}, f32[3,32,256]{2,1,0:T(8,128)S(1)}, u32[]{:S(2)}, u32[]{:S(2)}) %collective-permute-start.11) | collective-permute-done | bytes 98336 | tf_op jit(solution)/shard_map/ppermute | solution.py:362
  35.5 0.0 collective-permute-start.12
  35.5 0.0 collective-permute-done.8.rest_1_
  35.5 0.0 collective-permute-done.9.rest_3_
  35.5 0.0 collective-permute-done.10.rest_5_
  35.5 1.3 %collective-permute-done.12.rest_7_ = f32[3,32,256]{2,1,0:T(8,128)S(1)} collective-permute-done((f32[3,32,256]{2,1,0:T(8,128)S(1)}, f32[3,32,256]{2,1,0:T(8,128)S(1)}, u32[]{:S(2)}, u32[]{:S(2)}) %collective-permute-start.12) | collective-permute-done | bytes 98336 | tf_op jit(solution)/shard_map/ppermute | solution.py:362
  36.8 1.1 %place.1 = (f32[1,256,256]{2,1,0:T(8,128)}, f32[1,256,256]{2,1,0:T(8,128)}, f32[1,256,256]{2,1,0:T(8,128)}) custom-call(f32[3,32,256]{2,1,0:T(8,128)S(1)} %collective-permute-done.6.rest_0_, f32[3,32,256]{2,1,0:T(8,128)S(1)} %collective-permute-done.8.rest_1_, f32[3,32,256]{2,1,0:T(8,128)S(1)} %collective-permute-done.7.rest_2_, ...), custom_call_target="tpu_custom_call" | custom-call | bytes 1572864 | tf_op jit(solution)/shard_map/place/pallas_call | solution.py:348
  (4 shorter events, 0.1 us)
Async XLA Ops:
  1.7 10.4 %collective-permute-start = (f32[168,256]{1,0:T(8,128)S(1)}, f32[168,256]{1,0:T(8,128)S(1)}, u32[]{:S(2)}, u32[]{:S(2)}) collective-permute-start(f32[168,256]{1,0:T(8,128)S(1)} %get-tuple-element.26), channel_id=1, source_target_pairs={{0,1},{1,2},{2,3},{3,4},{4,5},{5,6},{6,7},{7,0},{8,9},{9,10},{10,1... | collective-permute-start | bytes 516104 | tf_op jit(solution)/shard_map/ppermute | solution.py:367
  5.4 6.8 %copy-start = (f32[25,256]{1,0:T(8,128)S(1)}, f32[25,256]{1,0:T(8,128)}, u32[]{:S(2)}) copy-start(f32[25,256]{1,0:T(8,128)} %w_ref.1) | copy-start | bytes 76804
  13.8 1.5 %collective-permute-start.2 = (f32[3,2,32,256]{3,2,1,0:T(8,128)S(1)}, f32[3,2,32,256]{3,2,1,0:T(8,128)S(1)}, u32[]{:S(2)}, u32[]{:S(2)}) collective-permute-start(f32[3,2,32,256]{3,2,1,0:T(8,128)S(1)} %get-tuple-element.35), channel_id=1, source_target_pairs={{0,8},{8,0},{16,24},{24,16},{1,9},{9,1},{17,25},{25,17},{2,10},{10... | collective-permute-start | bytes 589832 | tf_op jit(solution)/shard_map/ppermute | solution.py:362
  13.8 4.5 %collective-permute-start.1 = (f32[3,2,32,256]{3,2,1,0:T(8,128)S(1)}, f32[3,2,32,256]{3,2,1,0:T(8,128)S(1)}, u32[]{:S(2)}, u32[]{:S(2)}) collective-permute-start(f32[3,2,32,256]{3,2,1,0:T(8,128)S(1)} %get-tuple-element.31), channel_id=1, source_target_pairs={{0,8},{8,0},{16,24},{24,16},{1,9},{9,1},{17,25},{25,17},{2,10},{10... | collective-permute-start | bytes 589832 | tf_op jit(solution)/shard_map/ppermute | solution.py:362
  15.3 4.9 %collective-permute-start.5 = (f32[3,1,32,256]{3,2,1,0:T(8,128)S(1)}, f32[3,1,32,256]{3,2,1,0:T(8,128)S(1)}, u32[]{:S(2)}, u32[]{:S(2)}) collective-permute-start(f32[3,1,32,256]{3,2,1,0:T(8,128)S(1)} %get-tuple-element.36.rest_0_), channel_id=1, source_target_pairs={{0,16},{8,24},{16,0},{24,8},{1,17},{9,25},{17,1},{25,9},{2,18},{10... | collective-permute-start | bytes 294920 | tf_op jit(solution)/shard_map/ppermute | solution.py:362
  18.4 4.7 %collective-permute-start.3 = (f32[3,1,32,256]{3,2,1,0:T(8,128)S(1)}, f32[3,1,32,256]{3,2,1,0:T(8,128)S(1)}, u32[]{:S(2)}, u32[]{:S(2)}) collective-permute-start(f32[3,1,32,256]{3,2,1,0:T(8,128)S(1)} %get-tuple-element.39), channel_id=1, source_target_pairs={{0,16},{8,24},{16,0},{24,8},{1,17},{9,25},{17,1},{25,9},{2,18},{10... | collective-permute-start | bytes 294920 | tf_op jit(solution)/shard_map/ppermute | solution.py:362
  20.2 5.2 %collective-permute-start.6 = (f32[3,32,256]{2,1,0:T(8,128)S(1)}, f32[3,32,256]{2,1,0:T(8,128)S(1)}, u32[]{:S(2)}, u32[]{:S(2)}) collective-permute-start(f32[3,32,256]{2,1,0:T(8,128)S(1)} %mean.3), channel_id=1, source_target_pairs={{0,7},{1,0},{2,1},{3,2},{4,3},{5,4},{6,5},{7,6},{8,15},{9,8},{10,9... | collective-permute-start | bytes 294920 | tf_op jit(solution)/shard_map/ppermute | solution.py:377
  23.1 6.3 %collective-permute-start.4 = (f32[3,32,256]{2,1,0:T(8,128)S(1)}, f32[3,32,256]{2,1,0:T(8,128)S(1)}, u32[]{:S(2)}, u32[]{:S(2)}) collective-permute-start(f32[3,32,256]{2,1,0:T(8,128)S(1)} %mean.2), channel_id=1, source_target_pairs={{0,7},{1,0},{2,1},{3,2},{4,3},{5,4},{6,5},{7,6},{8,15},{9,8},{10,9... | collective-permute-start | bytes 294920 | tf_op jit(solution)/shard_map/ppermute | solution.py:377
  25.4 5.0 %collective-permute-start.7 = (f32[3,32,256]{2,1,0:T(8,128)S(1)}, f32[3,32,256]{2,1,0:T(8,128)S(1)}, u32[]{:S(2)}, u32[]{:S(2)}) collective-permute-start(f32[3,32,256]{2,1,0:T(8,128)S(1)} %collective-permute-done.6.rest_0_), channel_id=1, source_target_pairs={{0,16},{8,24},{16,0},{24,8},{1,17},{9,25},{17,1},{25,9},{2,18},{10... | collective-permute-start | bytes 294920 | tf_op jit(solution)/shard_map/ppermute | solution.py:362
  30.4 5.1 %collective-permute-start.11 = (f32[3,32,256]{2,1,0:T(8,128)S(1)}, f32[3,32,256]{2,1,0:T(8,128)S(1)}, u32[]{:S(2)}, u32[]{:S(2)}) collective-permute-start(f32[3,32,256]{2,1,0:T(8,128)S(1)} %collective-permute-done.4.rest_4_), channel_id=1, source_target_pairs={{0,16},{8,24},{16,0},{24,8},{1,17},{9,25},{17,1},{25,9},{2,18},{10... | collective-permute-start | bytes 294920 | tf_op jit(solution)/shard_map/ppermute | solution.py:362
  32.9 2.6 %collective-permute-start.8 = (f32[3,32,256]{2,1,0:T(8,128)S(1)}, f32[3,32,256]{2,1,0:T(8,128)S(1)}, u32[]{:S(2)}, u32[]{:S(2)}) collective-permute-start(f32[3,32,256]{2,1,0:T(8,128)S(1)} %collective-permute-done.6.rest_0_), channel_id=1, source_target_pairs={{0,8},{8,0},{16,24},{24,16},{1,9},{9,1},{17,25},{25,17},{2,10},{10... | collective-permute-start | bytes 294920 | tf_op jit(solution)/shard_map/ppermute | solution.py:362
  32.9 2.6 %collective-permute-start.10 = (f32[3,32,256]{2,1,0:T(8,128)S(1)}, f32[3,32,256]{2,1,0:T(8,128)S(1)}, u32[]{:S(2)}, u32[]{:S(2)}) collective-permute-start(f32[3,32,256]{2,1,0:T(8,128)S(1)} %collective-permute-done.4.rest_4_), channel_id=1, source_target_pairs={{0,8},{8,0},{16,24},{24,16},{1,9},{9,1},{17,25},{25,17},{2,10},{10... | collective-permute-start | bytes 294920 | tf_op jit(solution)/shard_map/ppermute | solution.py:362
  33.4 2.1 %collective-permute-start.9 = (f32[3,32,256]{2,1,0:T(8,128)S(1)}, f32[3,32,256]{2,1,0:T(8,128)S(1)}, u32[]{:S(2)}, u32[]{:S(2)}) collective-permute-start(f32[3,32,256]{2,1,0:T(8,128)S(1)} %collective-permute-done.7.rest_2_), channel_id=1, source_target_pairs={{0,8},{8,0},{16,24},{24,16},{1,9},{9,1},{17,25},{25,17},{2,10},{10... | collective-permute-start | bytes 294920 | tf_op jit(solution)/shard_map/ppermute | solution.py:362
  35.5 1.3 %collective-permute-start.12 = (f32[3,32,256]{2,1,0:T(8,128)S(1)}, f32[3,32,256]{2,1,0:T(8,128)S(1)}, u32[]{:S(2)}, u32[]{:S(2)}) collective-permute-start(f32[3,32,256]{2,1,0:T(8,128)S(1)} %collective-permute-done.11.rest_6_), channel_id=1, source_target_pairs={{0,8},{8,0},{16,24},{24,16},{1,9},{9,1},{17,25},{25,17},{2,10},{10... | collective-permute-start | bytes 294920 | tf_op jit(solution)/shard_map/ppermute | solution.py:362

commit v7 on v5

--- a/solution.py
+++ b/solution.py
@@ -202,77 +202,130 @@
     )(both, err, turned, *rest)
 
 
-def update_kernel(
-    count, pieces, lanes, stratum_ref, halo_ref, turned_ref, w_ref, gd_ref, x_ref, m_hbm, v_hbm, *rest
-):
-    outs, scratch = rest[: 2 * pieces], rest[2 * pieces :]
-    z_ref, r_ref, m_ref, v_ref, new_ref, sems = scratch
+def regress_kernel(lanes, turned_ref, w_ref, gd_ref, m_hbm, v_hbm, base_ref, m_ref, v_ref, z_ref, r_ref, sems):
     m_copy = pltpu.make_async_copy(m_hbm.at[0], m_ref, sems.at[0])
     v_copy = pltpu.make_async_copy(v_hbm.at[0], v_ref, sems.at[1])
     m_copy.start()
     v_copy.start()
     width, rank = turned_ref.shape
-    share = rank // count
-    block_index = lax.rem(lax.axis_index("blk") + stratum_ref[...], lax.axis_size("blk"))
     lags = list(range(1, w_ref.shape[0])) + [SEASON]
     for part in range(rank // lanes):
         columns = slice(part * lanes, (part + 1) * lanes)
-        z_ref[part, :SEASON, :] = jnp.where(block_index == 0, 0.0, halo_ref[:, columns])
+        z_ref[part, :SEASON, :] = jnp.zeros((SEASON, lanes), F32)
         z_ref[part, SEASON:, :] = turned_ref[:, columns]
+        r_ref[part, width:, :] = jnp.zeros((SEASON, lanes), F32)
         resid = turned_ref[:, columns]
         for index, lag in enumerate(lags):
             begin = SEASON - lag
             resid = resid - w_ref[index : index + 1, columns] * z_ref[part, begin : begin + width, :]
         r_ref[part, :width, :] = resid
-        r_ref[part, width:, :] = jnp.zeros((SEASON, lanes), F32)
-        back = resid
+        back = data_scale * gd_ref[:, columns] + resid
         for index, lag in enumerate(lags):
             back = back - w_ref[index : index + 1, columns] * r_ref[part, lag : lag + width, :]
-        z_ref[part, :width, :] = data_scale * gd_ref[:, columns] + back
+        base_ref[:, columns] = back
     m_copy.wait()
     v_copy.wait()
+
+
+def regress_step(turned, weights, gd, m, v):
+    width, rank = gd.shape
+    lanes = 128
+    return pl.pallas_call(
+        functools.partial(regress_kernel, lanes),
+        out_shape=(
+            jax.ShapeDtypeStruct((width, rank), F32),
+            jax.ShapeDtypeStruct((rank, width), F32),
+            jax.ShapeDtypeStruct((rank, width), F32),
+        ),
+        in_specs=[whole()] * 3 + [far()] * 2,
+        out_specs=(whole(),) * 3,
+        scratch_shapes=[
+            pltpu.VMEM((rank // lanes, SEASON + width, lanes), F32),
+            pltpu.VMEM((rank // lanes, SEASON + width, lanes), F32),
+            pltpu.SemaphoreType.DMA((2,)),
+        ],
+        compiler_params=params(),
+        cost_estimate=cost(100 * rank * width, 6 * rank * width * 4),
+        name="regress",
+    )(turned, weights, gd, held(m), held(v))
+
+
+def update_kernel(
+    count, sizes, lanes, stratum_ref, halo_ref, w_ref, base_ref, x_ref, m_ref, v_ref, *rest
+):
+    outs, (z_ref, r_ref, new_ref) = rest[: 2 * len(sizes)], rest[2 * len(sizes) :]
+    width, rank = base_ref.shape
+    share = rank // count
+    short = w_ref.shape[0] - 1
+    reach = -(-short // 8) * 8
+    block_index = lax.rem(lax.axis_index("blk") + stratum_ref[...], lax.axis_size("blk"))
+    for part in range(rank // lanes):
+        columns = slice(part * lanes, (part + 1) * lanes)
+        halo = jnp.where(block_index == 0, 0.0, halo_ref[:, columns])
+        z_ref[part, :SEASON, :] = halo
+        z_ref[part, SEASON:, :] = jnp.zeros((reach, lanes), F32)
+        r_ref[part, :SEASON, :] = -w_ref[short : short + 1, columns] * halo
+        r_ref[part, SEASON:, :] = jnp.zeros((reach, lanes), F32)
+        first_rows = r_ref[part, :reach, :]
+        for lag in range(1, short + 1):
+            begin = SEASON - lag
+            first_rows = first_rows - w_ref[lag - 1 : lag, columns] * z_ref[part, begin : begin + reach, :]
+        r_ref[part, :reach, :] = first_rows
+        back = r_ref[part, :SEASON, :]
+        for lag in range(1, short + 1):
+            back = back - w_ref[lag - 1 : lag, columns] * r_ref[part, lag : lag + SEASON, :]
+        base_ref[:SEASON, columns] += back
     for part in range(rank // lanes):
         rows = slice(part * lanes, (part + 1) * lanes)
-        gradient = z_ref[part, :width, :].T
+        gradient = base_ref[:, rows].T
         first = beta_one * m_ref[rows, :] + (1.0 - beta_one) * gradient
         second = beta_two * v_ref[rows, :] + (1.0 - beta_two) * gradient * gradient
         new_ref[0, rows, :] = x_ref[rows, :] - step_rate * first / (jnp.sqrt(second) + adam_eps)
         new_ref[1, rows, :] = first
         new_ref[2, rows, :] = second
-    size = share // pieces
     odd = lax.axis_index("grp") % 2
-    for piece in range(pieces):
+    begin = 0
+    for piece, size in enumerate(sizes):
         for line in range(count // 2):
             for side in range(2):
                 one = 2 * line + (odd if side == 0 else 1 - odd)
-                start = pl.multiple_of(one * share + piece * size, size)
+                start = pl.multiple_of(one * share + begin, 8)
                 for which in range(3):
                     outs[2 * piece + side][which, line] = new_ref[which, pl.ds(start, size), :]
-
-
-def update_step(stratum, halo, turned, weights, gd, x, m, v, count, pieces):
-    width, rank = gd.shape
+        begin += size
+
+
+def update_step(stratum, halo, weights, base, x, m, v, count, sizes):
+    width, rank = base.shape
     lanes = 128
-    size = rank // count // pieces
-    out = jax.ShapeDtypeStruct((3, count // 2, size, width), F32)
+    reach = -(-(weights.shape[0] - 1) // 8) * 8
+    kinds = []
+    for size in sizes:
+        kinds += [jax.ShapeDtypeStruct((3, count // 2, size, width), F32)] * 2
+
+    def kernel(stratum_ref, halo_ref, w_ref, base_ref, x_ref, m_ref, v_ref, *rest):
+        work = rest[-1]
+        work[...] = base_ref[...]
+        update_kernel(
+            count, sizes, lanes, stratum_ref, halo_ref, w_ref, work, x_ref, m_ref, v_ref, *rest[:-1]
+        )
+
     outs = pl.pallas_call(
-        functools.partial(update_kernel, count, pieces, lanes),
-        out_shape=(out,) * (2 * pieces),
-        in_specs=[whole()] * 6 + [far()] * 2,
-        out_specs=(whole(),) * (2 * pieces),
+        kernel,
+        out_shape=tuple(kinds),
+        in_specs=[whole()] * 7,
+        out_specs=(whole(),) * len(kinds),
         scratch_shapes=[
-            pltpu.VMEM((rank // lanes, SEASON + width, lanes), F32),
-            pltpu.VMEM((rank // lanes, SEASON + width, lanes), F32),
-            pltpu.VMEM((rank, width), F32),
-            pltpu.VMEM((rank, width), F32),
+            pltpu.VMEM((rank // lanes, SEASON + reach, lanes), F32),
+            pltpu.VMEM((rank // lanes, SEASON + reach, lanes), F32),
             pltpu.VMEM((3, rank, width), F32),
-            pltpu.SemaphoreType.DMA((2,)),
+            pltpu.VMEM((width, rank), F32),
         ],
         compiler_params=params(),
-        cost_estimate=cost(120 * rank * width, 10 * rank * width * 4),
+        cost_estimate=cost(60 * rank * width, 10 * rank * width * 4),
         name="update",
-    )(stratum.reshape(1, 1), halo, turned, weights, gd, x, held(m), held(v))
-    return [(outs[2 * piece], outs[2 * piece + 1]) for piece in range(pieces)]
+    )(stratum.reshape(1, 1), halo, weights, base, x, m, v)
+    return [(outs[2 * piece], outs[2 * piece + 1]) for piece in range(len(sizes))]
 
 
 def halve_kernel(level, kept_ref, got_ref, keep_ref, send_ref):
@@ -317,12 +370,12 @@
 
 def place_kernel(count, share, *rest):
     parts, outs, sems = rest[:-4], rest[-4:-1], rest[-1]
-    size = parts[0].shape[1]
     group = lax.axis_index("grp")
     copies = []
     for index, part in enumerate(parts):
-        piece, step = divmod(index, count)
-        start = pl.multiple_of((group ^ step) * share + piece * size, size)
+        begin = sum(before.shape[1] for before in parts[: index // count * count : count])
+        size = part.shape[1]
+        start = pl.multiple_of((group ^ (index % count)) * share + begin, 8)
         for which in range(3):
             copies.append(
                 pltpu.make_async_copy(
@@ -338,8 +391,8 @@
 def place(pieces):
     parts = [part for piece in pieces for part in piece]
     count = len(pieces[0])
-    _, size, width = parts[0].shape
-    share = size * len(pieces)
+    width = parts[0].shape[2]
+    share = sum(piece[0].shape[1] for piece in pieces)
     out = jax.ShapeDtypeStruct((1, count * share, width), F32)
     return pl.pallas_call(
         functools.partial(place_kernel, count, share),
@@ -381,8 +434,11 @@
     tail, turned, x = prepare(x_blocks)
     halo = shifted(tail, 1)
     err, kept, gd = error_step(obs, mask_bits.T, factors, turned)
+    base, first, second = regress_step(turned, ar_weights, gd, first_moment, second_moment)
+    share = x.shape[0] // count
+    lead = share // 2
     (keep0, send0), (keep1, send1) = update_step(
-        stratum, halo, turned, ar_weights, gd, x, first_moment, second_moment, count, 2
+        stratum, halo, ar_weights, base, x, first, second, count, (lead, share - lead)
     )
 
     got0 = crossed(send0, 1)
@@ -398,9 +454,8 @@
     near0 = delivered(mean0, 0)
     mean1 = mean(keep1, far1, count)
     near1 = delivered(mean1, 0)
+    side1 = delivered(mean1, 2)
     side0 = crossed(near0, 2)
-    mean1, _ = lax.optimization_barrier((mean1, near0))
-    side1 = delivered(mean1, 2)
     factor_new = factor_step(kept, err, turned, near0, factor_new, third, series - third)
     near1, factor_new = lax.optimization_barrier((near1, factor_new))
     pieces = [

time: 37.6 us -> 34.9 us (0.928); the launches traced: 36.9 us -> 34.8 us
  starting transfers between devices: 17.5 us -> 15.8 us
  waiting for transfers between devices: 5.33 us -> 4.38 us
  Pallas kernels: 12.7 us -> 13.2 us
    ppermute x9, starting transfers between devices: 5.97 us -> 4.67 us  [crossed(): lax.ppermute(value, 'grp', [(source, source ^ step) for source in range(c...]
    ppermute x1, waiting for transfers between devices: 1.17 us -> 0.01 us  [shifted(): lax.ppermute(value, 'blk', [(source, (source + steps) % count) for source...]
    pallas_call x1 -> x2, Pallas kernels: 1.59 us -> 1.99 us  [the longest x1 1.2 us: regress_step(): pl.pallas_call(functools.partial(regress_kernel, lanes), out_shape=(jax.S...]
    ppermute x9, waiting for transfers between devices: 3.98 us -> 4.37 us  [crossed(): lax.ppermute(value, 'grp', [(source, source ^ step) for source in range(c...]
  transfers between devices with their start and end apart: 13 -> 13, of which waited for: 8 -> 5; matrix products, arithmetic and copies ran while one was open for 0% -> 0% of each run, Pallas kernels for 24% -> 29%
where the time goes in v7:
time: 34.9 us; the launch traced here: 34.8 us
  starting transfers between devices  15.8 us (45%)
  Pallas kernels  13.2 us (38%)
  waiting for transfers between devices  4.38 us (13%)
  between operations  1.41 us (4%)
    ppermute x3, starting transfers between devices, delivered(): return lax.ppermute(value, ('grp', 'blk'), pairs)  8.14 us
    pallas_call x1, Pallas kernels, error_step(): pl.pallas_call(functools.partial(error_kernel, rows), out_shape=(jax.Shap...  5.57 us
    ppermute x9, starting transfers between devices, crossed(): lax.ppermute(value, 'grp', [(source, source ^ step) for source in range(c...  4.67 us
    ppermute x9, waiting for transfers between devices, crossed(): lax.ppermute(value, 'grp', [(source, source ^ step) for source in range(c...  4.37 us
    pallas_call x2, Pallas kernels, factor_step(): pl.pallas_call(functools.partial(factor_kernel, begin, rows, chunks), out...  3.33 us
    ppermute x1, starting transfers between devices, shifted(): lax.ppermute(value, 'blk', [(source, (source + steps) % count) for source...  3.02 us
    pallas_call x1, Pallas kernels, regress_step(): pl.pallas_call(functools.partial(regress_kernel, lanes), out_shape=(jax.S...  1.2 us
    pallas_call x1, Pallas kernels, prepare(): pl.pallas_call(prepare_kernel, out_shape=(jax.ShapeDtypeStruct((SEASON, r...  1.09 us
  transfers between devices with their start and end apart: 13, of which 5 were waited for; matrix products, arithmetic and copies ran while one was open for 0% of the time, Pallas kernels for 29%

profile of v7, /device:TPU:0, one launch (start us, length us, event | category | flops | bytes accessed | tf_op | source)
XLA Modules:
  0.0 34.8 jit_solution(5496145452032016242)
XLA Ops:
  0.6 1.1 %prepare.1 = (f32[168,256]{1,0:T(8,128)S(1)}, f32[256,256]{1,0:T(8,128)S(1)}, f32[256,256]{1,0:T(8,128)S(1)}) custom-call(f32[1,256,256]{2,1,0:T(8,128)} %x_hbm.1), custom_call_target="tpu_custom_call" | custom-call | bytes 1048576 | tf_op jit(solution)/shard_map/prepare/pallas_call | solution.py:66
  1.7 3.0 %collective-permute-start = (f32[168,256]{1,0:T(8,128)S(1)}, f32[168,256]{1,0:T(8,128)S(1)}, u32[]{:S(2)}, u32[]{:S(2)}) collective-permute-start(f32[168,256]{1,0:T(8,128)S(1)} %get-tuple-element.28), channel_id=1, source_target_pairs={{0,1},{1,2},{2,3},{3,4},{4,5},{5,6},{6,7},{7,0},{8,9},{9,10},{10,1... | collective-permute-start | bytes 516104 | tf_op jit(solution)/shard_map/ppermute | solution.py:416
  5.4 0.0 copy-start
  5.4 5.6 %errors.1 = (bf16[256,6144]{1,0:T(8,128)(2,1)S(1)}, bf16[6144,512]{1,0:T(8,128)(2,1)S(1)}, f32[256,256]{1,0:T(8,128)S(1)}) custom-call(bf16[6144,256]{1,0:T(8,128)(2,1)} %obs_hbm.1, s32[32,6144]{1,0:T(8,128)} %bitcast.3, bf16[6144,256]{1,0:T(8,128)(2,1)} %f_hbm.1, f32[256,256]{1,0:T(8,128)S(1)} %get-tuple-element.29.turned_ref), custom_call_target="tpu_custom_call" | custom-call | flops 3221225472 | bytes 10223616 | tf_op jit(solution)/shard_map/errors/pallas_call | solution.py:143
  11.0 0.0 copy-done
  11.0 1.2 %regress.1 = (f32[256,256]{1,0:T(8,128)S(1)}, f32[256,256]{1,0:T(8,128)S(1)}, f32[256,256]{1,0:T(8,128)S(1)}) custom-call(f32[256,256]{1,0:T(8,128)S(1)} %get-tuple-element.29.turned_ref, f32[25,256]{1,0:T(8,128)S(1)} %copy-done, f32[256,256]{1,0:T(8,128)S(1)} %get-tuple-element.30.gd_ref, f32[1,256,256]{2,1,0:T(8,128)} %m_hbm.1, f32[1,256,256]{2,1,0:T(8,128)} %v_hbm.1), custom_call_target="tpu_custom_call" | custom-call | flops 6553600 | bytes 1572864 | tf_op jit(solution)/shard_map/regress/pallas_call | solution.py:233
  12.2 0.0 collective-permute-done.halo_ref
  12.2 0.8 %update.1 = (f32[3,2,32,256]{3,2,1,0:T(8,128)S(1)}, f32[3,2,32,256]{3,2,1,0:T(8,128)S(1)}, f32[3,2,32,256]{3,2,1,0:T(8,128)S(1)}, f32[3,2,32,256]{3,2,1,0:T(8,128)S(1)}) custom-call(s32[1,1]{1,0:T(1,128)} %bitcast.2.stratum_ref, f32[168,256]{1,0:T(8,128)S(1)} %collective-permute-done.halo_ref, f32[25,256]{1,0:T(8,128)S(1)} %copy-done, ...), custom_call_target="tpu_custom_call" | custom-call | flops 3932160 | bytes 2621440 | tf_op jit(solution)/shard_map/update/pallas_call | solution.py:313
  13.0 0.1 collective-permute-start.2
  13.1 0.5 %collective-permute-start.1 = (f32[3,2,32,256]{3,2,1,0:T(8,128)S(1)}, f32[3,2,32,256]{3,2,1,0:T(8,128)S(1)}, u32[]{:S(2)}, u32[]{:S(2)}) collective-permute-start(f32[3,2,32,256]{3,2,1,0:T(8,128)S(1)} %get-tuple-element.36), channel_id=1, source_target_pairs={{0,8},{8,0},{16,24},{24,16},{1,9},{9,1},{17,25},{25,17},{2,10},{10... | collective-permute-start | bytes 589832 | tf_op jit(solution)/shard_map/ppermute | solution.py:411
  13.6 0.9 %collective-permute-done.2.got_ref = f32[3,2,32,256]{3,2,1,0:T(8,128)S(1)} collective-permute-done((f32[3,2,32,256]{3,2,1,0:T(8,128)S(1)}, f32[3,2,32,256]{3,2,1,0:T(8,128)S(1)}, u32[]{:S(2)}, u32[]{:S(2)}) %collective-permute-start.2) | collective-permute-done | bytes 196640 | tf_op jit(solution)/shard_map/ppermute | solution.py:411
  14.6 1.6 %collective-permute-start.5 = (f32[3,1,32,256]{3,2,1,0:T(8,128)S(1)}, f32[3,1,32,256]{3,2,1,0:T(8,128)S(1)}, u32[]{:S(2)}, u32[]{:S(2)}) collective-permute-start(f32[3,1,32,256]{3,2,1,0:T(8,128)S(1)} %get-tuple-element.41.rest_0_), channel_id=1, source_target_pairs={{0,16},{8,24},{16,0},{24,8},{1,17},{9,25},{17,1},{25,9},{2,18},{10... | collective-permute-start | bytes 294920 | tf_op jit(solution)/shard_map/ppermute | solution.py:411
  16.1 1.5 %factors.2.rest_1_ = bf16[6144,256]{1,0:T(8,128)(2,1)} custom-call(bf16[6144,512]{1,0:T(8,128)(2,1)S(1)} %get-tuple-element.37.both_ref, bf16[256,6144]{1,0:T(8,128)(2,1)S(1)} %get-tuple-element.38.err_ref, f32[256,256]{1,0:T(8,128)S(1)} %get-tuple-element.29.turned_ref, f32[3,1,32,256]{3,2,1,0:T(8,128)S(1)} %get-tuple-element.41.rest_0_), custom_call_target="tpu_custom_call" | custom-call | flops 268435456 | bytes 3145728 | tf_op jit(solution)/shard_map/factors/pallas_call | solution.py:192
  17.6 0.0 collective-permute-done.1.got_ref
  17.7 0.6 %collective-permute-start.3 = (f32[3,1,32,256]{3,2,1,0:T(8,128)S(1)}, f32[3,1,32,256]{3,2,1,0:T(8,128)S(1)}, u32[]{:S(2)}, u32[]{:S(2)}) collective-permute-start(f32[3,1,32,256]{3,2,1,0:T(8,128)S(1)} %get-tuple-element.44), channel_id=1, source_target_pairs={{0,16},{8,24},{16,0},{24,8},{1,17},{9,25},{17,1},{25,9},{2,18},{10... | collective-permute-start | bytes 294920 | tf_op jit(solution)/shard_map/ppermute | solution.py:411
  18.2 1.2 %collective-permute-done.5.got_ref = f32[3,1,32,256]{3,2,1,0:T(8,128)S(1)} collective-permute-done((f32[3,1,32,256]{3,2,1,0:T(8,128)S(1)}, f32[3,1,32,256]{3,2,1,0:T(8,128)S(1)}, u32[]{:S(2)}, u32[]{:S(2)}) %collective-permute-start.5) | collective-permute-done | bytes 98336 | tf_op jit(solution)/shard_map/ppermute | solution.py:411
  19.5 3.1 %collective-permute-start.6 = (f32[3,32,256]{2,1,0:T(8,128)S(1)}, f32[3,32,256]{2,1,0:T(8,128)S(1)}, u32[]{:S(2)}, u32[]{:S(2)}) collective-permute-start(f32[3,32,256]{2,1,0:T(8,128)S(1)} %mean.3), channel_id=1, source_target_pairs={{0,7},{1,0},{2,1},{3,2},{4,3},{5,4},{6,5},{7,6},{8,15},{9,8},{10,9... | collective-permute-start | bytes 294920 | tf_op jit(solution)/shard_map/ppermute | solution.py:426
  22.6 0.0 collective-permute-done.3.got_ref
  22.6 3.0 %collective-permute-start.4 = (f32[3,32,256]{2,1,0:T(8,128)S(1)}, f32[3,32,256]{2,1,0:T(8,128)S(1)}, u32[]{:S(2)}, u32[]{:S(2)}) collective-permute-start(f32[3,32,256]{2,1,0:T(8,128)S(1)} %mean.2), channel_id=1, source_target_pairs={{0,7},{1,0},{2,1},{3,2},{4,3},{5,4},{6,5},{7,6},{8,15},{9,8},{10,9... | collective-permute-start | bytes 294920 | tf_op jit(solution)/shard_map/ppermute | solution.py:426
  25.6 2.0 %collective-permute-start.11 = (f32[3,32,256]{2,1,0:T(8,128)S(1)}, f32[3,32,256]{2,1,0:T(8,128)S(1)}, u32[]{:S(2)}, u32[]{:S(2)}) collective-permute-start(f32[3,32,256]{2,1,0:T(8,128)S(1)} %mean.2), channel_id=1, source_target_pairs={{0,23},{1,16},{2,17},{3,18},{4,19},{5,20},{6,21},{7,22},{8,31},{9,... | collective-permute-start | bytes 294920 | tf_op jit(solution)/shard_map/ppermute | solution.py:426
  27.6 0.0 collective-permute-done.6.rest_0_
  27.6 1.3 %collective-permute-start.8 = (f32[3,32,256]{2,1,0:T(8,128)S(1)}, f32[3,32,256]{2,1,0:T(8,128)S(1)}, u32[]{:S(2)}, u32[]{:S(2)}) collective-permute-start(f32[3,32,256]{2,1,0:T(8,128)S(1)} %collective-permute-done.6.rest_0_), channel_id=1, source_target_pairs={{0,16},{8,24},{16,0},{24,8},{1,17},{9,25},{17,1},{25,9},{2,18},{10... | collective-permute-start | bytes 294920 | tf_op jit(solution)/shard_map/ppermute | solution.py:411
  28.9 1.9 %factors.3 = bf16[6144,256]{1,0:T(8,128)(2,1)} custom-call(bf16[6144,512]{1,0:T(8,128)(2,1)S(1)} %get-tuple-element.37.both_ref, bf16[256,6144]{1,0:T(8,128)(2,1)S(1)} %get-tuple-element.38.err_ref, f32[256,256]{1,0:T(8,128)S(1)} %get-tuple-element.29.turned_ref, f32[3,32,256]{2,1,0:T(8,128)S(1)} %collective-permute-done.6.rest_0_, ...), custom_call_target="tpu_custom_call", output_to_operand_aliasing={{}: (4, {})} | custom-call | flops 536870912 | bytes 6291456 | tf_op jit(solution)/shard_map/factors/pallas_call | solution.py:192
  30.8 0.0 collective-permute-done.4.rest_4_
  30.8 0.1 collective-permute-start.10
  30.9 0.5 %collective-permute-start.7 = (f32[3,32,256]{2,1,0:T(8,128)S(1)}, f32[3,32,256]{2,1,0:T(8,128)S(1)}, u32[]{:S(2)}, u32[]{:S(2)}) collective-permute-start(f32[3,32,256]{2,1,0:T(8,128)S(1)} %collective-permute-done.6.rest_0_), channel_id=1, source_target_pairs={{0,8},{8,0},{16,24},{24,16},{1,9},{9,1},{17,25},{25,17},{2,10},{10... | collective-permute-start | bytes 294920 | tf_op jit(solution)/shard_map/ppermute | solution.py:411
  31.4 0.0 collective-permute-done.11.rest_6_
  31.4 0.1 collective-permute-start.12
  31.5 0.9 %collective-permute-done.8.rest_2_ = f32[3,32,256]{2,1,0:T(8,128)S(1)} collective-permute-done((f32[3,32,256]{2,1,0:T(8,128)S(1)}, f32[3,32,256]{2,1,0:T(8,128)S(1)}, u32[]{:S(2)}, u32[]{:S(2)}) %collective-permute-start.8) | collective-permute-done | bytes 98336 | tf_op jit(solution)/shard_map/ppermute | solution.py:411
  32.4 0.0 collective-permute-start.9
  32.4 0.0 collective-permute-done.7.rest_1_
  32.4 0.0 collective-permute-done.10.rest_5_
  32.4 0.3 collective-permute-done.12.rest_7_
  32.7 1.0 %collective-permute-done.9.rest_3_ = f32[3,32,256]{2,1,0:T(8,128)S(1)} collective-permute-done((f32[3,32,256]{2,1,0:T(8,128)S(1)}, f32[3,32,256]{2,1,0:T(8,128)S(1)}, u32[]{:S(2)}, u32[]{:S(2)}) %collective-permute-start.9) | collective-permute-done | bytes 98336 | tf_op jit(solution)/shard_map/ppermute | solution.py:411
  33.7 1.1 %place.1 = (f32[1,256,256]{2,1,0:T(8,128)}, f32[1,256,256]{2,1,0:T(8,128)}, f32[1,256,256]{2,1,0:T(8,128)}) custom-call(f32[3,32,256]{2,1,0:T(8,128)S(1)} %collective-permute-done.6.rest_0_, f32[3,32,256]{2,1,0:T(8,128)S(1)} %collective-permute-done.7.rest_1_, f32[3,32,256]{2,1,0:T(8,128)S(1)} %collective-permute-done.8.rest_2_, ...), custom_call_target="tpu_custom_call" | custom-call | bytes 1572864 | tf_op jit(solution)/shard_map/place/pallas_call | solution.py:397
  (4 shorter events, 0.1 us)
Async XLA Ops:
  1.7 10.5 %collective-permute-start = (f32[168,256]{1,0:T(8,128)S(1)}, f32[168,256]{1,0:T(8,128)S(1)}, u32[]{:S(2)}, u32[]{:S(2)}) collective-permute-start(f32[168,256]{1,0:T(8,128)S(1)} %get-tuple-element.28), channel_id=1, source_target_pairs={{0,1},{1,2},{2,3},{3,4},{4,5},{5,6},{6,7},{7,0},{8,9},{9,10},{10,1... | collective-permute-start | bytes 516104 | tf_op jit(solution)/shard_map/ppermute | solution.py:416
  5.4 5.6 %copy-start = (f32[25,256]{1,0:T(8,128)S(1)}, f32[25,256]{1,0:T(8,128)}, u32[]{:S(2)}) copy-start(f32[25,256]{1,0:T(8,128)} %w_ref.3) | copy-start | bytes 76804
  13.0 1.5 %collective-permute-start.2 = (f32[3,2,32,256]{3,2,1,0:T(8,128)S(1)}, f32[3,2,32,256]{3,2,1,0:T(8,128)S(1)}, u32[]{:S(2)}, u32[]{:S(2)}) collective-permute-start(f32[3,2,32,256]{3,2,1,0:T(8,128)S(1)} %get-tuple-element.40), channel_id=1, source_target_pairs={{0,8},{8,0},{16,24},{24,16},{1,9},{9,1},{17,25},{25,17},{2,10},{10... | collective-permute-start | bytes 589832 | tf_op jit(solution)/shard_map/ppermute | solution.py:411
  13.1 4.5 %collective-permute-start.1 = (f32[3,2,32,256]{3,2,1,0:T(8,128)S(1)}, f32[3,2,32,256]{3,2,1,0:T(8,128)S(1)}, u32[]{:S(2)}, u32[]{:S(2)}) collective-permute-start(f32[3,2,32,256]{3,2,1,0:T(8,128)S(1)} %get-tuple-element.36), channel_id=1, source_target_pairs={{0,8},{8,0},{16,24},{24,16},{1,9},{9,1},{17,25},{25,17},{2,10},{10... | collective-permute-start | bytes 589832 | tf_op jit(solution)/shard_map/ppermute | solution.py:411
  14.6 4.9 %collective-permute-start.5 = (f32[3,1,32,256]{3,2,1,0:T(8,128)S(1)}, f32[3,1,32,256]{3,2,1,0:T(8,128)S(1)}, u32[]{:S(2)}, u32[]{:S(2)}) collective-permute-start(f32[3,1,32,256]{3,2,1,0:T(8,128)S(1)} %get-tuple-element.41.rest_0_), channel_id=1, source_target_pairs={{0,16},{8,24},{16,0},{24,8},{1,17},{9,25},{17,1},{25,9},{2,18},{10... | collective-permute-start | bytes 294920 | tf_op jit(solution)/shard_map/ppermute | solution.py:411
  17.7 4.9 %collective-permute-start.3 = (f32[3,1,32,256]{3,2,1,0:T(8,128)S(1)}, f32[3,1,32,256]{3,2,1,0:T(8,128)S(1)}, u32[]{:S(2)}, u32[]{:S(2)}) collective-permute-start(f32[3,1,32,256]{3,2,1,0:T(8,128)S(1)} %get-tuple-element.44), channel_id=1, source_target_pairs={{0,16},{8,24},{16,0},{24,8},{1,17},{9,25},{17,1},{25,9},{2,18},{10... | collective-permute-start | bytes 294920 | tf_op jit(solution)/shard_map/ppermute | solution.py:411
  19.5 8.2 %collective-permute-start.6 = (f32[3,32,256]{2,1,0:T(8,128)S(1)}, f32[3,32,256]{2,1,0:T(8,128)S(1)}, u32[]{:S(2)}, u32[]{:S(2)}) collective-permute-start(f32[3,32,256]{2,1,0:T(8,128)S(1)} %mean.3), channel_id=1, source_target_pairs={{0,7},{1,0},{2,1},{3,2},{4,3},{5,4},{6,5},{7,6},{8,15},{9,8},{10,9... | collective-permute-start | bytes 294920 | tf_op jit(solution)/shard_map/ppermute | solution.py:426
  22.6 8.2 %collective-permute-start.4 = (f32[3,32,256]{2,1,0:T(8,128)S(1)}, f32[3,32,256]{2,1,0:T(8,128)S(1)}, u32[]{:S(2)}, u32[]{:S(2)}) collective-permute-start(f32[3,32,256]{2,1,0:T(8,128)S(1)} %mean.2), channel_id=1, source_target_pairs={{0,7},{1,0},{2,1},{3,2},{4,3},{5,4},{6,5},{7,6},{8,15},{9,8},{10,9... | collective-permute-start | bytes 294920 | tf_op jit(solution)/shard_map/ppermute | solution.py:426
  25.6 5.8 %collective-permute-start.11 = (f32[3,32,256]{2,1,0:T(8,128)S(1)}, f32[3,32,256]{2,1,0:T(8,128)S(1)}, u32[]{:S(2)}, u32[]{:S(2)}) collective-permute-start(f32[3,32,256]{2,1,0:T(8,128)S(1)} %mean.2), channel_id=1, source_target_pairs={{0,23},{1,16},{2,17},{3,18},{4,19},{5,20},{6,21},{7,22},{8,31},{9,... | collective-permute-start | bytes 294920 | tf_op jit(solution)/shard_map/ppermute | solution.py:426
  27.6 4.8 %collective-permute-start.8 = (f32[3,32,256]{2,1,0:T(8,128)S(1)}, f32[3,32,256]{2,1,0:T(8,128)S(1)}, u32[]{:S(2)}, u32[]{:S(2)}) collective-permute-start(f32[3,32,256]{2,1,0:T(8,128)S(1)} %collective-permute-done.6.rest_0_), channel_id=1, source_target_pairs={{0,16},{8,24},{16,0},{24,8},{1,17},{9,25},{17,1},{25,9},{2,18},{10... | collective-permute-start | bytes 294920 | tf_op jit(solution)/shard_map/ppermute | solution.py:411
  30.8 1.6 %collective-permute-start.10 = (f32[3,32,256]{2,1,0:T(8,128)S(1)}, f32[3,32,256]{2,1,0:T(8,128)S(1)}, u32[]{:S(2)}, u32[]{:S(2)}) collective-permute-start(f32[3,32,256]{2,1,0:T(8,128)S(1)} %collective-permute-done.4.rest_4_), channel_id=1, source_target_pairs={{0,8},{8,0},{16,24},{24,16},{1,9},{9,1},{17,25},{25,17},{2,10},{10... | collective-permute-start | bytes 294920 | tf_op jit(solution)/shard_map/ppermute | solution.py:411
  30.9 1.5 %collective-permute-start.7 = (f32[3,32,256]{2,1,0:T(8,128)S(1)}, f32[3,32,256]{2,1,0:T(8,128)S(1)}, u32[]{:S(2)}, u32[]{:S(2)}) collective-permute-start(f32[3,32,256]{2,1,0:T(8,128)S(1)} %collective-permute-done.6.rest_0_), channel_id=1, source_target_pairs={{0,8},{8,0},{16,24},{24,16},{1,9},{9,1},{17,25},{25,17},{2,10},{10... | collective-permute-start | bytes 294920 | tf_op jit(solution)/shard_map/ppermute | solution.py:411
  31.4 1.3 %collective-permute-start.12 = (f32[3,32,256]{2,1,0:T(8,128)S(1)}, f32[3,32,256]{2,1,0:T(8,128)S(1)}, u32[]{:S(2)}, u32[]{:S(2)}) collective-permute-start(f32[3,32,256]{2,1,0:T(8,128)S(1)} %collective-permute-done.11.rest_6_), channel_id=1, source_target_pairs={{0,8},{8,0},{16,24},{24,16},{1,9},{9,1},{17,25},{25,17},{2,10},{10... | collective-permute-start | bytes 294920 | tf_op jit(solution)/shard_map/ppermute | solution.py:411
  32.4 1.3 %collective-permute-start.9 = (f32[3,32,256]{2,1,0:T(8,128)S(1)}, f32[3,32,256]{2,1,0:T(8,128)S(1)}, u32[]{:S(2)}, u32[]{:S(2)}) collective-permute-start(f32[3,32,256]{2,1,0:T(8,128)S(1)} %collective-permute-done.8.rest_2_), channel_id=1, source_target_pairs={{0,8},{8,0},{16,24},{24,16},{1,9},{9,1},{17,25},{25,17},{2,10},{10... | collective-permute-start | bytes 294920 | tf_op jit(solution)/shard_map/ppermute | solution.py:411

commit v8 on v7

--- a/solution.py
+++ b/solution.py
@@ -1,4 +1,5 @@
 import functools
+import math
 
 import jax
 import jax.numpy as jnp
@@ -53,33 +54,71 @@
     return best
 
 
-def prepare_kernel(x_hbm, tail_ref, turned_ref, x_ref, sem):
+def chunk_copies(rows, index, rank, hbm, both_ref, bits_ref, at, sems):
+    obs_hbm, bits_hbm, f_hbm = hbm
+    width = both_ref.shape[1] - rank
+    source, target = pl.ds(index * rows, rows), pl.ds(at, rows)
+    return (
+        pltpu.make_async_copy(bits_hbm.at[:, source], bits_ref.at[:, target], sems.at[0]),
+        pltpu.make_async_copy(
+            f_hbm.at[source, :], both_ref.at[target, pl.ds(0, rank)], sems.at[1]
+        ),
+        pltpu.make_async_copy(
+            obs_hbm.at[source, :], both_ref.at[target, pl.ds(rank, width)], sems.at[2]
+        ),
+    )
+
+
+def prepare_kernel(
+    rows, x_hbm, obs_hbm, bits_hbm, f_hbm, tail_ref, turned_ref, x_ref, both_ref, bits_ref, sem, sems
+):
     copy = pltpu.make_async_copy(x_hbm.at[0], x_ref, sem)
     copy.start()
+    rank = x_ref.shape[0]
+    first = chunk_copies(rows, 0, rank, (obs_hbm, bits_hbm, f_hbm), both_ref, bits_ref, 0, sems)
+    for other in first:
+        other.start()
     copy.wait()
     turned_ref[...] = x_ref[...].T
     tail_ref[...] = turned_ref[turned_ref.shape[0] - SEASON :, :]
-
-
-def prepare(x):
+    for other in first:
+        other.wait()
+
+
+def prepare(x, obs, bits, factors, rows):
     rank, width = x.shape[1:]
     return pl.pallas_call(
-        prepare_kernel,
+        functools.partial(prepare_kernel, rows),
         out_shape=(
             jax.ShapeDtypeStruct((SEASON, rank), F32),
             jax.ShapeDtypeStruct((width, rank), F32),
             jax.ShapeDtypeStruct((rank, width), F32),
+            jax.ShapeDtypeStruct((rows, rank + width), BF16),
+            jax.ShapeDtypeStruct((bits.shape[0], rows), jnp.int32),
         ),
-        in_specs=[far()],
-        out_specs=(whole(), whole(), whole()),
-        scratch_shapes=[pltpu.SemaphoreType.DMA(())],
-        compiler_params=params(),
-        cost_estimate=cost(0, 4 * rank * width * 4),
+        in_specs=[far()] * 4,
+        out_specs=(whole(),) * 5,
+        scratch_shapes=[pltpu.SemaphoreType.DMA(()), pltpu.SemaphoreType.DMA((3,))],
+        compiler_params=params(),
+        cost_estimate=cost(0, 4 * rank * width * 4 + rows * (rank + width) * 4),
         name="prepare",
-    )(held(x))
-
-
-def error_kernel(rows, obs_hbm, bits_hbm, f_hbm, turned_ref, err_ref, both_ref, gd_ref, bits_ref, sems):
+    )(held(x), held(obs), held(bits), held(factors))
+
+
+def error_kernel(
+    rows,
+    obs_hbm,
+    bits_hbm,
+    f_hbm,
+    turned_ref,
+    first_ref,
+    first_bits_ref,
+    err_ref,
+    both_ref,
+    gd_ref,
+    bits_ref,
+    sems,
+):
     width, series = err_ref.shape
     rank = turned_ref.shape[1]
     words = bits_ref.shape[0]
@@ -87,18 +126,18 @@
     chunks = series // rows
 
     def copies(index):
-        part = pl.ds(index * rows, rows)
-        return (
-            pltpu.make_async_copy(bits_hbm.at[:, part], bits_ref.at[:, part], sems.at[index, 0]),
-            pltpu.make_async_copy(
-                f_hbm.at[part, :], both_ref.at[part, pl.ds(0, rank)], sems.at[index, 1]
-            ),
-            pltpu.make_async_copy(
-                obs_hbm.at[part, :], both_ref.at[part, pl.ds(rank, width)], sems.at[index, 2]
-            ),
+        return chunk_copies(
+            rows, index, rank, (obs_hbm, bits_hbm, f_hbm),
+            both_ref, bits_ref, (index - 1) * rows, sems.at[index - 1],
         )
 
-    for index in range(chunks):
+    def pair(index):
+        if index == 0:
+            return first_ref[...], first_bits_ref[...]
+        part = pl.ds((index - 1) * rows, rows)
+        return both_ref[part, :], bits_ref[:, part]
+
+    for index in range(1, chunks):
         for copy in copies(index):
             copy.start()
     row = lax.broadcasted_iota(jnp.int32, (width, width), 0)
@@ -109,20 +148,21 @@
     flag = jnp.left_shift(1, lax.broadcasted_iota(jnp.int32, (1, per, 1), 1))
 
     def compare(index):
-        for copy in copies(index):
-            copy.wait()
-        part = pl.ds(index * rows, rows)
+        if index > 0:
+            for copy in copies(index):
+                copy.wait()
         return lax.dot_general(
-            weights, both_ref[part, :], (((1,), (1,)), ((), ())), preferred_element_type=F32
+            weights, pair(index)[0], (((1,), (1,)), ((), ())), preferred_element_type=F32
         )
 
     def settle(index, gap):
         part = pl.ds(index * rows, rows)
-        seen = jnp.bitwise_and(bits_ref[:, part][:, None, :], flag) != 0
+        both, bits = pair(index)
+        seen = jnp.bitwise_and(bits[:, None, :], flag) != 0
         error = jnp.where(seen, gap.reshape(words, per, rows), 0.0).reshape(width, rows)
         error = error.astype(BF16)
         err_ref[:, part] = error
-        term = jnp.dot(error, both_ref[part, pl.ds(0, rank)], preferred_element_type=F32)
+        term = jnp.dot(error, both[:, :rank], preferred_element_type=F32)
         if index == 0:
             gd_ref[...] = term
         else:
@@ -135,31 +175,32 @@
         gap = later
 
 
-def error_step(obs, bits, factors, turned):
+def error_step(obs, bits, factors, turned, first, first_bits):
     series, width = obs.shape
     rank = factors.shape[1]
     words = bits.shape[0]
-    rows = rows_of(series, 1024)
+    rows = first.shape[0]
+    others = max(series - rows, rows)
     return pl.pallas_call(
         functools.partial(error_kernel, rows),
         out_shape=(
             jax.ShapeDtypeStruct((width, series), BF16),
-            jax.ShapeDtypeStruct((series, rank + width), BF16),
+            jax.ShapeDtypeStruct((others, rank + width), BF16),
             jax.ShapeDtypeStruct((width, rank), F32),
         ),
-        in_specs=[far(), far(), far(), whole()],
+        in_specs=[far(), far(), far(), whole(), whole(), whole()],
         out_specs=(whole(), whole(), whole()),
         scratch_shapes=[
-            pltpu.VMEM((words, series), jnp.int32),
-            pltpu.SemaphoreType.DMA((series // rows, 3)),
+            pltpu.VMEM((words, others), jnp.int32),
+            pltpu.SemaphoreType.DMA((others // rows, 3)),
         ],
         compiler_params=params(),
         cost_estimate=cost(8 * series * width * rank, series * (3 * width * 2 + words * 4)),
         name="errors",
-    )(held(obs), held(bits), held(factors), turned)
-
-
-def factor_kernel(begin, rows, chunks, both_ref, err_ref, turned_ref, *rest):
+    )(held(obs), held(bits), held(factors), turned, first, first_bits)
+
+
+def factor_kernel(begin, rows, chunks, first_ref, both_ref, err_ref, turned_ref, *rest):
     out_hbm, out_ref, sems = rest[-3:]
     half = turned_ref[...].astype(BF16)
     size = rows // chunks
@@ -173,36 +214,43 @@
 
     for index in range(chunks):
         part = pl.ds(begin + index * size, size)
+        split = first_ref.shape[0]
+        if begin + index * size < split:
+            old = first_ref[part, pl.ds(0, half.shape[1])]
+        else:
+            old = both_ref[pl.ds(begin + index * size - split, size), pl.ds(0, half.shape[1])]
         gradient = lax.dot_general(
             err_ref[:, part], half, (((0,), (0,)), ((), ())), preferred_element_type=F32
         )
         out_ref[pl.ds(index * size, size), :] = (
-            both_ref[part, pl.ds(0, half.shape[1])].astype(F32) - factor_rate * gradient
+            old.astype(F32) - factor_rate * gradient
         ).astype(BF16)
         copy(index).start()
     for index in range(chunks):
         copy(index).wait()
 
 
-def factor_step(both, err, turned, after, sofar, begin, rows):
+def factor_step(first, both, err, turned, after, sofar, begin, rows):
     width, series = err.shape
     rank = turned.shape[1]
-    chunks = rows // rows_of(rows, 1024)
+    chunks = rows // math.gcd(first.shape[0], rows, begin)
     rest = (after,) if sofar is None else (after, sofar)
     return pl.pallas_call(
         functools.partial(factor_kernel, begin, rows, chunks),
         out_shape=jax.ShapeDtypeStruct((series, rank), BF16),
-        in_specs=[whole()] * 3 + [pl.BlockSpec(memory_space=pl.ANY)] * len(rest),
+        in_specs=[whole()] * 4 + [pl.BlockSpec(memory_space=pl.ANY)] * len(rest),
         out_specs=far(),
-        input_output_aliases={} if sofar is None else {4: 0},
+        input_output_aliases={} if sofar is None else {5: 0},
         scratch_shapes=[pltpu.VMEM((rows, rank), BF16), pltpu.SemaphoreType.DMA((chunks,))],
         compiler_params=params(),
         cost_estimate=cost(2 * rows * width * rank, rows * 3 * width * 2),
         name="factors",
-    )(both, err, turned, *rest)
-
-
-def regress_kernel(lanes, turned_ref, w_ref, gd_ref, m_hbm, v_hbm, base_ref, m_ref, v_ref, z_ref, r_ref, sems):
+    )(first, both, err, turned, *rest)
+
+
+def regress_kernel(
+    lanes, turned_ref, w_ref, gd_ref, m_hbm, v_hbm, base_ref, m_ref, v_ref, z_ref, r_ref, sems
+):
     m_copy = pltpu.make_async_copy(m_hbm.at[0], m_ref, sems.at[0])
     v_copy = pltpu.make_async_copy(v_hbm.at[0], v_ref, sems.at[1])
     m_copy.start()
@@ -429,23 +477,25 @@
 def body(obs, mask_bits, factors, x_blocks, first_moment, second_moment, ar_weights, stratum):
     count = lax.axis_size("grp")
     series = obs.shape[0]
-    third = series // 3 // 128 * 128
-
-    tail, turned, x = prepare(x_blocks)
+    rows = rows_of(series, 1024)
+    third = max(series // rows // 3, 1) * rows
+    bits = mask_bits.T
+
+    tail, turned, x, lead, lead_bits = prepare(x_blocks, obs, bits, factors, rows)
     halo = shifted(tail, 1)
-    err, kept, gd = error_step(obs, mask_bits.T, factors, turned)
+    err, kept, gd = error_step(obs, bits, factors, turned, lead, lead_bits)
     base, first, second = regress_step(turned, ar_weights, gd, first_moment, second_moment)
     share = x.shape[0] // count
-    lead = share // 2
+    half = share // 2
     (keep0, send0), (keep1, send1) = update_step(
-        stratum, halo, ar_weights, base, x, first, second, count, (lead, share - lead)
+        stratum, halo, ar_weights, base, x, first, second, count, (half, share - half)
     )
 
     got0 = crossed(send0, 1)
     got1 = crossed(send1, 1)
     keep0, send0 = halve(keep0, got0, 2)
     far0 = crossed(send0, 2)
-    factor_new = factor_step(kept, err, turned, send0, None, 0, third)
+    factor_new = factor_step(lead, kept, err, turned, send0, None, 0, third)
     got1, factor_new = lax.optimization_barrier((got1, factor_new))
     keep1, send1 = halve(keep1, got1, 2)
     far1 = crossed(send1, 2)
@@ -456,7 +506,7 @@
     near1 = delivered(mean1, 0)
     side1 = delivered(mean1, 2)
     side0 = crossed(near0, 2)
-    factor_new = factor_step(kept, err, turned, near0, factor_new, third, series - third)
+    factor_new = factor_step(lead, kept, err, turned, near0, factor_new, third, series - third)
     near1, factor_new = lax.optimization_barrier((near1, factor_new))
     pieces = [
         [near0, crossed(near0, 1), side0, crossed(side0, 1)],

time: 34.9 us -> 34.5 us (0.989)
  waiting for transfers between devices: 4.38 us -> 5.5 us
  starting transfers between devices: 15.8 us -> 14.7 us
  Pallas kernels: 13.2 us -> 12.7 us
    ppermute x3, starting transfers between devices: 8.14 us -> 7.03 us  [delivered(): return lax.ppermute(value, ('grp', 'blk'), pairs)]
    pallas_call x1, Pallas kernels: 5.57 us -> 4.84 us  [error_step(): pl.pallas_call(functools.partial(error_kernel, rows), out_shape=(jax.Shap...]
    ppermute x1, waiting for transfers between devices: 0.01 us -> 0.69 us  [shifted(): lax.ppermute(value, 'blk', [(source, (source + steps) % count) for source...]
    ppermute x9, waiting for transfers between devices: 4.37 us -> 4.81 us  [crossed(): lax.ppermute(value, 'grp', [(source, source ^ step) for source in range(c...]
  transfers between devices with their start and end apart: 13 -> 13, of which waited for: 5 -> 7; matrix products, arithmetic and copies ran while one was open for 0% -> 0% of each run, Pallas kernels for 29% -> 28%
where the time goes in v8:
time: 34.5 us; the launch traced here: 34.3 us
  starting transfers between devices  14.7 us (43%)
  Pallas kernels  12.7 us (37%)
  waiting for transfers between devices  5.5 us (16%)
  between operations  1.4 us (4%)
    ppermute x3, starting transfers between devices, delivered(): return lax.ppermute(value, ('grp', 'blk'), pairs)  7.03 us
    pallas_call x1, Pallas kernels, error_step(): pl.pallas_call(functools.partial(error_kernel, rows), out_shape=(jax.Shap...  4.84 us
    ppermute x9, waiting for transfers between devices, crossed(): lax.ppermute(value, 'grp', [(source, source ^ step) for source in range(c...  4.81 us
    ppermute x9, starting transfers between devices, crossed(): lax.ppermute(value, 'grp', [(source, source ^ step) for source in range(c...  4.67 us
    pallas_call x2, Pallas kernels, factor_step(): pl.pallas_call(functools.partial(factor_kernel, begin, rows, chunks), out...  3.32 us
    ppermute x1, starting transfers between devices, shifted(): lax.ppermute(value, 'blk', [(source, (source + steps) % count) for source...  3.02 us
    pallas_call x1, Pallas kernels, prepare(): pl.pallas_call(functools.partial(prepare_kernel, rows), out_shape=(jax.Sh...  1.39 us
    pallas_call x1, Pallas kernels, regress_step(): pl.pallas_call(functools.partial(regress_kernel, lanes), out_shape=(jax.S...  1.2 us
  transfers between devices with their start and end apart: 13, of which 7 were waited for; matrix products, arithmetic and copies ran while one was open for 0% of the time, Pallas kernels for 28%

profile of v8, /device:TPU:0, one launch (start us, length us, event | category | flops | bytes accessed | tf_op | source)
XLA Modules:
  0.0 34.3 jit_solution(18338973380899422488)
XLA Ops:
  0.6 1.4 %prepare.1 = (f32[168,256]{1,0:T(8,128)S(1)}, f32[256,256]{1,0:T(8,128)S(1)}, f32[256,256]{1,0:T(8,128)S(1)}, bf16[1024,512]{1,0:T(8,128)(2,1)S(1)}, s32[32,1024]{1,0:T(8,128)S(1)}) custom-call(f32[1,256,256]{2,1,0:T(8,128)} %x_hbm.1, bf16[6144,256]{1,0:T(8,128)(2,1)} %obs_hbm.3, s32[32,6144]{1,0:T(8,128)} %bitcast.3, bf16[6144,256]{1,0:T(8,128)(2,1)} %f_hbm.3), custom_call_target="tpu_custom_call" | custom-call | bytes 3145728 | tf_op jit(solution)/shard_map/prepare/pallas_call | solution.py:90
  2.0 3.0 %collective-permute-start = (f32[168,256]{1,0:T(8,128)S(1)}, f32[168,256]{1,0:T(8,128)S(1)}, u32[]{:S(2)}, u32[]{:S(2)}) collective-permute-start(f32[168,256]{1,0:T(8,128)S(1)} %get-tuple-element.30), channel_id=1, source_target_pairs={{0,1},{1,2},{2,3},{3,4},{4,5},{5,6},{6,7},{7,0},{8,9},{9,10},{10,1... | collective-permute-start | bytes 516104 | tf_op jit(solution)/shard_map/ppermute | solution.py:464
  5.7 0.0 copy-start
  5.7 4.8 %errors.1 = (bf16[256,6144]{1,0:T(8,128)(2,1)S(1)}, bf16[5120,512]{1,0:T(8,128)(2,1)S(1)}, f32[256,256]{1,0:T(8,128)S(1)}) custom-call(bf16[6144,256]{1,0:T(8,128)(2,1)} %obs_hbm.3, s32[32,6144]{1,0:T(8,128)} %bitcast.4, bf16[6144,256]{1,0:T(8,128)(2,1)} %f_hbm.3, f32[256,256]{1,0:T(8,128)S(1)} %get-tuple-element.31.turned_ref, ...), custom_call_target="tpu_custom_call" | custom-call | flops 3221225472 | bytes 10223616 | tf_op jit(solution)/shard_map/errors/pallas_call | solution.py:184
  10.6 0.0 copy-done
  10.6 1.2 %regress.1 = (f32[256,256]{1,0:T(8,128)S(1)}, f32[256,256]{1,0:T(8,128)S(1)}, f32[256,256]{1,0:T(8,128)S(1)}) custom-call(f32[256,256]{1,0:T(8,128)S(1)} %get-tuple-element.31.turned_ref, f32[25,256]{1,0:T(8,128)S(1)} %copy-done, f32[256,256]{1,0:T(8,128)S(1)} %get-tuple-element.34.gd_ref, f32[1,256,256]{2,1,0:T(8,128)} %m_hbm.1, f32[1,256,256]{2,1,0:T(8,128)} %v_hbm.1), custom_call_target="tpu_custom_call" | custom-call | flops 6553600 | bytes 1572864 | tf_op jit(solution)/shard_map/regress/pallas_call | solution.py:281
  11.8 0.7 %collective-permute-done.halo_ref = f32[168,256]{1,0:T(8,128)S(1)} collective-permute-done((f32[168,256]{1,0:T(8,128)S(1)}, f32[168,256]{1,0:T(8,128)S(1)}, u32[]{:S(2)}, u32[]{:S(2)}) %collective-permute-start) | collective-permute-done | bytes 172064 | tf_op jit(solution)/shard_map/ppermute | solution.py:464
  12.5 0.8 %update.1 = (f32[3,2,32,256]{3,2,1,0:T(8,128)S(1)}, f32[3,2,32,256]{3,2,1,0:T(8,128)S(1)}, f32[3,2,32,256]{3,2,1,0:T(8,128)S(1)}, f32[3,2,32,256]{3,2,1,0:T(8,128)S(1)}) custom-call(s32[1,1]{1,0:T(1,128)} %bitcast.2.stratum_ref, f32[168,256]{1,0:T(8,128)S(1)} %collective-permute-done.halo_ref, f32[25,256]{1,0:T(8,128)S(1)} %copy-done, ...), custom_call_target="tpu_custom_call" | custom-call | flops 3932160 | bytes 2621440 | tf_op jit(solution)/shard_map/update/pallas_call | solution.py:361
  13.2 0.1 collective-permute-start.2
  13.3 0.5 %collective-permute-start.1 = (f32[3,2,32,256]{3,2,1,0:T(8,128)S(1)}, f32[3,2,32,256]{3,2,1,0:T(8,128)S(1)}, u32[]{:S(2)}, u32[]{:S(2)}) collective-permute-start(f32[3,2,32,256]{3,2,1,0:T(8,128)S(1)} %get-tuple-element.40), channel_id=1, source_target_pairs={{0,8},{8,0},{16,24},{24,16},{1,9},{9,1},{17,25},{25,17},{2,10},{10... | collective-permute-start | bytes 589832 | tf_op jit(solution)/shard_map/ppermute | solution.py:459
  13.8 0.9 %collective-permute-done.2.got_ref = f32[3,2,32,256]{3,2,1,0:T(8,128)S(1)} collective-permute-done((f32[3,2,32,256]{3,2,1,0:T(8,128)S(1)}, f32[3,2,32,256]{3,2,1,0:T(8,128)S(1)}, u32[]{:S(2)}, u32[]{:S(2)}) %collective-permute-start.2) | collective-permute-done | bytes 196640 | tf_op jit(solution)/shard_map/ppermute | solution.py:459
  14.8 1.6 %collective-permute-start.5 = (f32[3,1,32,256]{3,2,1,0:T(8,128)S(1)}, f32[3,1,32,256]{3,2,1,0:T(8,128)S(1)}, u32[]{:S(2)}, u32[]{:S(2)}) collective-permute-start(f32[3,1,32,256]{3,2,1,0:T(8,128)S(1)} %get-tuple-element.45.rest_0_), channel_id=1, source_target_pairs={{0,16},{8,24},{16,0},{24,8},{1,17},{9,25},{17,1},{25,9},{2,18},{10... | collective-permute-start | bytes 294920 | tf_op jit(solution)/shard_map/ppermute | solution.py:459
  16.3 1.5 %factors.2.rest_1_ = bf16[6144,256]{1,0:T(8,128)(2,1)} custom-call(bf16[1024,512]{1,0:T(8,128)(2,1)S(1)} %get-tuple-element.32.first_ref, bf16[5120,512]{1,0:T(8,128)(2,1)S(1)} %get-tuple-element.41.both_ref, bf16[256,6144]{1,0:T(8,128)(2,1)S(1)} %get-tuple-element.42.err_ref, f32[256,256]{1,0:T(8,128)S(1)} %get-tuple-element.31.turned_ref, ...), custom_call_target="tpu_custom_call" | custom-call | flops 268435456 | bytes 3145728 | tf_op jit(solution)/shard_map/factors/pallas_call | solution.py:238
  17.8 0.0 collective-permute-done.1.got_ref
  17.9 0.6 %collective-permute-start.3 = (f32[3,1,32,256]{3,2,1,0:T(8,128)S(1)}, f32[3,1,32,256]{3,2,1,0:T(8,128)S(1)}, u32[]{:S(2)}, u32[]{:S(2)}) collective-permute-start(f32[3,1,32,256]{3,2,1,0:T(8,128)S(1)} %get-tuple-element.48), channel_id=1, source_target_pairs={{0,16},{8,24},{16,0},{24,8},{1,17},{9,25},{17,1},{25,9},{2,18},{10... | collective-permute-start | bytes 294920 | tf_op jit(solution)/shard_map/ppermute | solution.py:459
  18.5 1.2 %collective-permute-done.5.got_ref = f32[3,1,32,256]{3,2,1,0:T(8,128)S(1)} collective-permute-done((f32[3,1,32,256]{3,2,1,0:T(8,128)S(1)}, f32[3,1,32,256]{3,2,1,0:T(8,128)S(1)}, u32[]{:S(2)}, u32[]{:S(2)}) %collective-permute-start.5) | collective-permute-done | bytes 98336 | tf_op jit(solution)/shard_map/ppermute | solution.py:459
  19.7 2.4 %collective-permute-start.6 = (f32[3,32,256]{2,1,0:T(8,128)S(1)}, f32[3,32,256]{2,1,0:T(8,128)S(1)}, u32[]{:S(2)}, u32[]{:S(2)}) collective-permute-start(f32[3,32,256]{2,1,0:T(8,128)S(1)} %mean.3), channel_id=1, source_target_pairs={{0,7},{1,0},{2,1},{3,2},{4,3},{5,4},{6,5},{7,6},{8,15},{9,8},{10,9... | collective-permute-start | bytes 294920 | tf_op jit(solution)/shard_map/ppermute | solution.py:474
  22.1 0.4 %collective-permute-done.3.got_ref = f32[3,1,32,256]{3,2,1,0:T(8,128)S(1)} collective-permute-done((f32[3,1,32,256]{3,2,1,0:T(8,128)S(1)}, f32[3,1,32,256]{3,2,1,0:T(8,128)S(1)}, u32[]{:S(2)}, u32[]{:S(2)}) %collective-permute-start.3) | collective-permute-done | bytes 98336 | tf_op jit(solution)/shard_map/ppermute | solution.py:459
  22.6 2.6 %collective-permute-start.4 = (f32[3,32,256]{2,1,0:T(8,128)S(1)}, f32[3,32,256]{2,1,0:T(8,128)S(1)}, u32[]{:S(2)}, u32[]{:S(2)}) collective-permute-start(f32[3,32,256]{2,1,0:T(8,128)S(1)} %mean.2), channel_id=1, source_target_pairs={{0,7},{1,0},{2,1},{3,2},{4,3},{5,4},{6,5},{7,6},{8,15},{9,8},{10,9... | collective-permute-start | bytes 294920 | tf_op jit(solution)/shard_map/ppermute | solution.py:474
  25.1 2.0 %collective-permute-start.11 = (f32[3,32,256]{2,1,0:T(8,128)S(1)}, f32[3,32,256]{2,1,0:T(8,128)S(1)}, u32[]{:S(2)}, u32[]{:S(2)}) collective-permute-start(f32[3,32,256]{2,1,0:T(8,128)S(1)} %mean.2), channel_id=1, source_target_pairs={{0,23},{1,16},{2,17},{3,18},{4,19},{5,20},{6,21},{7,22},{8,31},{9,... | collective-permute-start | bytes 294920 | tf_op jit(solution)/shard_map/ppermute | solution.py:474
  27.2 0.0 collective-permute-done.6.rest_0_
  27.2 1.3 %collective-permute-start.8 = (f32[3,32,256]{2,1,0:T(8,128)S(1)}, f32[3,32,256]{2,1,0:T(8,128)S(1)}, u32[]{:S(2)}, u32[]{:S(2)}) collective-permute-start(f32[3,32,256]{2,1,0:T(8,128)S(1)} %collective-permute-done.6.rest_0_), channel_id=1, source_target_pairs={{0,16},{8,24},{16,0},{24,8},{1,17},{9,25},{17,1},{25,9},{2,18},{10... | collective-permute-start | bytes 294920 | tf_op jit(solution)/shard_map/ppermute | solution.py:459
  28.5 1.9 %factors.3 = bf16[6144,256]{1,0:T(8,128)(2,1)} custom-call(bf16[1024,512]{1,0:T(8,128)(2,1)S(1)} %get-tuple-element.32.first_ref, bf16[5120,512]{1,0:T(8,128)(2,1)S(1)} %get-tuple-element.41.both_ref, bf16[256,6144]{1,0:T(8,128)(2,1)S(1)} %get-tuple-element.42.err_ref, f32[256,256]{1,0:T(8,128)S(1)} %get-tuple-element.31.turned_ref, ...), custom_call_target="tpu_custom_call", output_to_operand_aliasing={{}: (5, {})} | custom-call | flops 536870912 | bytes 6291456 | tf_op jit(solution)/shard_map/factors/pallas_call | solution.py:238
  30.3 0.0 collective-permute-done.4.rest_4_
  30.3 0.1 collective-permute-start.10
  30.4 0.5 %collective-permute-start.7 = (f32[3,32,256]{2,1,0:T(8,128)S(1)}, f32[3,32,256]{2,1,0:T(8,128)S(1)}, u32[]{:S(2)}, u32[]{:S(2)}) collective-permute-start(f32[3,32,256]{2,1,0:T(8,128)S(1)} %collective-permute-done.6.rest_0_), channel_id=1, source_target_pairs={{0,8},{8,0},{16,24},{24,16},{1,9},{9,1},{17,25},{25,17},{2,10},{10... | collective-permute-start | bytes 294920 | tf_op jit(solution)/shard_map/ppermute | solution.py:459
  30.9 0.0 collective-permute-done.11.rest_6_
  30.9 0.1 collective-permute-start.12
  31.0 0.9 %collective-permute-done.8.rest_2_ = f32[3,32,256]{2,1,0:T(8,128)S(1)} collective-permute-done((f32[3,32,256]{2,1,0:T(8,128)S(1)}, f32[3,32,256]{2,1,0:T(8,128)S(1)}, u32[]{:S(2)}, u32[]{:S(2)}) %collective-permute-start.8) | collective-permute-done | bytes 98336 | tf_op jit(solution)/shard_map/ppermute | solution.py:459
  31.9 0.0 collective-permute-start.9
  31.9 0.0 collective-permute-done.7.rest_1_
  31.9 0.0 collective-permute-done.10.rest_5_
  32.0 0.3 collective-permute-done.12.rest_7_
  32.2 1.0 %collective-permute-done.9.rest_3_ = f32[3,32,256]{2,1,0:T(8,128)S(1)} collective-permute-done((f32[3,32,256]{2,1,0:T(8,128)S(1)}, f32[3,32,256]{2,1,0:T(8,128)S(1)}, u32[]{:S(2)}, u32[]{:S(2)}) %collective-permute-start.9) | collective-permute-done | bytes 98336 | tf_op jit(solution)/shard_map/ppermute | solution.py:459
  33.2 1.1 %place.1 = (f32[1,256,256]{2,1,0:T(8,128)}, f32[1,256,256]{2,1,0:T(8,128)}, f32[1,256,256]{2,1,0:T(8,128)}) custom-call(f32[3,32,256]{2,1,0:T(8,128)S(1)} %collective-permute-done.6.rest_0_, f32[3,32,256]{2,1,0:T(8,128)S(1)} %collective-permute-done.7.rest_1_, f32[3,32,256]{2,1,0:T(8,128)S(1)} %collective-permute-done.8.rest_2_, ...), custom_call_target="tpu_custom_call" | custom-call | bytes 1572864 | tf_op jit(solution)/shard_map/place/pallas_call | solution.py:445
  (4 shorter events, 0.1 us)
Async XLA Ops:
  2.0 10.4 %collective-permute-start = (f32[168,256]{1,0:T(8,128)S(1)}, f32[168,256]{1,0:T(8,128)S(1)}, u32[]{:S(2)}, u32[]{:S(2)}) collective-permute-start(f32[168,256]{1,0:T(8,128)S(1)} %get-tuple-element.30), channel_id=1, source_target_pairs={{0,1},{1,2},{2,3},{3,4},{4,5},{5,6},{6,7},{7,0},{8,9},{9,10},{10,1... | collective-permute-start | bytes 516104 | tf_op jit(solution)/shard_map/ppermute | solution.py:464
  5.7 4.9 %copy-start = (f32[25,256]{1,0:T(8,128)S(1)}, f32[25,256]{1,0:T(8,128)}, u32[]{:S(2)}) copy-start(f32[25,256]{1,0:T(8,128)} %w_ref.3) | copy-start | bytes 76804
  13.2 1.5 %collective-permute-start.2 = (f32[3,2,32,256]{3,2,1,0:T(8,128)S(1)}, f32[3,2,32,256]{3,2,1,0:T(8,128)S(1)}, u32[]{:S(2)}, u32[]{:S(2)}) collective-permute-start(f32[3,2,32,256]{3,2,1,0:T(8,128)S(1)} %get-tuple-element.44), channel_id=1, source_target_pairs={{0,8},{8,0},{16,24},{24,16},{1,9},{9,1},{17,25},{25,17},{2,10},{10... | collective-permute-start | bytes 589832 | tf_op jit(solution)/shard_map/ppermute | solution.py:459
  13.3 4.5 %collective-permute-start.1 = (f32[3,2,32,256]{3,2,1,0:T(8,128)S(1)}, f32[3,2,32,256]{3,2,1,0:T(8,128)S(1)}, u32[]{:S(2)}, u32[]{:S(2)}) collective-permute-start(f32[3,2,32,256]{3,2,1,0:T(8,128)S(1)} %get-tuple-element.40), channel_id=1, source_target_pairs={{0,8},{8,0},{16,24},{24,16},{1,9},{9,1},{17,25},{25,17},{2,10},{10... | collective-permute-start | bytes 589832 | tf_op jit(solution)/shard_map/ppermute | solution.py:459
  14.8 4.9 %collective-permute-start.5 = (f32[3,1,32,256]{3,2,1,0:T(8,128)S(1)}, f32[3,1,32,256]{3,2,1,0:T(8,128)S(1)}, u32[]{:S(2)}, u32[]{:S(2)}) collective-permute-start(f32[3,1,32,256]{3,2,1,0:T(8,128)S(1)} %get-tuple-element.45.rest_0_), channel_id=1, source_target_pairs={{0,16},{8,24},{16,0},{24,8},{1,17},{9,25},{17,1},{25,9},{2,18},{10... | collective-permute-start | bytes 294920 | tf_op jit(solution)/shard_map/ppermute | solution.py:459
  17.9 4.7 %collective-permute-start.3 = (f32[3,1,32,256]{3,2,1,0:T(8,128)S(1)}, f32[3,1,32,256]{3,2,1,0:T(8,128)S(1)}, u32[]{:S(2)}, u32[]{:S(2)}) collective-permute-start(f32[3,1,32,256]{3,2,1,0:T(8,128)S(1)} %get-tuple-element.48), channel_id=1, source_target_pairs={{0,16},{8,24},{16,0},{24,8},{1,17},{9,25},{17,1},{25,9},{2,18},{10... | collective-permute-start | bytes 294920 | tf_op jit(solution)/shard_map/ppermute | solution.py:459
  19.7 7.5 %collective-permute-start.6 = (f32[3,32,256]{2,1,0:T(8,128)S(1)}, f32[3,32,256]{2,1,0:T(8,128)S(1)}, u32[]{:S(2)}, u32[]{:S(2)}) collective-permute-start(f32[3,32,256]{2,1,0:T(8,128)S(1)} %mean.3), channel_id=1, source_target_pairs={{0,7},{1,0},{2,1},{3,2},{4,3},{5,4},{6,5},{7,6},{8,15},{9,8},{10,9... | collective-permute-start | bytes 294920 | tf_op jit(solution)/shard_map/ppermute | solution.py:474
  22.6 7.8 %collective-permute-start.4 = (f32[3,32,256]{2,1,0:T(8,128)S(1)}, f32[3,32,256]{2,1,0:T(8,128)S(1)}, u32[]{:S(2)}, u32[]{:S(2)}) collective-permute-start(f32[3,32,256]{2,1,0:T(8,128)S(1)} %mean.2), channel_id=1, source_target_pairs={{0,7},{1,0},{2,1},{3,2},{4,3},{5,4},{6,5},{7,6},{8,15},{9,8},{10,9... | collective-permute-start | bytes 294920 | tf_op jit(solution)/shard_map/ppermute | solution.py:474
  25.1 5.8 %collective-permute-start.11 = (f32[3,32,256]{2,1,0:T(8,128)S(1)}, f32[3,32,256]{2,1,0:T(8,128)S(1)}, u32[]{:S(2)}, u32[]{:S(2)}) collective-permute-start(f32[3,32,256]{2,1,0:T(8,128)S(1)} %mean.2), channel_id=1, source_target_pairs={{0,23},{1,16},{2,17},{3,18},{4,19},{5,20},{6,21},{7,22},{8,31},{9,... | collective-permute-start | bytes 294920 | tf_op jit(solution)/shard_map/ppermute | solution.py:474
  27.2 4.8 %collective-permute-start.8 = (f32[3,32,256]{2,1,0:T(8,128)S(1)}, f32[3,32,256]{2,1,0:T(8,128)S(1)}, u32[]{:S(2)}, u32[]{:S(2)}) collective-permute-start(f32[3,32,256]{2,1,0:T(8,128)S(1)} %collective-permute-done.6.rest_0_), channel_id=1, source_target_pairs={{0,16},{8,24},{16,0},{24,8},{1,17},{9,25},{17,1},{25,9},{2,18},{10... | collective-permute-start | bytes 294920 | tf_op jit(solution)/shard_map/ppermute | solution.py:459
  30.3 1.6 %collective-permute-start.10 = (f32[3,32,256]{2,1,0:T(8,128)S(1)}, f32[3,32,256]{2,1,0:T(8,128)S(1)}, u32[]{:S(2)}, u32[]{:S(2)}) collective-permute-start(f32[3,32,256]{2,1,0:T(8,128)S(1)} %collective-permute-done.4.rest_4_), channel_id=1, source_target_pairs={{0,8},{8,0},{16,24},{24,16},{1,9},{9,1},{17,25},{25,17},{2,10},{10... | collective-permute-start | bytes 294920 | tf_op jit(solution)/shard_map/ppermute | solution.py:459
  30.4 1.5 %collective-permute-start.7 = (f32[3,32,256]{2,1,0:T(8,128)S(1)}, f32[3,32,256]{2,1,0:T(8,128)S(1)}, u32[]{:S(2)}, u32[]{:S(2)}) collective-permute-start(f32[3,32,256]{2,1,0:T(8,128)S(1)} %collective-permute-done.6.rest_0_), channel_id=1, source_target_pairs={{0,8},{8,0},{16,24},{24,16},{1,9},{9,1},{17,25},{25,17},{2,10},{10... | collective-permute-start | bytes 294920 | tf_op jit(solution)/shard_map/ppermute | solution.py:459
  30.9 1.3 %collective-permute-start.12 = (f32[3,32,256]{2,1,0:T(8,128)S(1)}, f32[3,32,256]{2,1,0:T(8,128)S(1)}, u32[]{:S(2)}, u32[]{:S(2)}) collective-permute-start(f32[3,32,256]{2,1,0:T(8,128)S(1)} %collective-permute-done.11.rest_6_), channel_id=1, source_target_pairs={{0,8},{8,0},{16,24},{24,16},{1,9},{9,1},{17,25},{25,17},{2,10},{10... | collective-permute-start | bytes 294920 | tf_op jit(solution)/shard_map/ppermute | solution.py:459
  31.9 1.3 %collective-permute-start.9 = (f32[3,32,256]{2,1,0:T(8,128)S(1)}, f32[3,32,256]{2,1,0:T(8,128)S(1)}, u32[]{:S(2)}, u32[]{:S(2)}) collective-permute-start(f32[3,32,256]{2,1,0:T(8,128)S(1)} %collective-permute-done.8.rest_2_), channel_id=1, source_target_pairs={{0,8},{8,0},{16,24},{24,16},{1,9},{9,1},{17,25},{25,17},{2,10},{10... | collective-permute-start | bytes 294920 | tf_op jit(solution)/shard_map/ppermute | solution.py:459

commit v9 on v8

--- a/solution.py
+++ b/solution.py
@@ -464,14 +464,39 @@
     return lax.ppermute(value, "blk", [(source, (source + steps) % count) for source in range(count)])
 
 
-def delivered(value, step):
+def delivered(value, step, around=True):
     groups, slots = lax.axis_size("grp"), lax.axis_size("blk")
     pairs = [
         (group * slots + slot, (group ^ step) * slots + (slot - 1) % slots)
         for group in range(groups)
-        for slot in range(slots)
+        for slot in range(0 if around else 1, slots)
     ]
     return lax.ppermute(value, ("grp", "blk"), pairs)
+
+
+def crossed_last(value, step):
+    groups, slots = lax.axis_size("grp"), lax.axis_size("blk")
+    pairs = [
+        (group * slots + slots - 1, (group ^ step) * slots + slots - 1) for group in range(groups)
+    ]
+    return lax.ppermute(value, ("grp", "blk"), pairs)
+
+
+def choose_kernel(last_ref, other_ref, out_ref):
+    last = lax.axis_index("blk") == lax.axis_size("blk") - 1
+    out_ref[...] = jnp.where(last, last_ref[...], other_ref[...])
+
+
+def choose(last, other):
+    return pl.pallas_call(
+        choose_kernel,
+        out_shape=jax.ShapeDtypeStruct(last.shape, F32),
+        in_specs=[whole(), whole()],
+        out_specs=whole(),
+        compiler_params=params(),
+        cost_estimate=cost(last.size, 3 * last.size * 4),
+        name="choose",
+    )(last, other)
 
 
 def body(obs, mask_bits, factors, x_blocks, first_moment, second_moment, ar_weights, stratum):
@@ -502,12 +527,15 @@
     mean0 = mean(keep0, far0, count)
 
     near0 = delivered(mean0, 0)
+    far1, mean0 = lax.optimization_barrier((far1, mean0))
     mean1 = mean(keep1, far1, count)
     near1 = delivered(mean1, 0)
-    side1 = delivered(mean1, 2)
+    flip1 = delivered(mean1, 2, around=False)
     side0 = crossed(near0, 2)
+    last1 = crossed_last(near1, 2)
     factor_new = factor_step(lead, kept, err, turned, near0, factor_new, third, series - third)
-    near1, factor_new = lax.optimization_barrier((near1, factor_new))
+    flip1, side0, factor_new = lax.optimization_barrier((flip1, side0, factor_new))
+    side1 = choose(last1, flip1)
     pieces = [
         [near0, crossed(near0, 1), side0, crossed(side0, 1)],
         [near1, crossed(near1, 1), side1, crossed(side1, 1)],

time: 34.5 us -> 35.9 us (1.041)
  the two profiles are of different devices: /device:TPU:0 before, /device:TPU:29 now
where the time goes in v9:
time: 35.9 us; the launch traced here: 35.7 us
  starting transfers between devices  17.5 us (49%)
  Pallas kernels  12.7 us (35%)
  waiting for transfers between devices  4.1 us (11%)
  between operations  1.43 us (4%)
    ppermute x3, starting transfers between devices, delivered(): return lax.ppermute(value, ('grp', 'blk'), pairs)  7.15 us
    ppermute x9, starting transfers between devices, crossed(): lax.ppermute(value, 'grp', [(source, source ^ step) for source in range(c...  6.18 us
    pallas_call x1, Pallas kernels, error_step(): pl.pallas_call(functools.partial(error_kernel, rows), out_shape=(jax.Shap...  4.84 us
    ppermute x1, starting transfers between devices, crossed_last(): return lax.ppermute(value, ('grp', 'blk'), pairs)  4.1 us
    ppermute x9, waiting for transfers between devices, crossed(): lax.ppermute(value, 'grp', [(source, source ^ step) for source in range(c...  3.5 us
    pallas_call x2, Pallas kernels, factor_step(): pl.pallas_call(functools.partial(factor_kernel, begin, rows, chunks), out...  3.32 us
    pallas_call x1, Pallas kernels, prepare(): pl.pallas_call(functools.partial(prepare_kernel, rows), out_shape=(jax.Sh...  1.39 us
    pallas_call x1, Pallas kernels, regress_step(): pl.pallas_call(functools.partial(regress_kernel, lanes), out_shape=(jax.S...  1.2 us
  transfers between devices with their start and end apart: 14, of which 5 were waited for; matrix products, arithmetic and copies ran while one was open for 0% of the time, Pallas kernels for 27%

profile of v9, /device:TPU:29, one launch (start us, length us, event | category | flops | bytes accessed | tf_op | source)
XLA Modules:
  0.0 35.7 jit_solution(13710123312651879226)
XLA Ops:
  0.6 1.4 %prepare.1 = (f32[168,256]{1,0:T(8,128)S(1)}, f32[256,256]{1,0:T(8,128)S(1)}, f32[256,256]{1,0:T(8,128)S(1)}, bf16[1024,512]{1,0:T(8,128)(2,1)S(1)}, s32[32,1024]{1,0:T(8,128)S(1)}) custom-call(f32[1,256,256]{2,1,0:T(8,128)} %x_hbm.1, bf16[6144,256]{1,0:T(8,128)(2,1)} %obs_hbm.3, s32[32,6144]{1,0:T(8,128)} %bitcast.3, bf16[6144,256]{1,0:T(8,128)(2,1)} %f_hbm.3), custom_call_target="tpu_custom_call" | custom-call | bytes 3145728 | tf_op jit(solution)/shard_map/prepare/pallas_call | solution.py:90
  2.0 0.1 collective-permute-start
  2.7 0.0 copy-start
  2.8 4.8 %errors.1 = (bf16[256,6144]{1,0:T(8,128)(2,1)S(1)}, bf16[5120,512]{1,0:T(8,128)(2,1)S(1)}, f32[256,256]{1,0:T(8,128)S(1)}) custom-call(bf16[6144,256]{1,0:T(8,128)(2,1)} %obs_hbm.3, s32[32,6144]{1,0:T(8,128)} %bitcast.4, bf16[6144,256]{1,0:T(8,128)(2,1)} %f_hbm.3, f32[256,256]{1,0:T(8,128)S(1)} %get-tuple-element.33.turned_ref, ...), custom_call_target="tpu_custom_call" | custom-call | flops 3221225472 | bytes 10223616 | tf_op jit(solution)/shard_map/errors/pallas_call | solution.py:184
  7.6 0.0 copy-done
  7.6 1.2 %regress.1 = (f32[256,256]{1,0:T(8,128)S(1)}, f32[256,256]{1,0:T(8,128)S(1)}, f32[256,256]{1,0:T(8,128)S(1)}) custom-call(f32[256,256]{1,0:T(8,128)S(1)} %get-tuple-element.33.turned_ref, f32[25,256]{1,0:T(8,128)S(1)} %copy-done, f32[256,256]{1,0:T(8,128)S(1)} %get-tuple-element.36.gd_ref, f32[1,256,256]{2,1,0:T(8,128)} %m_hbm.1, f32[1,256,256]{2,1,0:T(8,128)} %v_hbm.1), custom_call_target="tpu_custom_call" | custom-call | flops 6553600 | bytes 1572864 | tf_op jit(solution)/shard_map/regress/pallas_call | solution.py:281
  8.8 0.0 collective-permute-done.halo_ref
  8.8 0.8 %update.1 = (f32[3,2,32,256]{3,2,1,0:T(8,128)S(1)}, f32[3,2,32,256]{3,2,1,0:T(8,128)S(1)}, f32[3,2,32,256]{3,2,1,0:T(8,128)S(1)}, f32[3,2,32,256]{3,2,1,0:T(8,128)S(1)}) custom-call(s32[1,1]{1,0:T(1,128)} %bitcast.2.stratum_ref, f32[168,256]{1,0:T(8,128)S(1)} %collective-permute-done.halo_ref, f32[25,256]{1,0:T(8,128)S(1)} %copy-done, ...), custom_call_target="tpu_custom_call" | custom-call | flops 3932160 | bytes 2621440 | tf_op jit(solution)/shard_map/update/pallas_call | solution.py:361
  9.6 0.7 %collective-permute-start.2 = (f32[3,2,32,256]{3,2,1,0:T(8,128)S(1)}, f32[3,2,32,256]{3,2,1,0:T(8,128)S(1)}, u32[]{:S(2)}, u32[]{:S(2)}) collective-permute-start(f32[3,2,32,256]{3,2,1,0:T(8,128)S(1)} %get-tuple-element.46), channel_id=1, source_target_pairs={{0,8},{8,0},{16,24},{24,16},{1,9},{9,1},{17,25},{25,17},{2,10},{10... | collective-permute-start | bytes 589832 | tf_op jit(solution)/shard_map/ppermute | solution.py:459
  10.3 0.1 collective-permute-start.1
  10.4 1.0 %collective-permute-done.2.got_ref = f32[3,2,32,256]{3,2,1,0:T(8,128)S(1)} collective-permute-done((f32[3,2,32,256]{3,2,1,0:T(8,128)S(1)}, f32[3,2,32,256]{3,2,1,0:T(8,128)S(1)}, u32[]{:S(2)}, u32[]{:S(2)}) %collective-permute-start.2) | collective-permute-done | bytes 196640 | tf_op jit(solution)/shard_map/ppermute | solution.py:459
  11.4 1.4 %collective-permute-start.4 = (f32[3,1,32,256]{3,2,1,0:T(8,128)S(1)}, f32[3,1,32,256]{3,2,1,0:T(8,128)S(1)}, u32[]{:S(2)}, u32[]{:S(2)}) collective-permute-start(f32[3,1,32,256]{3,2,1,0:T(8,128)S(1)} %get-tuple-element.47.rest_0_), channel_id=1, source_target_pairs={{0,16},{8,24},{16,0},{24,8},{1,17},{9,25},{17,1},{25,9},{2,18},{10... | collective-permute-start | bytes 294920 | tf_op jit(solution)/shard_map/ppermute | solution.py:459
  12.9 1.5 %factors.2.rest_1_ = bf16[6144,256]{1,0:T(8,128)(2,1)} custom-call(bf16[1024,512]{1,0:T(8,128)(2,1)S(1)} %get-tuple-element.34.first_ref, bf16[5120,512]{1,0:T(8,128)(2,1)S(1)} %get-tuple-element.43.both_ref, bf16[256,6144]{1,0:T(8,128)(2,1)S(1)} %get-tuple-element.44.err_ref, f32[256,256]{1,0:T(8,128)S(1)} %get-tuple-element.33.turned_ref, ...), custom_call_target="tpu_custom_call" | custom-call | flops 268435456 | bytes 3145728 | tf_op jit(solution)/shard_map/factors/pallas_call | solution.py:238
  14.3 0.0 collective-permute-done.1.got_ref
  14.4 0.2 collective-permute-start.3
  14.6 0.9 %collective-permute-done.4.got_ref = f32[3,1,32,256]{3,2,1,0:T(8,128)S(1)} collective-permute-done((f32[3,1,32,256]{3,2,1,0:T(8,128)S(1)}, f32[3,1,32,256]{3,2,1,0:T(8,128)S(1)}, u32[]{:S(2)}, u32[]{:S(2)}) %collective-permute-start.4) | collective-permute-done | bytes 98336 | tf_op jit(solution)/shard_map/ppermute | solution.py:459
  15.5 1.8 %collective-permute-start.6 = (f32[3,32,256]{2,1,0:T(8,128)S(1)}, f32[3,32,256]{2,1,0:T(8,128)S(1)}, u32[]{:S(2)}, u32[]{:S(2)}) collective-permute-start(f32[3,32,256]{2,1,0:T(8,128)S(1)} %mean.2), channel_id=1, source_target_pairs={{0,7},{1,0},{2,1},{3,2},{4,3},{5,4},{6,5},{7,6},{8,15},{9,8},{10,9... | collective-permute-start | bytes 294920 | tf_op jit(solution)/shard_map/ppermute | solution.py:474
  17.3 0.6 %collective-permute-done.3.got_ref = f32[3,1,32,256]{3,2,1,0:T(8,128)S(1)} collective-permute-done((f32[3,1,32,256]{3,2,1,0:T(8,128)S(1)}, f32[3,1,32,256]{3,2,1,0:T(8,128)S(1)}, u32[]{:S(2)}, u32[]{:S(2)}) %collective-permute-start.3) | collective-permute-done | bytes 98336 | tf_op jit(solution)/shard_map/ppermute | solution.py:459
  18.0 1.6 %collective-permute-start.10 = (f32[3,32,256]{2,1,0:T(8,128)S(1)}, f32[3,32,256]{2,1,0:T(8,128)S(1)}, u32[]{:S(2)}, u32[]{:S(2)}) collective-permute-start(f32[3,32,256]{2,1,0:T(8,128)S(1)} %mean.3), channel_id=1, source_target_pairs={{0,7},{1,0},{2,1},{3,2},{4,3},{5,4},{6,5},{7,6},{8,15},{9,8},{10,9... | collective-permute-start | bytes 294920 | tf_op jit(solution)/shard_map/ppermute | solution.py:474
  19.6 3.7 %collective-permute-start.5 = (f32[3,32,256]{2,1,0:T(8,128)S(1)}, f32[3,32,256]{2,1,0:T(8,128)S(1)}, u32[]{:S(2)}, u32[]{:S(2)}) collective-permute-start(f32[3,32,256]{2,1,0:T(8,128)S(1)} %mean.3), channel_id=1, source_target_pairs={{1,16},{2,17},{3,18},{4,19},{5,20},{6,21},{7,22},{9,24},{10,25},{1... | collective-permute-start | bytes 294920 | tf_op jit(solution)/shard_map/ppermute | solution.py:474
  23.3 0.0 collective-permute-done.6.rest_0_
  23.3 0.5 %collective-permute-start.7 = (f32[3,32,256]{2,1,0:T(8,128)S(1)}, f32[3,32,256]{2,1,0:T(8,128)S(1)}, u32[]{:S(2)}, u32[]{:S(2)}) collective-permute-start(f32[3,32,256]{2,1,0:T(8,128)S(1)} %collective-permute-done.6.rest_0_), channel_id=1, source_target_pairs={{0,16},{8,24},{16,0},{24,8},{1,17},{9,25},{17,1},{25,9},{2,18},{10... | collective-permute-start | bytes 294920 | tf_op jit(solution)/shard_map/ppermute | solution.py:459
  23.9 0.6 %collective-permute-done.10.rest_4_ = f32[3,32,256]{2,1,0:T(8,128)S(1)} collective-permute-done((f32[3,32,256]{2,1,0:T(8,128)S(1)}, f32[3,32,256]{2,1,0:T(8,128)S(1)}, u32[]{:S(2)}, u32[]{:S(2)}) %collective-permute-start.10) | collective-permute-done | bytes 98336 | tf_op jit(solution)/shard_map/ppermute | solution.py:474
  24.5 4.1 %collective-permute-start.12 = (f32[3,32,256]{2,1,0:T(8,128)S(1)}, f32[3,32,256]{2,1,0:T(8,128)S(1)}, u32[]{:S(2)}, u32[]{:S(2)}) collective-permute-start(f32[3,32,256]{2,1,0:T(8,128)S(1)} %collective-permute-done.10.rest_4_), channel_id=1, source_target_pairs={{7,23},{15,31},{23,7},{31,15}} | collective-permute-start | bytes 294920 | tf_op jit(solution)/shard_map/ppermute | solution.py:482
  28.6 1.7 %collective-permute-start.8 = (f32[3,32,256]{2,1,0:T(8,128)S(1)}, f32[3,32,256]{2,1,0:T(8,128)S(1)}, u32[]{:S(2)}, u32[]{:S(2)}) collective-permute-start(f32[3,32,256]{2,1,0:T(8,128)S(1)} %collective-permute-done.6.rest_0_), channel_id=1, source_target_pairs={{0,8},{8,0},{16,24},{24,16},{1,9},{9,1},{17,25},{25,17},{2,10},{10... | collective-permute-start | bytes 294920 | tf_op jit(solution)/shard_map/ppermute | solution.py:459
  30.3 0.1 collective-permute-start.11
  30.3 1.9 %factors.3 = bf16[6144,256]{1,0:T(8,128)(2,1)} custom-call(bf16[1024,512]{1,0:T(8,128)(2,1)S(1)} %get-tuple-element.34.first_ref, bf16[5120,512]{1,0:T(8,128)(2,1)S(1)} %get-tuple-element.43.both_ref, bf16[256,6144]{1,0:T(8,128)(2,1)S(1)} %get-tuple-element.44.err_ref, f32[256,256]{1,0:T(8,128)S(1)} %get-tuple-element.33.turned_ref, ...), custom_call_target="tpu_custom_call", output_to_operand_aliasing={{}: (5, {})} | custom-call | flops 536870912 | bytes 6291456 | tf_op jit(solution)/shard_map/factors/pallas_call | solution.py:238
  32.2 0.0 collective-permute-done.5.other_ref
  32.2 0.0 collective-permute-done.7.rest_2_
  32.2 0.5 %collective-permute-start.9 = (f32[3,32,256]{2,1,0:T(8,128)S(1)}, f32[3,32,256]{2,1,0:T(8,128)S(1)}, u32[]{:S(2)}, u32[]{:S(2)}) collective-permute-start(f32[3,32,256]{2,1,0:T(8,128)S(1)} %collective-permute-done.7.rest_2_), channel_id=1, source_target_pairs={{0,8},{8,0},{16,24},{24,16},{1,9},{9,1},{17,25},{25,17},{2,10},{10... | collective-permute-start | bytes 294920 | tf_op jit(solution)/shard_map/ppermute | solution.py:459
  32.7 0.0 collective-permute-done.12.last_ref
  32.8 1.0 %collective-permute-start.13 = (f32[3,32,256]{2,1,0:T(8,128)S(1)}, f32[3,32,256]{2,1,0:T(8,128)S(1)}, u32[]{:S(2)}, u32[]{:S(2)}) collective-permute-start(f32[3,32,256]{2,1,0:T(8,128)S(1)} %choose.1.rest_6_), channel_id=1, source_target_pairs={{0,8},{8,0},{16,24},{24,16},{1,9},{9,1},{17,25},{25,17},{2,10},{10... | collective-permute-start | bytes 294920 | tf_op jit(solution)/shard_map/ppermute | solution.py:459
  33.7 0.0 collective-permute-done.8.rest_1_
  33.7 0.0 collective-permute-done.11.rest_5_
  33.7 0.0 collective-permute-done.9.rest_3_
  33.7 0.9 %collective-permute-done.13.rest_7_ = f32[3,32,256]{2,1,0:T(8,128)S(1)} collective-permute-done((f32[3,32,256]{2,1,0:T(8,128)S(1)}, f32[3,32,256]{2,1,0:T(8,128)S(1)}, u32[]{:S(2)}, u32[]{:S(2)}) %collective-permute-start.13) | collective-permute-done | bytes 98336 | tf_op jit(solution)/shard_map/ppermute | solution.py:459
  34.7 1.1 %place.1 = (f32[1,256,256]{2,1,0:T(8,128)}, f32[1,256,256]{2,1,0:T(8,128)}, f32[1,256,256]{2,1,0:T(8,128)}) custom-call(f32[3,32,256]{2,1,0:T(8,128)S(1)} %collective-permute-done.6.rest_0_, f32[3,32,256]{2,1,0:T(8,128)S(1)} %collective-permute-done.8.rest_1_, f32[3,32,256]{2,1,0:T(8,128)S(1)} %collective-permute-done.7.rest_2_, ...), custom_call_target="tpu_custom_call" | custom-call | bytes 1572864 | tf_op jit(solution)/shard_map/place/pallas_call | solution.py:445
  (5 shorter events, 0.1 us)
Async XLA Ops:
  2.0 6.8 %collective-permute-start = (f32[168,256]{1,0:T(8,128)S(1)}, f32[168,256]{1,0:T(8,128)S(1)}, u32[]{:S(2)}, u32[]{:S(2)}) collective-permute-start(f32[168,256]{1,0:T(8,128)S(1)} %get-tuple-element.32), channel_id=1, source_target_pairs={{0,1},{1,2},{2,3},{3,4},{4,5},{5,6},{6,7},{7,0},{8,9},{9,10},{10,1... | collective-permute-start | bytes 516104 | tf_op jit(solution)/shard_map/ppermute | solution.py:464
  2.7 4.9 %copy-start = (f32[25,256]{1,0:T(8,128)S(1)}, f32[25,256]{1,0:T(8,128)}, u32[]{:S(2)}) copy-start(f32[25,256]{1,0:T(8,128)} %w_ref.3) | copy-start | bytes 76804
  9.6 1.8 %collective-permute-start.2 = (f32[3,2,32,256]{3,2,1,0:T(8,128)S(1)}, f32[3,2,32,256]{3,2,1,0:T(8,128)S(1)}, u32[]{:S(2)}, u32[]{:S(2)}) collective-permute-start(f32[3,2,32,256]{3,2,1,0:T(8,128)S(1)} %get-tuple-element.46), channel_id=1, source_target_pairs={{0,8},{8,0},{16,24},{24,16},{1,9},{9,1},{17,25},{25,17},{2,10},{10... | collective-permute-start | bytes 589832 | tf_op jit(solution)/shard_map/ppermute | solution.py:459
  10.3 4.0 %collective-permute-start.1 = (f32[3,2,32,256]{3,2,1,0:T(8,128)S(1)}, f32[3,2,32,256]{3,2,1,0:T(8,128)S(1)}, u32[]{:S(2)}, u32[]{:S(2)}) collective-permute-start(f32[3,2,32,256]{3,2,1,0:T(8,128)S(1)} %get-tuple-element.42), channel_id=1, source_target_pairs={{0,8},{8,0},{16,24},{24,16},{1,9},{9,1},{17,25},{25,17},{2,10},{10... | collective-permute-start | bytes 589832 | tf_op jit(solution)/shard_map/ppermute | solution.py:459
  11.4 4.1 %collective-permute-start.4 = (f32[3,1,32,256]{3,2,1,0:T(8,128)S(1)}, f32[3,1,32,256]{3,2,1,0:T(8,128)S(1)}, u32[]{:S(2)}, u32[]{:S(2)}) collective-permute-start(f32[3,1,32,256]{3,2,1,0:T(8,128)S(1)} %get-tuple-element.47.rest_0_), channel_id=1, source_target_pairs={{0,16},{8,24},{16,0},{24,8},{1,17},{9,25},{17,1},{25,9},{2,18},{10... | collective-permute-start | bytes 294920 | tf_op jit(solution)/shard_map/ppermute | solution.py:459
  14.4 3.5 %collective-permute-start.3 = (f32[3,1,32,256]{3,2,1,0:T(8,128)S(1)}, f32[3,1,32,256]{3,2,1,0:T(8,128)S(1)}, u32[]{:S(2)}, u32[]{:S(2)}) collective-permute-start(f32[3,1,32,256]{3,2,1,0:T(8,128)S(1)} %get-tuple-element.50), channel_id=1, source_target_pairs={{0,16},{8,24},{16,0},{24,8},{1,17},{9,25},{17,1},{25,9},{2,18},{10... | collective-permute-start | bytes 294920 | tf_op jit(solution)/shard_map/ppermute | solution.py:459
  15.5 7.8 %collective-permute-start.6 = (f32[3,32,256]{2,1,0:T(8,128)S(1)}, f32[3,32,256]{2,1,0:T(8,128)S(1)}, u32[]{:S(2)}, u32[]{:S(2)}) collective-permute-start(f32[3,32,256]{2,1,0:T(8,128)S(1)} %mean.2), channel_id=1, source_target_pairs={{0,7},{1,0},{2,1},{3,2},{4,3},{5,4},{6,5},{7,6},{8,15},{9,8},{10,9... | collective-permute-start | bytes 294920 | tf_op jit(solution)/shard_map/ppermute | solution.py:474
  18.0 6.5 %collective-permute-start.10 = (f32[3,32,256]{2,1,0:T(8,128)S(1)}, f32[3,32,256]{2,1,0:T(8,128)S(1)}, u32[]{:S(2)}, u32[]{:S(2)}) collective-permute-start(f32[3,32,256]{2,1,0:T(8,128)S(1)} %mean.3), channel_id=1, source_target_pairs={{0,7},{1,0},{2,1},{3,2},{4,3},{5,4},{6,5},{7,6},{8,15},{9,8},{10,9... | collective-permute-start | bytes 294920 | tf_op jit(solution)/shard_map/ppermute | solution.py:474
  19.6 12.6 %collective-permute-start.5 = (f32[3,32,256]{2,1,0:T(8,128)S(1)}, f32[3,32,256]{2,1,0:T(8,128)S(1)}, u32[]{:S(2)}, u32[]{:S(2)}) collective-permute-start(f32[3,32,256]{2,1,0:T(8,128)S(1)} %mean.3), channel_id=1, source_target_pairs={{1,16},{2,17},{3,18},{4,19},{5,20},{6,21},{7,22},{9,24},{10,25},{1... | collective-permute-start | bytes 294920 | tf_op jit(solution)/shard_map/ppermute | solution.py:474
  23.3 8.9 %collective-permute-start.7 = (f32[3,32,256]{2,1,0:T(8,128)S(1)}, f32[3,32,256]{2,1,0:T(8,128)S(1)}, u32[]{:S(2)}, u32[]{:S(2)}) collective-permute-start(f32[3,32,256]{2,1,0:T(8,128)S(1)} %collective-permute-done.6.rest_0_), channel_id=1, source_target_pairs={{0,16},{8,24},{16,0},{24,8},{1,17},{9,25},{17,1},{25,9},{2,18},{10... | collective-permute-start | bytes 294920 | tf_op jit(solution)/shard_map/ppermute | solution.py:459
  24.5 8.3 %collective-permute-start.12 = (f32[3,32,256]{2,1,0:T(8,128)S(1)}, f32[3,32,256]{2,1,0:T(8,128)S(1)}, u32[]{:S(2)}, u32[]{:S(2)}) collective-permute-start(f32[3,32,256]{2,1,0:T(8,128)S(1)} %collective-permute-done.10.rest_4_), channel_id=1, source_target_pairs={{7,23},{15,31},{23,7},{31,15}} | collective-permute-start | bytes 294920 | tf_op jit(solution)/shard_map/ppermute | solution.py:482
  28.6 5.1 %collective-permute-start.8 = (f32[3,32,256]{2,1,0:T(8,128)S(1)}, f32[3,32,256]{2,1,0:T(8,128)S(1)}, u32[]{:S(2)}, u32[]{:S(2)}) collective-permute-start(f32[3,32,256]{2,1,0:T(8,128)S(1)} %collective-permute-done.6.rest_0_), channel_id=1, source_target_pairs={{0,8},{8,0},{16,24},{24,16},{1,9},{9,1},{17,25},{25,17},{2,10},{10... | collective-permute-start | bytes 294920 | tf_op jit(solution)/shard_map/ppermute | solution.py:459
  30.3 3.5 %collective-permute-start.11 = (f32[3,32,256]{2,1,0:T(8,128)S(1)}, f32[3,32,256]{2,1,0:T(8,128)S(1)}, u32[]{:S(2)}, u32[]{:S(2)}) collective-permute-start(f32[3,32,256]{2,1,0:T(8,128)S(1)} %collective-permute-done.10.rest_4_), channel_id=1, source_target_pairs={{0,8},{8,0},{16,24},{24,16},{1,9},{9,1},{17,25},{25,17},{2,10},{10... | collective-permute-start | bytes 294920 | tf_op jit(solution)/shard_map/ppermute | solution.py:459
  32.2 1.5 %collective-permute-start.9 = (f32[3,32,256]{2,1,0:T(8,128)S(1)}, f32[3,32,256]{2,1,0:T(8,128)S(1)}, u32[]{:S(2)}, u32[]{:S(2)}) collective-permute-start(f32[3,32,256]{2,1,0:T(8,128)S(1)} %collective-permute-done.7.rest_2_), channel_id=1, source_target_pairs={{0,8},{8,0},{16,24},{24,16},{1,9},{9,1},{17,25},{25,17},{2,10},{10... | collective-permute-start | bytes 294920 | tf_op jit(solution)/shard_map/ppermute | solution.py:459
  32.8 1.9 %collective-permute-start.13 = (f32[3,32,256]{2,1,0:T(8,128)S(1)}, f32[3,32,256]{2,1,0:T(8,128)S(1)}, u32[]{:S(2)}, u32[]{:S(2)}) collective-permute-start(f32[3,32,256]{2,1,0:T(8,128)S(1)} %choose.1.rest_6_), channel_id=1, source_target_pairs={{0,8},{8,0},{16,24},{24,16},{1,9},{9,1},{17,25},{25,17},{2,10},{10... | collective-permute-start | bytes 294920 | tf_op jit(solution)/shard_map/ppermute | solution.py:459

commit v10 on v8

--- a/solution.py
+++ b/solution.py
@@ -416,18 +416,19 @@
     )(kept, got)
 
 
-def place_kernel(count, share, *rest):
-    parts, outs, sems = rest[:-4], rest[-4:-1], rest[-1]
+def place_kernel(share, spots, *rest):
+    outs, sems = rest[-4:-1], rest[-1]
     group = lax.axis_index("grp")
     copies = []
-    for index, part in enumerate(parts):
-        begin = sum(before.shape[1] for before in parts[: index // count * count : count])
-        size = part.shape[1]
-        start = pl.multiple_of((group ^ (index % count)) * share + begin, 8)
+    for index, (step, begin) in enumerate(spots):
+        part = rest[index]
+        start = pl.multiple_of((group ^ step) * share + begin, 8)
         for which in range(3):
             copies.append(
                 pltpu.make_async_copy(
-                    part.at[which], outs[which].at[0, pl.ds(start, size), :], sems.at[index, which]
+                    part.at[which],
+                    outs[which].at[0, pl.ds(start, part.shape[1]), :],
+                    sems.at[index, which],
                 )
             )
     for copy in copies:
@@ -436,22 +437,20 @@
         copy.wait()
 
 
-def place(pieces):
-    parts = [part for piece in pieces for part in piece]
-    count = len(pieces[0])
+def place(parts, spots, share, count, sofar):
     width = parts[0].shape[2]
-    share = sum(piece[0].shape[1] for piece in pieces)
     out = jax.ShapeDtypeStruct((1, count * share, width), F32)
     return pl.pallas_call(
-        functools.partial(place_kernel, count, share),
+        functools.partial(place_kernel, share, spots),
         out_shape=(out, out, out),
-        in_specs=[pl.BlockSpec(memory_space=pl.ANY)] * len(parts),
+        in_specs=[pl.BlockSpec(memory_space=pl.ANY)] * (len(parts) + len(sofar)),
         out_specs=(far(), far(), far()),
+        input_output_aliases={len(parts) + which: which for which in range(len(sofar))},
         scratch_shapes=[pltpu.SemaphoreType.DMA((len(parts), 3))],
         compiler_params=params(),
-        cost_estimate=cost(0, 6 * count * share * width * 4),
+        cost_estimate=cost(0, 6 * sum(part.size for part in parts) * 4),
         name="place",
-    )(*parts)
+    )(*parts, *sofar)
 
 
 def crossed(value, step):
@@ -508,11 +507,12 @@
     side0 = crossed(near0, 2)
     factor_new = factor_step(lead, kept, err, turned, near0, factor_new, third, series - third)
     near1, factor_new = lax.optimization_barrier((near1, factor_new))
-    pieces = [
-        [near0, crossed(near0, 1), side0, crossed(side0, 1)],
-        [near1, crossed(near1, 1), side1, crossed(side1, 1)],
-    ]
-    return (factor_new, *place(pieces))
+    parts = [near0, crossed(near0, 1), side0]
+    parts += [near1, crossed(near1, 1), side1, crossed(side1, 1)]
+    spots = [(0, 0), (1, 0), (2, 0), (0, half), (1, half), (2, half), (3, half)]
+    outs = place(parts, spots, share, count, ())
+    outs = place([crossed(side0, 1)], [(3, 0)], share, count, outs)
+    return (factor_new, *outs)
 
 
 def solution(mesh):

time: 34.5 us -> 34.1 us (0.988)
  waiting for transfers between devices: 5.5 us -> 4.49 us
  Pallas kernels: 12.7 us -> 13.3 us
    ppermute x9, waiting for transfers between devices: 4.81 us -> 3.79 us  [crossed(): lax.ppermute(value, 'grp', [(source, source ^ step) for source in range(c...]
    pallas_call x1 -> x2, Pallas kernels: 1.07 us -> 1.69 us  [place(): pl.pallas_call(functools.partial(place_kernel, share, spots), out_shape=(...]
  transfers between devices with their start and end apart: 13 -> 13, of which waited for: 7 -> 6; matrix products, arithmetic and copies ran while one was open for 0% -> 0% of each run, Pallas kernels for 28% -> 31%
where the time goes in v10:
time: 34.1 us; the launch traced here: 33.9 us
  starting transfers between devices  14.7 us (43%)
  Pallas kernels  13.3 us (39%)
  waiting for transfers between devices  4.49 us (13%)
  between operations  1.42 us (4%)
    ppermute x3, starting transfers between devices, delivered(): return lax.ppermute(value, ('grp', 'blk'), pairs)  7.03 us
    pallas_call x1, Pallas kernels, error_step(): pl.pallas_call(functools.partial(error_kernel, rows), out_shape=(jax.Shap...  4.84 us
    ppermute x9, starting transfers between devices, crossed(): lax.ppermute(value, 'grp', [(source, source ^ step) for source in range(c...  4.67 us
    ppermute x9, waiting for transfers between devices, crossed(): lax.ppermute(value, 'grp', [(source, source ^ step) for source in range(c...  3.79 us
    pallas_call x2, Pallas kernels, factor_step(): pl.pallas_call(functools.partial(factor_kernel, begin, rows, chunks), out...  3.32 us
    ppermute x1, starting transfers between devices, shifted(): lax.ppermute(value, 'blk', [(source, (source + steps) % count) for source...  3.02 us
    pallas_call x2, Pallas kernels, place(): pl.pallas_call(functools.partial(place_kernel, share, spots), out_shape=(...  1.69 us
    pallas_call x1, Pallas kernels, prepare(): pl.pallas_call(functools.partial(prepare_kernel, rows), out_shape=(jax.Sh...  1.39 us
  transfers between devices with their start and end apart: 13, of which 6 were waited for; matrix products, arithmetic and copies ran while one was open for 0% of the time, Pallas kernels for 31%

profile of v10, /device:TPU:0, one launch (start us, length us, event | category | flops | bytes accessed | tf_op | source)
XLA Modules:
  0.0 33.9 jit_solution(2264826092171129592)
XLA Ops:
  0.6 1.4 %prepare.1 = (f32[168,256]{1,0:T(8,128)S(1)}, f32[256,256]{1,0:T(8,128)S(1)}, f32[256,256]{1,0:T(8,128)S(1)}, bf16[1024,512]{1,0:T(8,128)(2,1)S(1)}, s32[32,1024]{1,0:T(8,128)S(1)}) custom-call(f32[1,256,256]{2,1,0:T(8,128)} %x_hbm.1, bf16[6144,256]{1,0:T(8,128)(2,1)} %obs_hbm.3, s32[32,6144]{1,0:T(8,128)} %bitcast.3, bf16[6144,256]{1,0:T(8,128)(2,1)} %f_hbm.3), custom_call_target="tpu_custom_call" | custom-call | bytes 3145728 | tf_op jit(solution)/shard_map/prepare/pallas_call | solution.py:90
  2.0 3.0 %collective-permute-start = (f32[168,256]{1,0:T(8,128)S(1)}, f32[168,256]{1,0:T(8,128)S(1)}, u32[]{:S(2)}, u32[]{:S(2)}) collective-permute-start(f32[168,256]{1,0:T(8,128)S(1)} %get-tuple-element.33), channel_id=1, source_target_pairs={{0,1},{1,2},{2,3},{3,4},{4,5},{5,6},{6,7},{7,0},{8,9},{9,10},{10,1... | collective-permute-start | bytes 516104 | tf_op jit(solution)/shard_map/ppermute | solution.py:463
  5.7 0.0 copy-start
  5.7 4.8 %errors.1 = (bf16[256,6144]{1,0:T(8,128)(2,1)S(1)}, bf16[5120,512]{1,0:T(8,128)(2,1)S(1)}, f32[256,256]{1,0:T(8,128)S(1)}) custom-call(bf16[6144,256]{1,0:T(8,128)(2,1)} %obs_hbm.3, s32[32,6144]{1,0:T(8,128)} %bitcast.4, bf16[6144,256]{1,0:T(8,128)(2,1)} %f_hbm.3, f32[256,256]{1,0:T(8,128)S(1)} %get-tuple-element.34.turned_ref, ...), custom_call_target="tpu_custom_call" | custom-call | flops 3221225472 | bytes 10223616 | tf_op jit(solution)/shard_map/errors/pallas_call | solution.py:184
  10.6 0.0 copy-done
  10.6 1.2 %regress.1 = (f32[256,256]{1,0:T(8,128)S(1)}, f32[256,256]{1,0:T(8,128)S(1)}, f32[256,256]{1,0:T(8,128)S(1)}) custom-call(f32[256,256]{1,0:T(8,128)S(1)} %get-tuple-element.34.turned_ref, f32[25,256]{1,0:T(8,128)S(1)} %copy-done, f32[256,256]{1,0:T(8,128)S(1)} %get-tuple-element.37.gd_ref, f32[1,256,256]{2,1,0:T(8,128)} %m_hbm.1, f32[1,256,256]{2,1,0:T(8,128)} %v_hbm.1), custom_call_target="tpu_custom_call" | custom-call | flops 6553600 | bytes 1572864 | tf_op jit(solution)/shard_map/regress/pallas_call | solution.py:281
  11.8 0.7 %collective-permute-done.halo_ref = f32[168,256]{1,0:T(8,128)S(1)} collective-permute-done((f32[168,256]{1,0:T(8,128)S(1)}, f32[168,256]{1,0:T(8,128)S(1)}, u32[]{:S(2)}, u32[]{:S(2)}) %collective-permute-start) | collective-permute-done | bytes 172064 | tf_op jit(solution)/shard_map/ppermute | solution.py:463
  12.5 0.8 %update.1 = (f32[3,2,32,256]{3,2,1,0:T(8,128)S(1)}, f32[3,2,32,256]{3,2,1,0:T(8,128)S(1)}, f32[3,2,32,256]{3,2,1,0:T(8,128)S(1)}, f32[3,2,32,256]{3,2,1,0:T(8,128)S(1)}) custom-call(s32[1,1]{1,0:T(1,128)} %bitcast.2.stratum_ref, f32[168,256]{1,0:T(8,128)S(1)} %collective-permute-done.halo_ref, f32[25,256]{1,0:T(8,128)S(1)} %copy-done, ...), custom_call_target="tpu_custom_call" | custom-call | flops 3932160 | bytes 2621440 | tf_op jit(solution)/shard_map/update/pallas_call | solution.py:361
  13.2 0.1 collective-permute-start.2
  13.3 0.5 %collective-permute-start.1 = (f32[3,2,32,256]{3,2,1,0:T(8,128)S(1)}, f32[3,2,32,256]{3,2,1,0:T(8,128)S(1)}, u32[]{:S(2)}, u32[]{:S(2)}) collective-permute-start(f32[3,2,32,256]{3,2,1,0:T(8,128)S(1)} %get-tuple-element.43), channel_id=1, source_target_pairs={{0,8},{8,0},{16,24},{24,16},{1,9},{9,1},{17,25},{25,17},{2,10},{10... | collective-permute-start | bytes 589832 | tf_op jit(solution)/shard_map/ppermute | solution.py:458
  13.8 0.9 %collective-permute-done.2.got_ref = f32[3,2,32,256]{3,2,1,0:T(8,128)S(1)} collective-permute-done((f32[3,2,32,256]{3,2,1,0:T(8,128)S(1)}, f32[3,2,32,256]{3,2,1,0:T(8,128)S(1)}, u32[]{:S(2)}, u32[]{:S(2)}) %collective-permute-start.2) | collective-permute-done | bytes 196640 | tf_op jit(solution)/shard_map/ppermute | solution.py:458
  14.8 1.6 %collective-permute-start.5 = (f32[3,1,32,256]{3,2,1,0:T(8,128)S(1)}, f32[3,1,32,256]{3,2,1,0:T(8,128)S(1)}, u32[]{:S(2)}, u32[]{:S(2)}) collective-permute-start(f32[3,1,32,256]{3,2,1,0:T(8,128)S(1)} %get-tuple-element.48.rest_0_), channel_id=1, source_target_pairs={{0,16},{8,24},{16,0},{24,8},{1,17},{9,25},{17,1},{25,9},{2,18},{10... | collective-permute-start | bytes 294920 | tf_op jit(solution)/shard_map/ppermute | solution.py:458
  16.3 1.5 %factors.2.rest_1_ = bf16[6144,256]{1,0:T(8,128)(2,1)} custom-call(bf16[1024,512]{1,0:T(8,128)(2,1)S(1)} %get-tuple-element.35.first_ref, bf16[5120,512]{1,0:T(8,128)(2,1)S(1)} %get-tuple-element.44.both_ref, bf16[256,6144]{1,0:T(8,128)(2,1)S(1)} %get-tuple-element.45.err_ref, f32[256,256]{1,0:T(8,128)S(1)} %get-tuple-element.34.turned_ref, ...), custom_call_target="tpu_custom_call" | custom-call | flops 268435456 | bytes 3145728 | tf_op jit(solution)/shard_map/factors/pallas_call | solution.py:238
  17.8 0.0 collective-permute-done.1.got_ref
  17.9 0.6 %collective-permute-start.3 = (f32[3,1,32,256]{3,2,1,0:T(8,128)S(1)}, f32[3,1,32,256]{3,2,1,0:T(8,128)S(1)}, u32[]{:S(2)}, u32[]{:S(2)}) collective-permute-start(f32[3,1,32,256]{3,2,1,0:T(8,128)S(1)} %get-tuple-element.51), channel_id=1, source_target_pairs={{0,16},{8,24},{16,0},{24,8},{1,17},{9,25},{17,1},{25,9},{2,18},{10... | collective-permute-start | bytes 294920 | tf_op jit(solution)/shard_map/ppermute | solution.py:458
  18.5 1.2 %collective-permute-done.5.got_ref = f32[3,1,32,256]{3,2,1,0:T(8,128)S(1)} collective-permute-done((f32[3,1,32,256]{3,2,1,0:T(8,128)S(1)}, f32[3,1,32,256]{3,2,1,0:T(8,128)S(1)}, u32[]{:S(2)}, u32[]{:S(2)}) %collective-permute-start.5) | collective-permute-done | bytes 98336 | tf_op jit(solution)/shard_map/ppermute | solution.py:458
  19.7 2.4 %collective-permute-start.6 = (f32[3,32,256]{2,1,0:T(8,128)S(1)}, f32[3,32,256]{2,1,0:T(8,128)S(1)}, u32[]{:S(2)}, u32[]{:S(2)}) collective-permute-start(f32[3,32,256]{2,1,0:T(8,128)S(1)} %mean.3), channel_id=1, source_target_pairs={{0,7},{1,0},{2,1},{3,2},{4,3},{5,4},{6,5},{7,6},{8,15},{9,8},{10,9... | collective-permute-start | bytes 294920 | tf_op jit(solution)/shard_map/ppermute | solution.py:473
  22.1 0.4 %collective-permute-done.3.got_ref = f32[3,1,32,256]{3,2,1,0:T(8,128)S(1)} collective-permute-done((f32[3,1,32,256]{3,2,1,0:T(8,128)S(1)}, f32[3,1,32,256]{3,2,1,0:T(8,128)S(1)}, u32[]{:S(2)}, u32[]{:S(2)}) %collective-permute-start.3) | collective-permute-done | bytes 98336 | tf_op jit(solution)/shard_map/ppermute | solution.py:458
  22.6 2.6 %collective-permute-start.4 = (f32[3,32,256]{2,1,0:T(8,128)S(1)}, f32[3,32,256]{2,1,0:T(8,128)S(1)}, u32[]{:S(2)}, u32[]{:S(2)}) collective-permute-start(f32[3,32,256]{2,1,0:T(8,128)S(1)} %mean.2), channel_id=1, source_target_pairs={{0,7},{1,0},{2,1},{3,2},{4,3},{5,4},{6,5},{7,6},{8,15},{9,8},{10,9... | collective-permute-start | bytes 294920 | tf_op jit(solution)/shard_map/ppermute | solution.py:473
  25.1 2.0 %collective-permute-start.11 = (f32[3,32,256]{2,1,0:T(8,128)S(1)}, f32[3,32,256]{2,1,0:T(8,128)S(1)}, u32[]{:S(2)}, u32[]{:S(2)}) collective-permute-start(f32[3,32,256]{2,1,0:T(8,128)S(1)} %mean.2), channel_id=1, source_target_pairs={{0,23},{1,16},{2,17},{3,18},{4,19},{5,20},{6,21},{7,22},{8,31},{9,... | collective-permute-start | bytes 294920 | tf_op jit(solution)/shard_map/ppermute | solution.py:473
  27.2 0.0 collective-permute-done.6.rest_0_
  27.2 1.3 %collective-permute-start.7 = (f32[3,32,256]{2,1,0:T(8,128)S(1)}, f32[3,32,256]{2,1,0:T(8,128)S(1)}, u32[]{:S(2)}, u32[]{:S(2)}) collective-permute-start(f32[3,32,256]{2,1,0:T(8,128)S(1)} %collective-permute-done.6.rest_0_), channel_id=1, source_target_pairs={{0,16},{8,24},{16,0},{24,8},{1,17},{9,25},{17,1},{25,9},{2,18},{10... | collective-permute-start | bytes 294920 | tf_op jit(solution)/shard_map/ppermute | solution.py:458
  28.5 1.9 %factors.3 = bf16[6144,256]{1,0:T(8,128)(2,1)} custom-call(bf16[1024,512]{1,0:T(8,128)(2,1)S(1)} %get-tuple-element.35.first_ref, bf16[5120,512]{1,0:T(8,128)(2,1)S(1)} %get-tuple-element.44.both_ref, bf16[256,6144]{1,0:T(8,128)(2,1)S(1)} %get-tuple-element.45.err_ref, f32[256,256]{1,0:T(8,128)S(1)} %get-tuple-element.34.turned_ref, ...), custom_call_target="tpu_custom_call", output_to_operand_aliasing={{}: (5, {})} | custom-call | flops 536870912 | bytes 6291456 | tf_op jit(solution)/shard_map/factors/pallas_call | solution.py:238
  30.3 0.0 collective-permute-done.4.rest_3_
  30.3 0.1 collective-permute-start.10
  30.4 0.5 %collective-permute-start.9 = (f32[3,32,256]{2,1,0:T(8,128)S(1)}, f32[3,32,256]{2,1,0:T(8,128)S(1)}, u32[]{:S(2)}, u32[]{:S(2)}) collective-permute-start(f32[3,32,256]{2,1,0:T(8,128)S(1)} %collective-permute-done.6.rest_0_), channel_id=1, source_target_pairs={{0,8},{8,0},{16,24},{24,16},{1,9},{9,1},{17,25},{25,17},{2,10},{10... | collective-permute-start | bytes 294920 | tf_op jit(solution)/shard_map/ppermute | solution.py:458
  30.9 0.0 collective-permute-done.11.rest_5_
  30.9 0.1 collective-permute-start.12
  31.0 0.9 %collective-permute-done.7.rest_2_ = f32[3,32,256]{2,1,0:T(8,128)S(1)} collective-permute-done((f32[3,32,256]{2,1,0:T(8,128)S(1)}, f32[3,32,256]{2,1,0:T(8,128)S(1)}, u32[]{:S(2)}, u32[]{:S(2)}) %collective-permute-start.7) | collective-permute-done | bytes 98336 | tf_op jit(solution)/shard_map/ppermute | solution.py:458
  31.9 0.0 collective-permute-start.8
  31.9 0.0 collective-permute-done.9.rest_1_
  31.9 0.0 collective-permute-done.10.rest_4_
  32.0 0.3 collective-permute-done.12.rest_6_
  32.2 1.0 %place.2 = (f32[1,256,256]{2,1,0:T(8,128)}, f32[1,256,256]{2,1,0:T(8,128)}, f32[1,256,256]{2,1,0:T(8,128)}) custom-call(f32[3,32,256]{2,1,0:T(8,128)S(1)} %collective-permute-done.6.rest_0_, f32[3,32,256]{2,1,0:T(8,128)S(1)} %collective-permute-done.9.rest_1_, f32[3,32,256]{2,1,0:T(8,128)S(1)} %collective-permute-done.7.rest_2_, ...), custom_call_target="tpu_custom_call" | custom-call | bytes 4128768 | tf_op jit(solution)/shard_map/place/pallas_call | solution.py:443
  33.2 0.0 collective-permute-done.8.rest_0_
  33.3 0.7 %place.3 = (f32[1,256,256]{2,1,0:T(8,128)}, f32[1,256,256]{2,1,0:T(8,128)}, f32[1,256,256]{2,1,0:T(8,128)}) custom-call(f32[3,32,256]{2,1,0:T(8,128)S(1)} %collective-permute-done.8.rest_0_, f32[1,256,256]{2,1,0:T(8,128)} %get-tuple-element.56.rest_1_, ...), custom_call_target="tpu_custom_call", output_to_operand_aliasing={{0}: (1, {}), {1}: (2, {}), {2}: (3, {})} | custom-call | bytes 589824 | tf_op jit(solution)/shard_map/place/pallas_call | solution.py:443
  (4 shorter events, 0.1 us)
Async XLA Ops:
  2.0 10.4 %collective-permute-start = (f32[168,256]{1,0:T(8,128)S(1)}, f32[168,256]{1,0:T(8,128)S(1)}, u32[]{:S(2)}, u32[]{:S(2)}) collective-permute-start(f32[168,256]{1,0:T(8,128)S(1)} %get-tuple-element.33), channel_id=1, source_target_pairs={{0,1},{1,2},{2,3},{3,4},{4,5},{5,6},{6,7},{7,0},{8,9},{9,10},{10,1... | collective-permute-start | bytes 516104 | tf_op jit(solution)/shard_map/ppermute | solution.py:463
  5.7 4.9 %copy-start = (f32[25,256]{1,0:T(8,128)S(1)}, f32[25,256]{1,0:T(8,128)}, u32[]{:S(2)}) copy-start(f32[25,256]{1,0:T(8,128)} %w_ref.3) | copy-start | bytes 76804
  13.2 1.5 %collective-permute-start.2 = (f32[3,2,32,256]{3,2,1,0:T(8,128)S(1)}, f32[3,2,32,256]{3,2,1,0:T(8,128)S(1)}, u32[]{:S(2)}, u32[]{:S(2)}) collective-permute-start(f32[3,2,32,256]{3,2,1,0:T(8,128)S(1)} %get-tuple-element.47), channel_id=1, source_target_pairs={{0,8},{8,0},{16,24},{24,16},{1,9},{9,1},{17,25},{25,17},{2,10},{10... | collective-permute-start | bytes 589832 | tf_op jit(solution)/shard_map/ppermute | solution.py:458
  13.3 4.5 %collective-permute-start.1 = (f32[3,2,32,256]{3,2,1,0:T(8,128)S(1)}, f32[3,2,32,256]{3,2,1,0:T(8,128)S(1)}, u32[]{:S(2)}, u32[]{:S(2)}) collective-permute-start(f32[3,2,32,256]{3,2,1,0:T(8,128)S(1)} %get-tuple-element.43), channel_id=1, source_target_pairs={{0,8},{8,0},{16,24},{24,16},{1,9},{9,1},{17,25},{25,17},{2,10},{10... | collective-permute-start | bytes 589832 | tf_op jit(solution)/shard_map/ppermute | solution.py:458
  14.8 4.9 %collective-permute-start.5 = (f32[3,1,32,256]{3,2,1,0:T(8,128)S(1)}, f32[3,1,32,256]{3,2,1,0:T(8,128)S(1)}, u32[]{:S(2)}, u32[]{:S(2)}) collective-permute-start(f32[3,1,32,256]{3,2,1,0:T(8,128)S(1)} %get-tuple-element.48.rest_0_), channel_id=1, source_target_pairs={{0,16},{8,24},{16,0},{24,8},{1,17},{9,25},{17,1},{25,9},{2,18},{10... | collective-permute-start | bytes 294920 | tf_op jit(solution)/shard_map/ppermute | solution.py:458
  17.9 4.7 %collective-permute-start.3 = (f32[3,1,32,256]{3,2,1,0:T(8,128)S(1)}, f32[3,1,32,256]{3,2,1,0:T(8,128)S(1)}, u32[]{:S(2)}, u32[]{:S(2)}) collective-permute-start(f32[3,1,32,256]{3,2,1,0:T(8,128)S(1)} %get-tuple-element.51), channel_id=1, source_target_pairs={{0,16},{8,24},{16,0},{24,8},{1,17},{9,25},{17,1},{25,9},{2,18},{10... | collective-permute-start | bytes 294920 | tf_op jit(solution)/shard_map/ppermute | solution.py:458
  19.7 7.5 %collective-permute-start.6 = (f32[3,32,256]{2,1,0:T(8,128)S(1)}, f32[3,32,256]{2,1,0:T(8,128)S(1)}, u32[]{:S(2)}, u32[]{:S(2)}) collective-permute-start(f32[3,32,256]{2,1,0:T(8,128)S(1)} %mean.3), channel_id=1, source_target_pairs={{0,7},{1,0},{2,1},{3,2},{4,3},{5,4},{6,5},{7,6},{8,15},{9,8},{10,9... | collective-permute-start | bytes 294920 | tf_op jit(solution)/shard_map/ppermute | solution.py:473
  22.6 7.8 %collective-permute-start.4 = (f32[3,32,256]{2,1,0:T(8,128)S(1)}, f32[3,32,256]{2,1,0:T(8,128)S(1)}, u32[]{:S(2)}, u32[]{:S(2)}) collective-permute-start(f32[3,32,256]{2,1,0:T(8,128)S(1)} %mean.2), channel_id=1, source_target_pairs={{0,7},{1,0},{2,1},{3,2},{4,3},{5,4},{6,5},{7,6},{8,15},{9,8},{10,9... | collective-permute-start | bytes 294920 | tf_op jit(solution)/shard_map/ppermute | solution.py:473
  25.1 5.8 %collective-permute-start.11 = (f32[3,32,256]{2,1,0:T(8,128)S(1)}, f32[3,32,256]{2,1,0:T(8,128)S(1)}, u32[]{:S(2)}, u32[]{:S(2)}) collective-permute-start(f32[3,32,256]{2,1,0:T(8,128)S(1)} %mean.2), channel_id=1, source_target_pairs={{0,23},{1,16},{2,17},{3,18},{4,19},{5,20},{6,21},{7,22},{8,31},{9,... | collective-permute-start | bytes 294920 | tf_op jit(solution)/shard_map/ppermute | solution.py:473
  27.2 4.8 %collective-permute-start.7 = (f32[3,32,256]{2,1,0:T(8,128)S(1)}, f32[3,32,256]{2,1,0:T(8,128)S(1)}, u32[]{:S(2)}, u32[]{:S(2)}) collective-permute-start(f32[3,32,256]{2,1,0:T(8,128)S(1)} %collective-permute-done.6.rest_0_), channel_id=1, source_target_pairs={{0,16},{8,24},{16,0},{24,8},{1,17},{9,25},{17,1},{25,9},{2,18},{10... | collective-permute-start | bytes 294920 | tf_op jit(solution)/shard_map/ppermute | solution.py:458
  30.3 1.6 %collective-permute-start.10 = (f32[3,32,256]{2,1,0:T(8,128)S(1)}, f32[3,32,256]{2,1,0:T(8,128)S(1)}, u32[]{:S(2)}, u32[]{:S(2)}) collective-permute-start(f32[3,32,256]{2,1,0:T(8,128)S(1)} %collective-permute-done.4.rest_3_), channel_id=1, source_target_pairs={{0,8},{8,0},{16,24},{24,16},{1,9},{9,1},{17,25},{25,17},{2,10},{10... | collective-permute-start | bytes 294920 | tf_op jit(solution)/shard_map/ppermute | solution.py:458
  30.4 1.5 %collective-permute-start.9 = (f32[3,32,256]{2,1,0:T(8,128)S(1)}, f32[3,32,256]{2,1,0:T(8,128)S(1)}, u32[]{:S(2)}, u32[]{:S(2)}) collective-permute-start(f32[3,32,256]{2,1,0:T(8,128)S(1)} %collective-permute-done.6.rest_0_), channel_id=1, source_target_pairs={{0,8},{8,0},{16,24},{24,16},{1,9},{9,1},{17,25},{25,17},{2,10},{10... | collective-permute-start | bytes 294920 | tf_op jit(solution)/shard_map/ppermute | solution.py:458
  30.9 1.3 %collective-permute-start.12 = (f32[3,32,256]{2,1,0:T(8,128)S(1)}, f32[3,32,256]{2,1,0:T(8,128)S(1)}, u32[]{:S(2)}, u32[]{:S(2)}) collective-permute-start(f32[3,32,256]{2,1,0:T(8,128)S(1)} %collective-permute-done.11.rest_5_), channel_id=1, source_target_pairs={{0,8},{8,0},{16,24},{24,16},{1,9},{9,1},{17,25},{25,17},{2,10},{10... | collective-permute-start | bytes 294920 | tf_op jit(solution)/shard_map/ppermute | solution.py:458
  31.9 1.3 %collective-permute-start.8 = (f32[3,32,256]{2,1,0:T(8,128)S(1)}, f32[3,32,256]{2,1,0:T(8,128)S(1)}, u32[]{:S(2)}, u32[]{:S(2)}) collective-permute-start(f32[3,32,256]{2,1,0:T(8,128)S(1)} %collective-permute-done.7.rest_2_), channel_id=1, source_target_pairs={{0,8},{8,0},{16,24},{24,16},{1,9},{9,1},{17,25},{25,17},{2,10},{10... | collective-permute-start | bytes 294920 | tf_op jit(solution)/shard_map/ppermute | solution.py:458

commit v11 on v10

--- a/solution.py
+++ b/solution.py
@@ -398,22 +398,29 @@
     )(kept, got)
 
 
-def mean_kernel(count, kept_ref, got_ref, out_ref):
-    for which in range(3):
-        out_ref[which] = (kept_ref[which, 0] + got_ref[which, 0]) / count
-
-
-def mean(kept, got, count):
-    _, _, size, width = kept.shape
-    return pl.pallas_call(
-        functools.partial(mean_kernel, count),
+def mean_kernel(count, bounds, *rest):
+    out_ref = rest[-1]
+    at = 0
+    for index, (low, high) in enumerate(bounds):
+        kept_ref, got_ref = rest[2 * index : 2 * index + 2]
+        for which in range(3):
+            total = kept_ref[which, 0, low:high, :] + got_ref[which, 0, low:high, :]
+            out_ref[which, at : at + high - low, :] = total / count
+        at += high - low
+
+
+def mean(pairs, bounds, count):
+    width = pairs[0][0].shape[3]
+    size = sum(high - low for low, high in bounds)
+    return pl.pallas_call(
+        functools.partial(mean_kernel, count, bounds),
         out_shape=jax.ShapeDtypeStruct((3, size, width), F32),
-        in_specs=[whole(), whole()],
+        in_specs=[whole()] * (2 * len(pairs)),
         out_specs=whole(),
         compiler_params=params(),
-        cost_estimate=cost(2 * kept.size, 3 * kept.size * 4),
+        cost_estimate=cost(6 * size * width, 36 * size * width),
         name="mean",
-    )(kept, got)
+    )(*[part for pair in pairs for part in pair])
 
 
 def place_kernel(share, spots, *rest):
@@ -498,10 +505,13 @@
     got1, factor_new = lax.optimization_barrier((got1, factor_new))
     keep1, send1 = halve(keep1, got1, 2)
     far1 = crossed(send1, 2)
-    mean0 = mean(keep0, far0, count)
+    small = max(half * 3 // 4 // 8 * 8, 8)
+    mean0 = mean([(keep0, far0)], [(0, small)], count)
 
     near0 = delivered(mean0, 0)
-    mean1 = mean(keep1, far1, count)
+    mean1 = mean(
+        [(keep0, far0), (keep1, far1)], [(small, half), (0, share - half)], count
+    )
     near1 = delivered(mean1, 0)
     side1 = delivered(mean1, 2)
     side0 = crossed(near0, 2)
@@ -509,7 +519,7 @@
     near1, factor_new = lax.optimization_barrier((near1, factor_new))
     parts = [near0, crossed(near0, 1), side0]
     parts += [near1, crossed(near1, 1), side1, crossed(side1, 1)]
-    spots = [(0, 0), (1, 0), (2, 0), (0, half), (1, half), (2, half), (3, half)]
+    spots = [(0, 0), (1, 0), (2, 0), (0, small), (1, small), (2, small), (3, small)]
     outs = place(parts, spots, share, count, ())
     outs = place([crossed(side0, 1)], [(3, 0)], share, count, outs)
     return (factor_new, *outs)

time: 34.1 us -> 34.2 us (level)
    ppermute x3, waiting for transfers between devices: 0.01 us -> 0.51 us  [delivered(): return lax.ppermute(value, ('grp', 'blk'), pairs)]
  transfers between devices with their start and end apart: 13 -> 13, of which waited for: 6 -> 7; matrix products, arithmetic and copies ran while one was open for 0% -> 0% of each run, Pallas kernels for 31% -> 31%
where the time goes in v11:
time: 34.2 us; the launch traced here: 34.1 us
  starting transfers between devices  14.7 us (43%)
  Pallas kernels  13.3 us (39%)
  waiting for transfers between devices  4.71 us (14%)
  between operations  1.41 us (4%)
    ppermute x3, starting transfers between devices, delivered(): return lax.ppermute(value, ('grp', 'blk'), pairs)  7.03 us
    pallas_call x1, Pallas kernels, error_step(): pl.pallas_call(functools.partial(error_kernel, rows), out_shape=(jax.Shap...  4.84 us
    ppermute x9, starting transfers between devices, crossed(): lax.ppermute(value, 'grp', [(source, source ^ step) for source in range(c...  4.6 us
    ppermute x9, waiting for transfers between devices, crossed(): lax.ppermute(value, 'grp', [(source, source ^ step) for source in range(c...  3.51 us
    pallas_call x2, Pallas kernels, factor_step(): pl.pallas_call(functools.partial(factor_kernel, begin, rows, chunks), out...  3.31 us
    ppermute x1, starting transfers between devices, shifted(): lax.ppermute(value, 'blk', [(source, (source + steps) % count) for source...  3.02 us
    pallas_call x2, Pallas kernels, place(): pl.pallas_call(functools.partial(place_kernel, share, spots), out_shape=(...  1.69 us
    pallas_call x1, Pallas kernels, prepare(): pl.pallas_call(functools.partial(prepare_kernel, rows), out_shape=(jax.Sh...  1.39 us
  transfers between devices with their start and end apart: 13, of which 7 were waited for; matrix products, arithmetic and copies ran while one was open for 0% of the time, Pallas kernels for 31%

profile of v11, /device:TPU:0, one launch (start us, length us, event | category | flops | bytes accessed | tf_op | source)
XLA Modules:
  0.0 34.1 jit_solution(11712659669751904228)
XLA Ops:
  0.6 1.4 %prepare.1 = (f32[168,256]{1,0:T(8,128)S(1)}, f32[256,256]{1,0:T(8,128)S(1)}, f32[256,256]{1,0:T(8,128)S(1)}, bf16[1024,512]{1,0:T(8,128)(2,1)S(1)}, s32[32,1024]{1,0:T(8,128)S(1)}) custom-call(f32[1,256,256]{2,1,0:T(8,128)} %x_hbm.1, bf16[6144,256]{1,0:T(8,128)(2,1)} %obs_hbm.3, s32[32,6144]{1,0:T(8,128)} %bitcast.3, bf16[6144,256]{1,0:T(8,128)(2,1)} %f_hbm.3), custom_call_target="tpu_custom_call" | custom-call | bytes 3145728 | tf_op jit(solution)/shard_map/prepare/pallas_call | solution.py:90
  2.0 3.0 %collective-permute-start = (f32[168,256]{1,0:T(8,128)S(1)}, f32[168,256]{1,0:T(8,128)S(1)}, u32[]{:S(2)}, u32[]{:S(2)}) collective-permute-start(f32[168,256]{1,0:T(8,128)S(1)} %get-tuple-element.33), channel_id=1, source_target_pairs={{0,1},{1,2},{2,3},{3,4},{4,5},{5,6},{6,7},{7,0},{8,9},{9,10},{10,1... | collective-permute-start | bytes 516104 | tf_op jit(solution)/shard_map/ppermute | solution.py:470
  5.7 0.0 copy-start
  5.7 4.8 %errors.1 = (bf16[256,6144]{1,0:T(8,128)(2,1)S(1)}, bf16[5120,512]{1,0:T(8,128)(2,1)S(1)}, f32[256,256]{1,0:T(8,128)S(1)}) custom-call(bf16[6144,256]{1,0:T(8,128)(2,1)} %obs_hbm.3, s32[32,6144]{1,0:T(8,128)} %bitcast.4, bf16[6144,256]{1,0:T(8,128)(2,1)} %f_hbm.3, f32[256,256]{1,0:T(8,128)S(1)} %get-tuple-element.34.turned_ref, ...), custom_call_target="tpu_custom_call" | custom-call | flops 3221225472 | bytes 10223616 | tf_op jit(solution)/shard_map/errors/pallas_call | solution.py:184
  10.6 0.0 copy-done
  10.6 1.2 %regress.1 = (f32[256,256]{1,0:T(8,128)S(1)}, f32[256,256]{1,0:T(8,128)S(1)}, f32[256,256]{1,0:T(8,128)S(1)}) custom-call(f32[256,256]{1,0:T(8,128)S(1)} %get-tuple-element.34.turned_ref, f32[25,256]{1,0:T(8,128)S(1)} %copy-done, f32[256,256]{1,0:T(8,128)S(1)} %get-tuple-element.37.gd_ref, f32[1,256,256]{2,1,0:T(8,128)} %m_hbm.1, f32[1,256,256]{2,1,0:T(8,128)} %v_hbm.1), custom_call_target="tpu_custom_call" | custom-call | flops 6553600 | bytes 1572864 | tf_op jit(solution)/shard_map/regress/pallas_call | solution.py:281
  11.8 0.7 %collective-permute-done.halo_ref = f32[168,256]{1,0:T(8,128)S(1)} collective-permute-done((f32[168,256]{1,0:T(8,128)S(1)}, f32[168,256]{1,0:T(8,128)S(1)}, u32[]{:S(2)}, u32[]{:S(2)}) %collective-permute-start) | collective-permute-done | bytes 172064 | tf_op jit(solution)/shard_map/ppermute | solution.py:470
  12.5 0.8 %update.1 = (f32[3,2,32,256]{3,2,1,0:T(8,128)S(1)}, f32[3,2,32,256]{3,2,1,0:T(8,128)S(1)}, f32[3,2,32,256]{3,2,1,0:T(8,128)S(1)}, f32[3,2,32,256]{3,2,1,0:T(8,128)S(1)}) custom-call(s32[1,1]{1,0:T(1,128)} %bitcast.2.stratum_ref, f32[168,256]{1,0:T(8,128)S(1)} %collective-permute-done.halo_ref, f32[25,256]{1,0:T(8,128)S(1)} %copy-done, ...), custom_call_target="tpu_custom_call" | custom-call | flops 3932160 | bytes 2621440 | tf_op jit(solution)/shard_map/update/pallas_call | solution.py:361
  13.2 0.1 collective-permute-start.1
  13.3 0.5 %collective-permute-start.3 = (f32[3,2,32,256]{3,2,1,0:T(8,128)S(1)}, f32[3,2,32,256]{3,2,1,0:T(8,128)S(1)}, u32[]{:S(2)}, u32[]{:S(2)}) collective-permute-start(f32[3,2,32,256]{3,2,1,0:T(8,128)S(1)} %get-tuple-element.47), channel_id=1, source_target_pairs={{0,8},{8,0},{16,24},{24,16},{1,9},{9,1},{17,25},{25,17},{2,10},{10... | collective-permute-start | bytes 589832 | tf_op jit(solution)/shard_map/ppermute | solution.py:465
  13.8 0.9 %collective-permute-done.1.got_ref = f32[3,2,32,256]{3,2,1,0:T(8,128)S(1)} collective-permute-done((f32[3,2,32,256]{3,2,1,0:T(8,128)S(1)}, f32[3,2,32,256]{3,2,1,0:T(8,128)S(1)}, u32[]{:S(2)}, u32[]{:S(2)}) %collective-permute-start.1) | collective-permute-done | bytes 196640 | tf_op jit(solution)/shard_map/ppermute | solution.py:465
  14.8 1.6 %collective-permute-start.2 = (f32[3,1,32,256]{3,2,1,0:T(8,128)S(1)}, f32[3,1,32,256]{3,2,1,0:T(8,128)S(1)}, u32[]{:S(2)}, u32[]{:S(2)}) collective-permute-start(f32[3,1,32,256]{3,2,1,0:T(8,128)S(1)} %get-tuple-element.45.rest_0_), channel_id=1, source_target_pairs={{0,16},{8,24},{16,0},{24,8},{1,17},{9,25},{17,1},{25,9},{2,18},{10... | collective-permute-start | bytes 294920 | tf_op jit(solution)/shard_map/ppermute | solution.py:465
  16.3 1.5 %factors.2.rest_1_ = bf16[6144,256]{1,0:T(8,128)(2,1)} custom-call(bf16[1024,512]{1,0:T(8,128)(2,1)S(1)} %get-tuple-element.35.first_ref, bf16[5120,512]{1,0:T(8,128)(2,1)S(1)} %get-tuple-element.48.both_ref, bf16[256,6144]{1,0:T(8,128)(2,1)S(1)} %get-tuple-element.49.err_ref, f32[256,256]{1,0:T(8,128)S(1)} %get-tuple-element.34.turned_ref, ...), custom_call_target="tpu_custom_call" | custom-call | flops 268435456 | bytes 3145728 | tf_op jit(solution)/shard_map/factors/pallas_call | solution.py:238
  17.8 0.0 collective-permute-done.3.got_ref
  17.9 0.6 %collective-permute-start.4 = (f32[3,1,32,256]{3,2,1,0:T(8,128)S(1)}, f32[3,1,32,256]{3,2,1,0:T(8,128)S(1)}, u32[]{:S(2)}, u32[]{:S(2)}) collective-permute-start(f32[3,1,32,256]{3,2,1,0:T(8,128)S(1)} %get-tuple-element.52), channel_id=1, source_target_pairs={{0,16},{8,24},{16,0},{24,8},{1,17},{9,25},{17,1},{25,9},{2,18},{10... | collective-permute-start | bytes 294920 | tf_op jit(solution)/shard_map/ppermute | solution.py:465
  18.5 1.2 %collective-permute-done.2.rest_1_ = f32[3,1,32,256]{3,2,1,0:T(8,128)S(1)} collective-permute-done((f32[3,1,32,256]{3,2,1,0:T(8,128)S(1)}, f32[3,1,32,256]{3,2,1,0:T(8,128)S(1)}, u32[]{:S(2)}, u32[]{:S(2)}) %collective-permute-start.2) | collective-permute-done | bytes 98336 | tf_op jit(solution)/shard_map/ppermute | solution.py:465
  19.7 2.4 %collective-permute-start.6 = (f32[3,24,256]{2,1,0:T(8,128)S(1)}, f32[3,24,256]{2,1,0:T(8,128)S(1)}, u32[]{:S(2)}, u32[]{:S(2)}) collective-permute-start(f32[3,24,256]{2,1,0:T(8,128)S(1)} %mean.3), channel_id=1, source_target_pairs={{0,7},{1,0},{2,1},{3,2},{4,3},{5,4},{6,5},{7,6},{8,15},{9,8},{10,9... | collective-permute-start | bytes 221192 | tf_op jit(solution)/shard_map/ppermute | solution.py:480
  22.1 0.4 %collective-permute-done.4.rest_3_ = f32[3,1,32,256]{3,2,1,0:T(8,128)S(1)} collective-permute-done((f32[3,1,32,256]{3,2,1,0:T(8,128)S(1)}, f32[3,1,32,256]{3,2,1,0:T(8,128)S(1)}, u32[]{:S(2)}, u32[]{:S(2)}) %collective-permute-start.4) | collective-permute-done | bytes 98336 | tf_op jit(solution)/shard_map/ppermute | solution.py:465
  22.6 2.6 %collective-permute-start.5 = (f32[3,40,256]{2,1,0:T(8,128)S(1)}, f32[3,40,256]{2,1,0:T(8,128)S(1)}, u32[]{:S(2)}, u32[]{:S(2)}) collective-permute-start(f32[3,40,256]{2,1,0:T(8,128)S(1)} %mean.2), channel_id=1, source_target_pairs={{0,7},{1,0},{2,1},{3,2},{4,3},{5,4},{6,5},{7,6},{8,15},{9,8},{10,9... | collective-permute-start | bytes 368648 | tf_op jit(solution)/shard_map/ppermute | solution.py:480
  25.1 2.0 %collective-permute-start.11 = (f32[3,40,256]{2,1,0:T(8,128)S(1)}, f32[3,40,256]{2,1,0:T(8,128)S(1)}, u32[]{:S(2)}, u32[]{:S(2)}) collective-permute-start(f32[3,40,256]{2,1,0:T(8,128)S(1)} %mean.2), channel_id=1, source_target_pairs={{0,23},{1,16},{2,17},{3,18},{4,19},{5,20},{6,21},{7,22},{8,31},{9,... | collective-permute-start | bytes 368648 | tf_op jit(solution)/shard_map/ppermute | solution.py:480
  27.2 0.0 collective-permute-done.6.rest_0_
  27.2 1.3 %collective-permute-start.7 = (f32[3,24,256]{2,1,0:T(8,128)S(1)}, f32[3,24,256]{2,1,0:T(8,128)S(1)}, u32[]{:S(2)}, u32[]{:S(2)}) collective-permute-start(f32[3,24,256]{2,1,0:T(8,128)S(1)} %collective-permute-done.6.rest_0_), channel_id=1, source_target_pairs={{0,16},{8,24},{16,0},{24,8},{1,17},{9,25},{17,1},{25,9},{2,18},{10... | collective-permute-start | bytes 221192 | tf_op jit(solution)/shard_map/ppermute | solution.py:465
  28.5 1.9 %factors.3 = bf16[6144,256]{1,0:T(8,128)(2,1)} custom-call(bf16[1024,512]{1,0:T(8,128)(2,1)S(1)} %get-tuple-element.35.first_ref, bf16[5120,512]{1,0:T(8,128)(2,1)S(1)} %get-tuple-element.48.both_ref, bf16[256,6144]{1,0:T(8,128)(2,1)S(1)} %get-tuple-element.49.err_ref, f32[256,256]{1,0:T(8,128)S(1)} %get-tuple-element.34.turned_ref, ...), custom_call_target="tpu_custom_call", output_to_operand_aliasing={{}: (5, {})} | custom-call | flops 536870912 | bytes 6291456 | tf_op jit(solution)/shard_map/factors/pallas_call | solution.py:238
  30.3 0.0 collective-permute-done.5.rest_3_
  30.3 0.1 collective-permute-start.10
  30.4 0.5 %collective-permute-done.11.rest_5_ = f32[3,40,256]{2,1,0:T(8,128)S(1)} collective-permute-done((f32[3,40,256]{2,1,0:T(8,128)S(1)}, f32[3,40,256]{2,1,0:T(8,128)S(1)}, u32[]{:S(2)}, u32[]{:S(2)}) %collective-permute-start.11) | collective-permute-done | bytes 122912 | tf_op jit(solution)/shard_map/ppermute | solution.py:480
  30.9 0.0 collective-permute-start.12
  30.9 0.5 %collective-permute-start.9 = (f32[3,24,256]{2,1,0:T(8,128)S(1)}, f32[3,24,256]{2,1,0:T(8,128)S(1)}, u32[]{:S(2)}, u32[]{:S(2)}) collective-permute-start(f32[3,24,256]{2,1,0:T(8,128)S(1)} %collective-permute-done.6.rest_0_), channel_id=1, source_target_pairs={{0,8},{8,0},{16,24},{24,16},{1,9},{9,1},{17,25},{25,17},{2,10},{10... | collective-permute-start | bytes 221192 | tf_op jit(solution)/shard_map/ppermute | solution.py:465
  31.4 0.5 %collective-permute-done.7.rest_2_ = f32[3,24,256]{2,1,0:T(8,128)S(1)} collective-permute-done((f32[3,24,256]{2,1,0:T(8,128)S(1)}, f32[3,24,256]{2,1,0:T(8,128)S(1)}, u32[]{:S(2)}, u32[]{:S(2)}) %collective-permute-start.7) | collective-permute-done | bytes 73760 | tf_op jit(solution)/shard_map/ppermute | solution.py:465
  32.0 0.0 collective-permute-start.8
  32.0 0.4 %collective-permute-done.9.rest_1_ = f32[3,24,256]{2,1,0:T(8,128)S(1)} collective-permute-done((f32[3,24,256]{2,1,0:T(8,128)S(1)}, f32[3,24,256]{2,1,0:T(8,128)S(1)}, u32[]{:S(2)}, u32[]{:S(2)}) %collective-permute-start.9) | collective-permute-done | bytes 73760 | tf_op jit(solution)/shard_map/ppermute | solution.py:465
  32.4 0.0 collective-permute-done.10.rest_4_
  32.4 0.0 collective-permute-done.12.rest_6_
  32.4 1.0 %place.2 = (f32[1,256,256]{2,1,0:T(8,128)}, f32[1,256,256]{2,1,0:T(8,128)}, f32[1,256,256]{2,1,0:T(8,128)}) custom-call(f32[3,24,256]{2,1,0:T(8,128)S(1)} %collective-permute-done.6.rest_0_, f32[3,24,256]{2,1,0:T(8,128)S(1)} %collective-permute-done.9.rest_1_, f32[3,24,256]{2,1,0:T(8,128)S(1)} %collective-permute-done.7.rest_2_, ...), custom_call_target="tpu_custom_call" | custom-call | bytes 4276224 | tf_op jit(solution)/shard_map/place/pallas_call | solution.py:450
  33.4 0.0 collective-permute-done.8.rest_0_
  33.4 0.7 %place.3 = (f32[1,256,256]{2,1,0:T(8,128)}, f32[1,256,256]{2,1,0:T(8,128)}, f32[1,256,256]{2,1,0:T(8,128)}) custom-call(f32[3,24,256]{2,1,0:T(8,128)S(1)} %collective-permute-done.8.rest_0_, f32[1,256,256]{2,1,0:T(8,128)} %get-tuple-element.56.rest_1_, ...), custom_call_target="tpu_custom_call", output_to_operand_aliasing={{0}: (1, {}), {1}: (2, {}), {2}: (3, {})} | custom-call | bytes 442368 | tf_op jit(solution)/shard_map/place/pallas_call | solution.py:450
  (4 shorter events, 0.1 us)
Async XLA Ops:
  2.0 10.4 %collective-permute-start = (f32[168,256]{1,0:T(8,128)S(1)}, f32[168,256]{1,0:T(8,128)S(1)}, u32[]{:S(2)}, u32[]{:S(2)}) collective-permute-start(f32[168,256]{1,0:T(8,128)S(1)} %get-tuple-element.33), channel_id=1, source_target_pairs={{0,1},{1,2},{2,3},{3,4},{4,5},{5,6},{6,7},{7,0},{8,9},{9,10},{10,1... | collective-permute-start | bytes 516104 | tf_op jit(solution)/shard_map/ppermute | solution.py:470
  5.7 4.9 %copy-start = (f32[25,256]{1,0:T(8,128)S(1)}, f32[25,256]{1,0:T(8,128)}, u32[]{:S(2)}) copy-start(f32[25,256]{1,0:T(8,128)} %w_ref.3) | copy-start | bytes 76804
  13.2 1.5 %collective-permute-start.1 = (f32[3,2,32,256]{3,2,1,0:T(8,128)S(1)}, f32[3,2,32,256]{3,2,1,0:T(8,128)S(1)}, u32[]{:S(2)}, u32[]{:S(2)}) collective-permute-start(f32[3,2,32,256]{3,2,1,0:T(8,128)S(1)} %get-tuple-element.43), channel_id=1, source_target_pairs={{0,8},{8,0},{16,24},{24,16},{1,9},{9,1},{17,25},{25,17},{2,10},{10... | collective-permute-start | bytes 589832 | tf_op jit(solution)/shard_map/ppermute | solution.py:465
  13.3 4.5 %collective-permute-start.3 = (f32[3,2,32,256]{3,2,1,0:T(8,128)S(1)}, f32[3,2,32,256]{3,2,1,0:T(8,128)S(1)}, u32[]{:S(2)}, u32[]{:S(2)}) collective-permute-start(f32[3,2,32,256]{3,2,1,0:T(8,128)S(1)} %get-tuple-element.47), channel_id=1, source_target_pairs={{0,8},{8,0},{16,24},{24,16},{1,9},{9,1},{17,25},{25,17},{2,10},{10... | collective-permute-start | bytes 589832 | tf_op jit(solution)/shard_map/ppermute | solution.py:465
  14.8 4.9 %collective-permute-start.2 = (f32[3,1,32,256]{3,2,1,0:T(8,128)S(1)}, f32[3,1,32,256]{3,2,1,0:T(8,128)S(1)}, u32[]{:S(2)}, u32[]{:S(2)}) collective-permute-start(f32[3,1,32,256]{3,2,1,0:T(8,128)S(1)} %get-tuple-element.45.rest_0_), channel_id=1, source_target_pairs={{0,16},{8,24},{16,0},{24,8},{1,17},{9,25},{17,1},{25,9},{2,18},{10... | collective-permute-start | bytes 294920 | tf_op jit(solution)/shard_map/ppermute | solution.py:465
  17.9 4.7 %collective-permute-start.4 = (f32[3,1,32,256]{3,2,1,0:T(8,128)S(1)}, f32[3,1,32,256]{3,2,1,0:T(8,128)S(1)}, u32[]{:S(2)}, u32[]{:S(2)}) collective-permute-start(f32[3,1,32,256]{3,2,1,0:T(8,128)S(1)} %get-tuple-element.52), channel_id=1, source_target_pairs={{0,16},{8,24},{16,0},{24,8},{1,17},{9,25},{17,1},{25,9},{2,18},{10... | collective-permute-start | bytes 294920 | tf_op jit(solution)/shard_map/ppermute | solution.py:465
  19.7 7.5 %collective-permute-start.6 = (f32[3,24,256]{2,1,0:T(8,128)S(1)}, f32[3,24,256]{2,1,0:T(8,128)S(1)}, u32[]{:S(2)}, u32[]{:S(2)}) collective-permute-start(f32[3,24,256]{2,1,0:T(8,128)S(1)} %mean.3), channel_id=1, source_target_pairs={{0,7},{1,0},{2,1},{3,2},{4,3},{5,4},{6,5},{7,6},{8,15},{9,8},{10,9... | collective-permute-start | bytes 221192 | tf_op jit(solution)/shard_map/ppermute | solution.py:480
  22.6 7.8 %collective-permute-start.5 = (f32[3,40,256]{2,1,0:T(8,128)S(1)}, f32[3,40,256]{2,1,0:T(8,128)S(1)}, u32[]{:S(2)}, u32[]{:S(2)}) collective-permute-start(f32[3,40,256]{2,1,0:T(8,128)S(1)} %mean.2), channel_id=1, source_target_pairs={{0,7},{1,0},{2,1},{3,2},{4,3},{5,4},{6,5},{7,6},{8,15},{9,8},{10,9... | collective-permute-start | bytes 368648 | tf_op jit(solution)/shard_map/ppermute | solution.py:480
  25.1 5.8 %collective-permute-start.11 = (f32[3,40,256]{2,1,0:T(8,128)S(1)}, f32[3,40,256]{2,1,0:T(8,128)S(1)}, u32[]{:S(2)}, u32[]{:S(2)}) collective-permute-start(f32[3,40,256]{2,1,0:T(8,128)S(1)} %mean.2), channel_id=1, source_target_pairs={{0,23},{1,16},{2,17},{3,18},{4,19},{5,20},{6,21},{7,22},{8,31},{9,... | collective-permute-start | bytes 368648 | tf_op jit(solution)/shard_map/ppermute | solution.py:480
  27.2 4.8 %collective-permute-start.7 = (f32[3,24,256]{2,1,0:T(8,128)S(1)}, f32[3,24,256]{2,1,0:T(8,128)S(1)}, u32[]{:S(2)}, u32[]{:S(2)}) collective-permute-start(f32[3,24,256]{2,1,0:T(8,128)S(1)} %collective-permute-done.6.rest_0_), channel_id=1, source_target_pairs={{0,16},{8,24},{16,0},{24,8},{1,17},{9,25},{17,1},{25,9},{2,18},{10... | collective-permute-start | bytes 221192 | tf_op jit(solution)/shard_map/ppermute | solution.py:465
  30.3 2.0 %collective-permute-start.10 = (f32[3,40,256]{2,1,0:T(8,128)S(1)}, f32[3,40,256]{2,1,0:T(8,128)S(1)}, u32[]{:S(2)}, u32[]{:S(2)}) collective-permute-start(f32[3,40,256]{2,1,0:T(8,128)S(1)} %collective-permute-done.5.rest_3_), channel_id=1, source_target_pairs={{0,8},{8,0},{16,24},{24,16},{1,9},{9,1},{17,25},{25,17},{2,10},{10... | collective-permute-start | bytes 368648 | tf_op jit(solution)/shard_map/ppermute | solution.py:465
  30.9 1.4 %collective-permute-start.12 = (f32[3,40,256]{2,1,0:T(8,128)S(1)}, f32[3,40,256]{2,1,0:T(8,128)S(1)}, u32[]{:S(2)}, u32[]{:S(2)}) collective-permute-start(f32[3,40,256]{2,1,0:T(8,128)S(1)} %collective-permute-done.11.rest_5_), channel_id=1, source_target_pairs={{0,8},{8,0},{16,24},{24,16},{1,9},{9,1},{17,25},{25,17},{2,10},{10... | collective-permute-start | bytes 368648 | tf_op jit(solution)/shard_map/ppermute | solution.py:465
  30.9 1.4 %collective-permute-start.9 = (f32[3,24,256]{2,1,0:T(8,128)S(1)}, f32[3,24,256]{2,1,0:T(8,128)S(1)}, u32[]{:S(2)}, u32[]{:S(2)}) collective-permute-start(f32[3,24,256]{2,1,0:T(8,128)S(1)} %collective-permute-done.6.rest_0_), channel_id=1, source_target_pairs={{0,8},{8,0},{16,24},{24,16},{1,9},{9,1},{17,25},{25,17},{2,10},{10... | collective-permute-start | bytes 221192 | tf_op jit(solution)/shard_map/ppermute | solution.py:465
  32.0 1.4 %collective-permute-start.8 = (f32[3,24,256]{2,1,0:T(8,128)S(1)}, f32[3,24,256]{2,1,0:T(8,128)S(1)}, u32[]{:S(2)}, u32[]{:S(2)}) collective-permute-start(f32[3,24,256]{2,1,0:T(8,128)S(1)} %collective-permute-done.7.rest_2_), channel_id=1, source_target_pairs={{0,8},{8,0},{16,24},{24,16},{1,9},{9,1},{17,25},{25,17},{2,10},{10... | collective-permute-start | bytes 221192 | tf_op jit(solution)/shard_map/ppermute | solution.py:465

commit v12 on v10

--- a/solution.py
+++ b/solution.py
@@ -491,8 +491,9 @@
     )
 
     got0 = crossed(send0, 1)
+    keep0, send0 = halve(keep0, got0, 2)
+    send1, keep0 = lax.optimization_barrier((send1, keep0))
     got1 = crossed(send1, 1)
-    keep0, send0 = halve(keep0, got0, 2)
     far0 = crossed(send0, 2)
     factor_new = factor_step(lead, kept, err, turned, send0, None, 0, third)
     got1, factor_new = lax.optimization_barrier((got1, factor_new))

time: 34.1 us -> 34.6 us (1.015)
  waiting for transfers between devices: 4.49 us -> 5.31 us
    ppermute x9, waiting for transfers between devices: 3.79 us -> 4.62 us  [crossed(): lax.ppermute(value, 'grp', [(source, source ^ step) for source in range(c...]
    ppermute x9, starting transfers between devices: 4.67 us -> 4.29 us  [crossed(): lax.ppermute(value, 'grp', [(source, source ^ step) for source in range(c...]
  transfers between devices with their start and end apart: 13 -> 13, of which waited for: 6 -> 7; matrix products, arithmetic and copies ran while one was open for 0% -> 0% of each run, Pallas kernels for 31% -> 30%
where the time goes in v12:
time: 34.6 us; the launch traced here: 34.4 us
  starting transfers between devices  14.4 us (42%)
  Pallas kernels  13.3 us (38%)
  waiting for transfers between devices  5.31 us (15%)
  between operations  1.4 us (4%)
    ppermute x3, starting transfers between devices, delivered(): return lax.ppermute(value, ('grp', 'blk'), pairs)  7.09 us
    pallas_call x1, Pallas kernels, error_step(): pl.pallas_call(functools.partial(error_kernel, rows), out_shape=(jax.Shap...  4.84 us
    ppermute x9, waiting for transfers between devices, crossed(): lax.ppermute(value, 'grp', [(source, source ^ step) for source in range(c...  4.62 us
    ppermute x9, starting transfers between devices, crossed(): lax.ppermute(value, 'grp', [(source, source ^ step) for source in range(c...  4.29 us
    pallas_call x2, Pallas kernels, factor_step(): pl.pallas_call(functools.partial(factor_kernel, begin, rows, chunks), out...  3.31 us
    ppermute x1, starting transfers between devices, shifted(): lax.ppermute(value, 'blk', [(source, (source + steps) % count) for source...  3.02 us
    pallas_call x2, Pallas kernels, place(): pl.pallas_call(functools.partial(place_kernel, share, spots), out_shape=(...  1.67 us
    pallas_call x1, Pallas kernels, prepare(): pl.pallas_call(functools.partial(prepare_kernel, rows), out_shape=(jax.Sh...  1.39 us
  transfers between devices with their start and end apart: 13, of which 7 were waited for; matrix products, arithmetic and copies ran while one was open for 0% of the time, Pallas kernels for 30%

profile of v12, /device:TPU:0, one launch (start us, length us, event | category | flops | bytes accessed | tf_op | source)
XLA Modules:
  0.0 34.4 jit_solution(4636348902506887103)
XLA Ops:
  0.6 1.4 %prepare.1 = (f32[168,256]{1,0:T(8,128)S(1)}, f32[256,256]{1,0:T(8,128)S(1)}, f32[256,256]{1,0:T(8,128)S(1)}, bf16[1024,512]{1,0:T(8,128)(2,1)S(1)}, s32[32,1024]{1,0:T(8,128)S(1)}) custom-call(f32[1,256,256]{2,1,0:T(8,128)} %x_hbm.1, bf16[6144,256]{1,0:T(8,128)(2,1)} %obs_hbm.3, s32[32,6144]{1,0:T(8,128)} %bitcast.3, bf16[6144,256]{1,0:T(8,128)(2,1)} %f_hbm.3), custom_call_target="tpu_custom_call" | custom-call | bytes 3145728 | tf_op jit(solution)/shard_map/prepare/pallas_call | solution.py:90
  2.0 3.0 %collective-permute-start = (f32[168,256]{1,0:T(8,128)S(1)}, f32[168,256]{1,0:T(8,128)S(1)}, u32[]{:S(2)}, u32[]{:S(2)}) collective-permute-start(f32[168,256]{1,0:T(8,128)S(1)} %get-tuple-element.35), channel_id=1, source_target_pairs={{0,1},{1,2},{2,3},{3,4},{4,5},{5,6},{6,7},{7,0},{8,9},{9,10},{10,1... | collective-permute-start | bytes 516104 | tf_op jit(solution)/shard_map/ppermute | solution.py:463
  5.7 0.0 copy-start
  5.7 4.8 %errors.1 = (bf16[256,6144]{1,0:T(8,128)(2,1)S(1)}, bf16[5120,512]{1,0:T(8,128)(2,1)S(1)}, f32[256,256]{1,0:T(8,128)S(1)}) custom-call(bf16[6144,256]{1,0:T(8,128)(2,1)} %obs_hbm.3, s32[32,6144]{1,0:T(8,128)} %bitcast.4, bf16[6144,256]{1,0:T(8,128)(2,1)} %f_hbm.3, f32[256,256]{1,0:T(8,128)S(1)} %get-tuple-element.36.turned_ref, ...), custom_call_target="tpu_custom_call" | custom-call | flops 3221225472 | bytes 10223616 | tf_op jit(solution)/shard_map/errors/pallas_call | solution.py:184
  10.6 0.0 copy-done
  10.6 1.2 %regress.1 = (f32[256,256]{1,0:T(8,128)S(1)}, f32[256,256]{1,0:T(8,128)S(1)}, f32[256,256]{1,0:T(8,128)S(1)}) custom-call(f32[256,256]{1,0:T(8,128)S(1)} %get-tuple-element.36.turned_ref, f32[25,256]{1,0:T(8,128)S(1)} %copy-done, f32[256,256]{1,0:T(8,128)S(1)} %get-tuple-element.39.gd_ref, f32[1,256,256]{2,1,0:T(8,128)} %m_hbm.1, f32[1,256,256]{2,1,0:T(8,128)} %v_hbm.1), custom_call_target="tpu_custom_call" | custom-call | flops 6553600 | bytes 1572864 | tf_op jit(solution)/shard_map/regress/pallas_call | solution.py:281
  11.8 0.7 %collective-permute-done.halo_ref = f32[168,256]{1,0:T(8,128)S(1)} collective-permute-done((f32[168,256]{1,0:T(8,128)S(1)}, f32[168,256]{1,0:T(8,128)S(1)}, u32[]{:S(2)}, u32[]{:S(2)}) %collective-permute-start) | collective-permute-done | bytes 172064 | tf_op jit(solution)/shard_map/ppermute | solution.py:463
  12.5 0.8 %update.1 = (f32[3,2,32,256]{3,2,1,0:T(8,128)S(1)}, f32[3,2,32,256]{3,2,1,0:T(8,128)S(1)}, f32[3,2,32,256]{3,2,1,0:T(8,128)S(1)}, f32[3,2,32,256]{3,2,1,0:T(8,128)S(1)}) custom-call(s32[1,1]{1,0:T(1,128)} %bitcast.2.stratum_ref, f32[168,256]{1,0:T(8,128)S(1)} %collective-permute-done.halo_ref, f32[25,256]{1,0:T(8,128)S(1)} %copy-done, ...), custom_call_target="tpu_custom_call" | custom-call | flops 3932160 | bytes 2621440 | tf_op jit(solution)/shard_map/update/pallas_call | solution.py:361
  13.2 0.1 collective-permute-start.1
  13.3 1.4 %collective-permute-done.1.got_ref = f32[3,2,32,256]{3,2,1,0:T(8,128)S(1)} collective-permute-done((f32[3,2,32,256]{3,2,1,0:T(8,128)S(1)}, f32[3,2,32,256]{3,2,1,0:T(8,128)S(1)}, u32[]{:S(2)}, u32[]{:S(2)}) %collective-permute-start.1) | collective-permute-done | bytes 196640 | tf_op jit(solution)/shard_map/ppermute | solution.py:458
  14.8 0.2 collective-permute-start.2
  15.0 1.5 %collective-permute-start.5 = (f32[3,1,32,256]{3,2,1,0:T(8,128)S(1)}, f32[3,1,32,256]{3,2,1,0:T(8,128)S(1)}, u32[]{:S(2)}, u32[]{:S(2)}) collective-permute-start(f32[3,1,32,256]{3,2,1,0:T(8,128)S(1)} %get-tuple-element.52.rest_0_), channel_id=1, source_target_pairs={{0,16},{8,24},{16,0},{24,8},{1,17},{9,25},{17,1},{25,9},{2,18},{10... | collective-permute-start | bytes 294920 | tf_op jit(solution)/shard_map/ppermute | solution.py:458
  16.5 1.5 %factors.2.rest_1_ = bf16[6144,256]{1,0:T(8,128)(2,1)} custom-call(bf16[1024,512]{1,0:T(8,128)(2,1)S(1)} %get-tuple-element.37.first_ref, bf16[5120,512]{1,0:T(8,128)(2,1)S(1)} %get-tuple-element.50.both_ref, bf16[256,6144]{1,0:T(8,128)(2,1)S(1)} %get-tuple-element.51.err_ref, f32[256,256]{1,0:T(8,128)S(1)} %get-tuple-element.36.turned_ref, ...), custom_call_target="tpu_custom_call" | custom-call | flops 268435456 | bytes 3145728 | tf_op jit(solution)/shard_map/factors/pallas_call | solution.py:238
  18.0 0.0 collective-permute-done.2.got_ref
  18.0 0.6 %collective-permute-start.3 = (f32[3,1,32,256]{3,2,1,0:T(8,128)S(1)}, f32[3,1,32,256]{3,2,1,0:T(8,128)S(1)}, u32[]{:S(2)}, u32[]{:S(2)}) collective-permute-start(f32[3,1,32,256]{3,2,1,0:T(8,128)S(1)} %get-tuple-element.55), channel_id=1, source_target_pairs={{0,16},{8,24},{16,0},{24,8},{1,17},{9,25},{17,1},{25,9},{2,18},{10... | collective-permute-start | bytes 294920 | tf_op jit(solution)/shard_map/ppermute | solution.py:458
  18.6 1.4 %collective-permute-done.5.got_ref = f32[3,1,32,256]{3,2,1,0:T(8,128)S(1)} collective-permute-done((f32[3,1,32,256]{3,2,1,0:T(8,128)S(1)}, f32[3,1,32,256]{3,2,1,0:T(8,128)S(1)}, u32[]{:S(2)}, u32[]{:S(2)}) %collective-permute-start.5) | collective-permute-done | bytes 98336 | tf_op jit(solution)/shard_map/ppermute | solution.py:458
  20.1 2.4 %collective-permute-start.6 = (f32[3,32,256]{2,1,0:T(8,128)S(1)}, f32[3,32,256]{2,1,0:T(8,128)S(1)}, u32[]{:S(2)}, u32[]{:S(2)}) collective-permute-start(f32[3,32,256]{2,1,0:T(8,128)S(1)} %mean.3), channel_id=1, source_target_pairs={{0,7},{1,0},{2,1},{3,2},{4,3},{5,4},{6,5},{7,6},{8,15},{9,8},{10,9... | collective-permute-start | bytes 294920 | tf_op jit(solution)/shard_map/ppermute | solution.py:473
  22.5 0.4 %collective-permute-done.3.got_ref = f32[3,1,32,256]{3,2,1,0:T(8,128)S(1)} collective-permute-done((f32[3,1,32,256]{3,2,1,0:T(8,128)S(1)}, f32[3,1,32,256]{3,2,1,0:T(8,128)S(1)}, u32[]{:S(2)}, u32[]{:S(2)}) %collective-permute-start.3) | collective-permute-done | bytes 98336 | tf_op jit(solution)/shard_map/ppermute | solution.py:458
  22.9 2.6 %collective-permute-start.4 = (f32[3,32,256]{2,1,0:T(8,128)S(1)}, f32[3,32,256]{2,1,0:T(8,128)S(1)}, u32[]{:S(2)}, u32[]{:S(2)}) collective-permute-start(f32[3,32,256]{2,1,0:T(8,128)S(1)} %mean.2), channel_id=1, source_target_pairs={{0,7},{1,0},{2,1},{3,2},{4,3},{5,4},{6,5},{7,6},{8,15},{9,8},{10,9... | collective-permute-start | bytes 294920 | tf_op jit(solution)/shard_map/ppermute | solution.py:473
  25.5 2.1 %collective-permute-start.11 = (f32[3,32,256]{2,1,0:T(8,128)S(1)}, f32[3,32,256]{2,1,0:T(8,128)S(1)}, u32[]{:S(2)}, u32[]{:S(2)}) collective-permute-start(f32[3,32,256]{2,1,0:T(8,128)S(1)} %mean.2), channel_id=1, source_target_pairs={{0,23},{1,16},{2,17},{3,18},{4,19},{5,20},{6,21},{7,22},{8,31},{9,... | collective-permute-start | bytes 294920 | tf_op jit(solution)/shard_map/ppermute | solution.py:473
  27.5 0.0 collective-permute-done.6.rest_0_
  27.5 1.2 %collective-permute-start.7 = (f32[3,32,256]{2,1,0:T(8,128)S(1)}, f32[3,32,256]{2,1,0:T(8,128)S(1)}, u32[]{:S(2)}, u32[]{:S(2)}) collective-permute-start(f32[3,32,256]{2,1,0:T(8,128)S(1)} %collective-permute-done.6.rest_0_), channel_id=1, source_target_pairs={{0,16},{8,24},{16,0},{24,8},{1,17},{9,25},{17,1},{25,9},{2,18},{10... | collective-permute-start | bytes 294920 | tf_op jit(solution)/shard_map/ppermute | solution.py:458
  28.8 0.0 collective-permute-start.9
  28.8 1.9 %factors.3 = bf16[6144,256]{1,0:T(8,128)(2,1)} custom-call(bf16[1024,512]{1,0:T(8,128)(2,1)S(1)} %get-tuple-element.37.first_ref, bf16[5120,512]{1,0:T(8,128)(2,1)S(1)} %get-tuple-element.50.both_ref, bf16[256,6144]{1,0:T(8,128)(2,1)S(1)} %get-tuple-element.51.err_ref, f32[256,256]{1,0:T(8,128)S(1)} %get-tuple-element.36.turned_ref, ...), custom_call_target="tpu_custom_call", output_to_operand_aliasing={{}: (5, {})} | custom-call | flops 536870912 | bytes 6291456 | tf_op jit(solution)/shard_map/factors/pallas_call | solution.py:238
  30.6 0.0 collective-permute-done.4.rest_3_
  30.7 0.6 %collective-permute-start.10 = (f32[3,32,256]{2,1,0:T(8,128)S(1)}, f32[3,32,256]{2,1,0:T(8,128)S(1)}, u32[]{:S(2)}, u32[]{:S(2)}) collective-permute-start(f32[3,32,256]{2,1,0:T(8,128)S(1)} %collective-permute-done.4.rest_3_), channel_id=1, source_target_pairs={{0,8},{8,0},{16,24},{24,16},{1,9},{9,1},{17,25},{25,17},{2,10},{10... | collective-permute-start | bytes 294920 | tf_op jit(solution)/shard_map/ppermute | solution.py:458
  31.2 0.0 collective-permute-done.11.rest_5_
  31.2 0.1 collective-permute-start.12
  31.3 1.1 %collective-permute-done.7.rest_2_ = f32[3,32,256]{2,1,0:T(8,128)S(1)} collective-permute-done((f32[3,32,256]{2,1,0:T(8,128)S(1)}, f32[3,32,256]{2,1,0:T(8,128)S(1)}, u32[]{:S(2)}, u32[]{:S(2)}) %collective-permute-start.7) | collective-permute-done | bytes 98336 | tf_op jit(solution)/shard_map/ppermute | solution.py:458
  32.4 0.0 collective-permute-start.8
  32.4 0.0 collective-permute-done.9.rest_1_
  32.4 0.0 collective-permute-done.10.rest_4_
  32.4 0.1 collective-permute-done.12.rest_6_
  32.5 1.0 %place.2 = (f32[1,256,256]{2,1,0:T(8,128)}, f32[1,256,256]{2,1,0:T(8,128)}, f32[1,256,256]{2,1,0:T(8,128)}) custom-call(f32[3,32,256]{2,1,0:T(8,128)S(1)} %collective-permute-done.6.rest_0_, f32[3,32,256]{2,1,0:T(8,128)S(1)} %collective-permute-done.9.rest_1_, f32[3,32,256]{2,1,0:T(8,128)S(1)} %collective-permute-done.7.rest_2_, ...), custom_call_target="tpu_custom_call" | custom-call | bytes 4128768 | tf_op jit(solution)/shard_map/place/pallas_call | solution.py:443
  33.6 0.2 collective-permute-done.8.rest_0_
  33.7 0.7 %place.3 = (f32[1,256,256]{2,1,0:T(8,128)}, f32[1,256,256]{2,1,0:T(8,128)}, f32[1,256,256]{2,1,0:T(8,128)}) custom-call(f32[3,32,256]{2,1,0:T(8,128)S(1)} %collective-permute-done.8.rest_0_, f32[1,256,256]{2,1,0:T(8,128)} %get-tuple-element.60.rest_1_, ...), custom_call_target="tpu_custom_call", output_to_operand_aliasing={{0}: (1, {}), {1}: (2, {}), {2}: (3, {})} | custom-call | bytes 589824 | tf_op jit(solution)/shard_map/place/pallas_call | solution.py:443
  (4 shorter events, 0.1 us)
Async XLA Ops:
  2.0 10.4 %collective-permute-start = (f32[168,256]{1,0:T(8,128)S(1)}, f32[168,256]{1,0:T(8,128)S(1)}, u32[]{:S(2)}, u32[]{:S(2)}) collective-permute-start(f32[168,256]{1,0:T(8,128)S(1)} %get-tuple-element.35), channel_id=1, source_target_pairs={{0,1},{1,2},{2,3},{3,4},{4,5},{5,6},{6,7},{7,0},{8,9},{9,10},{10,1... | collective-permute-start | bytes 516104 | tf_op jit(solution)/shard_map/ppermute | solution.py:463
  5.7 4.9 %copy-start = (f32[25,256]{1,0:T(8,128)S(1)}, f32[25,256]{1,0:T(8,128)}, u32[]{:S(2)}) copy-start(f32[25,256]{1,0:T(8,128)} %w_ref.3) | copy-start | bytes 76804
  13.2 1.5 %collective-permute-start.1 = (f32[3,2,32,256]{3,2,1,0:T(8,128)S(1)}, f32[3,2,32,256]{3,2,1,0:T(8,128)S(1)}, u32[]{:S(2)}, u32[]{:S(2)}) collective-permute-start(f32[3,2,32,256]{3,2,1,0:T(8,128)S(1)} %get-tuple-element.47), channel_id=1, source_target_pairs={{0,8},{8,0},{16,24},{24,16},{1,9},{9,1},{17,25},{25,17},{2,10},{10... | collective-permute-start | bytes 589832 | tf_op jit(solution)/shard_map/ppermute | solution.py:458
  14.8 3.2 %collective-permute-start.2 = (f32[3,2,32,256]{3,2,1,0:T(8,128)S(1)}, f32[3,2,32,256]{3,2,1,0:T(8,128)S(1)}, u32[]{:S(2)}, u32[]{:S(2)}) collective-permute-start(f32[3,2,32,256]{3,2,1,0:T(8,128)S(1)} %get-tuple-element.49), channel_id=1, source_target_pairs={{0,8},{8,0},{16,24},{24,16},{1,9},{9,1},{17,25},{25,17},{2,10},{10... | collective-permute-start | bytes 589832 | tf_op jit(solution)/shard_map/ppermute | solution.py:458
  15.0 5.1 %collective-permute-start.5 = (f32[3,1,32,256]{3,2,1,0:T(8,128)S(1)}, f32[3,1,32,256]{3,2,1,0:T(8,128)S(1)}, u32[]{:S(2)}, u32[]{:S(2)}) collective-permute-start(f32[3,1,32,256]{3,2,1,0:T(8,128)S(1)} %get-tuple-element.52.rest_0_), channel_id=1, source_target_pairs={{0,16},{8,24},{16,0},{24,8},{1,17},{9,25},{17,1},{25,9},{2,18},{10... | collective-permute-start | bytes 294920 | tf_op jit(solution)/shard_map/ppermute | solution.py:458
  18.0 4.8 %collective-permute-start.3 = (f32[3,1,32,256]{3,2,1,0:T(8,128)S(1)}, f32[3,1,32,256]{3,2,1,0:T(8,128)S(1)}, u32[]{:S(2)}, u32[]{:S(2)}) collective-permute-start(f32[3,1,32,256]{3,2,1,0:T(8,128)S(1)} %get-tuple-element.55), channel_id=1, source_target_pairs={{0,16},{8,24},{16,0},{24,8},{1,17},{9,25},{17,1},{25,9},{2,18},{10... | collective-permute-start | bytes 294920 | tf_op jit(solution)/shard_map/ppermute | solution.py:458
  20.1 7.5 %collective-permute-start.6 = (f32[3,32,256]{2,1,0:T(8,128)S(1)}, f32[3,32,256]{2,1,0:T(8,128)S(1)}, u32[]{:S(2)}, u32[]{:S(2)}) collective-permute-start(f32[3,32,256]{2,1,0:T(8,128)S(1)} %mean.3), channel_id=1, source_target_pairs={{0,7},{1,0},{2,1},{3,2},{4,3},{5,4},{6,5},{7,6},{8,15},{9,8},{10,9... | collective-permute-start | bytes 294920 | tf_op jit(solution)/shard_map/ppermute | solution.py:473
  22.9 7.8 %collective-permute-start.4 = (f32[3,32,256]{2,1,0:T(8,128)S(1)}, f32[3,32,256]{2,1,0:T(8,128)S(1)}, u32[]{:S(2)}, u32[]{:S(2)}) collective-permute-start(f32[3,32,256]{2,1,0:T(8,128)S(1)} %mean.2), channel_id=1, source_target_pairs={{0,7},{1,0},{2,1},{3,2},{4,3},{5,4},{6,5},{7,6},{8,15},{9,8},{10,9... | collective-permute-start | bytes 294920 | tf_op jit(solution)/shard_map/ppermute | solution.py:473
  25.5 5.8 %collective-permute-start.11 = (f32[3,32,256]{2,1,0:T(8,128)S(1)}, f32[3,32,256]{2,1,0:T(8,128)S(1)}, u32[]{:S(2)}, u32[]{:S(2)}) collective-permute-start(f32[3,32,256]{2,1,0:T(8,128)S(1)} %mean.2), channel_id=1, source_target_pairs={{0,23},{1,16},{2,17},{3,18},{4,19},{5,20},{6,21},{7,22},{8,31},{9,... | collective-permute-start | bytes 294920 | tf_op jit(solution)/shard_map/ppermute | solution.py:473
  27.5 4.9 %collective-permute-start.7 = (f32[3,32,256]{2,1,0:T(8,128)S(1)}, f32[3,32,256]{2,1,0:T(8,128)S(1)}, u32[]{:S(2)}, u32[]{:S(2)}) collective-permute-start(f32[3,32,256]{2,1,0:T(8,128)S(1)} %collective-permute-done.6.rest_0_), channel_id=1, source_target_pairs={{0,16},{8,24},{16,0},{24,8},{1,17},{9,25},{17,1},{25,9},{2,18},{10... | collective-permute-start | bytes 294920 | tf_op jit(solution)/shard_map/ppermute | solution.py:458
  28.8 3.7 %collective-permute-start.9 = (f32[3,32,256]{2,1,0:T(8,128)S(1)}, f32[3,32,256]{2,1,0:T(8,128)S(1)}, u32[]{:S(2)}, u32[]{:S(2)}) collective-permute-start(f32[3,32,256]{2,1,0:T(8,128)S(1)} %collective-permute-done.6.rest_0_), channel_id=1, source_target_pairs={{0,8},{8,0},{16,24},{24,16},{1,9},{9,1},{17,25},{25,17},{2,10},{10... | collective-permute-start | bytes 294920 | tf_op jit(solution)/shard_map/ppermute | solution.py:458
  30.7 1.8 %collective-permute-start.10 = (f32[3,32,256]{2,1,0:T(8,128)S(1)}, f32[3,32,256]{2,1,0:T(8,128)S(1)}, u32[]{:S(2)}, u32[]{:S(2)}) collective-permute-start(f32[3,32,256]{2,1,0:T(8,128)S(1)} %collective-permute-done.4.rest_3_), channel_id=1, source_target_pairs={{0,8},{8,0},{16,24},{24,16},{1,9},{9,1},{17,25},{25,17},{2,10},{10... | collective-permute-start | bytes 294920 | tf_op jit(solution)/shard_map/ppermute | solution.py:458
  31.2 1.3 %collective-permute-start.12 = (f32[3,32,256]{2,1,0:T(8,128)S(1)}, f32[3,32,256]{2,1,0:T(8,128)S(1)}, u32[]{:S(2)}, u32[]{:S(2)}) collective-permute-start(f32[3,32,256]{2,1,0:T(8,128)S(1)} %collective-permute-done.11.rest_5_), channel_id=1, source_target_pairs={{0,8},{8,0},{16,24},{24,16},{1,9},{9,1},{17,25},{25,17},{2,10},{10... | collective-permute-start | bytes 294920 | tf_op jit(solution)/shard_map/ppermute | solution.py:458
  32.4 1.3 %collective-permute-start.8 = (f32[3,32,256]{2,1,0:T(8,128)S(1)}, f32[3,32,256]{2,1,0:T(8,128)S(1)}, u32[]{:S(2)}, u32[]{:S(2)}) collective-permute-start(f32[3,32,256]{2,1,0:T(8,128)S(1)} %collective-permute-done.7.rest_2_), channel_id=1, source_target_pairs={{0,8},{8,0},{16,24},{24,16},{1,9},{9,1},{17,25},{25,17},{2,10},{10... | collective-permute-start | bytes 294920 | tf_op jit(solution)/shard_map/ppermute | solution.py:458

commit v13 on v10

--- a/solution.py
+++ b/solution.py
@@ -476,7 +476,7 @@
 def body(obs, mask_bits, factors, x_blocks, first_moment, second_moment, ar_weights, stratum):
     count = lax.axis_size("grp")
     series = obs.shape[0]
-    rows = rows_of(series, 1024)
+    rows = rows_of(series, 768)
     third = max(series // rows // 3, 1) * rows
     bits = mask_bits.T
 

time: 34.1 us -> 34.5 us (1.012)
  starting transfers between devices: 14.7 us -> 15.3 us
  waiting for transfers between devices: 4.49 us -> 4.11 us
    ppermute x3, starting transfers between devices: 7.03 us -> 7.81 us  [delivered(): return lax.ppermute(value, ('grp', 'blk'), pairs)]
    ppermute x1, waiting for transfers between devices: 0.69 us -> 0.34 us  [shifted(): lax.ppermute(value, 'blk', [(source, (source + steps) % count) for source...]
    pallas_call x1, Pallas kernels: 4.84 us -> 5.18 us  [error_step(): pl.pallas_call(functools.partial(error_kernel, rows), out_shape=(jax.Shap...]
  transfers between devices with their start and end apart: 13 -> 13, of which waited for: 6 -> 5; matrix products, arithmetic and copies ran while one was open for 0% -> 0% of each run, Pallas kernels for 31% -> 31%
where the time goes in v13:
time: 34.5 us; the launch traced here: 34.3 us
  starting transfers between devices  15.3 us (44%)
  Pallas kernels  13.5 us (39%)
  waiting for transfers between devices  4.11 us (12%)
  between operations  1.4 us (4%)
    ppermute x3, starting transfers between devices, delivered(): return lax.ppermute(value, ('grp', 'blk'), pairs)  7.81 us
    pallas_call x1, Pallas kernels, error_step(): pl.pallas_call(functools.partial(error_kernel, rows), out_shape=(jax.Shap...  5.18 us
    ppermute x9, starting transfers between devices, crossed(): lax.ppermute(value, 'grp', [(source, source ^ step) for source in range(c...  4.51 us
    ppermute x9, waiting for transfers between devices, crossed(): lax.ppermute(value, 'grp', [(source, source ^ step) for source in range(c...  3.77 us
    pallas_call x2, Pallas kernels, factor_step(): pl.pallas_call(functools.partial(factor_kernel, begin, rows, chunks), out...  3.22 us
    ppermute x1, starting transfers between devices, shifted(): lax.ppermute(value, 'blk', [(source, (source + steps) % count) for source...  3.02 us
    pallas_call x2, Pallas kernels, place(): pl.pallas_call(functools.partial(place_kernel, share, spots), out_shape=(...  1.68 us
    pallas_call x1, Pallas kernels, prepare(): pl.pallas_call(functools.partial(prepare_kernel, rows), out_shape=(jax.Sh...  1.3 us
  transfers between devices with their start and end apart: 13, of which 5 were waited for; matrix products, arithmetic and copies ran while one was open for 0% of the time, Pallas kernels for 31%

profile of v13, /device:TPU:0, one launch (start us, length us, event | category | flops | bytes accessed | tf_op | source)
XLA Modules:
  0.0 34.3 jit_solution(18002132258714828994)
XLA Ops:
  0.6 1.3 %prepare.1 = (f32[168,256]{1,0:T(8,128)S(1)}, f32[256,256]{1,0:T(8,128)S(1)}, f32[256,256]{1,0:T(8,128)S(1)}, bf16[768,512]{1,0:T(8,128)(2,1)S(1)}, s32[32,768]{1,0:T(8,128)S(1)}) custom-call(f32[1,256,256]{2,1,0:T(8,128)} %x_hbm.1, bf16[6144,256]{1,0:T(8,128)(2,1)} %obs_hbm.3, s32[32,6144]{1,0:T(8,128)} %bitcast.3, bf16[6144,256]{1,0:T(8,128)(2,1)} %f_hbm.3), custom_call_target="tpu_custom_call" | custom-call | bytes 2621440 | tf_op jit(solution)/shard_map/prepare/pallas_call | solution.py:90
  1.9 3.0 %collective-permute-start = (f32[168,256]{1,0:T(8,128)S(1)}, f32[168,256]{1,0:T(8,128)S(1)}, u32[]{:S(2)}, u32[]{:S(2)}) collective-permute-start(f32[168,256]{1,0:T(8,128)S(1)} %get-tuple-element.33), channel_id=1, source_target_pairs={{0,1},{1,2},{2,3},{3,4},{4,5},{5,6},{6,7},{7,0},{8,9},{9,10},{10,1... | collective-permute-start | bytes 516104 | tf_op jit(solution)/shard_map/ppermute | solution.py:463
  5.6 0.0 copy-start
  5.6 5.2 %errors.1 = (bf16[256,6144]{1,0:T(8,128)(2,1)S(1)}, bf16[5376,512]{1,0:T(8,128)(2,1)S(1)}, f32[256,256]{1,0:T(8,128)S(1)}) custom-call(bf16[6144,256]{1,0:T(8,128)(2,1)} %obs_hbm.3, s32[32,6144]{1,0:T(8,128)} %bitcast.4, bf16[6144,256]{1,0:T(8,128)(2,1)} %f_hbm.3, f32[256,256]{1,0:T(8,128)S(1)} %get-tuple-element.34.turned_ref, ...), custom_call_target="tpu_custom_call" | custom-call | flops 3221225472 | bytes 10223616 | tf_op jit(solution)/shard_map/errors/pallas_call | solution.py:184
  10.8 0.0 copy-done
  10.8 1.2 %regress.1 = (f32[256,256]{1,0:T(8,128)S(1)}, f32[256,256]{1,0:T(8,128)S(1)}, f32[256,256]{1,0:T(8,128)S(1)}) custom-call(f32[256,256]{1,0:T(8,128)S(1)} %get-tuple-element.34.turned_ref, f32[25,256]{1,0:T(8,128)S(1)} %copy-done, f32[256,256]{1,0:T(8,128)S(1)} %get-tuple-element.37.gd_ref, f32[1,256,256]{2,1,0:T(8,128)} %m_hbm.1, f32[1,256,256]{2,1,0:T(8,128)} %v_hbm.1), custom_call_target="tpu_custom_call" | custom-call | flops 6553600 | bytes 1572864 | tf_op jit(solution)/shard_map/regress/pallas_call | solution.py:281
  12.0 0.3 collective-permute-done.halo_ref
  12.4 0.8 %update.1 = (f32[3,2,32,256]{3,2,1,0:T(8,128)S(1)}, f32[3,2,32,256]{3,2,1,0:T(8,128)S(1)}, f32[3,2,32,256]{3,2,1,0:T(8,128)S(1)}, f32[3,2,32,256]{3,2,1,0:T(8,128)S(1)}) custom-call(s32[1,1]{1,0:T(1,128)} %bitcast.2.stratum_ref, f32[168,256]{1,0:T(8,128)S(1)} %collective-permute-done.halo_ref, f32[25,256]{1,0:T(8,128)S(1)} %copy-done, ...), custom_call_target="tpu_custom_call" | custom-call | flops 3932160 | bytes 2621440 | tf_op jit(solution)/shard_map/update/pallas_call | solution.py:361
  13.2 0.1 collective-permute-start.2
  13.2 0.5 %collective-permute-start.1 = (f32[3,2,32,256]{3,2,1,0:T(8,128)S(1)}, f32[3,2,32,256]{3,2,1,0:T(8,128)S(1)}, u32[]{:S(2)}, u32[]{:S(2)}) collective-permute-start(f32[3,2,32,256]{3,2,1,0:T(8,128)S(1)} %get-tuple-element.43), channel_id=1, source_target_pairs={{0,8},{8,0},{16,24},{24,16},{1,9},{9,1},{17,25},{25,17},{2,10},{10... | collective-permute-start | bytes 589832 | tf_op jit(solution)/shard_map/ppermute | solution.py:458
  13.7 0.9 %collective-permute-done.2.got_ref = f32[3,2,32,256]{3,2,1,0:T(8,128)S(1)} collective-permute-done((f32[3,2,32,256]{3,2,1,0:T(8,128)S(1)}, f32[3,2,32,256]{3,2,1,0:T(8,128)S(1)}, u32[]{:S(2)}, u32[]{:S(2)}) %collective-permute-start.2) | collective-permute-done | bytes 196640 | tf_op jit(solution)/shard_map/ppermute | solution.py:458
  14.7 1.6 %collective-permute-start.5 = (f32[3,1,32,256]{3,2,1,0:T(8,128)S(1)}, f32[3,1,32,256]{3,2,1,0:T(8,128)S(1)}, u32[]{:S(2)}, u32[]{:S(2)}) collective-permute-start(f32[3,1,32,256]{3,2,1,0:T(8,128)S(1)} %get-tuple-element.48.rest_0_), channel_id=1, source_target_pairs={{0,16},{8,24},{16,0},{24,8},{1,17},{9,25},{17,1},{25,9},{2,18},{10... | collective-permute-start | bytes 294920 | tf_op jit(solution)/shard_map/ppermute | solution.py:458
  16.2 1.3 %factors.2.rest_1_ = bf16[6144,256]{1,0:T(8,128)(2,1)} custom-call(bf16[768,512]{1,0:T(8,128)(2,1)S(1)} %get-tuple-element.35.first_ref, bf16[5376,512]{1,0:T(8,128)(2,1)S(1)} %get-tuple-element.44.both_ref, bf16[256,6144]{1,0:T(8,128)(2,1)S(1)} %get-tuple-element.45.err_ref, f32[256,256]{1,0:T(8,128)S(1)} %get-tuple-element.34.turned_ref, ...), custom_call_target="tpu_custom_call" | custom-call | flops 201326592 | bytes 2359296 | tf_op jit(solution)/shard_map/factors/pallas_call | solution.py:238
  17.6 0.0 collective-permute-done.1.got_ref
  17.6 0.6 %collective-permute-start.3 = (f32[3,1,32,256]{3,2,1,0:T(8,128)S(1)}, f32[3,1,32,256]{3,2,1,0:T(8,128)S(1)}, u32[]{:S(2)}, u32[]{:S(2)}) collective-permute-start(f32[3,1,32,256]{3,2,1,0:T(8,128)S(1)} %get-tuple-element.51), channel_id=1, source_target_pairs={{0,16},{8,24},{16,0},{24,8},{1,17},{9,25},{17,1},{25,9},{2,18},{10... | collective-permute-start | bytes 294920 | tf_op jit(solution)/shard_map/ppermute | solution.py:458
  18.2 1.4 %collective-permute-done.5.got_ref = f32[3,1,32,256]{3,2,1,0:T(8,128)S(1)} collective-permute-done((f32[3,1,32,256]{3,2,1,0:T(8,128)S(1)}, f32[3,1,32,256]{3,2,1,0:T(8,128)S(1)}, u32[]{:S(2)}, u32[]{:S(2)}) %collective-permute-start.5) | collective-permute-done | bytes 98336 | tf_op jit(solution)/shard_map/ppermute | solution.py:458
  19.6 2.8 %collective-permute-start.6 = (f32[3,32,256]{2,1,0:T(8,128)S(1)}, f32[3,32,256]{2,1,0:T(8,128)S(1)}, u32[]{:S(2)}, u32[]{:S(2)}) collective-permute-start(f32[3,32,256]{2,1,0:T(8,128)S(1)} %mean.3), channel_id=1, source_target_pairs={{0,7},{1,0},{2,1},{3,2},{4,3},{5,4},{6,5},{7,6},{8,15},{9,8},{10,9... | collective-permute-start | bytes 294920 | tf_op jit(solution)/shard_map/ppermute | solution.py:473
  22.4 0.0 collective-permute-done.3.got_ref
  22.4 2.8 %collective-permute-start.4 = (f32[3,32,256]{2,1,0:T(8,128)S(1)}, f32[3,32,256]{2,1,0:T(8,128)S(1)}, u32[]{:S(2)}, u32[]{:S(2)}) collective-permute-start(f32[3,32,256]{2,1,0:T(8,128)S(1)} %mean.2), channel_id=1, source_target_pairs={{0,7},{1,0},{2,1},{3,2},{4,3},{5,4},{6,5},{7,6},{8,15},{9,8},{10,9... | collective-permute-start | bytes 294920 | tf_op jit(solution)/shard_map/ppermute | solution.py:473
  25.3 2.2 %collective-permute-start.11 = (f32[3,32,256]{2,1,0:T(8,128)S(1)}, f32[3,32,256]{2,1,0:T(8,128)S(1)}, u32[]{:S(2)}, u32[]{:S(2)}) collective-permute-start(f32[3,32,256]{2,1,0:T(8,128)S(1)} %mean.2), channel_id=1, source_target_pairs={{0,23},{1,16},{2,17},{3,18},{4,19},{5,20},{6,21},{7,22},{8,31},{9,... | collective-permute-start | bytes 294920 | tf_op jit(solution)/shard_map/ppermute | solution.py:473
  27.4 0.0 collective-permute-done.6.rest_0_
  27.4 1.1 %collective-permute-start.7 = (f32[3,32,256]{2,1,0:T(8,128)S(1)}, f32[3,32,256]{2,1,0:T(8,128)S(1)}, u32[]{:S(2)}, u32[]{:S(2)}) collective-permute-start(f32[3,32,256]{2,1,0:T(8,128)S(1)} %collective-permute-done.6.rest_0_), channel_id=1, source_target_pairs={{0,16},{8,24},{16,0},{24,8},{1,17},{9,25},{17,1},{25,9},{2,18},{10... | collective-permute-start | bytes 294920 | tf_op jit(solution)/shard_map/ppermute | solution.py:458
  28.6 1.9 %factors.3 = bf16[6144,256]{1,0:T(8,128)(2,1)} custom-call(bf16[768,512]{1,0:T(8,128)(2,1)S(1)} %get-tuple-element.35.first_ref, bf16[5376,512]{1,0:T(8,128)(2,1)S(1)} %get-tuple-element.44.both_ref, bf16[256,6144]{1,0:T(8,128)(2,1)S(1)} %get-tuple-element.45.err_ref, f32[256,256]{1,0:T(8,128)S(1)} %get-tuple-element.34.turned_ref, ...), custom_call_target="tpu_custom_call", output_to_operand_aliasing={{}: (5, {})} | custom-call | flops 603979776 | bytes 7077888 | tf_op jit(solution)/shard_map/factors/pallas_call | solution.py:238
  30.5 0.0 collective-permute-done.4.rest_3_
  30.5 0.1 collective-permute-start.10
  30.6 0.5 %collective-permute-start.9 = (f32[3,32,256]{2,1,0:T(8,128)S(1)}, f32[3,32,256]{2,1,0:T(8,128)S(1)}, u32[]{:S(2)}, u32[]{:S(2)}) collective-permute-start(f32[3,32,256]{2,1,0:T(8,128)S(1)} %collective-permute-done.6.rest_0_), channel_id=1, source_target_pairs={{0,8},{8,0},{16,24},{24,16},{1,9},{9,1},{17,25},{25,17},{2,10},{10... | collective-permute-start | bytes 294920 | tf_op jit(solution)/shard_map/ppermute | solution.py:458
  31.1 0.0 collective-permute-done.11.rest_5_
  31.1 0.1 collective-permute-start.12
  31.2 1.2 %collective-permute-done.7.rest_2_ = f32[3,32,256]{2,1,0:T(8,128)S(1)} collective-permute-done((f32[3,32,256]{2,1,0:T(8,128)S(1)}, f32[3,32,256]{2,1,0:T(8,128)S(1)}, u32[]{:S(2)}, u32[]{:S(2)}) %collective-permute-start.7) | collective-permute-done | bytes 98336 | tf_op jit(solution)/shard_map/ppermute | solution.py:458
  32.4 0.0 collective-permute-start.8
  32.4 0.0 collective-permute-done.9.rest_1_
  32.4 0.0 collective-permute-done.10.rest_4_
  32.4 0.0 collective-permute-done.12.rest_6_
  32.4 1.0 %place.2 = (f32[1,256,256]{2,1,0:T(8,128)}, f32[1,256,256]{2,1,0:T(8,128)}, f32[1,256,256]{2,1,0:T(8,128)}) custom-call(f32[3,32,256]{2,1,0:T(8,128)S(1)} %collective-permute-done.6.rest_0_, f32[3,32,256]{2,1,0:T(8,128)S(1)} %collective-permute-done.9.rest_1_, f32[3,32,256]{2,1,0:T(8,128)S(1)} %collective-permute-done.7.rest_2_, ...), custom_call_target="tpu_custom_call" | custom-call | bytes 4128768 | tf_op jit(solution)/shard_map/place/pallas_call | solution.py:443
  33.4 0.2 collective-permute-done.8.rest_0_
  33.7 0.7 %place.3 = (f32[1,256,256]{2,1,0:T(8,128)}, f32[1,256,256]{2,1,0:T(8,128)}, f32[1,256,256]{2,1,0:T(8,128)}) custom-call(f32[3,32,256]{2,1,0:T(8,128)S(1)} %collective-permute-done.8.rest_0_, f32[1,256,256]{2,1,0:T(8,128)} %get-tuple-element.56.rest_1_, ...), custom_call_target="tpu_custom_call", output_to_operand_aliasing={{0}: (1, {}), {1}: (2, {}), {2}: (3, {})} | custom-call | bytes 589824 | tf_op jit(solution)/shard_map/place/pallas_call | solution.py:443
  (4 shorter events, 0.1 us)
Async XLA Ops:
  1.9 10.4 %collective-permute-start = (f32[168,256]{1,0:T(8,128)S(1)}, f32[168,256]{1,0:T(8,128)S(1)}, u32[]{:S(2)}, u32[]{:S(2)}) collective-permute-start(f32[168,256]{1,0:T(8,128)S(1)} %get-tuple-element.33), channel_id=1, source_target_pairs={{0,1},{1,2},{2,3},{3,4},{4,5},{5,6},{6,7},{7,0},{8,9},{9,10},{10,1... | collective-permute-start | bytes 516104 | tf_op jit(solution)/shard_map/ppermute | solution.py:463
  5.6 5.2 %copy-start = (f32[25,256]{1,0:T(8,128)S(1)}, f32[25,256]{1,0:T(8,128)}, u32[]{:S(2)}) copy-start(f32[25,256]{1,0:T(8,128)} %w_ref.3) | copy-start | bytes 76804
  13.2 1.5 %collective-permute-start.2 = (f32[3,2,32,256]{3,2,1,0:T(8,128)S(1)}, f32[3,2,32,256]{3,2,1,0:T(8,128)S(1)}, u32[]{:S(2)}, u32[]{:S(2)}) collective-permute-start(f32[3,2,32,256]{3,2,1,0:T(8,128)S(1)} %get-tuple-element.47), channel_id=1, source_target_pairs={{0,8},{8,0},{16,24},{24,16},{1,9},{9,1},{17,25},{25,17},{2,10},{10... | collective-permute-start | bytes 589832 | tf_op jit(solution)/shard_map/ppermute | solution.py:458
  13.2 4.3 %collective-permute-start.1 = (f32[3,2,32,256]{3,2,1,0:T(8,128)S(1)}, f32[3,2,32,256]{3,2,1,0:T(8,128)S(1)}, u32[]{:S(2)}, u32[]{:S(2)}) collective-permute-start(f32[3,2,32,256]{3,2,1,0:T(8,128)S(1)} %get-tuple-element.43), channel_id=1, source_target_pairs={{0,8},{8,0},{16,24},{24,16},{1,9},{9,1},{17,25},{25,17},{2,10},{10... | collective-permute-start | bytes 589832 | tf_op jit(solution)/shard_map/ppermute | solution.py:458
  14.7 4.9 %collective-permute-start.5 = (f32[3,1,32,256]{3,2,1,0:T(8,128)S(1)}, f32[3,1,32,256]{3,2,1,0:T(8,128)S(1)}, u32[]{:S(2)}, u32[]{:S(2)}) collective-permute-start(f32[3,1,32,256]{3,2,1,0:T(8,128)S(1)} %get-tuple-element.48.rest_0_), channel_id=1, source_target_pairs={{0,16},{8,24},{16,0},{24,8},{1,17},{9,25},{17,1},{25,9},{2,18},{10... | collective-permute-start | bytes 294920 | tf_op jit(solution)/shard_map/ppermute | solution.py:458
  17.6 4.8 %collective-permute-start.3 = (f32[3,1,32,256]{3,2,1,0:T(8,128)S(1)}, f32[3,1,32,256]{3,2,1,0:T(8,128)S(1)}, u32[]{:S(2)}, u32[]{:S(2)}) collective-permute-start(f32[3,1,32,256]{3,2,1,0:T(8,128)S(1)} %get-tuple-element.51), channel_id=1, source_target_pairs={{0,16},{8,24},{16,0},{24,8},{1,17},{9,25},{17,1},{25,9},{2,18},{10... | collective-permute-start | bytes 294920 | tf_op jit(solution)/shard_map/ppermute | solution.py:458
  19.6 7.8 %collective-permute-start.6 = (f32[3,32,256]{2,1,0:T(8,128)S(1)}, f32[3,32,256]{2,1,0:T(8,128)S(1)}, u32[]{:S(2)}, u32[]{:S(2)}) collective-permute-start(f32[3,32,256]{2,1,0:T(8,128)S(1)} %mean.3), channel_id=1, source_target_pairs={{0,7},{1,0},{2,1},{3,2},{4,3},{5,4},{6,5},{7,6},{8,15},{9,8},{10,9... | collective-permute-start | bytes 294920 | tf_op jit(solution)/shard_map/ppermute | solution.py:473
  22.4 8.1 %collective-permute-start.4 = (f32[3,32,256]{2,1,0:T(8,128)S(1)}, f32[3,32,256]{2,1,0:T(8,128)S(1)}, u32[]{:S(2)}, u32[]{:S(2)}) collective-permute-start(f32[3,32,256]{2,1,0:T(8,128)S(1)} %mean.2), channel_id=1, source_target_pairs={{0,7},{1,0},{2,1},{3,2},{4,3},{5,4},{6,5},{7,6},{8,15},{9,8},{10,9... | collective-permute-start | bytes 294920 | tf_op jit(solution)/shard_map/ppermute | solution.py:473
  25.3 5.8 %collective-permute-start.11 = (f32[3,32,256]{2,1,0:T(8,128)S(1)}, f32[3,32,256]{2,1,0:T(8,128)S(1)}, u32[]{:S(2)}, u32[]{:S(2)}) collective-permute-start(f32[3,32,256]{2,1,0:T(8,128)S(1)} %mean.2), channel_id=1, source_target_pairs={{0,23},{1,16},{2,17},{3,18},{4,19},{5,20},{6,21},{7,22},{8,31},{9,... | collective-permute-start | bytes 294920 | tf_op jit(solution)/shard_map/ppermute | solution.py:473
  27.4 4.9 %collective-permute-start.7 = (f32[3,32,256]{2,1,0:T(8,128)S(1)}, f32[3,32,256]{2,1,0:T(8,128)S(1)}, u32[]{:S(2)}, u32[]{:S(2)}) collective-permute-start(f32[3,32,256]{2,1,0:T(8,128)S(1)} %collective-permute-done.6.rest_0_), channel_id=1, source_target_pairs={{0,16},{8,24},{16,0},{24,8},{1,17},{9,25},{17,1},{25,9},{2,18},{10... | collective-permute-start | bytes 294920 | tf_op jit(solution)/shard_map/ppermute | solution.py:458
  30.5 1.9 %collective-permute-start.10 = (f32[3,32,256]{2,1,0:T(8,128)S(1)}, f32[3,32,256]{2,1,0:T(8,128)S(1)}, u32[]{:S(2)}, u32[]{:S(2)}) collective-permute-start(f32[3,32,256]{2,1,0:T(8,128)S(1)} %collective-permute-done.4.rest_3_), channel_id=1, source_target_pairs={{0,8},{8,0},{16,24},{24,16},{1,9},{9,1},{17,25},{25,17},{2,10},{10... | collective-permute-start | bytes 294920 | tf_op jit(solution)/shard_map/ppermute | solution.py:458
  30.6 1.8 %collective-permute-start.9 = (f32[3,32,256]{2,1,0:T(8,128)S(1)}, f32[3,32,256]{2,1,0:T(8,128)S(1)}, u32[]{:S(2)}, u32[]{:S(2)}) collective-permute-start(f32[3,32,256]{2,1,0:T(8,128)S(1)} %collective-permute-done.6.rest_0_), channel_id=1, source_target_pairs={{0,8},{8,0},{16,24},{24,16},{1,9},{9,1},{17,25},{25,17},{2,10},{10... | collective-permute-start | bytes 294920 | tf_op jit(solution)/shard_map/ppermute | solution.py:458
  31.1 1.3 %collective-permute-start.12 = (f32[3,32,256]{2,1,0:T(8,128)S(1)}, f32[3,32,256]{2,1,0:T(8,128)S(1)}, u32[]{:S(2)}, u32[]{:S(2)}) collective-permute-start(f32[3,32,256]{2,1,0:T(8,128)S(1)} %collective-permute-done.11.rest_5_), channel_id=1, source_target_pairs={{0,8},{8,0},{16,24},{24,16},{1,9},{9,1},{17,25},{25,17},{2,10},{10... | collective-permute-start | bytes 294920 | tf_op jit(solution)/shard_map/ppermute | solution.py:458
  32.4 1.3 %collective-permute-start.8 = (f32[3,32,256]{2,1,0:T(8,128)S(1)}, f32[3,32,256]{2,1,0:T(8,128)S(1)}, u32[]{:S(2)}, u32[]{:S(2)}) collective-permute-start(f32[3,32,256]{2,1,0:T(8,128)S(1)} %collective-permute-done.7.rest_2_), channel_id=1, source_target_pairs={{0,8},{8,0},{16,24},{24,16},{1,9},{9,1},{17,25},{25,17},{2,10},{10... | collective-permute-start | bytes 294920 | tf_op jit(solution)/shard_map/ppermute | solution.py:458

commit v14 on v10

--- a/solution.py
+++ b/solution.py
@@ -477,7 +477,7 @@
     count = lax.axis_size("grp")
     series = obs.shape[0]
     rows = rows_of(series, 1024)
-    third = max(series // rows // 3, 1) * rows
+    third = max(series // rows // 6, 1) * rows
     bits = mask_bits.T
 
     tail, turned, x, lead, lead_bits = prepare(x_blocks, obs, bits, factors, rows)

time: 34.1 us -> 34.3 us (level)
  waiting for transfers between devices: 4.49 us -> 4.86 us
    ppermute x9, waiting for transfers between devices: 3.79 us -> 4.17 us  [crossed(): lax.ppermute(value, 'grp', [(source, source ^ step) for source in range(c...]
  transfers between devices with their start and end apart: 13 -> 13, of which waited for: 6 -> 6; matrix products, arithmetic and copies ran while one was open for 0% -> 0% of each run, Pallas kernels for 31% -> 30%
where the time goes in v14:
time: 34.3 us; the launch traced here: 34.2 us
  starting transfers between devices  14.7 us (43%)
  Pallas kernels  13.2 us (38%)
  waiting for transfers between devices  4.86 us (14%)
  between operations  1.42 us (4%)
    ppermute x3, starting transfers between devices, delivered(): return lax.ppermute(value, ('grp', 'blk'), pairs)  7.33 us
    pallas_call x1, Pallas kernels, error_step(): pl.pallas_call(functools.partial(error_kernel, rows), out_shape=(jax.Shap...  4.84 us
    ppermute x9, starting transfers between devices, crossed(): lax.ppermute(value, 'grp', [(source, source ^ step) for source in range(c...  4.37 us
    ppermute x9, waiting for transfers between devices, crossed(): lax.ppermute(value, 'grp', [(source, source ^ step) for source in range(c...  4.17 us
    pallas_call x2, Pallas kernels, factor_step(): pl.pallas_call(functools.partial(factor_kernel, begin, rows, chunks), out...  3.19 us
    ppermute x1, starting transfers between devices, shifted(): lax.ppermute(value, 'blk', [(source, (source + steps) % count) for source...  3.02 us
    pallas_call x2, Pallas kernels, place(): pl.pallas_call(functools.partial(place_kernel, share, spots), out_shape=(...  1.69 us
    pallas_call x1, Pallas kernels, prepare(): pl.pallas_call(functools.partial(prepare_kernel, rows), out_shape=(jax.Sh...  1.39 us
  transfers between devices with their start and end apart: 13, of which 6 were waited for; matrix products, arithmetic and copies ran while one was open for 0% of the time, Pallas kernels for 30%

profile of v14, /device:TPU:0, one launch (start us, length us, event | category | flops | bytes accessed | tf_op | source)
XLA Modules:
  0.0 34.2 jit_solution(17414759099207538058)
XLA Ops:
  0.6 1.4 %prepare.1 = (f32[168,256]{1,0:T(8,128)S(1)}, f32[256,256]{1,0:T(8,128)S(1)}, f32[256,256]{1,0:T(8,128)S(1)}, bf16[1024,512]{1,0:T(8,128)(2,1)S(1)}, s32[32,1024]{1,0:T(8,128)S(1)}) custom-call(f32[1,256,256]{2,1,0:T(8,128)} %x_hbm.1, bf16[6144,256]{1,0:T(8,128)(2,1)} %obs_hbm.3, s32[32,6144]{1,0:T(8,128)} %bitcast.3, bf16[6144,256]{1,0:T(8,128)(2,1)} %f_hbm.3), custom_call_target="tpu_custom_call" | custom-call | bytes 3145728 | tf_op jit(solution)/shard_map/prepare/pallas_call | solution.py:90
  2.0 3.0 %collective-permute-start = (f32[168,256]{1,0:T(8,128)S(1)}, f32[168,256]{1,0:T(8,128)S(1)}, u32[]{:S(2)}, u32[]{:S(2)}) collective-permute-start(f32[168,256]{1,0:T(8,128)S(1)} %get-tuple-element.33), channel_id=1, source_target_pairs={{0,1},{1,2},{2,3},{3,4},{4,5},{5,6},{6,7},{7,0},{8,9},{9,10},{10,1... | collective-permute-start | bytes 516104 | tf_op jit(solution)/shard_map/ppermute | solution.py:463
  5.7 0.0 copy-start
  5.7 4.8 %errors.1 = (bf16[256,6144]{1,0:T(8,128)(2,1)S(1)}, bf16[5120,512]{1,0:T(8,128)(2,1)S(1)}, f32[256,256]{1,0:T(8,128)S(1)}) custom-call(bf16[6144,256]{1,0:T(8,128)(2,1)} %obs_hbm.3, s32[32,6144]{1,0:T(8,128)} %bitcast.4, bf16[6144,256]{1,0:T(8,128)(2,1)} %f_hbm.3, f32[256,256]{1,0:T(8,128)S(1)} %get-tuple-element.34.turned_ref, ...), custom_call_target="tpu_custom_call" | custom-call | flops 3221225472 | bytes 10223616 | tf_op jit(solution)/shard_map/errors/pallas_call | solution.py:184
  10.6 0.0 copy-done
  10.6 1.2 %regress.1 = (f32[256,256]{1,0:T(8,128)S(1)}, f32[256,256]{1,0:T(8,128)S(1)}, f32[256,256]{1,0:T(8,128)S(1)}) custom-call(f32[256,256]{1,0:T(8,128)S(1)} %get-tuple-element.34.turned_ref, f32[25,256]{1,0:T(8,128)S(1)} %copy-done, f32[256,256]{1,0:T(8,128)S(1)} %get-tuple-element.37.gd_ref, f32[1,256,256]{2,1,0:T(8,128)} %m_hbm.1, f32[1,256,256]{2,1,0:T(8,128)} %v_hbm.1), custom_call_target="tpu_custom_call" | custom-call | flops 6553600 | bytes 1572864 | tf_op jit(solution)/shard_map/regress/pallas_call | solution.py:281
  11.8 0.7 %collective-permute-done.halo_ref = f32[168,256]{1,0:T(8,128)S(1)} collective-permute-done((f32[168,256]{1,0:T(8,128)S(1)}, f32[168,256]{1,0:T(8,128)S(1)}, u32[]{:S(2)}, u32[]{:S(2)}) %collective-permute-start) | collective-permute-done | bytes 172064 | tf_op jit(solution)/shard_map/ppermute | solution.py:463
  12.5 0.8 %update.1 = (f32[3,2,32,256]{3,2,1,0:T(8,128)S(1)}, f32[3,2,32,256]{3,2,1,0:T(8,128)S(1)}, f32[3,2,32,256]{3,2,1,0:T(8,128)S(1)}, f32[3,2,32,256]{3,2,1,0:T(8,128)S(1)}) custom-call(s32[1,1]{1,0:T(1,128)} %bitcast.2.stratum_ref, f32[168,256]{1,0:T(8,128)S(1)} %collective-permute-done.halo_ref, f32[25,256]{1,0:T(8,128)S(1)} %copy-done, ...), custom_call_target="tpu_custom_call" | custom-call | flops 3932160 | bytes 2621440 | tf_op jit(solution)/shard_map/update/pallas_call | solution.py:361
  13.2 0.1 collective-permute-start.2
  13.3 0.5 %collective-permute-start.1 = (f32[3,2,32,256]{3,2,1,0:T(8,128)S(1)}, f32[3,2,32,256]{3,2,1,0:T(8,128)S(1)}, u32[]{:S(2)}, u32[]{:S(2)}) collective-permute-start(f32[3,2,32,256]{3,2,1,0:T(8,128)S(1)} %get-tuple-element.43), channel_id=1, source_target_pairs={{0,8},{8,0},{16,24},{24,16},{1,9},{9,1},{17,25},{25,17},{2,10},{10... | collective-permute-start | bytes 589832 | tf_op jit(solution)/shard_map/ppermute | solution.py:458
  13.8 0.9 %collective-permute-done.2.got_ref = f32[3,2,32,256]{3,2,1,0:T(8,128)S(1)} collective-permute-done((f32[3,2,32,256]{3,2,1,0:T(8,128)S(1)}, f32[3,2,32,256]{3,2,1,0:T(8,128)S(1)}, u32[]{:S(2)}, u32[]{:S(2)}) %collective-permute-start.2) | collective-permute-done | bytes 196640 | tf_op jit(solution)/shard_map/ppermute | solution.py:458
  14.8 1.6 %collective-permute-start.5 = (f32[3,1,32,256]{3,2,1,0:T(8,128)S(1)}, f32[3,1,32,256]{3,2,1,0:T(8,128)S(1)}, u32[]{:S(2)}, u32[]{:S(2)}) collective-permute-start(f32[3,1,32,256]{3,2,1,0:T(8,128)S(1)} %get-tuple-element.48.rest_0_), channel_id=1, source_target_pairs={{0,16},{8,24},{16,0},{24,8},{1,17},{9,25},{17,1},{25,9},{2,18},{10... | collective-permute-start | bytes 294920 | tf_op jit(solution)/shard_map/ppermute | solution.py:458
  16.3 1.2 %factors.2.rest_1_ = bf16[6144,256]{1,0:T(8,128)(2,1)} custom-call(bf16[1024,512]{1,0:T(8,128)(2,1)S(1)} %get-tuple-element.35.first_ref, bf16[5120,512]{1,0:T(8,128)(2,1)S(1)} %get-tuple-element.44.both_ref, bf16[256,6144]{1,0:T(8,128)(2,1)S(1)} %get-tuple-element.45.err_ref, f32[256,256]{1,0:T(8,128)S(1)} %get-tuple-element.34.turned_ref, ...), custom_call_target="tpu_custom_call" | custom-call | flops 134217728 | bytes 1572864 | tf_op jit(solution)/shard_map/factors/pallas_call | solution.py:238
  17.5 0.0 collective-permute-done.1.got_ref
  17.6 0.6 %collective-permute-start.3 = (f32[3,1,32,256]{3,2,1,0:T(8,128)S(1)}, f32[3,1,32,256]{3,2,1,0:T(8,128)S(1)}, u32[]{:S(2)}, u32[]{:S(2)}) collective-permute-start(f32[3,1,32,256]{3,2,1,0:T(8,128)S(1)} %get-tuple-element.51), channel_id=1, source_target_pairs={{0,16},{8,24},{16,0},{24,8},{1,17},{9,25},{17,1},{25,9},{2,18},{10... | collective-permute-start | bytes 294920 | tf_op jit(solution)/shard_map/ppermute | solution.py:458
  18.2 1.5 %collective-permute-done.5.got_ref = f32[3,1,32,256]{3,2,1,0:T(8,128)S(1)} collective-permute-done((f32[3,1,32,256]{3,2,1,0:T(8,128)S(1)}, f32[3,1,32,256]{3,2,1,0:T(8,128)S(1)}, u32[]{:S(2)}, u32[]{:S(2)}) %collective-permute-start.5) | collective-permute-done | bytes 98336 | tf_op jit(solution)/shard_map/ppermute | solution.py:458
  19.7 2.4 %collective-permute-start.6 = (f32[3,32,256]{2,1,0:T(8,128)S(1)}, f32[3,32,256]{2,1,0:T(8,128)S(1)}, u32[]{:S(2)}, u32[]{:S(2)}) collective-permute-start(f32[3,32,256]{2,1,0:T(8,128)S(1)} %mean.3), channel_id=1, source_target_pairs={{0,7},{1,0},{2,1},{3,2},{4,3},{5,4},{6,5},{7,6},{8,15},{9,8},{10,9... | collective-permute-start | bytes 294920 | tf_op jit(solution)/shard_map/ppermute | solution.py:473
  22.1 0.1 collective-permute-done.3.got_ref
  22.3 2.6 %collective-permute-start.4 = (f32[3,32,256]{2,1,0:T(8,128)S(1)}, f32[3,32,256]{2,1,0:T(8,128)S(1)}, u32[]{:S(2)}, u32[]{:S(2)}) collective-permute-start(f32[3,32,256]{2,1,0:T(8,128)S(1)} %mean.2), channel_id=1, source_target_pairs={{0,7},{1,0},{2,1},{3,2},{4,3},{5,4},{6,5},{7,6},{8,15},{9,8},{10,9... | collective-permute-start | bytes 294920 | tf_op jit(solution)/shard_map/ppermute | solution.py:473
  24.8 2.3 %collective-permute-start.11 = (f32[3,32,256]{2,1,0:T(8,128)S(1)}, f32[3,32,256]{2,1,0:T(8,128)S(1)}, u32[]{:S(2)}, u32[]{:S(2)}) collective-permute-start(f32[3,32,256]{2,1,0:T(8,128)S(1)} %mean.2), channel_id=1, source_target_pairs={{0,23},{1,16},{2,17},{3,18},{4,19},{5,20},{6,21},{7,22},{8,31},{9,... | collective-permute-start | bytes 294920 | tf_op jit(solution)/shard_map/ppermute | solution.py:473
  27.2 0.0 collective-permute-done.6.rest_0_
  27.2 1.0 %collective-permute-start.7 = (f32[3,32,256]{2,1,0:T(8,128)S(1)}, f32[3,32,256]{2,1,0:T(8,128)S(1)}, u32[]{:S(2)}, u32[]{:S(2)}) collective-permute-start(f32[3,32,256]{2,1,0:T(8,128)S(1)} %collective-permute-done.6.rest_0_), channel_id=1, source_target_pairs={{0,16},{8,24},{16,0},{24,8},{1,17},{9,25},{17,1},{25,9},{2,18},{10... | collective-permute-start | bytes 294920 | tf_op jit(solution)/shard_map/ppermute | solution.py:458
  28.2 2.0 %factors.3 = bf16[6144,256]{1,0:T(8,128)(2,1)} custom-call(bf16[1024,512]{1,0:T(8,128)(2,1)S(1)} %get-tuple-element.35.first_ref, bf16[5120,512]{1,0:T(8,128)(2,1)S(1)} %get-tuple-element.44.both_ref, bf16[256,6144]{1,0:T(8,128)(2,1)S(1)} %get-tuple-element.45.err_ref, f32[256,256]{1,0:T(8,128)S(1)} %get-tuple-element.34.turned_ref, ...), custom_call_target="tpu_custom_call", output_to_operand_aliasing={{}: (5, {})} | custom-call | flops 671088640 | bytes 7864320 | tf_op jit(solution)/shard_map/factors/pallas_call | solution.py:238
  30.2 0.0 collective-permute-done.4.rest_3_
  30.2 0.1 collective-permute-start.10
  30.3 0.5 %collective-permute-start.9 = (f32[3,32,256]{2,1,0:T(8,128)S(1)}, f32[3,32,256]{2,1,0:T(8,128)S(1)}, u32[]{:S(2)}, u32[]{:S(2)}) collective-permute-start(f32[3,32,256]{2,1,0:T(8,128)S(1)} %collective-permute-done.6.rest_0_), channel_id=1, source_target_pairs={{0,8},{8,0},{16,24},{24,16},{1,9},{9,1},{17,25},{25,17},{2,10},{10... | collective-permute-start | bytes 294920 | tf_op jit(solution)/shard_map/ppermute | solution.py:458
  30.8 0.0 collective-permute-done.11.rest_5_
  30.8 0.1 collective-permute-start.12
  30.9 1.3 %collective-permute-done.7.rest_2_ = f32[3,32,256]{2,1,0:T(8,128)S(1)} collective-permute-done((f32[3,32,256]{2,1,0:T(8,128)S(1)}, f32[3,32,256]{2,1,0:T(8,128)S(1)}, u32[]{:S(2)}, u32[]{:S(2)}) %collective-permute-start.7) | collective-permute-done | bytes 98336 | tf_op jit(solution)/shard_map/ppermute | solution.py:458
  32.2 0.0 collective-permute-start.8
  32.2 0.0 collective-permute-done.9.rest_1_
  32.2 0.0 collective-permute-done.10.rest_4_
  32.2 0.0 collective-permute-done.12.rest_6_
  32.2 1.0 %place.2 = (f32[1,256,256]{2,1,0:T(8,128)}, f32[1,256,256]{2,1,0:T(8,128)}, f32[1,256,256]{2,1,0:T(8,128)}) custom-call(f32[3,32,256]{2,1,0:T(8,128)S(1)} %collective-permute-done.6.rest_0_, f32[3,32,256]{2,1,0:T(8,128)S(1)} %collective-permute-done.9.rest_1_, f32[3,32,256]{2,1,0:T(8,128)S(1)} %collective-permute-done.7.rest_2_, ...), custom_call_target="tpu_custom_call" | custom-call | bytes 4128768 | tf_op jit(solution)/shard_map/place/pallas_call | solution.py:443
  33.3 0.2 collective-permute-done.8.rest_0_
  33.5 0.7 %place.3 = (f32[1,256,256]{2,1,0:T(8,128)}, f32[1,256,256]{2,1,0:T(8,128)}, f32[1,256,256]{2,1,0:T(8,128)}) custom-call(f32[3,32,256]{2,1,0:T(8,128)S(1)} %collective-permute-done.8.rest_0_, f32[1,256,256]{2,1,0:T(8,128)} %get-tuple-element.56.rest_1_, ...), custom_call_target="tpu_custom_call", output_to_operand_aliasing={{0}: (1, {}), {1}: (2, {}), {2}: (3, {})} | custom-call | bytes 589824 | tf_op jit(solution)/shard_map/place/pallas_call | solution.py:443
  (4 shorter events, 0.1 us)
Async XLA Ops:
  2.0 10.4 %collective-permute-start = (f32[168,256]{1,0:T(8,128)S(1)}, f32[168,256]{1,0:T(8,128)S(1)}, u32[]{:S(2)}, u32[]{:S(2)}) collective-permute-start(f32[168,256]{1,0:T(8,128)S(1)} %get-tuple-element.33), channel_id=1, source_target_pairs={{0,1},{1,2},{2,3},{3,4},{4,5},{5,6},{6,7},{7,0},{8,9},{9,10},{10,1... | collective-permute-start | bytes 516104 | tf_op jit(solution)/shard_map/ppermute | solution.py:463
  5.7 4.9 %copy-start = (f32[25,256]{1,0:T(8,128)S(1)}, f32[25,256]{1,0:T(8,128)}, u32[]{:S(2)}) copy-start(f32[25,256]{1,0:T(8,128)} %w_ref.3) | copy-start | bytes 76804
  13.2 1.5 %collective-permute-start.2 = (f32[3,2,32,256]{3,2,1,0:T(8,128)S(1)}, f32[3,2,32,256]{3,2,1,0:T(8,128)S(1)}, u32[]{:S(2)}, u32[]{:S(2)}) collective-permute-start(f32[3,2,32,256]{3,2,1,0:T(8,128)S(1)} %get-tuple-element.47), channel_id=1, source_target_pairs={{0,8},{8,0},{16,24},{24,16},{1,9},{9,1},{17,25},{25,17},{2,10},{10... | collective-permute-start | bytes 589832 | tf_op jit(solution)/shard_map/ppermute | solution.py:458
  13.3 4.2 %collective-permute-start.1 = (f32[3,2,32,256]{3,2,1,0:T(8,128)S(1)}, f32[3,2,32,256]{3,2,1,0:T(8,128)S(1)}, u32[]{:S(2)}, u32[]{:S(2)}) collective-permute-start(f32[3,2,32,256]{3,2,1,0:T(8,128)S(1)} %get-tuple-element.43), channel_id=1, source_target_pairs={{0,8},{8,0},{16,24},{24,16},{1,9},{9,1},{17,25},{25,17},{2,10},{10... | collective-permute-start | bytes 589832 | tf_op jit(solution)/shard_map/ppermute | solution.py:458
  14.8 4.9 %collective-permute-start.5 = (f32[3,1,32,256]{3,2,1,0:T(8,128)S(1)}, f32[3,1,32,256]{3,2,1,0:T(8,128)S(1)}, u32[]{:S(2)}, u32[]{:S(2)}) collective-permute-start(f32[3,1,32,256]{3,2,1,0:T(8,128)S(1)} %get-tuple-element.48.rest_0_), channel_id=1, source_target_pairs={{0,16},{8,24},{16,0},{24,8},{1,17},{9,25},{17,1},{25,9},{2,18},{10... | collective-permute-start | bytes 294920 | tf_op jit(solution)/shard_map/ppermute | solution.py:458
  17.6 4.7 %collective-permute-start.3 = (f32[3,1,32,256]{3,2,1,0:T(8,128)S(1)}, f32[3,1,32,256]{3,2,1,0:T(8,128)S(1)}, u32[]{:S(2)}, u32[]{:S(2)}) collective-permute-start(f32[3,1,32,256]{3,2,1,0:T(8,128)S(1)} %get-tuple-element.51), channel_id=1, source_target_pairs={{0,16},{8,24},{16,0},{24,8},{1,17},{9,25},{17,1},{25,9},{2,18},{10... | collective-permute-start | bytes 294920 | tf_op jit(solution)/shard_map/ppermute | solution.py:458
  19.7 7.5 %collective-permute-start.6 = (f32[3,32,256]{2,1,0:T(8,128)S(1)}, f32[3,32,256]{2,1,0:T(8,128)S(1)}, u32[]{:S(2)}, u32[]{:S(2)}) collective-permute-start(f32[3,32,256]{2,1,0:T(8,128)S(1)} %mean.3), channel_id=1, source_target_pairs={{0,7},{1,0},{2,1},{3,2},{4,3},{5,4},{6,5},{7,6},{8,15},{9,8},{10,9... | collective-permute-start | bytes 294920 | tf_op jit(solution)/shard_map/ppermute | solution.py:473
  22.3 7.9 %collective-permute-start.4 = (f32[3,32,256]{2,1,0:T(8,128)S(1)}, f32[3,32,256]{2,1,0:T(8,128)S(1)}, u32[]{:S(2)}, u32[]{:S(2)}) collective-permute-start(f32[3,32,256]{2,1,0:T(8,128)S(1)} %mean.2), channel_id=1, source_target_pairs={{0,7},{1,0},{2,1},{3,2},{4,3},{5,4},{6,5},{7,6},{8,15},{9,8},{10,9... | collective-permute-start | bytes 294920 | tf_op jit(solution)/shard_map/ppermute | solution.py:473
  24.8 6.0 %collective-permute-start.11 = (f32[3,32,256]{2,1,0:T(8,128)S(1)}, f32[3,32,256]{2,1,0:T(8,128)S(1)}, u32[]{:S(2)}, u32[]{:S(2)}) collective-permute-start(f32[3,32,256]{2,1,0:T(8,128)S(1)} %mean.2), channel_id=1, source_target_pairs={{0,23},{1,16},{2,17},{3,18},{4,19},{5,20},{6,21},{7,22},{8,31},{9,... | collective-permute-start | bytes 294920 | tf_op jit(solution)/shard_map/ppermute | solution.py:473
  27.2 5.0 %collective-permute-start.7 = (f32[3,32,256]{2,1,0:T(8,128)S(1)}, f32[3,32,256]{2,1,0:T(8,128)S(1)}, u32[]{:S(2)}, u32[]{:S(2)}) collective-permute-start(f32[3,32,256]{2,1,0:T(8,128)S(1)} %collective-permute-done.6.rest_0_), channel_id=1, source_target_pairs={{0,16},{8,24},{16,0},{24,8},{1,17},{9,25},{17,1},{25,9},{2,18},{10... | collective-permute-start | bytes 294920 | tf_op jit(solution)/shard_map/ppermute | solution.py:458
  30.2 2.0 %collective-permute-start.10 = (f32[3,32,256]{2,1,0:T(8,128)S(1)}, f32[3,32,256]{2,1,0:T(8,128)S(1)}, u32[]{:S(2)}, u32[]{:S(2)}) collective-permute-start(f32[3,32,256]{2,1,0:T(8,128)S(1)} %collective-permute-done.4.rest_3_), channel_id=1, source_target_pairs={{0,8},{8,0},{16,24},{24,16},{1,9},{9,1},{17,25},{25,17},{2,10},{10... | collective-permute-start | bytes 294920 | tf_op jit(solution)/shard_map/ppermute | solution.py:458
  30.3 1.9 %collective-permute-start.9 = (f32[3,32,256]{2,1,0:T(8,128)S(1)}, f32[3,32,256]{2,1,0:T(8,128)S(1)}, u32[]{:S(2)}, u32[]{:S(2)}) collective-permute-start(f32[3,32,256]{2,1,0:T(8,128)S(1)} %collective-permute-done.6.rest_0_), channel_id=1, source_target_pairs={{0,8},{8,0},{16,24},{24,16},{1,9},{9,1},{17,25},{25,17},{2,10},{10... | collective-permute-start | bytes 294920 | tf_op jit(solution)/shard_map/ppermute | solution.py:458
  30.8 1.4 %collective-permute-start.12 = (f32[3,32,256]{2,1,0:T(8,128)S(1)}, f32[3,32,256]{2,1,0:T(8,128)S(1)}, u32[]{:S(2)}, u32[]{:S(2)}) collective-permute-start(f32[3,32,256]{2,1,0:T(8,128)S(1)} %collective-permute-done.11.rest_5_), channel_id=1, source_target_pairs={{0,8},{8,0},{16,24},{24,16},{1,9},{9,1},{17,25},{25,17},{2,10},{10... | collective-permute-start | bytes 294920 | tf_op jit(solution)/shard_map/ppermute | solution.py:458
  32.2 1.3 %collective-permute-start.8 = (f32[3,32,256]{2,1,0:T(8,128)S(1)}, f32[3,32,256]{2,1,0:T(8,128)S(1)}, u32[]{:S(2)}, u32[]{:S(2)}) collective-permute-start(f32[3,32,256]{2,1,0:T(8,128)S(1)} %collective-permute-done.7.rest_2_), channel_id=1, source_target_pairs={{0,8},{8,0},{16,24},{24,16},{1,9},{9,1},{17,25},{25,17},{2,10},{10... | collective-permute-start | bytes 294920 | tf_op jit(solution)/shard_map/ppermute | solution.py:458

commit v15 on v10

--- a/solution.py
+++ b/solution.py
@@ -59,13 +59,13 @@
     width = both_ref.shape[1] - rank
     source, target = pl.ds(index * rows, rows), pl.ds(at, rows)
     return (
-        pltpu.make_async_copy(bits_hbm.at[:, source], bits_ref.at[:, target], sems.at[0]),
         pltpu.make_async_copy(
             f_hbm.at[source, :], both_ref.at[target, pl.ds(0, rank)], sems.at[1]
         ),
         pltpu.make_async_copy(
             obs_hbm.at[source, :], both_ref.at[target, pl.ds(rank, width)], sems.at[2]
         ),
+        pltpu.make_async_copy(bits_hbm.at[:, source], bits_ref.at[:, target], sems.at[0]),
     )
 
 
@@ -149,7 +149,7 @@
 
     def compare(index):
         if index > 0:
-            for copy in copies(index):
+            for copy in copies(index)[:2]:
                 copy.wait()
         return lax.dot_general(
             weights, pair(index)[0], (((1,), (1,)), ((), ())), preferred_element_type=F32
@@ -157,6 +157,8 @@
 
     def settle(index, gap):
         part = pl.ds(index * rows, rows)
+        if index > 0:
+            copies(index)[2].wait()
         both, bits = pair(index)
         seen = jnp.bitwise_and(bits[:, None, :], flag) != 0
         error = jnp.where(seen, gap.reshape(words, per, rows), 0.0).reshape(width, rows)

time: 34.1 us -> 35.4 us (1.038)
  Pallas kernels: 13.3 us -> 14.6 us
  waiting for transfers between devices: 4.49 us -> 3.38 us
  starting transfers between devices: 14.7 us -> 15.8 us
    pallas_call x1, Pallas kernels: 4.84 us -> 6.08 us  [error_step(): pl.pallas_call(functools.partial(error_kernel, rows), out_shape=(jax.Shap...]
    ppermute x3, starting transfers between devices: 7.03 us -> 8.12 us  [delivered(): return lax.ppermute(value, ('grp', 'blk'), pairs)]
    ppermute x1, waiting for transfers between devices: 0.69 us -> 0.01 us  [shifted(): lax.ppermute(value, 'blk', [(source, (source + steps) % count) for source...]
    ppermute x9, waiting for transfers between devices: 3.79 us -> 3.37 us  [crossed(): lax.ppermute(value, 'grp', [(source, source ^ step) for source in range(c...]
  transfers between devices with their start and end apart: 13 -> 13, of which waited for: 6 -> 4; matrix products, arithmetic and copies ran while one was open for 0% -> 0% of each run, Pallas kernels for 31% -> 33%
where the time goes in v15:
time: 35.4 us; the launch traced here: 35.2 us
  starting transfers between devices  15.8 us (45%)
  Pallas kernels  14.6 us (41%)
  waiting for transfers between devices  3.38 us (10%)
  between operations  1.42 us (4%)
    ppermute x3, starting transfers between devices, delivered(): return lax.ppermute(value, ('grp', 'blk'), pairs)  8.12 us
    pallas_call x1, Pallas kernels, error_step(): pl.pallas_call(functools.partial(error_kernel, rows), out_shape=(jax.Shap...  6.08 us
    ppermute x9, starting transfers between devices, crossed(): lax.ppermute(value, 'grp', [(source, source ^ step) for source in range(c...  4.67 us
    ppermute x9, waiting for transfers between devices, crossed(): lax.ppermute(value, 'grp', [(source, source ^ step) for source in range(c...  3.37 us
    pallas_call x2, Pallas kernels, factor_step(): pl.pallas_call(functools.partial(factor_kernel, begin, rows, chunks), out...  3.31 us
    ppermute x1, starting transfers between devices, shifted(): lax.ppermute(value, 'blk', [(source, (source + steps) % count) for source...  3.02 us
    pallas_call x2, Pallas kernels, place(): pl.pallas_call(functools.partial(place_kernel, share, spots), out_shape=(...  1.69 us
    pallas_call x1, Pallas kernels, prepare(): pl.pallas_call(functools.partial(prepare_kernel, rows), out_shape=(jax.Sh...  1.44 us
  transfers between devices with their start and end apart: 13, of which 4 were waited for; matrix products, arithmetic and copies ran while one was open for 0% of the time, Pallas kernels for 33%

profile of v15, /device:TPU:0, one launch (start us, length us, event | category | flops | bytes accessed | tf_op | source)
XLA Modules:
  0.0 35.2 jit_solution(17551541440421699160)
XLA Ops:
  0.6 1.4 %prepare.1 = (f32[168,256]{1,0:T(8,128)S(1)}, f32[256,256]{1,0:T(8,128)S(1)}, f32[256,256]{1,0:T(8,128)S(1)}, bf16[1024,512]{1,0:T(8,128)(2,1)S(1)}, s32[32,1024]{1,0:T(8,128)S(1)}) custom-call(f32[1,256,256]{2,1,0:T(8,128)} %x_hbm.1, bf16[6144,256]{1,0:T(8,128)(2,1)} %obs_hbm.3, s32[32,6144]{1,0:T(8,128)} %bitcast.3, bf16[6144,256]{1,0:T(8,128)(2,1)} %f_hbm.3), custom_call_target="tpu_custom_call" | custom-call | bytes 3145728 | tf_op jit(solution)/shard_map/prepare/pallas_call | solution.py:90
  2.1 3.0 %collective-permute-start = (f32[168,256]{1,0:T(8,128)S(1)}, f32[168,256]{1,0:T(8,128)S(1)}, u32[]{:S(2)}, u32[]{:S(2)}) collective-permute-start(f32[168,256]{1,0:T(8,128)S(1)} %get-tuple-element.33), channel_id=1, source_target_pairs={{0,1},{1,2},{2,3},{3,4},{4,5},{5,6},{6,7},{7,0},{8,9},{9,10},{10,1... | collective-permute-start | bytes 516104 | tf_op jit(solution)/shard_map/ppermute | solution.py:465
  5.8 0.0 copy-start
  5.8 6.1 %errors.1 = (bf16[256,6144]{1,0:T(8,128)(2,1)S(1)}, bf16[5120,512]{1,0:T(8,128)(2,1)S(1)}, f32[256,256]{1,0:T(8,128)S(1)}) custom-call(bf16[6144,256]{1,0:T(8,128)(2,1)} %obs_hbm.3, s32[32,6144]{1,0:T(8,128)} %bitcast.4, bf16[6144,256]{1,0:T(8,128)(2,1)} %f_hbm.3, f32[256,256]{1,0:T(8,128)S(1)} %get-tuple-element.34.turned_ref, ...), custom_call_target="tpu_custom_call" | custom-call | flops 3221225472 | bytes 10223616 | tf_op jit(solution)/shard_map/errors/pallas_call | solution.py:186
  11.8 0.0 copy-done
  11.9 1.2 %regress.1 = (f32[256,256]{1,0:T(8,128)S(1)}, f32[256,256]{1,0:T(8,128)S(1)}, f32[256,256]{1,0:T(8,128)S(1)}) custom-call(f32[256,256]{1,0:T(8,128)S(1)} %get-tuple-element.34.turned_ref, f32[25,256]{1,0:T(8,128)S(1)} %copy-done, f32[256,256]{1,0:T(8,128)S(1)} %get-tuple-element.37.gd_ref, f32[1,256,256]{2,1,0:T(8,128)} %m_hbm.1, f32[1,256,256]{2,1,0:T(8,128)} %v_hbm.1), custom_call_target="tpu_custom_call" | custom-call | flops 6553600 | bytes 1572864 | tf_op jit(solution)/shard_map/regress/pallas_call | solution.py:283
  13.1 0.0 collective-permute-done.halo_ref
  13.1 0.8 %update.1 = (f32[3,2,32,256]{3,2,1,0:T(8,128)S(1)}, f32[3,2,32,256]{3,2,1,0:T(8,128)S(1)}, f32[3,2,32,256]{3,2,1,0:T(8,128)S(1)}, f32[3,2,32,256]{3,2,1,0:T(8,128)S(1)}) custom-call(s32[1,1]{1,0:T(1,128)} %bitcast.2.stratum_ref, f32[168,256]{1,0:T(8,128)S(1)} %collective-permute-done.halo_ref, f32[25,256]{1,0:T(8,128)S(1)} %copy-done, ...), custom_call_target="tpu_custom_call" | custom-call | flops 3932160 | bytes 2621440 | tf_op jit(solution)/shard_map/update/pallas_call | solution.py:363
  13.9 0.1 collective-permute-start.2
  13.9 0.5 %collective-permute-start.1 = (f32[3,2,32,256]{3,2,1,0:T(8,128)S(1)}, f32[3,2,32,256]{3,2,1,0:T(8,128)S(1)}, u32[]{:S(2)}, u32[]{:S(2)}) collective-permute-start(f32[3,2,32,256]{3,2,1,0:T(8,128)S(1)} %get-tuple-element.43), channel_id=1, source_target_pairs={{0,8},{8,0},{16,24},{24,16},{1,9},{9,1},{17,25},{25,17},{2,10},{10... | collective-permute-start | bytes 589832 | tf_op jit(solution)/shard_map/ppermute | solution.py:460
  14.4 0.9 %collective-permute-done.2.got_ref = f32[3,2,32,256]{3,2,1,0:T(8,128)S(1)} collective-permute-done((f32[3,2,32,256]{3,2,1,0:T(8,128)S(1)}, f32[3,2,32,256]{3,2,1,0:T(8,128)S(1)}, u32[]{:S(2)}, u32[]{:S(2)}) %collective-permute-start.2) | collective-permute-done | bytes 196640 | tf_op jit(solution)/shard_map/ppermute | solution.py:460
  15.4 1.6 %collective-permute-start.5 = (f32[3,1,32,256]{3,2,1,0:T(8,128)S(1)}, f32[3,1,32,256]{3,2,1,0:T(8,128)S(1)}, u32[]{:S(2)}, u32[]{:S(2)}) collective-permute-start(f32[3,1,32,256]{3,2,1,0:T(8,128)S(1)} %get-tuple-element.48.rest_0_), channel_id=1, source_target_pairs={{0,16},{8,24},{16,0},{24,8},{1,17},{9,25},{17,1},{25,9},{2,18},{10... | collective-permute-start | bytes 294920 | tf_op jit(solution)/shard_map/ppermute | solution.py:460
  16.9 1.5 %factors.2.rest_1_ = bf16[6144,256]{1,0:T(8,128)(2,1)} custom-call(bf16[1024,512]{1,0:T(8,128)(2,1)S(1)} %get-tuple-element.35.first_ref, bf16[5120,512]{1,0:T(8,128)(2,1)S(1)} %get-tuple-element.44.both_ref, bf16[256,6144]{1,0:T(8,128)(2,1)S(1)} %get-tuple-element.45.err_ref, f32[256,256]{1,0:T(8,128)S(1)} %get-tuple-element.34.turned_ref, ...), custom_call_target="tpu_custom_call" | custom-call | flops 268435456 | bytes 3145728 | tf_op jit(solution)/shard_map/factors/pallas_call | solution.py:240
  18.4 0.0 collective-permute-done.1.got_ref
  18.5 0.6 %collective-permute-start.3 = (f32[3,1,32,256]{3,2,1,0:T(8,128)S(1)}, f32[3,1,32,256]{3,2,1,0:T(8,128)S(1)}, u32[]{:S(2)}, u32[]{:S(2)}) collective-permute-start(f32[3,1,32,256]{3,2,1,0:T(8,128)S(1)} %get-tuple-element.51), channel_id=1, source_target_pairs={{0,16},{8,24},{16,0},{24,8},{1,17},{9,25},{17,1},{25,9},{2,18},{10... | collective-permute-start | bytes 294920 | tf_op jit(solution)/shard_map/ppermute | solution.py:460
  19.1 1.2 %collective-permute-done.5.got_ref = f32[3,1,32,256]{3,2,1,0:T(8,128)S(1)} collective-permute-done((f32[3,1,32,256]{3,2,1,0:T(8,128)S(1)}, f32[3,1,32,256]{3,2,1,0:T(8,128)S(1)}, u32[]{:S(2)}, u32[]{:S(2)}) %collective-permute-start.5) | collective-permute-done | bytes 98336 | tf_op jit(solution)/shard_map/ppermute | solution.py:460
  20.3 3.1 %collective-permute-start.6 = (f32[3,32,256]{2,1,0:T(8,128)S(1)}, f32[3,32,256]{2,1,0:T(8,128)S(1)}, u32[]{:S(2)}, u32[]{:S(2)}) collective-permute-start(f32[3,32,256]{2,1,0:T(8,128)S(1)} %mean.3), channel_id=1, source_target_pairs={{0,7},{1,0},{2,1},{3,2},{4,3},{5,4},{6,5},{7,6},{8,15},{9,8},{10,9... | collective-permute-start | bytes 294920 | tf_op jit(solution)/shard_map/ppermute | solution.py:475
  23.4 0.0 collective-permute-done.3.got_ref
  23.4 3.0 %collective-permute-start.4 = (f32[3,32,256]{2,1,0:T(8,128)S(1)}, f32[3,32,256]{2,1,0:T(8,128)S(1)}, u32[]{:S(2)}, u32[]{:S(2)}) collective-permute-start(f32[3,32,256]{2,1,0:T(8,128)S(1)} %mean.2), channel_id=1, source_target_pairs={{0,7},{1,0},{2,1},{3,2},{4,3},{5,4},{6,5},{7,6},{8,15},{9,8},{10,9... | collective-permute-start | bytes 294920 | tf_op jit(solution)/shard_map/ppermute | solution.py:475
  26.4 2.0 %collective-permute-start.11 = (f32[3,32,256]{2,1,0:T(8,128)S(1)}, f32[3,32,256]{2,1,0:T(8,128)S(1)}, u32[]{:S(2)}, u32[]{:S(2)}) collective-permute-start(f32[3,32,256]{2,1,0:T(8,128)S(1)} %mean.2), channel_id=1, source_target_pairs={{0,23},{1,16},{2,17},{3,18},{4,19},{5,20},{6,21},{7,22},{8,31},{9,... | collective-permute-start | bytes 294920 | tf_op jit(solution)/shard_map/ppermute | solution.py:475
  28.5 0.0 collective-permute-done.6.rest_0_
  28.5 1.3 %collective-permute-start.7 = (f32[3,32,256]{2,1,0:T(8,128)S(1)}, f32[3,32,256]{2,1,0:T(8,128)S(1)}, u32[]{:S(2)}, u32[]{:S(2)}) collective-permute-start(f32[3,32,256]{2,1,0:T(8,128)S(1)} %collective-permute-done.6.rest_0_), channel_id=1, source_target_pairs={{0,16},{8,24},{16,0},{24,8},{1,17},{9,25},{17,1},{25,9},{2,18},{10... | collective-permute-start | bytes 294920 | tf_op jit(solution)/shard_map/ppermute | solution.py:460
  29.7 1.9 %factors.3 = bf16[6144,256]{1,0:T(8,128)(2,1)} custom-call(bf16[1024,512]{1,0:T(8,128)(2,1)S(1)} %get-tuple-element.35.first_ref, bf16[5120,512]{1,0:T(8,128)(2,1)S(1)} %get-tuple-element.44.both_ref, bf16[256,6144]{1,0:T(8,128)(2,1)S(1)} %get-tuple-element.45.err_ref, f32[256,256]{1,0:T(8,128)S(1)} %get-tuple-element.34.turned_ref, ...), custom_call_target="tpu_custom_call", output_to_operand_aliasing={{}: (5, {})} | custom-call | flops 536870912 | bytes 6291456 | tf_op jit(solution)/shard_map/factors/pallas_call | solution.py:240
  31.6 0.0 collective-permute-done.4.rest_3_
  31.6 0.1 collective-permute-start.10
  31.7 0.5 %collective-permute-start.9 = (f32[3,32,256]{2,1,0:T(8,128)S(1)}, f32[3,32,256]{2,1,0:T(8,128)S(1)}, u32[]{:S(2)}, u32[]{:S(2)}) collective-permute-start(f32[3,32,256]{2,1,0:T(8,128)S(1)} %collective-permute-done.6.rest_0_), channel_id=1, source_target_pairs={{0,8},{8,0},{16,24},{24,16},{1,9},{9,1},{17,25},{25,17},{2,10},{10... | collective-permute-start | bytes 294920 | tf_op jit(solution)/shard_map/ppermute | solution.py:460
  32.2 0.0 collective-permute-done.11.rest_5_
  32.2 0.1 collective-permute-start.12
  32.3 0.9 %collective-permute-done.7.rest_2_ = f32[3,32,256]{2,1,0:T(8,128)S(1)} collective-permute-done((f32[3,32,256]{2,1,0:T(8,128)S(1)}, f32[3,32,256]{2,1,0:T(8,128)S(1)}, u32[]{:S(2)}, u32[]{:S(2)}) %collective-permute-start.7) | collective-permute-done | bytes 98336 | tf_op jit(solution)/shard_map/ppermute | solution.py:460
  33.2 0.0 collective-permute-start.8
  33.2 0.0 collective-permute-done.9.rest_1_
  33.2 0.0 collective-permute-done.10.rest_4_
  33.2 0.3 collective-permute-done.12.rest_6_
  33.5 1.0 %place.2 = (f32[1,256,256]{2,1,0:T(8,128)}, f32[1,256,256]{2,1,0:T(8,128)}, f32[1,256,256]{2,1,0:T(8,128)}) custom-call(f32[3,32,256]{2,1,0:T(8,128)S(1)} %collective-permute-done.6.rest_0_, f32[3,32,256]{2,1,0:T(8,128)S(1)} %collective-permute-done.9.rest_1_, f32[3,32,256]{2,1,0:T(8,128)S(1)} %collective-permute-done.7.rest_2_, ...), custom_call_target="tpu_custom_call" | custom-call | bytes 4128768 | tf_op jit(solution)/shard_map/place/pallas_call | solution.py:445
  34.5 0.0 collective-permute-done.8.rest_0_
  34.5 0.7 %place.3 = (f32[1,256,256]{2,1,0:T(8,128)}, f32[1,256,256]{2,1,0:T(8,128)}, f32[1,256,256]{2,1,0:T(8,128)}) custom-call(f32[3,32,256]{2,1,0:T(8,128)S(1)} %collective-permute-done.8.rest_0_, f32[1,256,256]{2,1,0:T(8,128)} %get-tuple-element.56.rest_1_, ...), custom_call_target="tpu_custom_call", output_to_operand_aliasing={{0}: (1, {}), {1}: (2, {}), {2}: (3, {})} | custom-call | bytes 589824 | tf_op jit(solution)/shard_map/place/pallas_call | solution.py:445
  (4 shorter events, 0.1 us)
Async XLA Ops:
  2.1 11.0 %collective-permute-start = (f32[168,256]{1,0:T(8,128)S(1)}, f32[168,256]{1,0:T(8,128)S(1)}, u32[]{:S(2)}, u32[]{:S(2)}) collective-permute-start(f32[168,256]{1,0:T(8,128)S(1)} %get-tuple-element.33), channel_id=1, source_target_pairs={{0,1},{1,2},{2,3},{3,4},{4,5},{5,6},{6,7},{7,0},{8,9},{9,10},{10,1... | collective-permute-start | bytes 516104 | tf_op jit(solution)/shard_map/ppermute | solution.py:465
  5.8 6.1 %copy-start = (f32[25,256]{1,0:T(8,128)S(1)}, f32[25,256]{1,0:T(8,128)}, u32[]{:S(2)}) copy-start(f32[25,256]{1,0:T(8,128)} %w_ref.3) | copy-start | bytes 76804
  13.9 1.5 %collective-permute-start.2 = (f32[3,2,32,256]{3,2,1,0:T(8,128)S(1)}, f32[3,2,32,256]{3,2,1,0:T(8,128)S(1)}, u32[]{:S(2)}, u32[]{:S(2)}) collective-permute-start(f32[3,2,32,256]{3,2,1,0:T(8,128)S(1)} %get-tuple-element.47), channel_id=1, source_target_pairs={{0,8},{8,0},{16,24},{24,16},{1,9},{9,1},{17,25},{25,17},{2,10},{10... | collective-permute-start | bytes 589832 | tf_op jit(solution)/shard_map/ppermute | solution.py:460
  13.9 4.5 %collective-permute-start.1 = (f32[3,2,32,256]{3,2,1,0:T(8,128)S(1)}, f32[3,2,32,256]{3,2,1,0:T(8,128)S(1)}, u32[]{:S(2)}, u32[]{:S(2)}) collective-permute-start(f32[3,2,32,256]{3,2,1,0:T(8,128)S(1)} %get-tuple-element.43), channel_id=1, source_target_pairs={{0,8},{8,0},{16,24},{24,16},{1,9},{9,1},{17,25},{25,17},{2,10},{10... | collective-permute-start | bytes 589832 | tf_op jit(solution)/shard_map/ppermute | solution.py:460
  15.4 4.9 %collective-permute-start.5 = (f32[3,1,32,256]{3,2,1,0:T(8,128)S(1)}, f32[3,1,32,256]{3,2,1,0:T(8,128)S(1)}, u32[]{:S(2)}, u32[]{:S(2)}) collective-permute-start(f32[3,1,32,256]{3,2,1,0:T(8,128)S(1)} %get-tuple-element.48.rest_0_), channel_id=1, source_target_pairs={{0,16},{8,24},{16,0},{24,8},{1,17},{9,25},{17,1},{25,9},{2,18},{10... | collective-permute-start | bytes 294920 | tf_op jit(solution)/shard_map/ppermute | solution.py:460
  18.5 4.9 %collective-permute-start.3 = (f32[3,1,32,256]{3,2,1,0:T(8,128)S(1)}, f32[3,1,32,256]{3,2,1,0:T(8,128)S(1)}, u32[]{:S(2)}, u32[]{:S(2)}) collective-permute-start(f32[3,1,32,256]{3,2,1,0:T(8,128)S(1)} %get-tuple-element.51), channel_id=1, source_target_pairs={{0,16},{8,24},{16,0},{24,8},{1,17},{9,25},{17,1},{25,9},{2,18},{10... | collective-permute-start | bytes 294920 | tf_op jit(solution)/shard_map/ppermute | solution.py:460
  20.3 8.1 %collective-permute-start.6 = (f32[3,32,256]{2,1,0:T(8,128)S(1)}, f32[3,32,256]{2,1,0:T(8,128)S(1)}, u32[]{:S(2)}, u32[]{:S(2)}) collective-permute-start(f32[3,32,256]{2,1,0:T(8,128)S(1)} %mean.3), channel_id=1, source_target_pairs={{0,7},{1,0},{2,1},{3,2},{4,3},{5,4},{6,5},{7,6},{8,15},{9,8},{10,9... | collective-permute-start | bytes 294920 | tf_op jit(solution)/shard_map/ppermute | solution.py:475
  23.4 8.2 %collective-permute-start.4 = (f32[3,32,256]{2,1,0:T(8,128)S(1)}, f32[3,32,256]{2,1,0:T(8,128)S(1)}, u32[]{:S(2)}, u32[]{:S(2)}) collective-permute-start(f32[3,32,256]{2,1,0:T(8,128)S(1)} %mean.2), channel_id=1, source_target_pairs={{0,7},{1,0},{2,1},{3,2},{4,3},{5,4},{6,5},{7,6},{8,15},{9,8},{10,9... | collective-permute-start | bytes 294920 | tf_op jit(solution)/shard_map/ppermute | solution.py:475
  26.4 5.8 %collective-permute-start.11 = (f32[3,32,256]{2,1,0:T(8,128)S(1)}, f32[3,32,256]{2,1,0:T(8,128)S(1)}, u32[]{:S(2)}, u32[]{:S(2)}) collective-permute-start(f32[3,32,256]{2,1,0:T(8,128)S(1)} %mean.2), channel_id=1, source_target_pairs={{0,23},{1,16},{2,17},{3,18},{4,19},{5,20},{6,21},{7,22},{8,31},{9,... | collective-permute-start | bytes 294920 | tf_op jit(solution)/shard_map/ppermute | solution.py:475
  28.5 4.8 %collective-permute-start.7 = (f32[3,32,256]{2,1,0:T(8,128)S(1)}, f32[3,32,256]{2,1,0:T(8,128)S(1)}, u32[]{:S(2)}, u32[]{:S(2)}) collective-permute-start(f32[3,32,256]{2,1,0:T(8,128)S(1)} %collective-permute-done.6.rest_0_), channel_id=1, source_target_pairs={{0,16},{8,24},{16,0},{24,8},{1,17},{9,25},{17,1},{25,9},{2,18},{10... | collective-permute-start | bytes 294920 | tf_op jit(solution)/shard_map/ppermute | solution.py:460
  31.6 1.6 %collective-permute-start.10 = (f32[3,32,256]{2,1,0:T(8,128)S(1)}, f32[3,32,256]{2,1,0:T(8,128)S(1)}, u32[]{:S(2)}, u32[]{:S(2)}) collective-permute-start(f32[3,32,256]{2,1,0:T(8,128)S(1)} %collective-permute-done.4.rest_3_), channel_id=1, source_target_pairs={{0,8},{8,0},{16,24},{24,16},{1,9},{9,1},{17,25},{25,17},{2,10},{10... | collective-permute-start | bytes 294920 | tf_op jit(solution)/shard_map/ppermute | solution.py:460
  31.7 1.5 %collective-permute-start.9 = (f32[3,32,256]{2,1,0:T(8,128)S(1)}, f32[3,32,256]{2,1,0:T(8,128)S(1)}, u32[]{:S(2)}, u32[]{:S(2)}) collective-permute-start(f32[3,32,256]{2,1,0:T(8,128)S(1)} %collective-permute-done.6.rest_0_), channel_id=1, source_target_pairs={{0,8},{8,0},{16,24},{24,16},{1,9},{9,1},{17,25},{25,17},{2,10},{10... | collective-permute-start | bytes 294920 | tf_op jit(solution)/shard_map/ppermute | solution.py:460
  32.2 1.3 %collective-permute-start.12 = (f32[3,32,256]{2,1,0:T(8,128)S(1)}, f32[3,32,256]{2,1,0:T(8,128)S(1)}, u32[]{:S(2)}, u32[]{:S(2)}) collective-permute-start(f32[3,32,256]{2,1,0:T(8,128)S(1)} %collective-permute-done.11.rest_5_), channel_id=1, source_target_pairs={{0,8},{8,0},{16,24},{24,16},{1,9},{9,1},{17,25},{25,17},{2,10},{10... | collective-permute-start | bytes 294920 | tf_op jit(solution)/shard_map/ppermute | solution.py:460
  33.2 1.3 %collective-permute-start.8 = (f32[3,32,256]{2,1,0:T(8,128)S(1)}, f32[3,32,256]{2,1,0:T(8,128)S(1)}, u32[]{:S(2)}, u32[]{:S(2)}) collective-permute-start(f32[3,32,256]{2,1,0:T(8,128)S(1)} %collective-permute-done.7.rest_2_), channel_id=1, source_target_pairs={{0,8},{8,0},{16,24},{24,16},{1,9},{9,1},{17,25},{25,17},{2,10},{10... | collective-permute-start | bytes 294920 | tf_op jit(solution)/shard_map/ppermute | solution.py:460
